TPU v7x, 256 devices: a whole 4x4x8 slice. The times are simulated.
256 devices in a mesh: seq: 64 (over y, z, core), head: 4 (over x).
Axes of the slice: x: 4, y: 4, z: 8, core: 2. Of those that a mesh axis runs over, the one named last changes fastest.
Arguments:
- query_vectors: float32 [16384, 2048], P('seq', 'head'), may hold values from -8 to 8
- key_vectors: float32 [16384, 2048], P('seq', 'head'), may hold values from -4 to 4
- value_vectors: float32 [16384, 2048], P('seq', 'head'), may hold values from -24 to 24
- norm_gain: float32 [2048], P('head'), may hold values from 0.5 to 1.5
- upstream: float32 [16384, 2048], P('seq', 'head'), may hold values from -6 to 6
Outputs:
- attended: float32 [16384, 2048], P('seq', 'head')
- query_grad: float32 [16384, 2048], P('seq', 'head')
- key_grad: float32 [16384, 2048], P('seq', 'head')
- value_grad: float32 [16384, 2048], P('seq', 'head')
All inputs are finite; a program needn't handle non-finite values.
Results may differ from a plain program's by a relative error of at most 0.0012.
Values sent between devices are 32-bit elements; how exact they have to be, the bound alone decides.
No kernel may reach another device: no remote copies, remote signals or barrier semaphores. Data moves between devices by JAX's collectives and lax.ppermute only.
A program may use at most 64 MiB of HBM per device.

v0:
```python
import math

import jax
import jax.numpy as jnp
import numpy as np
from jax import lax
from jax.experimental import pallas as pl
from jax.experimental.pallas import tpu as pltpu
from jax.sharding import PartitionSpec as P

DHEAD = 128
BLOCK = 256
FEAT = 2048
HEADS = 4
WIDTH = HEADS * DHEAD
NEGATIVE_FILL = -1e30
FLOOR = -1e25
EPSILON = 1e-06
INV_ROOT = 1.0 / math.sqrt(DHEAD)
LN4 = math.log(4.0)
VMEM_BYTES = 48 * 1024 * 1024

OWN = 96
LEVEL_ROWS = ((0, 64), (64, 80), (80, 84))
FAR = 512
KV = 2 * WIDTH
GRAD = 2 * WIDTH + DHEAD

QUAD = (4, 8, 12)
HALF2_BLOCKS = QUAD + tuple(2 ^ o for o in QUAD)
HALF3_BLOCKS = (0,) + QUAD + tuple(2 ^ o for o in (0,) + QUAD)
YZ3_BLOCKS = tuple(y ^ o for y in (16, 32, 48) for o in HALF3_BLOCKS)
SLOTS = (
    ((2, 3), 64),
    (HALF2_BLOCKS + tuple(1 ^ o for o in HALF2_BLOCKS), 16),
    (YZ3_BLOCKS + tuple(1 ^ o for o in YZ3_BLOCKS), 4),
)


def slot_table():
    offset = np.concatenate([np.repeat(np.array(blocks, np.int32), rows) for blocks, rows in SLOTS])
    level = np.concatenate([np.full(len(blocks) * rows, n + 1, np.int32) for n, (blocks, rows) in enumerate(SLOTS)])
    own = np.zeros(OWN, np.int32)
    for n, (start, stop) in enumerate(LEVEL_ROWS):
        own[start:stop] = n + 1
    return offset[None, :], level[None, :], own[:, None]


def split3(x):
    high = x.astype(jnp.bfloat16)
    rest = x - high.astype(jnp.float32)
    middle = rest.astype(jnp.bfloat16)
    return high, middle, (rest - middle.astype(jnp.float32)).astype(jnp.bfloat16)


def dot(a, b, dims):
    return lax.dot_general(a, b, (dims, ((), ())), preferred_element_type=jnp.float32)


def nt3(a, b):
    a1, a2, a3 = split3(a)
    b1, b2, b3 = split3(b)
    left = jnp.concatenate([a1, a2, a1, a2, a1, a3], axis=1)
    right = jnp.concatenate([b1, b1, b2, b2, b3, b1], axis=1)
    return dot(left, right, ((1,), (1,)))


def nn3(a, b):
    a1, a2, a3 = split3(a)
    b1, b2, b3 = split3(b)
    right = jnp.concatenate([b1, b2], axis=1)
    main = dot(jnp.concatenate([a1, a2], axis=1), jnp.concatenate([right, right], axis=0), ((1,), (0,)))
    small = dot(jnp.concatenate([a1, a3], axis=1), jnp.concatenate([b3, b1], axis=0), ((1,), (0,)))
    return main[:, :DHEAD] + (main[:, DHEAD:] + small)


def cols(h, base=0):
    return slice(base + h * DHEAD, base + (h + 1) * DHEAD)


def quarters(ref, value):
    rows = value.shape[0] // 4
    ref[pl.ds(0, 4 * rows), :] = value
    return [ref[pl.ds(j, rows, stride=4), :] for j in range(4)]


def mean4(ref, value):
    parts = quarters(ref, value)
    return ((parts[0] + parts[1]) + (parts[2] + parts[3])) * 0.25


def expand(ref, value):
    rows = value.shape[0]
    for j in range(4):
        ref[pl.ds(j, rows, stride=4), :] = value
    return ref[pl.ds(0, 4 * rows), :]


def expand_levels(ref, value, scales):
    total = value[80:84] * scales[2]
    total = value[64:80] * scales[1] + expand(ref, total)
    total = value[0:64] * scales[0] + expand(ref, total)
    return expand(ref, total)


def lane_index(rows):
    return lax.broadcasted_iota(jnp.int32, (rows, DHEAD), 1)


def wide(column):
    return jnp.broadcast_to(column, (column.shape[0], DHEAD))


def gathered(refs, lanes):
    l1a, l1b, l2a, l2b, l2c, l2d, l3a, l3b = refs
    pieces = [l1a[:, lanes], l1b[:, lanes]]
    pieces += [ref[0:48, lanes] for ref in (l2a, l2b, l2c, l2d)]
    pieces += [l3a[:, lanes], l3b[:, lanes]]
    return jnp.concatenate(pieces, axis=0)


def pool_kernel(
    k_ref, v_ref, q_ref, own_ref, first_ref, rest_ref, pair_ref, query_ref, e0_ref, e1_ref, e2_ref, in_ref, sems
):
    copies = [pltpu.make_async_copy(ref, in_ref.at[i], sems.at[i]) for i, ref in enumerate((k_ref, v_ref, q_ref))]
    for copy in copies:
        copy.start()
    own_ref[84:96, :] = jnp.zeros((12, 3 * WIDTH), jnp.float32)
    for part, copy in enumerate(copies):
        copy.wait()
        for h in range(HEADS):
            dst = cols(h, part * WIDTH)
            value = in_ref[part, :, cols(h)]
            one = mean4(e0_ref.at[(part * HEADS + h) % 2], value)
            two = mean4(e1_ref, one)
            three = mean4(e2_ref, two)
            own_ref[0:64, dst] = one
            own_ref[64:80, dst] = two
            own_ref[80:84, dst] = three
            if part < 2:
                first_ref[:, dst] = one
                rest_ref[0:16, dst] = two
                rest_ref[16:20, dst] = three
                pair_ref[:, dst] = value
            else:
                query_ref[:, cols(h)] = value


def merge_kernel(own_ref, a_ref, b_ref, c_ref, out_ref):
    for i, ref in enumerate((a_ref, b_ref, c_ref)):
        out_ref[16 * i : 16 * i + 16, :] = ref[0:16, :]
    out_ref[48:52, :] = own_ref[16:20, :]
    for i, ref in enumerate((a_ref, b_ref, c_ref)):
        out_ref[52 + 4 * i : 56 + 4 * i, :] = ref[16:20, :]


def thirds_kernel(a_ref, b_ref, out_ref):
    out_ref[0:16, :] = a_ref[48:64, :]
    out_ref[16:32, :] = b_ref[48:64, :]


def stack_kernel(a_ref, b_ref, c_ref, out_ref):
    out_ref[0:32, :] = a_ref[...]
    out_ref[32:64, :] = b_ref[...]
    out_ref[64:96, :] = c_ref[...]


def near_forward_kernel(
    edge_ref, q_ref, kp_ref, ko_ref, kn_ref, vp_ref, vo_ref, vn_ref, w_ref, peak_ref, mass_ref, sum_ref
):
    keys = jnp.concatenate([kp_ref[...], ko_ref[...], kn_ref[...]], axis=0)
    values = jnp.concatenate([vp_ref[...], vo_ref[...], vn_ref[...]], axis=0)
    scores = nt3(q_ref[...], keys) * INV_ROOT + edge_ref[0:1, :]
    peak = jnp.max(scores, axis=1, keepdims=True)
    weights = jnp.exp(scores - peak)
    w_ref[0] = weights
    peak_ref[...] = wide(peak)
    mass_ref[...] = wide(jnp.sum(weights, axis=1, keepdims=True))
    sum_ref[...] = nn3(weights, values)


def merge(one, two):
    peak = jnp.maximum(one[0], two[0])
    left = jnp.exp(one[0] - peak)
    right = jnp.exp(two[0] - peak)
    return peak, left * one[1] + right * two[1], left * one[2] + right * two[2]


def far_forward_kernel(
    bias_ref, own_ref, a0, a1, a2, a3, a4, a5, a6, a7,
    peak_ref, mass_ref, sum_ref, up_ref, gain_ref,
    att_ref, lse_ref, stat_ref,
    e0_ref, e1_ref, e2_ref, square_ref, cross_ref,
):
    far = (a0, a1, a2, a3, a4, a5, a6, a7)
    bias = bias_ref[...]
    for h in range(HEADS):
        k = cols(h)
        v = cols(h, WIDTH)
        scores = nt3(own_ref[:, cols(h, 2 * WIDTH)], gathered(far, k)) * INV_ROOT + bias
        peak = jnp.maximum(jnp.max(scores, axis=1, keepdims=True), FLOOR)
        weights = jnp.exp(scores - peak)
        mass = jnp.sum(weights, axis=1, keepdims=True)
        levels = (wide(peak), wide(mass), nn3(weights, gathered(far, v)))
        state = tuple(x[80:84] for x in levels)
        for start, stop in (LEVEL_ROWS[1], LEVEL_ROWS[0]):
            state = tuple(expand(ref.at[h % 2], x) for ref, x in zip((e0_ref, e1_ref, e2_ref), state))
            state = merge(state, tuple(x[start:stop] for x in levels))
        state = tuple(expand(ref.at[h % 2], x) for ref, x in zip((e0_ref, e1_ref, e2_ref), state))
        state = merge(state, (peak_ref[:, k], mass_ref[:, k], sum_ref[:, k]))
        attention = state[2] / state[1]
        att_ref[:, k] = attention
        lse_ref[:, k] = state[0] + jnp.log(state[1])
        square = attention * attention
        cross = up_ref[:, k] * gain_ref[0:1, k] * attention
        if h == 0:
            square_ref[...] = square
            cross_ref[...] = cross
        else:
            square_ref[...] += square
            cross_ref[...] += cross
    square = wide(jnp.sum(square_ref[...], axis=1, keepdims=True))
    cross = wide(jnp.sum(cross_ref[...], axis=1, keepdims=True))
    packed = jnp.where(lane_index(BLOCK) == 0, square, cross)
    stat_ref[...] = jnp.transpose(packed)[0:8, :]


def pooled_cotangent(scratch, lows, dots, grads):
    lows, dots, grads = (quarters(ref, x) for ref, x in zip(scratch, (lows, dots, grads)))
    low = jnp.minimum(jnp.minimum(lows[0], lows[1]), jnp.minimum(lows[2], lows[3]))
    scale = [jnp.exp(low - x) for x in lows]
    total = scale[0] * dots[0]
    grad = scale[0] * grads[0]
    for j in range(1, 4):
        total = total + scale[j] * dots[j]
        grad = grad + scale[j] * grads[j]
    return low, total, grad


def cotangent_kernel(
    s0_ref, s1_ref, s2_ref, s3_ref, own_ref, att_ref, lse_ref, up_ref, gain_ref,
    out_ref, dout_ref, delta_ref, first_ref, rest_ref,
    e0_ref, e1_ref, e2_ref,
):
    total = (s0_ref[...] + s1_ref[...]) + (s2_ref[...] + s3_ref[...])
    square = jnp.transpose(jnp.broadcast_to(total[0:1, :], (DHEAD, BLOCK)))
    cross = jnp.transpose(jnp.broadcast_to(total[1:2, :], (DHEAD, BLOCK)))
    inverse = lax.rsqrt(square / FEAT + EPSILON)
    pull = inverse * inverse * inverse * cross / FEAT
    lane = lane_index(BLOCK)
    packed = jnp.zeros((BLOCK, DHEAD), jnp.float32)
    stats = [jnp.zeros((rows, DHEAD), jnp.float32) for rows in (64, 16, 4)]
    first_ref[:, WIDTH:KV] = own_ref[0:64, KV:]
    rest_ref[:, WIDTH:KV] = own_ref[64:84, KV:]
    for h in range(HEADS):
        k = cols(h)
        attention = att_ref[:, k]
        out_ref[:, k] = attention * inverse * gain_ref[0:1, k]
        d_out = inverse * (up_ref[:, k] * gain_ref[0:1, k]) - attention * pull
        dout_ref[0:BLOCK, k] = d_out
        delta = wide(jnp.sum(d_out * attention, axis=1, keepdims=True))
        delta_ref[:, k] = delta
        packed = jnp.where(lane == h, lse_ref[:, k], packed)
        packed = jnp.where(lane == HEADS + h, delta, packed)
        level = (lse_ref[:, k], delta, d_out)
        for n, (ref, start) in enumerate(((first_ref, 0), (rest_ref, 0), (rest_ref, 16))):
            level = pooled_cotangent([e.at[h % 2] for e in (e0_ref, e1_ref, e2_ref)], *level)
            rows = level[0].shape[0]
            ref[start : start + rows, k] = level[2]
            short = lane[0:rows]
            stats[n] = jnp.where(short == h, level[0], jnp.where(short == HEADS + h, level[1], stats[n]))
    first_ref[:, KV:] = stats[0]
    rest_ref[0:16, KV:] = stats[1]
    rest_ref[16:20, KV:] = stats[2]
    dout_ref[BLOCK:, 0:256] = jnp.transpose(packed)[0:8, :]
    dout_ref[BLOCK:, 256:] = jnp.zeros((8, 256), jnp.float32)


def near_query_kernel(
    w_ref, peak_ref, lse_ref, delta_ref, dout_ref, kp_ref, ko_ref, kn_ref, vp_ref, vo_ref, vn_ref, dq_ref
):
    keys = jnp.concatenate([kp_ref[...], ko_ref[...], kn_ref[...]], axis=0)
    values = jnp.concatenate([vp_ref[...], vo_ref[...], vn_ref[...]], axis=0)
    factor = jnp.exp(peak_ref[:, 0:1] - lse_ref[:, 0:1])
    weights = w_ref[0] * factor
    d_scores = weights * (nt3(dout_ref[...], values) - delta_ref[:, 0:1])
    dq_ref[...] = nn3(d_scores, keys) * INV_ROOT


def far_query_kernel(
    bias_ref, own_ref, a0, a1, a2, a3, a4, a5, a6, a7, first_ref, rest_ref, near_ref, dq_ref, e0_ref
):
    far = (a0, a1, a2, a3, a4, a5, a6, a7)
    bias = bias_ref[...]

    def grads(lanes):
        fill = jnp.zeros((12, DHEAD), jnp.float32)
        return jnp.concatenate([first_ref[:, lanes], rest_ref[0:16, lanes], rest_ref[16:20, lanes], fill], axis=0)

    stats = grads(slice(KV, GRAD))
    for h in range(HEADS):
        k = cols(h)
        keys = gathered(far, k)
        scores = nt3(own_ref[:, cols(h, 2 * WIDTH)], keys) * INV_ROOT + bias
        weights = jnp.exp(scores - stats[:, h : h + 1])
        d_probs = nt3(grads(k), gathered(far, cols(h, WIDTH)))
        d_scores = weights * (d_probs - stats[:, HEADS + h : HEADS + h + 1])
        grad = nn3(d_scores, keys)
        scales = [INV_ROOT / 4**n for n in (1, 2, 3)]
        dq_ref[:, k] = near_ref[:, k] + expand_levels(e0_ref.at[h % 2], grad, scales)


def near_key_kernel(
    k_ref, v_ref, qp_ref, qo_ref, qn_ref, dp_ref, do_ref, dn_ref, tp_ref, to_ref, tn_ref, dk_ref, dv_ref
):
    h = pl.program_id(0)
    queries = jnp.concatenate([qp_ref[...], qo_ref[...], qn_ref[...]], axis=0)
    grads = jnp.concatenate([dp_ref[...], do_ref[...], dn_ref[...]], axis=0)
    low = jnp.concatenate([ref[pl.ds(h, 1), :] for ref in (tp_ref, to_ref, tn_ref)], axis=1)
    total = jnp.concatenate([ref[pl.ds(h + HEADS, 1), :] for ref in (tp_ref, to_ref, tn_ref)], axis=1)
    weights = jnp.exp(nt3(k_ref[...], queries) * INV_ROOT - low)
    d_scores = weights * (nt3(v_ref[...], grads) - total)
    dk_ref[...] = nn3(d_scores, queries) * INV_ROOT
    dv_ref[...] = nn3(weights, grads)


def far_key_kernel(
    bias_ref, own_ref, a0, a1, a2, a3, a4, a5, a6, a7, dk_in_ref, dv_in_ref, dk_ref, dv_ref, e0_ref, e1_ref
):
    far = (a0, a1, a2, a3, a4, a5, a6, a7)
    bias = bias_ref[...]
    stats = jnp.transpose(gathered(far, slice(KV, GRAD)))[0:8, :]
    for h in range(HEADS):
        k = cols(h)
        queries = gathered(far, cols(h, WIDTH))
        grads = gathered(far, k)
        scores = nt3(own_ref[:, k], queries) * INV_ROOT + bias
        weights = jnp.exp(scores - stats[h : h + 1, :])
        d_scores = weights * (nt3(own_ref[:, cols(h, WIDTH)], grads) - stats[HEADS + h : HEADS + h + 1, :])
        scales = [1.0 / 4**n for n in (1, 2, 3)]
        d_keys = nn3(d_scores, queries) * INV_ROOT
        dk_ref[:, k] = dk_in_ref[:, k] + expand_levels(e0_ref.at[h % 2], d_keys, scales)
        dv_ref[:, k] = dv_in_ref[:, k] + expand_levels(e1_ref.at[h % 2], nn3(weights, grads), scales)


def f32(*shape):
    return jax.ShapeDtypeStruct(shape, jnp.float32)


def params():
    return pltpu.CompilerParams(vmem_limit_bytes=VMEM_BYTES)


def cost(flops, size):
    return pl.CostEstimate(flops=int(flops), bytes_accessed=int(size), transcendentals=0)


def whole_call(kernel, outs, scratch, flops, size, *operands):
    spec = pl.BlockSpec(memory_space=pltpu.VMEM)
    return pl.pallas_call(
        kernel,
        out_shape=outs,
        in_specs=[spec] * len(operands),
        out_specs=[spec] * len(outs),
        scratch_shapes=[pltpu.VMEM(shape, jnp.float32) for shape in scratch],
        compiler_params=params(),
        cost_estimate=cost(flops, size),
    )(*operands)


BLOCK_FLOPS = 2.0 * BLOCK * BLOCK * DHEAD * HEADS * 6


def column():
    return pl.BlockSpec((BLOCK, DHEAD), lambda h: (0, h))


def column_at(first):
    return pl.BlockSpec((BLOCK, DHEAD), lambda h: (0, first + h))


def near_forward(edge, query, kvp, pair, kvn):
    slab = pl.BlockSpec((1, BLOCK, 3 * BLOCK), lambda h: (h, 0, 0))
    edge_spec = pl.BlockSpec((1, 3 * BLOCK), lambda h: (0, 0))
    k, v = column_at(0), column_at(HEADS)
    return pl.pallas_call(
        near_forward_kernel,
        grid=(HEADS,),
        out_shape=[f32(HEADS, BLOCK, 3 * BLOCK), f32(BLOCK, WIDTH), f32(BLOCK, WIDTH), f32(BLOCK, WIDTH)],
        in_specs=[edge_spec, k, k, k, k, v, v, v],
        out_specs=[slab, k, k, k],
        compiler_params=params(),
        cost_estimate=cost(6 * BLOCK_FLOPS, 8e6),
    )(edge, query, kvp, pair, kvn, kvp, pair, kvn)


def near_query(weights, peak, lse, delta, d_out, kvp, pair, kvn):
    slab = pl.BlockSpec((1, BLOCK, 3 * BLOCK), lambda h: (h, 0, 0))
    k, v = column_at(0), column_at(HEADS)
    return pl.pallas_call(
        near_query_kernel,
        grid=(HEADS,),
        out_shape=f32(BLOCK, WIDTH),
        in_specs=[slab, k, k, k, k, k, k, k, v, v, v],
        out_specs=k,
        compiler_params=params(),
        cost_estimate=cost(6 * BLOCK_FLOPS, 8e6),
    )(weights, peak, lse, delta, d_out, kvp, pair, kvn, kvp, pair, kvn)


def near_key(pair, qp, query, qn, dp, d_out, dn):
    stat = pl.BlockSpec((8, 256), lambda h: (BLOCK // 8, 0))
    k, v = column_at(0), column_at(HEADS)
    return pl.pallas_call(
        near_key_kernel,
        grid=(HEADS,),
        out_shape=[f32(BLOCK, WIDTH)] * 2,
        in_specs=[k, v] + [k] * 6 + [stat] * 3,
        out_specs=[k] * 2,
        compiler_params=params(),
        cost_estimate=cost(12 * BLOCK_FLOPS, 8e6),
    )(pair, pair, qp, query, qn, dp, d_out, dn, dp, d_out, dn)


def pool(key, value, query):
    vmem = pl.BlockSpec(memory_space=pltpu.VMEM)
    hbm = pl.BlockSpec(memory_space=pltpu.HBM)
    return pl.pallas_call(
        pool_kernel,
        out_shape=[f32(OWN, 3 * WIDTH), f32(64, KV), f32(20, KV), f32(BLOCK, KV), f32(BLOCK, WIDTH)],
        in_specs=[hbm] * 3,
        out_specs=[vmem] * 5,
        scratch_shapes=[
            pltpu.VMEM((2, BLOCK, DHEAD), jnp.float32),
            pltpu.VMEM((64, DHEAD), jnp.float32),
            pltpu.VMEM((16, DHEAD), jnp.float32),
            pltpu.VMEM((3, BLOCK, WIDTH), jnp.float32),
            pltpu.SemaphoreType.DMA((3,)),
        ],
        compiler_params=params(),
        cost_estimate=cost(1e6, 2e6),
    )(key, value, query)


def far_forward(bias, own, far, peak, mass, summed, upstream, gain):
    return whole_call(
        far_forward_kernel,
        [f32(BLOCK, WIDTH), f32(BLOCK, WIDTH), f32(8, 256)],
        [(2, BLOCK, DHEAD)] * 3 + [(BLOCK, DHEAD)] * 2,
        BLOCK_FLOPS,
        8e6,
        bias, own, *far, peak, mass, summed, upstream, gain,
    )


def cotangent(stats, others, own, attention, lse, upstream, gain):
    return whole_call(
        cotangent_kernel,
        [f32(BLOCK, WIDTH), f32(BLOCK + 8, WIDTH), f32(BLOCK, WIDTH), f32(64, GRAD), f32(20, GRAD)],
        [(2, BLOCK, DHEAD)] * 3,
        1e6,
        4e6,
        stats, *others, own, attention, lse, upstream, gain,
    )


def far_query(bias, own, far, first, rest, near):
    (grad,) = whole_call(
        far_query_kernel,
        [f32(BLOCK, WIDTH)],
        [(2, BLOCK, DHEAD)],
        BLOCK_FLOPS,
        6e6,
        bias, own, *far, first, rest, near,
    )
    return grad


def far_key(bias, own, grads, near_dk, near_dv):
    return whole_call(
        far_key_kernel,
        [f32(BLOCK, WIDTH)] * 2,
        [(2, BLOCK, DHEAD)] * 2,
        BLOCK_FLOPS,
        6e6,
        bias, own, *grads, near_dk, near_dv,
    )


def body(query, key, value, norm_gain, upstream):
    position = lax.axis_index("seq")
    count = lax.axis_size("seq")

    def exchange(array, mask):
        return lax.ppermute(array, "seq", [(i, i ^ mask) for i in range(count)])

    def from_before(array):
        return lax.ppermute(array, "seq", [(i, i + 1) for i in range(count - 1)])

    def from_after(array):
        return lax.ppermute(array, "seq", [(i + 1, i) for i in range(count - 1)])

    head_count = lax.axis_size("head")
    gain = norm_gain.reshape(1, WIDTH)
    offset, slot_level, own_level = slot_table()
    apart = jnp.abs((position ^ offset) - position) > 1
    bias = jnp.where(apart & (slot_level == own_level), slot_level.astype(np.float32) * LN4, NEGATIVE_FILL)
    block = jnp.arange(3 * BLOCK, dtype=jnp.int32)[None, :] // BLOCK + position - 1
    edge = jnp.where((block >= 0) & (block < count), 0.0, NEGATIVE_FILL)

    def after(array, *tokens):
        return lax.optimization_barrier((array,) + tokens)[0]

    def gather(first, rest, hook, work0=None, work1=None):
        width = first.shape[1]
        quads = [exchange(rest, mask) for mask in (8, 4, 12)]
        l1a = exchange(first, 2)
        head_rest = after(rest, l1a) if work0 is None else after(rest, l1a, work0)
        (l2a,) = whole_call(merge_kernel, [f32(64, width)], [], 1e4, 1e5, head_rest, quads[1], quads[0], quads[2])
        l2b = exchange(l2a, 2)
        hook(0, l2a)
        head_l2a = l2a if work1 is None else after(l2a, work1)
        (thirds,) = whole_call(thirds_kernel, [f32(32, width)], [], 1e4, 1e5, head_l2a, l2b)
        many = [exchange(thirds, mask) for mask in (16, 32, 48)]
        l1b = exchange(after(l1a, thirds), 1)
        l2c = exchange(after(l2a, thirds), 1)
        l2d = exchange(l2b, 1)
        (l3a,) = whole_call(stack_kernel, [f32(96, width)], [], 1e4, 1e5, *many)
        l3b = exchange(l3a, 1)
        return l1a, l1b, l2a, l2b, l2c, l2d, l3a, l3b

    own, first, rest, pair, query = pool(key, value, query)
    state = {}

    def forward_hook(stage, token):
        if stage == 0:
            held = after(pair, token)
            state["kvp"], state["kvn"] = from_before(held), from_after(held)

    far = gather(first, rest, forward_hook)
    kvp, kvn = state["kvp"], state["kvn"]
    held = after(query, kvp, kvn)
    qp, qn = from_before(held), from_after(held)

    weights, peak, mass, summed = near_forward(edge, query, kvp, pair, kvn)
    attention, lse, stats = far_forward(bias, own, far, peak, mass, summed, upstream, gain)
    stats = after(stats, qp, qn)
    others = [
        lax.ppermute(stats, "head", [(i, i ^ mask) for i in range(head_count)]) for mask in range(1, head_count)
    ]
    attended, d_out, delta, g1, g23 = cotangent(stats, others, own, attention, lse, upstream, gain)
    near_dq = near_query(weights, peak, lse, delta, d_out, kvp, pair, kvn)
    query_grad = far_query(bias, own, far, g1, g23, near_dq)

    def backward_hook(stage, token):
        if stage == 0:
            held = after(d_out, token)
            state["dp"], state["dn"] = from_before(held), from_after(held)

    grads = gather(g1, g23, backward_hook, near_dq, query_grad)
    near_dk, near_dv = near_key(pair, qp, query, qn, state["dp"], d_out, state["dn"])
    key_grad, value_grad = far_key(bias, own, grads, near_dk, near_dv)
    return attended, query_grad, key_grad, value_grad


def solution(mesh):
    return jax.shard_map(
        body,
        mesh=mesh,
        in_specs=(
            P("seq", "head"),
            P("seq", "head"),
            P("seq", "head"),
            P("head"),
            P("seq", "head"),
        ),
        out_specs=(P("seq", "head"), P("seq", "head"), P("seq", "head"), P("seq", "head")),
        check_vma=False,
    )
```

profile of v0, /device:TPU:1, one launch (start us, length us, event | category | flops | bytes accessed | tf_op | source)
XLA Modules:
  0.0 151.5 jit_solution(11964306098419294240)
XLA Ops:
  0.6 1.0 copy-done.7
  1.7 1.0 copy-done.8
  2.7 1.0 copy-done.9
  3.8 0.6 shard_map.111
  4.4 0.8 copy-done
  5.2 0.8 copy-done.11
  6.0 2.5 %collective-permute-start = (f32[64,1024]{1,0:T(8,128)S(1)}, f32[64,1024]{1,0:T(8,128)S(1)}, u32[]{:S(2)}, u32[]{:S(2)}) collective-permute-start(f32[64,1024]{1,0:T(8,128)S(1)} %get-tuple-element.37), channel_id=1, source_target_pairs={{0,8},{4,12},{8,0},{12,4},{16,24},{20,28},{24,16},{28,20},{32,40},... | collective-permute-start | bytes 786440 | tf_op jit(solution)/shard_map/ppermute | solution.py:495
  8.5 5.1 %collective-permute-start.3 = (f32[20,1024]{1,0:T(8,128)S(1)}, f32[20,1024]{1,0:T(8,128)S(1)}, u32[]{:S(2)}, u32[]{:S(2)}) collective-permute-start(f32[20,1024]{1,0:T(8,128)S(1)} %get-tuple-element.39.own_ref), channel_id=1, source_target_pairs={{0,48},{4,52},{8,56},{12,60},{16,32},{20,36},{24,40},{28,44},{32,1... | collective-permute-start | bytes 245768 | tf_op jit(solution)/shard_map/ppermute | solution.py:495
  13.6 1.2 collective-permute-start.2
  14.8 0.9 collective-permute-start.1
  15.7 0.0 collective-permute-done.a0
  15.7 6.6 %collective-permute-done.3.c_ref = f32[20,1024]{1,0:T(8,128)S(1)} collective-permute-done((f32[20,1024]{1,0:T(8,128)S(1)}, f32[20,1024]{1,0:T(8,128)S(1)}, u32[]{:S(2)}, u32[]{:S(2)}) %collective-permute-start.3) | collective-permute-done | bytes 81952 | tf_op jit(solution)/shard_map/ppermute | solution.py:495
  22.3 1.8 %collective-permute-done.2.b_ref = f32[20,1024]{1,0:T(8,128)S(1)} collective-permute-done((f32[20,1024]{1,0:T(8,128)S(1)}, f32[20,1024]{1,0:T(8,128)S(1)}, u32[]{:S(2)}, u32[]{:S(2)}) %collective-permute-start.2) | collective-permute-done | bytes 81952 | tf_op jit(solution)/shard_map/ppermute | solution.py:495
  24.2 5.9 %collective-permute-start.13 = (f32[256,1024]{1,0:T(8,128)S(1)}, f32[256,1024]{1,0:T(8,128)S(1)}, u32[]{:S(2)}, u32[]{:S(2)}) collective-permute-start(f32[256,1024]{1,0:T(8,128)S(1)} %get-tuple-element.44.ko_ref.vo_ref.k_ref.v_ref), channel_id=1, source_target_pairs={{4,0},{8,4},{12,8},{16,12},{20,16},{24,20},{28,24},{32,28},{36,32}... | collective-permute-start | bytes 3145736 | tf_op jit(solution)/shard_map/ppermute | solution.py:501
  30.1 4.6 %collective-permute-start.12 = (f32[256,1024]{1,0:T(8,128)S(1)}, f32[256,1024]{1,0:T(8,128)S(1)}, u32[]{:S(2)}, u32[]{:S(2)}) collective-permute-start(f32[256,1024]{1,0:T(8,128)S(1)} %get-tuple-element.44.ko_ref.vo_ref.k_ref.v_ref), channel_id=1, source_target_pairs={{0,4},{4,8},{8,12},{12,16},{16,20},{20,24},{24,28},{28,32},{32,36}... | collective-permute-start | bytes 3145736 | tf_op jit(solution)/shard_map/ppermute | solution.py:498
  34.7 0.7 collective-permute-start.4
  35.4 16.6 %collective-permute-done.4.b_ref.a3 = f32[64,1024]{1,0:T(8,128)S(1)} collective-permute-done((f32[64,1024]{1,0:T(8,128)S(1)}, f32[64,1024]{1,0:T(8,128)S(1)}, u32[]{:S(2)}, u32[]{:S(2)}) %collective-permute-start.4) | collective-permute-done | bytes 262176 | tf_op jit(solution)/shard_map/ppermute | solution.py:495
  52.0 0.0 copy-start.2
  52.0 0.7 copy-done.2
  52.7 2.7 %collective-permute-start.10 = (f32[32,1024]{1,0:T(8,128)S(1)}, f32[32,1024]{1,0:T(8,128)}, u32[]{:S(2)}, u32[]{:S(2)}) collective-permute-start(f32[32,1024]{1,0:T(8,128)S(1)} %shard_map.113), channel_id=1, source_target_pairs={{0,192},{4,196},{8,200},{12,204},{16,208},{20,212},{24,216},{28,22... | collective-permute-start | bytes 393224 | tf_op jit(solution)/shard_map/ppermute | solution.py:495
  55.5 0.3 collective-permute-start.9
  55.8 0.2 collective-permute-start.8
  56.0 5.5 %collective-permute-done.10.c_ref = f32[32,1024]{1,0:T(8,128)} collective-permute-done((f32[32,1024]{1,0:T(8,128)S(1)}, f32[32,1024]{1,0:T(8,128)}, u32[]{:S(2)}, u32[]{:S(2)}) %collective-permute-start.10) | collective-permute-done | bytes 131104 | tf_op jit(solution)/shard_map/ppermute | solution.py:495
  61.6 0.3 collective-permute-start.5
  61.9 0.7 compare_reduce_fusion
  62.6 0.2 collective-permute-done.8.a_ref
  62.9 1.1 shard_map.114.a6
  63.9 0.7 collective-permute-start.11
  64.6 1.9 %collective-permute-start.15 = (f32[256,512]{1,0:T(8,128)}, f32[256,512]{1,0:T(8,128)S(1)}, u32[]{:S(2)}, u32[]{:S(2)}) collective-permute-start(f32[256,512]{1,0:T(8,128)} %copy-done.11), channel_id=1, source_target_pairs={{4,0},{8,4},{12,8},{16,12},{20,16},{24,20},{28,24},{32,28},{36,32}... | collective-permute-start | bytes 1572872 | tf_op jit(solution)/shard_map/ppermute | solution.py:501
  66.5 3.6 %collective-permute-start.14 = (f32[256,512]{1,0:T(8,128)}, f32[256,512]{1,0:T(8,128)S(1)}, u32[]{:S(2)}, u32[]{:S(2)}) collective-permute-start(f32[256,512]{1,0:T(8,128)} %copy-done.11), channel_id=1, source_target_pairs={{0,4},{4,8},{8,12},{12,16},{16,20},{20,24},{24,28},{28,32},{32,36}... | collective-permute-start | bytes 1572872 | tf_op jit(solution)/shard_map/ppermute | solution.py:498
  70.2 0.8 and_select_fusion.bias_ref
  71.0 0.1 collective-permute-start.6
  71.1 0.5 collective-permute-start.7
  71.6 0.0 copy-start.12
  71.6 1.0 copy-done.12
  72.7 6.4 %shard_map.115 = (f32[4,256,768]{2,1,0:T(8,128)}, f32[256,512]{1,0:T(8,128)S(1)}, f32[256,512]{1,0:T(8,128)S(1)}, f32[256,512]{1,0:T(8,128)S(1)}) custom-call(f32[1,768]{1,0:T(1,128)S(1)} %and_select_fusion.1.edge_ref, f32[256,512]{1,0:T(8,128)S(1)} %copy-done.12, f32[256,1024]{1,0:T(8,128)S(1)} %collective-permute-done.12.kp_ref.vp_ref, ...), custom_call_target="tpu_custom_call" | custom-call | flops 2415919104 | bytes 8000000 | tf_op jit(solution)/shard_map/pallas_call | solution.py:386
  79.1 3.9 %shard_map.116 = (f32[256,512]{1,0:T(8,128)S(1)}, f32[256,512]{1,0:T(8,128)S(1)}, f32[8,256]{1,0:T(8,128)S(1)}) custom-call(f32[96,512]{1,0:T(8,128)S(1)} %and_select_fusion.bias_ref, f32[96,1536]{1,0:T(8,128)} %copy-done, f32[64,1024]{1,0:T(8,128)S(1)} %copy-done.6, f32[64,1024]{1,0:T(8,128)S(1)} %collective-permute-done.5.a1, ...), custom_call_target="tpu_custom_call" | custom-call | flops 402653184 | bytes 8000000 | tf_op jit(solution)/shard_map/pallas_call | solution.py:360
  83.0 2.8 %collective-permute-start.18 = (f32[8,256]{1,0:T(8,128)S(1)}, f32[8,256]{1,0:T(8,128)S(1)}, u32[]{:S(2)}, u32[]{:S(2)}) collective-permute-start(f32[8,256]{1,0:T(8,128)S(1)} %get-tuple-element.50.s0_ref), channel_id=1, source_target_pairs={{0,3},{1,2},{2,1},{3,0},{4,7},{5,6},{6,5},{7,4},{8,11},{9,10},{10,... | collective-permute-start | bytes 24584 | tf_op jit(solution)/shard_map/ppermute | solution.py:549
  85.8 0.5 collective-permute-start.17
  86.3 0.3 collective-permute-start.16
  86.5 0.5 collective-permute-done.18.s3_ref
  87.0 2.8 %collective-permute-done.17.s2_ref = f32[8,256]{1,0:T(8,128)S(1)} collective-permute-done((f32[8,256]{1,0:T(8,128)S(1)}, f32[8,256]{1,0:T(8,128)S(1)}, u32[]{:S(2)}, u32[]{:S(2)}) %collective-permute-start.17) | collective-permute-done | bytes 8224 | tf_op jit(solution)/shard_map/ppermute | solution.py:549
  89.8 1.3 shard_map.117
  91.1 3.0 %collective-permute-start.22 = (f32[20,1152]{1,0:T(8,128)S(1)}, f32[20,1152]{1,0:T(8,128)S(1)}, u32[]{:S(2)}, u32[]{:S(2)}) collective-permute-start(f32[20,1152]{1,0:T(8,128)S(1)} %get-tuple-element.59.rest_ref.own_ref), channel_id=1, source_target_pairs={{0,48},{4,52},{8,56},{12,60},{16,32},{20,36},{24,40},{28,44},{32,1... | collective-permute-start | bytes 276488 | tf_op jit(solution)/shard_map/ppermute | solution.py:495
  94.1 1.7 %collective-permute-start.21 = (f32[20,1152]{1,0:T(8,128)S(1)}, f32[20,1152]{1,0:T(8,128)S(1)}, u32[]{:S(2)}, u32[]{:S(2)}) collective-permute-start(f32[20,1152]{1,0:T(8,128)S(1)} %get-tuple-element.59.rest_ref.own_ref), channel_id=1, source_target_pairs={{0,32},{4,36},{8,40},{12,44},{16,48},{20,52},{24,56},{28,60},{32,0... | collective-permute-start | bytes 276488 | tf_op jit(solution)/shard_map/ppermute | solution.py:495
  95.8 0.9 collective-permute-start.20
  96.8 5.8 %shard_map.118.near_ref = f32[256,512]{1,0:T(8,128)S(1)} custom-call(f32[4,256,768]{2,1,0:T(8,128)} %get-tuple-element.56.w_ref, f32[256,512]{1,0:T(8,128)S(1)} %get-tuple-element.45.peak_ref, f32[256,512]{1,0:T(8,128)S(1)} %get-tuple-element.52.lse_ref, f32[256,512]{1,0:T(8,128)S(1)} %get-tuple-element.57.delta_ref, ...), custom_call_target="tpu_custom_call" | custom-call | flops 2415919104 | bytes 8000000 | tf_op jit(solution)/shard_map/pallas_call | solution.py:400
  102.6 3.8 %collective-permute-done.22.c_ref = f32[20,1152]{1,0:T(8,128)S(1)} collective-permute-done((f32[20,1152]{1,0:T(8,128)S(1)}, f32[20,1152]{1,0:T(8,128)S(1)}, u32[]{:S(2)}, u32[]{:S(2)}) %collective-permute-start.22) | collective-permute-done | bytes 92192 | tf_op jit(solution)/shard_map/ppermute | solution.py:495
  106.4 0.0 copy-start.13
  106.4 6.0 %collective-permute-start.32 = (f32[264,512]{1,0:T(8,128)S(1)}, f32[264,512]{1,0:T(8,128)S(1)}, u32[]{:S(2)}, u32[]{:S(2)}) collective-permute-start(f32[264,512]{1,0:T(8,128)S(1)} %get-tuple-element.63.dout_ref.do_ref.to_ref), channel_id=1, source_target_pairs={{4,0},{8,4},{12,8},{16,12},{20,16},{24,20},{28,24},{32,28},{36,32}... | collective-permute-start | bytes 1622024 | tf_op jit(solution)/shard_map/ppermute | solution.py:501
  112.5 2.3 %collective-permute-start.31 = (f32[264,512]{1,0:T(8,128)S(1)}, f32[264,512]{1,0:T(8,128)S(1)}, u32[]{:S(2)}, u32[]{:S(2)}) collective-permute-start(f32[264,512]{1,0:T(8,128)S(1)} %get-tuple-element.63.dout_ref.do_ref.to_ref), channel_id=1, source_target_pairs={{0,4},{4,8},{8,12},{12,16},{16,20},{20,24},{24,28},{28,32},{32,36}... | collective-permute-start | bytes 1622024 | tf_op jit(solution)/shard_map/ppermute | solution.py:498
  114.8 3.1 %collective-permute-start.23 = (f32[64,1152]{1,0:T(8,128)S(1)}, f32[64,1152]{1,0:T(8,128)S(1)}, u32[]{:S(2)}, u32[]{:S(2)}) collective-permute-start(f32[64,1152]{1,0:T(8,128)S(1)} %shard_map.120.a_ref.a2), channel_id=1, source_target_pairs={{0,8},{4,12},{8,0},{12,4},{16,24},{20,28},{24,16},{28,20},{32,40},... | collective-permute-start | bytes 884744 | tf_op jit(solution)/shard_map/ppermute | solution.py:495
  117.9 3.7 %shard_map.119 = f32[256,512]{1,0:T(8,128)} custom-call(f32[96,512]{1,0:T(8,128)S(1)} %and_select_fusion.bias_ref, f32[96,1536]{1,0:T(8,128)S(1)} %copy-done.1, f32[64,1024]{1,0:T(8,128)S(1)} %copy-done.6, f32[64,1024]{1,0:T(8,128)S(1)} %collective-permute-done.5.a1, f32[64,1024]{1,0:T(8,128)S(1)} %shard_map.112.a_ref.a2, f32[64,1024]{1,0:T(8,128)S(1)} %copy-done.3, ...), custom_call_target="tpu_custom_call" | custom-call | flops 402653184 | bytes 6000000 | tf_op jit(solution)/shard_map/pallas_call | solution.py:360
  121.6 5.8 %collective-permute-done.23.b_ref.a3 = f32[64,1152]{1,0:T(8,128)S(1)} collective-permute-done((f32[64,1152]{1,0:T(8,128)S(1)}, f32[64,1152]{1,0:T(8,128)S(1)}, u32[]{:S(2)}, u32[]{:S(2)}) %collective-permute-start.23) | collective-permute-done | bytes 294944 | tf_op jit(solution)/shard_map/ppermute | solution.py:495
  127.4 3.3 %collective-permute-start.29 = (f32[32,1152]{1,0:T(8,128)S(1)}, f32[32,1152]{1,0:T(8,128)S(1)}, u32[]{:S(2)}, u32[]{:S(2)}) collective-permute-start(f32[32,1152]{1,0:T(8,128)S(1)} %shard_map.121), channel_id=1, source_target_pairs={{0,192},{4,196},{8,200},{12,204},{16,208},{20,212},{24,216},{28,22... | collective-permute-start | bytes 442376 | tf_op jit(solution)/shard_map/ppermute | solution.py:495
  130.7 0.7 collective-permute-start.27
  131.3 6.1 %collective-permute-done.29.c_ref = f32[32,1152]{1,0:T(8,128)S(1)} collective-permute-done((f32[32,1152]{1,0:T(8,128)S(1)}, f32[32,1152]{1,0:T(8,128)S(1)}, u32[]{:S(2)}, u32[]{:S(2)}) %collective-permute-start.29) | collective-permute-done | bytes 147488 | tf_op jit(solution)/shard_map/ppermute | solution.py:495
  137.5 0.3 collective-permute-start.24
  137.8 0.9 collective-permute-start.25
  138.7 0.2 collective-permute-done.27.a_ref
  138.9 0.4 collective-permute-start.26
  139.3 0.4 collective-permute-start.30
  139.7 7.3 %shard_map.123 = (f32[256,512]{1,0:T(8,128)S(1)}, f32[256,512]{1,0:T(8,128)S(1)}) custom-call(f32[256,1024]{1,0:T(8,128)S(1)} %get-tuple-element.44.ko_ref.vo_ref.k_ref.v_ref, f32[256,1024]{1,0:T(8,128)S(1)} %get-tuple-element.44.ko_ref.vo_ref.k_ref.v_ref, f32[256,512]{1,0:T(8,128)S(1)} %collective-permute-done.14.qp_ref, f32[256,512]{1,0:T(8,128)S(1)} %copy-done.13, ...), custom_call_target="tpu_custom_call" | custom-call | flops 4831838208 | bytes 8000000 | tf_op jit(solution)/shard_map/pallas_call | solution.py:414
  147.1 4.4 %shard_map.124 = (f32[256,512]{1,0:T(8,128)}, f32[256,512]{1,0:T(8,128)}) custom-call(f32[96,512]{1,0:T(8,128)S(1)} %and_select_fusion.bias_ref, f32[96,1536]{1,0:T(8,128)S(1)} %copy-done.1, f32[64,1152]{1,0:T(8,128)S(1)} %collective-permute-done.19.a0, f32[64,1152]{1,0:T(8,128)S(1)} %collective-permute-done.24.a1, f32[64,1152]{1,0:T(8,128)S(1)} %shard_map.120.a_ref.a2, ...), custom_call_target="tpu_custom_call" | custom-call | flops 402653184 | bytes 6000000 | tf_op jit(solution)/shard_map/pallas_call | solution.py:360
  (49 shorter events, 0.2 us)
Async XLA Ops:
  0.6 1.0 copy-start.7
  1.7 1.0 copy-start.8
  2.7 1.0 copy-start.9
  3.8 66.4 %copy-start.14 = (f32[512]{0:T(512)S(1)}, f32[512]{0:T(512)}, u32[]{:S(2)}) copy-start(f32[512]{0:T(512)} %constant.43) | copy-start | bytes 6148
  4.4 0.8 copy-start
  5.2 0.8 copy-start.11
  6.0 9.7 %collective-permute-start = (f32[64,1024]{1,0:T(8,128)S(1)}, f32[64,1024]{1,0:T(8,128)S(1)}, u32[]{:S(2)}, u32[]{:S(2)}) collective-permute-start(f32[64,1024]{1,0:T(8,128)S(1)} %get-tuple-element.37), channel_id=1, source_target_pairs={{0,8},{4,12},{8,0},{12,4},{16,24},{20,28},{24,16},{28,20},{32,40},... | collective-permute-start | bytes 786440 | tf_op jit(solution)/shard_map/ppermute | solution.py:495
  8.5 13.9 %collective-permute-start.3 = (f32[20,1024]{1,0:T(8,128)S(1)}, f32[20,1024]{1,0:T(8,128)S(1)}, u32[]{:S(2)}, u32[]{:S(2)}) collective-permute-start(f32[20,1024]{1,0:T(8,128)S(1)} %get-tuple-element.39.own_ref), channel_id=1, source_target_pairs={{0,48},{4,52},{8,56},{12,60},{16,32},{20,36},{24,40},{28,44},{32,1... | collective-permute-start | bytes 245768 | tf_op jit(solution)/shard_map/ppermute | solution.py:495
  13.6 10.5 %collective-permute-start.2 = (f32[20,1024]{1,0:T(8,128)S(1)}, f32[20,1024]{1,0:T(8,128)S(1)}, u32[]{:S(2)}, u32[]{:S(2)}) collective-permute-start(f32[20,1024]{1,0:T(8,128)S(1)} %get-tuple-element.39.own_ref), channel_id=1, source_target_pairs={{0,32},{4,36},{8,40},{12,44},{16,48},{20,52},{24,56},{28,60},{32,0... | collective-permute-start | bytes 245768 | tf_op jit(solution)/shard_map/ppermute | solution.py:495
  14.8 9.4 %collective-permute-start.1 = (f32[20,1024]{1,0:T(8,128)S(1)}, f32[20,1024]{1,0:T(8,128)S(1)}, u32[]{:S(2)}, u32[]{:S(2)}) collective-permute-start(f32[20,1024]{1,0:T(8,128)S(1)} %get-tuple-element.39.own_ref), channel_id=1, source_target_pairs={{0,16},{4,20},{8,24},{12,28},{16,0},{20,4},{24,8},{28,12},{32,48},... | collective-permute-start | bytes 245768 | tf_op jit(solution)/shard_map/ppermute | solution.py:495
  15.7 8.4 %copy-start.5 = (f32[64,1024]{1,0:T(8,128)}, f32[64,1024]{1,0:T(8,128)S(1)}, u32[]{:S(2)}) copy-start(f32[64,1024]{1,0:T(8,128)S(1)} %collective-permute-done.a0) | copy-start | bytes 786436
  24.2 40.4 %collective-permute-start.13 = (f32[256,1024]{1,0:T(8,128)S(1)}, f32[256,1024]{1,0:T(8,128)S(1)}, u32[]{:S(2)}, u32[]{:S(2)}) collective-permute-start(f32[256,1024]{1,0:T(8,128)S(1)} %get-tuple-element.44.ko_ref.vo_ref.k_ref.v_ref), channel_id=1, source_target_pairs={{4,0},{8,4},{12,8},{16,12},{20,16},{24,20},{28,24},{32,28},{36,32}... | collective-permute-start | bytes 3145736 | tf_op jit(solution)/shard_map/ppermute | solution.py:501
  30.1 34.5 %collective-permute-start.12 = (f32[256,1024]{1,0:T(8,128)S(1)}, f32[256,1024]{1,0:T(8,128)S(1)}, u32[]{:S(2)}, u32[]{:S(2)}) collective-permute-start(f32[256,1024]{1,0:T(8,128)S(1)} %get-tuple-element.44.ko_ref.vo_ref.k_ref.v_ref), channel_id=1, source_target_pairs={{0,4},{4,8},{8,12},{12,16},{16,20},{20,24},{24,28},{28,32},{32,36}... | collective-permute-start | bytes 3145736 | tf_op jit(solution)/shard_map/ppermute | solution.py:498
  34.7 17.3 %collective-permute-start.4 = (f32[64,1024]{1,0:T(8,128)S(1)}, f32[64,1024]{1,0:T(8,128)S(1)}, u32[]{:S(2)}, u32[]{:S(2)}) collective-permute-start(f32[64,1024]{1,0:T(8,128)S(1)} %shard_map.112.a_ref.a2), channel_id=1, source_target_pairs={{0,8},{4,12},{8,0},{12,4},{16,24},{20,28},{24,16},{28,20},{32,40},... | collective-permute-start | bytes 786440 | tf_op jit(solution)/shard_map/ppermute | solution.py:495
  52.0 0.7 copy-start.2
  52.7 8.9 %collective-permute-start.10 = (f32[32,1024]{1,0:T(8,128)S(1)}, f32[32,1024]{1,0:T(8,128)}, u32[]{:S(2)}, u32[]{:S(2)}) collective-permute-start(f32[32,1024]{1,0:T(8,128)S(1)} %shard_map.113), channel_id=1, source_target_pairs={{0,192},{4,196},{8,200},{12,204},{16,208},{20,212},{24,216},{28,22... | collective-permute-start | bytes 393224 | tf_op jit(solution)/shard_map/ppermute | solution.py:495
  55.5 7.2 %collective-permute-start.9 = (f32[32,1024]{1,0:T(8,128)S(1)}, f32[32,1024]{1,0:T(8,128)}, u32[]{:S(2)}, u32[]{:S(2)}) collective-permute-start(f32[32,1024]{1,0:T(8,128)S(1)} %shard_map.113), channel_id=1, source_target_pairs={{0,128},{4,132},{8,136},{12,140},{16,144},{20,148},{24,152},{28,15... | collective-permute-start | bytes 393224 | tf_op jit(solution)/shard_map/ppermute | solution.py:495
  55.8 7.0 %collective-permute-start.8 = (f32[32,1024]{1,0:T(8,128)S(1)}, f32[32,1024]{1,0:T(8,128)}, u32[]{:S(2)}, u32[]{:S(2)}) collective-permute-start(f32[32,1024]{1,0:T(8,128)S(1)} %shard_map.113), channel_id=1, source_target_pairs={{0,64},{4,68},{8,72},{12,76},{16,80},{20,84},{24,88},{28,92},{32,9... | collective-permute-start | bytes 393224 | tf_op jit(solution)/shard_map/ppermute | solution.py:495
  61.6 9.5 %collective-permute-start.5 = (f32[64,1024]{1,0:T(8,128)}, f32[64,1024]{1,0:T(8,128)S(1)}, u32[]{:S(2)}, u32[]{:S(2)}) collective-permute-start(f32[64,1024]{1,0:T(8,128)} %copy-done.5), channel_id=1, source_target_pairs={{0,4},{4,0},{8,12},{12,8},{16,20},{20,16},{24,28},{28,24},{32,36},... | collective-permute-start | bytes 786440 | tf_op jit(solution)/shard_map/ppermute | solution.py:495
  63.9 15.1 %collective-permute-start.11 = (f32[96,1024]{1,0:T(8,128)S(1)}, f32[96,1024]{1,0:T(8,128)S(1)}, u32[]{:S(2)}, u32[]{:S(2)}) collective-permute-start(f32[96,1024]{1,0:T(8,128)S(1)} %shard_map.114.a6), channel_id=1, source_target_pairs={{0,4},{4,0},{8,12},{12,8},{16,20},{20,16},{24,28},{28,24},{32,36},... | collective-permute-start | bytes 1179656 | tf_op jit(solution)/shard_map/ppermute | solution.py:495
  64.6 18.4 %collective-permute-start.15 = (f32[256,512]{1,0:T(8,128)}, f32[256,512]{1,0:T(8,128)S(1)}, u32[]{:S(2)}, u32[]{:S(2)}) collective-permute-start(f32[256,512]{1,0:T(8,128)} %copy-done.11), channel_id=1, source_target_pairs={{4,0},{8,4},{12,8},{16,12},{20,16},{24,20},{28,24},{32,28},{36,32}... | collective-permute-start | bytes 1572872 | tf_op jit(solution)/shard_map/ppermute | solution.py:501
  66.5 16.5 %collective-permute-start.14 = (f32[256,512]{1,0:T(8,128)}, f32[256,512]{1,0:T(8,128)S(1)}, u32[]{:S(2)}, u32[]{:S(2)}) collective-permute-start(f32[256,512]{1,0:T(8,128)} %copy-done.11), channel_id=1, source_target_pairs={{0,4},{4,8},{8,12},{12,16},{16,20},{20,24},{24,28},{28,32},{32,36}... | collective-permute-start | bytes 1572872 | tf_op jit(solution)/shard_map/ppermute | solution.py:498
  71.0 8.0 %collective-permute-start.6 = (f32[64,1024]{1,0:T(8,128)S(1)}, f32[64,1024]{1,0:T(8,128)S(1)}, u32[]{:S(2)}, u32[]{:S(2)}) collective-permute-start(f32[64,1024]{1,0:T(8,128)S(1)} %shard_map.112.a_ref.a2), channel_id=1, source_target_pairs={{0,4},{4,0},{8,12},{12,8},{16,20},{20,16},{24,28},{28,24},{32,36},... | collective-permute-start | bytes 786440 | tf_op jit(solution)/shard_map/ppermute | solution.py:495
  71.1 7.9 %collective-permute-start.7 = (f32[64,1024]{1,0:T(8,128)}, f32[64,1024]{1,0:T(8,128)S(1)}, u32[]{:S(2)}, u32[]{:S(2)}) collective-permute-start(f32[64,1024]{1,0:T(8,128)} %copy-done.2), channel_id=1, source_target_pairs={{0,4},{4,0},{8,12},{12,8},{16,20},{20,16},{24,28},{28,24},{32,36},... | collective-permute-start | bytes 786440 | tf_op jit(solution)/shard_map/ppermute | solution.py:495
  71.6 1.0 copy-start.12
  72.7 6.4 %copy-start.3 = (f32[64,1024]{1,0:T(8,128)S(1)}, f32[64,1024]{1,0:T(8,128)}, u32[]{:S(2)}) copy-start(f32[64,1024]{1,0:T(8,128)} %copy-done.2) | copy-start | bytes 786436
  72.7 6.4 %copy-start.4 = (f32[256,512]{1,0:T(8,128)S(1)}, f32[256,512]{1,0:T(8,128)}, u32[]{:S(2)}) copy-start(f32[256,512]{1,0:T(8,128)} %up_ref.3) | copy-start | bytes 1572868
  72.7 6.4 %copy-start.6 = (f32[64,1024]{1,0:T(8,128)S(1)}, f32[64,1024]{1,0:T(8,128)}, u32[]{:S(2)}) copy-start(f32[64,1024]{1,0:T(8,128)} %copy-done.5) | copy-start | bytes 786436
  72.7 6.4 %copy-start.10 = (f32[512]{0:T(512)S(1)}, f32[512]{0:T(512)}, u32[]{:S(2)}) copy-start(f32[512]{0:T(512)} %param.11) | copy-start | bytes 6148
  79.0 10.7 %copy-start.1 = (f32[96,1536]{1,0:T(8,128)S(1)}, f32[96,1536]{1,0:T(8,128)}, u32[]{:S(2)}) copy-start(f32[96,1536]{1,0:T(8,128)} %copy-done) | copy-start | bytes 1769476
  83.0 4.0 %collective-permute-start.18 = (f32[8,256]{1,0:T(8,128)S(1)}, f32[8,256]{1,0:T(8,128)S(1)}, u32[]{:S(2)}, u32[]{:S(2)}) collective-permute-start(f32[8,256]{1,0:T(8,128)S(1)} %get-tuple-element.50.s0_ref), channel_id=1, source_target_pairs={{0,3},{1,2},{2,1},{3,0},{4,7},{5,6},{6,5},{7,4},{8,11},{9,10},{10,... | collective-permute-start | bytes 24584 | tf_op jit(solution)/shard_map/ppermute | solution.py:549
  85.8 4.0 %collective-permute-start.17 = (f32[8,256]{1,0:T(8,128)S(1)}, f32[8,256]{1,0:T(8,128)S(1)}, u32[]{:S(2)}, u32[]{:S(2)}) collective-permute-start(f32[8,256]{1,0:T(8,128)S(1)} %get-tuple-element.50.s0_ref), channel_id=1, source_target_pairs={{0,2},{1,3},{2,0},{3,1},{4,6},{5,7},{6,4},{7,5},{8,10},{9,11},{10,... | collective-permute-start | bytes 24584 | tf_op jit(solution)/shard_map/ppermute | solution.py:549
  86.3 3.5 %collective-permute-start.16 = (f32[8,256]{1,0:T(8,128)S(1)}, f32[8,256]{1,0:T(8,128)S(1)}, u32[]{:S(2)}, u32[]{:S(2)}) collective-permute-start(f32[8,256]{1,0:T(8,128)S(1)} %get-tuple-element.50.s0_ref), channel_id=1, source_target_pairs={{0,1},{1,0},{2,3},{3,2},{4,5},{5,4},{6,7},{7,6},{8,9},{9,8},{10,11... | collective-permute-start | bytes 24584 | tf_op jit(solution)/shard_map/ppermute | solution.py:549
  91.1 11.5 %collective-permute-start.19 = (f32[64,1152]{1,0:T(8,128)S(1)}, f32[64,1152]{1,0:T(8,128)S(1)}, u32[]{:S(2)}, u32[]{:S(2)}) collective-permute-start(f32[64,1152]{1,0:T(8,128)S(1)} %get-tuple-element.54.first_ref), channel_id=1, source_target_pairs={{0,8},{4,12},{8,0},{12,4},{16,24},{20,28},{24,16},{28,20},{32,40},... | collective-permute-start | bytes 884744 | tf_op jit(solution)/shard_map/ppermute | solution.py:495
  91.1 15.2 %collective-permute-start.22 = (f32[20,1152]{1,0:T(8,128)S(1)}, f32[20,1152]{1,0:T(8,128)S(1)}, u32[]{:S(2)}, u32[]{:S(2)}) collective-permute-start(f32[20,1152]{1,0:T(8,128)S(1)} %get-tuple-element.59.rest_ref.own_ref), channel_id=1, source_target_pairs={{0,48},{4,52},{8,56},{12,60},{16,32},{20,36},{24,40},{28,44},{32,1... | collective-permute-start | bytes 276488 | tf_op jit(solution)/shard_map/ppermute | solution.py:495
  94.1 12.3 %collective-permute-start.21 = (f32[20,1152]{1,0:T(8,128)S(1)}, f32[20,1152]{1,0:T(8,128)S(1)}, u32[]{:S(2)}, u32[]{:S(2)}) collective-permute-start(f32[20,1152]{1,0:T(8,128)S(1)} %get-tuple-element.59.rest_ref.own_ref), channel_id=1, source_target_pairs={{0,32},{4,36},{8,40},{12,44},{16,48},{20,52},{24,56},{28,60},{32,0... | collective-permute-start | bytes 276488 | tf_op jit(solution)/shard_map/ppermute | solution.py:495
  95.8 10.5 %collective-permute-start.20 = (f32[20,1152]{1,0:T(8,128)S(1)}, f32[20,1152]{1,0:T(8,128)S(1)}, u32[]{:S(2)}, u32[]{:S(2)}) collective-permute-start(f32[20,1152]{1,0:T(8,128)S(1)} %get-tuple-element.59.rest_ref.own_ref), channel_id=1, source_target_pairs={{0,16},{4,20},{8,24},{12,28},{16,0},{20,4},{24,8},{28,12},{32,48},... | collective-permute-start | bytes 276488 | tf_op jit(solution)/shard_map/ppermute | solution.py:495
  106.4 33.3 %copy-start.13 = (f32[256,512]{1,0:T(8,128)S(1)}, f32[256,512]{1,0:T(8,128)}, u32[]{:S(2)}) copy-start(f32[256,512]{1,0:T(8,128)} %copy-done.11) | copy-start | bytes 1572868
  106.4 32.9 %collective-permute-start.32 = (f32[264,512]{1,0:T(8,128)S(1)}, f32[264,512]{1,0:T(8,128)S(1)}, u32[]{:S(2)}, u32[]{:S(2)}) collective-permute-start(f32[264,512]{1,0:T(8,128)S(1)} %get-tuple-element.63.dout_ref.do_ref.to_ref), channel_id=1, source_target_pairs={{4,0},{8,4},{12,8},{16,12},{20,16},{24,20},{28,24},{32,28},{36,32}... | collective-permute-start | bytes 1622024 | tf_op jit(solution)/shard_map/ppermute | solution.py:501
  112.5 27.3 %collective-permute-start.31 = (f32[264,512]{1,0:T(8,128)S(1)}, f32[264,512]{1,0:T(8,128)S(1)}, u32[]{:S(2)}, u32[]{:S(2)}) collective-permute-start(f32[264,512]{1,0:T(8,128)S(1)} %get-tuple-element.63.dout_ref.do_ref.to_ref), channel_id=1, source_target_pairs={{0,4},{4,8},{8,12},{12,16},{16,20},{20,24},{24,28},{28,32},{32,36}... | collective-permute-start | bytes 1622024 | tf_op jit(solution)/shard_map/ppermute | solution.py:498
  114.8 12.6 %collective-permute-start.23 = (f32[64,1152]{1,0:T(8,128)S(1)}, f32[64,1152]{1,0:T(8,128)S(1)}, u32[]{:S(2)}, u32[]{:S(2)}) collective-permute-start(f32[64,1152]{1,0:T(8,128)S(1)} %shard_map.120.a_ref.a2), channel_id=1, source_target_pairs={{0,8},{4,12},{8,0},{12,4},{16,24},{20,28},{24,16},{28,20},{32,40},... | collective-permute-start | bytes 884744 | tf_op jit(solution)/shard_map/ppermute | solution.py:495
  127.4 10.1 %collective-permute-start.29 = (f32[32,1152]{1,0:T(8,128)S(1)}, f32[32,1152]{1,0:T(8,128)S(1)}, u32[]{:S(2)}, u32[]{:S(2)}) collective-permute-start(f32[32,1152]{1,0:T(8,128)S(1)} %shard_map.121), channel_id=1, source_target_pairs={{0,192},{4,196},{8,200},{12,204},{16,208},{20,212},{24,216},{28,22... | collective-permute-start | bytes 442376 | tf_op jit(solution)/shard_map/ppermute | solution.py:495
  130.7 7.2 %collective-permute-start.28 = (f32[32,1152]{1,0:T(8,128)S(1)}, f32[32,1152]{1,0:T(8,128)S(1)}, u32[]{:S(2)}, u32[]{:S(2)}) collective-permute-start(f32[32,1152]{1,0:T(8,128)S(1)} %shard_map.121), channel_id=1, source_target_pairs={{0,128},{4,132},{8,136},{12,140},{16,144},{20,148},{24,152},{28,15... | collective-permute-start | bytes 442376 | tf_op jit(solution)/shard_map/ppermute | solution.py:495
  130.7 8.2 %collective-permute-start.27 = (f32[32,1152]{1,0:T(8,128)S(1)}, f32[32,1152]{1,0:T(8,128)S(1)}, u32[]{:S(2)}, u32[]{:S(2)}) collective-permute-start(f32[32,1152]{1,0:T(8,128)S(1)} %shard_map.121), channel_id=1, source_target_pairs={{0,64},{4,68},{8,72},{12,76},{16,80},{20,84},{24,88},{28,92},{32,9... | collective-permute-start | bytes 442376 | tf_op jit(solution)/shard_map/ppermute | solution.py:495
  137.5 9.6 %collective-permute-start.24 = (f32[64,1152]{1,0:T(8,128)S(1)}, f32[64,1152]{1,0:T(8,128)S(1)}, u32[]{:S(2)}, u32[]{:S(2)}) collective-permute-start(f32[64,1152]{1,0:T(8,128)S(1)} %collective-permute-done.19.a0), channel_id=1, source_target_pairs={{0,4},{4,0},{8,12},{12,8},{16,20},{20,16},{24,28},{28,24},{32,36},... | collective-permute-start | bytes 884744 | tf_op jit(solution)/shard_map/ppermute | solution.py:495
  137.8 9.3 %collective-permute-start.25 = (f32[64,1152]{1,0:T(8,128)S(1)}, f32[64,1152]{1,0:T(8,128)S(1)}, u32[]{:S(2)}, u32[]{:S(2)}) collective-permute-start(f32[64,1152]{1,0:T(8,128)S(1)} %shard_map.120.a_ref.a2), channel_id=1, source_target_pairs={{0,4},{4,0},{8,12},{12,8},{16,20},{20,16},{24,28},{28,24},{32,36},... | collective-permute-start | bytes 884744 | tf_op jit(solution)/shard_map/ppermute | solution.py:495
  138.9 8.2 %collective-permute-start.26 = (f32[64,1152]{1,0:T(8,128)S(1)}, f32[64,1152]{1,0:T(8,128)S(1)}, u32[]{:S(2)}, u32[]{:S(2)}) collective-permute-start(f32[64,1152]{1,0:T(8,128)S(1)} %collective-permute-done.23.b_ref.a3), channel_id=1, source_target_pairs={{0,4},{4,0},{8,12},{12,8},{16,20},{20,16},{24,28},{28,24},{32,36},... | collective-permute-start | bytes 884744 | tf_op jit(solution)/shard_map/ppermute | solution.py:495
  139.3 7.8 %collective-permute-start.30 = (f32[96,1152]{1,0:T(8,128)S(1)}, f32[96,1152]{1,0:T(8,128)S(1)}, u32[]{:S(2)}, u32[]{:S(2)}) collective-permute-start(f32[96,1152]{1,0:T(8,128)S(1)} %shard_map.122.a6), channel_id=1, source_target_pairs={{0,4},{4,0},{8,12},{12,8},{16,20},{20,16},{24,28},{28,24},{32,36},... | collective-permute-start | bytes 1327112 | tf_op jit(solution)/shard_map/ppermute | solution.py:495
where the time goes:
time: 152 us
  starting transfers between devices  58 us (38%)
  waiting for transfers between devices  50 us (33%)
  Pallas kernels  34.6 us (23%)
  local copies, waits for them, and re-layouts  6.48 us (4%)
  other arithmetic  1.55 us (1%)
    ppermute x24, waiting for transfers between devices, exchange(): return lax.ppermute(array, 'seq', [(i, i ^ mask) for i in range(count)])  46.7 us
    ppermute x24, starting transfers between devices, exchange(): return lax.ppermute(array, 'seq', [(i, i ^ mask) for i in range(count)])  30 us
    pallas_call x10, Pallas kernels, whole_call(): pl.pallas_call(kernel, out_shape=outs, in_specs=[spec] * len(operands), o...  14.5 us
    ppermute x3, starting transfers between devices, from_after(): return lax.ppermute(array, 'seq', [(i + 1, i) for i in range(count - 1)])  13.9 us
    ppermute x3, starting transfers between devices, from_before(): return lax.ppermute(array, 'seq', [(i, i + 1) for i in range(count - 1)])  10.5 us
    pallas_call x1, Pallas kernels, near_key(): pl.pallas_call(near_key_kernel, grid=(HEADS,), out_shape=[f32(BLOCK, WIDT...  7.35 us
    unnamed x30, local copies, waits for them, and re-layouts  6.48 us
    pallas_call x1, Pallas kernels, near_forward(): pl.pallas_call(near_forward_kernel, grid=(HEADS,), out_shape=[f32(HEADS,...  6.36 us
  transfers between devices with their start and end apart: 33, of which 11 were waited for; matrix products, arithmetic and copies ran while one was open for 1% of the time, Pallas kernels for 19%

commit v1 on v0

v1 whole, which is shorter than its diff:
```python
import math

import jax
import jax.numpy as jnp
import numpy as np
from jax import lax
from jax.experimental import pallas as pl
from jax.experimental.pallas import tpu as pltpu
from jax.sharding import PartitionSpec as P

DHEAD = 128
BLOCK = 256
FEAT = 2048
HEADS = 4
WIDTH = HEADS * DHEAD
NEGATIVE_FILL = -1e30
FLOOR = -1e25
EPSILON = 1e-06
INV_ROOT = 1.0 / math.sqrt(DHEAD)
LN4 = math.log(4.0)
VMEM_BYTES = 24 * 1024 * 1024
POOL_VMEM_BYTES = 56 * 1024 * 1024

OWN = 96
LEVEL_ROWS = ((0, 64), (64, 80), (80, 84))
FAR = 512
KV = 2 * WIDTH
GRAD = 2 * WIDTH + DHEAD

QUAD = (4, 8, 12)
PLANES = (16, 32, 48)
HALF2_BLOCKS = QUAD + tuple(2 ^ o for o in QUAD)
QUARTER3_BLOCKS = tuple(y ^ o for o in (0,) + QUAD for y in PLANES)
HALF3_BLOCKS = QUARTER3_BLOCKS + tuple(2 ^ o for o in QUARTER3_BLOCKS)
SLOTS = (
    ((2, 3), 64),
    (HALF2_BLOCKS + tuple(1 ^ o for o in HALF2_BLOCKS), 16),
    (HALF3_BLOCKS + tuple(1 ^ o for o in HALF3_BLOCKS), 4),
)


def slot_table():
    offset = np.concatenate([np.repeat(np.array(blocks, np.int32), rows) for blocks, rows in SLOTS])
    level = np.concatenate([np.full(len(blocks) * rows, n + 1, np.int32) for n, (blocks, rows) in enumerate(SLOTS)])
    table = np.zeros((8, FAR), np.int32)
    table[0], table[1] = offset, level
    return table


def split3(x):
    high = x.astype(jnp.bfloat16)
    rest = x - high.astype(jnp.float32)
    middle = rest.astype(jnp.bfloat16)
    return high, middle, (rest - middle.astype(jnp.float32)).astype(jnp.bfloat16)


def dot(a, b, dims):
    return lax.dot_general(a, b, (dims, ((), ())), preferred_element_type=jnp.float32)


def nt3(a, b):
    a1, a2, a3 = split3(a)
    b1, b2, b3 = split3(b)
    left = jnp.concatenate([a1, a2, a1, a2, a1, a3], axis=1)
    right = jnp.concatenate([b1, b1, b2, b2, b3, b1], axis=1)
    return dot(left, right, ((1,), (1,)))


def nn3(a, b):
    a1, a2, a3 = split3(a)
    b1, b2, b3 = split3(b)
    right = jnp.concatenate([b1, b2], axis=1)
    main = dot(jnp.concatenate([a1, a2], axis=1), jnp.concatenate([right, right], axis=0), ((1,), (0,)))
    small = dot(jnp.concatenate([a1, a3], axis=1), jnp.concatenate([b3, b1], axis=0), ((1,), (0,)))
    return main[:, :DHEAD] + (main[:, DHEAD:] + small)


def cols(h, base=0):
    return slice(base + h * DHEAD, base + (h + 1) * DHEAD)


def quarters(ref, value):
    rows = value.shape[0] // 4
    ref[pl.ds(0, 4 * rows), :] = value
    return [ref[pl.ds(j, rows, stride=4), :] for j in range(4)]


def mean4(ref, value):
    parts = quarters(ref, value)
    return ((parts[0] + parts[1]) + (parts[2] + parts[3])) * 0.25


def expand(ref, value):
    rows = value.shape[0]
    for j in range(4):
        ref[pl.ds(j, rows, stride=4), :] = value
    return ref[pl.ds(0, 4 * rows), :]


def expand_levels(ref, value, scales):
    total = value[80:84] * scales[2]
    total = value[64:80] * scales[1] + expand(ref, total)
    total = value[0:64] * scales[0] + expand(ref, total)
    return expand(ref, total)


def lane_index(rows):
    return lax.broadcasted_iota(jnp.int32, (rows, DHEAD), 1)


def wide(column):
    return jnp.broadcast_to(column, (column.shape[0], DHEAD))


def gathered(refs, lanes):
    l1a, l2a, l2b, core1, core2 = refs
    pieces = [l1a[:, lanes], core1[0:64, lanes]]
    pieces += [l2a[0:48, lanes], l2b[0:48, lanes], core1[64:112, lanes], core2[0:48, lanes]]
    pieces += [l2a[48:96, lanes], l2b[48:96, lanes], core1[112:160, lanes], core2[48:96, lanes]]
    return jnp.concatenate(pieces, axis=0)


def pool_kernel(
    table_ref, k_ref, v_ref, q_ref,
    own_ref, first_ref, second_ref, third_ref, trio_ref, bias_ref, edge_ref,
    e0_ref, e1_ref, e2_ref, in_ref, sems, out_sems,
):
    copies = []
    for i, ref in enumerate((k_ref, v_ref, q_ref)):
        for j in range(4):
            rows = pl.ds(64 * j, 64)
            copies.append(pltpu.make_async_copy(ref.at[rows, :], in_ref.at[i, rows, :], sems.at[i, j]))
    for copy in copies:
        copy.start()
    place = lax.axis_index("seq")
    last = lax.axis_size("seq") - 1
    offset = table_ref[0:1, :]
    level = table_ref[1:2, :]
    row = lax.broadcasted_iota(jnp.int32, (OWN, FAR), 0)
    mine = jnp.where(row < 64, 1, jnp.where(row < 80, 2, jnp.where(row < 84, 3, 0)))
    allowed = (jnp.abs((offset ^ place) - place) > 1) & (level == mine)
    bias_ref[...] = jnp.where(allowed, level.astype(jnp.float32) * LN4, NEGATIVE_FILL)
    alone = (place == 0) | (place == last)
    edge_ref[...] = jnp.full((8, BLOCK), jnp.where(alone, NEGATIVE_FILL, 0.0), jnp.float32)
    own_ref[84:96, :] = jnp.zeros((12, 3 * WIDTH), jnp.float32)
    stores = []
    for part in range(3):
        for copy in copies[4 * part : 4 * part + 4]:
            copy.wait()
        lanes = pl.ds(part * WIDTH, WIDTH)
        stores.append(pltpu.make_async_copy(in_ref.at[part], trio_ref.at[:, lanes], out_sems.at[part]))
        stores[-1].start()
        for h in range(HEADS):
            dst = cols(h, part * WIDTH)
            value = in_ref[part, :, cols(h)]
            one = mean4(e0_ref.at[(part * HEADS + h) % 2], value)
            two = mean4(e1_ref, one)
            three = mean4(e2_ref, two)
            own_ref[0:64, dst] = one
            own_ref[64:80, dst] = two
            own_ref[80:84, dst] = three
            if part < 2:
                first_ref[:, dst] = one
                second_ref[:, dst] = two
                third_ref[:, dst] = three
    for store in stores:
        store.wait()


def pack_kernel(second_ref, a_ref, b_ref, c_ref, out_ref):
    out_ref[0:16, :] = second_ref[...]
    out_ref[16:20, :] = a_ref[...]
    out_ref[20:24, :] = b_ref[...]
    out_ref[24:28, :] = c_ref[...]


def merge_kernel(first_ref, own_ref, a_ref, b_ref, c_ref, out_ref, bundle_ref):
    bundle_ref[0:64, :] = first_ref[...]
    pieces = [(16 * i, ref[0:16, :]) for i, ref in enumerate((a_ref, b_ref, c_ref))]
    pieces += [(48 + 12 * i, ref[16:28, :]) for i, ref in enumerate((own_ref, a_ref, b_ref, c_ref))]
    for start, piece in pieces:
        stop = start + piece.shape[0]
        out_ref[start:stop, :] = piece
        bundle_ref[64 + start : 64 + stop, :] = piece


def near_state(scores, values, w_ref, peak_ref, mass_ref, sum_ref):
    peak = jnp.maximum(jnp.max(scores, axis=1, keepdims=True), FLOOR)
    weights = jnp.exp(scores - peak)
    w_ref[0] = weights
    peak_ref[...] = wide(peak)
    mass_ref[...] = wide(jnp.sum(weights, axis=1, keepdims=True))
    sum_ref[...] = nn3(weights, values)


def near_inner_kernel(q_ref, ko_ref, ki_ref, vo_ref, vi_ref, *outs):
    keys = jnp.concatenate([ko_ref[...], ki_ref[...]], axis=0)
    values = jnp.concatenate([vo_ref[...], vi_ref[...]], axis=0)
    near_state(nt3(q_ref[...], keys) * INV_ROOT, values, *outs)


def near_outer_kernel(edge_ref, q_ref, k_ref, v_ref, *outs):
    near_state(nt3(q_ref[...], k_ref[...]) * INV_ROOT + edge_ref[0:1, :], v_ref[...], *outs)


def merge(one, two):
    peak = jnp.maximum(one[0], two[0])
    left = jnp.exp(one[0] - peak)
    right = jnp.exp(two[0] - peak)
    return peak, left * one[1] + right * two[1], left * one[2] + right * two[2]


def far_forward_kernel(
    bias_ref, own_ref, a0, a1, a2, a3, a4,
    peak0_ref, mass0_ref, sum0_ref, peak1_ref, mass1_ref, sum1_ref, up_ref, gain_ref,
    att_ref, lse_ref, stat_ref,
    e0_ref, e1_ref, e2_ref, square_ref, cross_ref,
):
    far = (a0, a1, a2, a3, a4)
    bias = bias_ref[...]
    for h in range(HEADS):
        k = cols(h)
        v = cols(h, WIDTH)
        scores = nt3(own_ref[:, cols(h, 2 * WIDTH)], gathered(far, k)) * INV_ROOT + bias
        peak = jnp.maximum(jnp.max(scores, axis=1, keepdims=True), FLOOR)
        weights = jnp.exp(scores - peak)
        mass = jnp.sum(weights, axis=1, keepdims=True)
        levels = (wide(peak), wide(mass), nn3(weights, gathered(far, v)))
        state = tuple(x[80:84] for x in levels)
        for start, stop in (LEVEL_ROWS[1], LEVEL_ROWS[0]):
            state = tuple(expand(ref.at[h % 2], x) for ref, x in zip((e0_ref, e1_ref, e2_ref), state))
            state = merge(state, tuple(x[start:stop] for x in levels))
        state = tuple(expand(ref.at[h % 2], x) for ref, x in zip((e0_ref, e1_ref, e2_ref), state))
        near = merge(
            (peak0_ref[:, k], mass0_ref[:, k], sum0_ref[:, k]), (peak1_ref[:, k], mass1_ref[:, k], sum1_ref[:, k])
        )
        state = merge(state, near)
        attention = state[2] / state[1]
        att_ref[:, k] = attention
        lse_ref[:, k] = state[0] + jnp.log(state[1])
        square = attention * attention
        cross = up_ref[:, k] * gain_ref[0:1, k] * attention
        if h == 0:
            square_ref[...] = square
            cross_ref[...] = cross
        else:
            square_ref[...] += square
            cross_ref[...] += cross
    square = wide(jnp.sum(square_ref[...], axis=1, keepdims=True))
    cross = wide(jnp.sum(cross_ref[...], axis=1, keepdims=True))
    packed = jnp.where(lane_index(BLOCK) == 0, square, cross)
    stat_ref[...] = jnp.transpose(packed)[0:8, :]


def pooled_cotangent(scratch, lows, dots, grads):
    lows, dots, grads = (quarters(ref, x) for ref, x in zip(scratch, (lows, dots, grads)))
    low = jnp.minimum(jnp.minimum(lows[0], lows[1]), jnp.minimum(lows[2], lows[3]))
    scale = [jnp.exp(low - x) for x in lows]
    total = scale[0] * dots[0]
    grad = scale[0] * grads[0]
    for j in range(1, 4):
        total = total + scale[j] * dots[j]
        grad = grad + scale[j] * grads[j]
    return low, total, grad


def cotangent_kernel(
    s0_ref, s1_ref, s2_ref, s3_ref, own_ref, att_ref, lse_ref, up_ref, gain_ref,
    out_ref, dout_ref, delta_ref, first_ref, second_ref, third_ref,
    e0_ref, e1_ref, e2_ref,
):
    total = (s0_ref[...] + s1_ref[...]) + (s2_ref[...] + s3_ref[...])
    square = jnp.transpose(jnp.broadcast_to(total[0:1, :], (DHEAD, BLOCK)))
    cross = jnp.transpose(jnp.broadcast_to(total[1:2, :], (DHEAD, BLOCK)))
    inverse = lax.rsqrt(square / FEAT + EPSILON)
    pull = inverse * inverse * inverse * cross / FEAT
    lane = lane_index(BLOCK)
    packed = jnp.zeros((BLOCK, DHEAD), jnp.float32)
    stats = [jnp.zeros((rows, DHEAD), jnp.float32) for rows in (64, 16, 4)]
    first_ref[:, WIDTH:KV] = own_ref[0:64, KV:]
    second_ref[:, WIDTH:KV] = own_ref[64:80, KV:]
    third_ref[:, WIDTH:KV] = own_ref[80:84, KV:]
    for h in range(HEADS):
        k = cols(h)
        attention = att_ref[:, k]
        out_ref[:, k] = attention * inverse * gain_ref[0:1, k]
        d_out = inverse * (up_ref[:, k] * gain_ref[0:1, k]) - attention * pull
        dout_ref[0:BLOCK, k] = d_out
        delta = wide(jnp.sum(d_out * attention, axis=1, keepdims=True))
        delta_ref[:, k] = delta
        packed = jnp.where(lane == h, lse_ref[:, k], packed)
        packed = jnp.where(lane == HEADS + h, delta, packed)
        level = (lse_ref[:, k], delta, d_out)
        for n, ref in enumerate((first_ref, second_ref, third_ref)):
            level = pooled_cotangent([e.at[h % 2] for e in (e0_ref, e1_ref, e2_ref)], *level)
            rows = level[0].shape[0]
            ref[:, k] = level[2]
            short = lane[0:rows]
            stats[n] = jnp.where(short == h, level[0], jnp.where(short == HEADS + h, level[1], stats[n]))
    first_ref[:, KV:] = stats[0]
    second_ref[:, KV:] = stats[1]
    third_ref[:, KV:] = stats[2]
    dout_ref[BLOCK:, 0:256] = jnp.transpose(packed)[0:8, :]
    dout_ref[BLOCK:, 256:] = jnp.zeros((8, 256), jnp.float32)


def near_query_kernel(
    w0_ref, w1_ref, peak0_ref, peak1_ref, lse_ref, delta_ref, dout_ref,
    k0_ref, k1_ref, k2_ref, v0_ref, v1_ref, v2_ref, dq_ref,
):
    keys = jnp.concatenate([k0_ref[...], k1_ref[...], k2_ref[...]], axis=0)
    values = jnp.concatenate([v0_ref[...], v1_ref[...], v2_ref[...]], axis=0)
    lse = lse_ref[:, 0:1]
    inner = w0_ref[0] * jnp.exp(peak0_ref[:, 0:1] - lse)
    outer = w1_ref[0] * jnp.exp(peak1_ref[:, 0:1] - lse)
    weights = jnp.concatenate([inner, outer], axis=1)
    d_scores = weights * (nt3(dout_ref[...], values) - delta_ref[:, 0:1])
    dq_ref[...] = nn3(d_scores, keys) * INV_ROOT


def far_query_kernel(
    bias_ref, own_ref, a0, a1, a2, a3, a4, first_ref, second_ref, third_ref, near_ref, dq_ref, e0_ref
):
    far = (a0, a1, a2, a3, a4)
    bias = bias_ref[...]

    def grads(lanes):
        fill = jnp.zeros((12, DHEAD), jnp.float32)
        return jnp.concatenate([first_ref[:, lanes], second_ref[:, lanes], third_ref[:, lanes], fill], axis=0)

    stats = grads(slice(KV, GRAD))
    for h in range(HEADS):
        k = cols(h)
        keys = gathered(far, k)
        scores = nt3(own_ref[:, cols(h, 2 * WIDTH)], keys) * INV_ROOT + bias
        weights = jnp.exp(scores - stats[:, h : h + 1])
        d_probs = nt3(grads(k), gathered(far, cols(h, WIDTH)))
        d_scores = weights * (d_probs - stats[:, HEADS + h : HEADS + h + 1])
        grad = nn3(d_scores, keys)
        scales = [INV_ROOT / 4**n for n in (1, 2, 3)]
        dq_ref[:, k] = near_ref[:, k] + expand_levels(e0_ref.at[h % 2], grad, scales)


def near_key_parts(k_ref, v_ref, queries, grads, stats):
    h = pl.program_id(0)
    low = jnp.concatenate([ref[pl.ds(h, 1), :] for ref in stats], axis=1)
    total = jnp.concatenate([ref[pl.ds(h + HEADS, 1), :] for ref in stats], axis=1)
    weights = jnp.exp(nt3(k_ref[...], queries) * INV_ROOT - low)
    d_scores = weights * (nt3(v_ref[...], grads) - total)
    return nn3(d_scores, queries) * INV_ROOT, nn3(weights, grads)


def inner_key_kernel(k_ref, v_ref, q0_ref, q1_ref, d0_ref, d1_ref, t0_ref, t1_ref, dk_ref, dv_ref):
    queries = jnp.concatenate([q0_ref[...], q1_ref[...]], axis=0)
    grads = jnp.concatenate([d0_ref[...], d1_ref[...]], axis=0)
    dk_ref[...], dv_ref[...] = near_key_parts(k_ref, v_ref, queries, grads, (t0_ref, t1_ref))


def outer_key_kernel(k_ref, v_ref, q_ref, d_ref, t_ref, dk_in_ref, dv_in_ref, dk_ref, dv_ref):
    d_keys, d_values = near_key_parts(k_ref, v_ref, q_ref[...], d_ref[...], (t_ref,))
    dk_ref[...] = dk_in_ref[...] + d_keys
    dv_ref[...] = dv_in_ref[...] + d_values


def far_key_kernel(
    bias_ref, own_ref, a0, a1, a2, a3, a4, dk_in_ref, dv_in_ref, dk_ref, dv_ref, e0_ref, e1_ref
):
    far = (a0, a1, a2, a3, a4)
    bias = bias_ref[...]
    stats = jnp.transpose(gathered(far, slice(KV, GRAD)))[0:8, :]
    for h in range(HEADS):
        k = cols(h)
        queries = gathered(far, cols(h, WIDTH))
        grads = gathered(far, k)
        scores = nt3(own_ref[:, k], queries) * INV_ROOT + bias
        weights = jnp.exp(scores - stats[h : h + 1, :])
        d_scores = weights * (nt3(own_ref[:, cols(h, WIDTH)], grads) - stats[HEADS + h : HEADS + h + 1, :])
        scales = [1.0 / 4**n for n in (1, 2, 3)]
        d_keys = nn3(d_scores, queries) * INV_ROOT
        dk_ref[:, k] = dk_in_ref[:, k] + expand_levels(e0_ref.at[h % 2], d_keys, scales)
        dv_ref[:, k] = dv_in_ref[:, k] + expand_levels(e1_ref.at[h % 2], nn3(weights, grads), scales)


def f32(*shape):
    return jax.ShapeDtypeStruct(shape, jnp.float32)


def params():
    return pltpu.CompilerParams(vmem_limit_bytes=VMEM_BYTES)


def cost(flops, size):
    return pl.CostEstimate(flops=int(flops), bytes_accessed=int(size), transcendentals=0)


def whole_call(kernel, outs, scratch, flops, size, *operands):
    spec = pl.BlockSpec(memory_space=pltpu.VMEM)
    return pl.pallas_call(
        kernel,
        out_shape=outs,
        in_specs=[spec] * len(operands),
        out_specs=[spec] * len(outs),
        scratch_shapes=[pltpu.VMEM(shape, jnp.float32) for shape in scratch],
        compiler_params=params(),
        cost_estimate=cost(flops, size),
    )(*operands)


BLOCK_FLOPS = 2.0 * BLOCK * BLOCK * DHEAD * HEADS * 6


def column_at(first):
    return pl.BlockSpec((BLOCK, DHEAD), lambda h: (0, first + h))


def slab(blocks):
    return pl.BlockSpec((1, BLOCK, blocks * BLOCK), lambda h: (h, 0, 0))


def head_call(kernel, outs, out_specs, in_specs, blocks, *operands):
    return pl.pallas_call(
        kernel,
        grid=(HEADS,),
        out_shape=outs,
        in_specs=in_specs,
        out_specs=out_specs,
        compiler_params=params(),
        cost_estimate=cost(blocks * BLOCK_FLOPS, 4e6),
    )(*operands)


def near_inner(trio, inn):
    k, v, q = column_at(0), column_at(HEADS), column_at(2 * HEADS)
    outs = [f32(HEADS, BLOCK, 2 * BLOCK)] + [f32(BLOCK, WIDTH)] * 3
    return head_call(near_inner_kernel, outs, [slab(2), k, k, k], [q, k, k, v, v], 4, trio, trio, inn, trio, inn)


def near_outer(edge, trio, out):
    k, v, q = column_at(0), column_at(HEADS), column_at(2 * HEADS)
    outs = [f32(HEADS, BLOCK, BLOCK)] + [f32(BLOCK, WIDTH)] * 3
    edge_spec = pl.BlockSpec((8, BLOCK), lambda h: (0, 0))
    return head_call(near_outer_kernel, outs, [slab(1), k, k, k], [edge_spec, q, k, v], 2, edge, trio, out, out)


def near_query(w0, w1, peak0, peak1, lse, delta, d_out, trio, inn, out):
    k, v = column_at(0), column_at(HEADS)
    specs = [slab(2), slab(1)] + [k] * 8 + [v] * 3
    return head_call(
        near_query_kernel, f32(BLOCK, WIDTH), k, specs, 6,
        w0, w1, peak0, peak1, lse, delta, d_out, trio, inn, out, trio, inn, out,
    )


def stat_rows():
    return pl.BlockSpec((8, 256), lambda h: (BLOCK // 8, 0))


def inner_key(trio, inn, d_out, d_in):
    k, v, q, t = column_at(0), column_at(HEADS), column_at(2 * HEADS), stat_rows()
    return head_call(
        inner_key_kernel, [f32(BLOCK, WIDTH)] * 2, [k, k], [k, v, q, q, k, k, t, t], 8,
        trio, trio, trio, inn, d_out, d_in, d_out, d_in,
    )


def outer_key(trio, out, d_far, dk, dv):
    k, v, q, t = column_at(0), column_at(HEADS), column_at(2 * HEADS), stat_rows()
    return head_call(
        outer_key_kernel, [f32(BLOCK, WIDTH)] * 2, [k, k], [k, v, q, k, t, k, k], 4,
        trio, trio, out, d_far, d_far, dk, dv,
    )


def pool(key, value, query):
    vmem = pl.BlockSpec(memory_space=pltpu.VMEM)
    hbm = pl.BlockSpec(memory_space=pltpu.HBM)
    return pl.pallas_call(
        pool_kernel,
        out_shape=[
            f32(OWN, 3 * WIDTH), f32(64, KV), f32(16, KV), f32(4, KV), f32(BLOCK, 3 * WIDTH), f32(OWN, FAR), f32(8, BLOCK),
        ],
        in_specs=[vmem] + [hbm] * 3,
        out_specs=[vmem] * 4 + [hbm] + [vmem] * 2,
        scratch_shapes=[
            pltpu.VMEM((2, BLOCK, DHEAD), jnp.float32),
            pltpu.VMEM((64, DHEAD), jnp.float32),
            pltpu.VMEM((16, DHEAD), jnp.float32),
            pltpu.VMEM((3, BLOCK, WIDTH), jnp.float32),
            pltpu.SemaphoreType.DMA((3, 4)),
            pltpu.SemaphoreType.DMA((3,)),
        ],
        compiler_params=pltpu.CompilerParams(vmem_limit_bytes=POOL_VMEM_BYTES),
        cost_estimate=cost(1e6, 2e6),
    )(jnp.asarray(slot_table()), key, value, query)


def far_forward(bias, own, far, inner, outer, upstream, gain):
    return whole_call(
        far_forward_kernel,
        [f32(BLOCK, WIDTH), f32(BLOCK, WIDTH), f32(8, 256)],
        [(2, BLOCK, DHEAD)] * 3 + [(BLOCK, DHEAD)] * 2,
        BLOCK_FLOPS,
        8e6,
        bias, own, *far, *inner, *outer, upstream, gain,
    )


def cotangent(stats, others, own, attention, lse, upstream, gain):
    return whole_call(
        cotangent_kernel,
        [f32(BLOCK, WIDTH), f32(BLOCK + 8, WIDTH), f32(BLOCK, WIDTH), f32(64, GRAD), f32(16, GRAD), f32(4, GRAD)],
        [(2, BLOCK, DHEAD)] * 3,
        1e6,
        4e6,
        stats, *others, own, attention, lse, upstream, gain,
    )


def far_query(bias, own, far, first, second, third, near):
    (grad,) = whole_call(
        far_query_kernel,
        [f32(BLOCK, WIDTH)],
        [(2, BLOCK, DHEAD)],
        BLOCK_FLOPS,
        6e6,
        bias, own, *far, first, second, third, near,
    )
    return grad


def far_key(bias, own, grads, near_dk, near_dv):
    return whole_call(
        far_key_kernel,
        [f32(BLOCK, WIDTH)] * 2,
        [(2, BLOCK, DHEAD)] * 2,
        BLOCK_FLOPS,
        6e6,
        bias, own, *grads, near_dk, near_dv,
    )


def body(query, key, value, norm_gain, upstream):
    count = lax.axis_size("seq")
    head_count = lax.axis_size("head")

    def exchange(array, mask):
        return lax.ppermute(array, "seq", [(i, i ^ mask) for i in range(count)])

    def exchange_outer(array):
        pairs = [(i, i + 1 if i % 2 else i - 1) for i in range(1, count - 1)]
        return lax.ppermute(array, "seq", pairs)

    def after(array, *tokens):
        return lax.optimization_barrier((array,) + tokens)[0]

    def packed(second, thirds):
        return whole_call(pack_kernel, [f32(28, second.shape[1])], [], 1e4, 1e5, second, *thirds)[0]

    def merged(first, pack, quads):
        width = first.shape[1]
        return whole_call(merge_kernel, [f32(96, width), f32(160, width)], [], 1e4, 1e5, first, pack, *quads)

    gain = norm_gain.reshape(1, WIDTH)
    own, first, second, third, trio, bias, edge = pool(key, value, query)

    planes = [exchange(third, mask) for mask in PLANES]
    l1a = exchange(first, 2)
    inn = exchange(trio, 1)
    pack = packed(second, planes)
    quads = [exchange(pack, mask) for mask in QUAD]
    out = exchange_outer(after(trio, pack))
    w0, *inner = near_inner(trio, inn)
    l2a, bundle = merged(l1a, after(pack, w0), quads)
    l2b = exchange(l2a, 2)
    core1 = exchange(bundle, 1)
    core2 = exchange(l2b, 1)
    w1, *outer = near_outer(edge, trio, out)
    far = (l1a, l2a, l2b, core1, core2)
    attention, lse, stats = far_forward(bias, own, far, inner, outer, upstream, gain)

    others = [
        lax.ppermute(stats, "head", [(i, i ^ mask) for i in range(head_count)]) for mask in range(1, head_count)
    ]
    attended, d_out, delta, g1, g2, g3 = cotangent(stats, others, own, attention, lse, upstream, gain)

    planes = [exchange(g3, mask) for mask in PLANES]
    l1a = exchange(g1, 2)
    d_in = exchange(d_out, 1)
    pack = packed(g2, planes)
    quads = [exchange(pack, mask) for mask in QUAD]
    near_dq = near_query(w0, w1, inner[0], outer[0], lse, delta, after(d_out, pack), trio, inn, out)
    near_dk, near_dv = inner_key(trio, inn, d_out, d_in)
    l2a, bundle = merged(l1a, after(pack, near_dq, near_dk), quads)
    l2b = exchange(l2a, 2)
    core1 = exchange(bundle, 1)
    d_far = exchange_outer(after(d_out, l2a))
    query_grad = far_query(bias, own, far, g1, g2, g3, near_dq)
    core2 = exchange(after(l2b, query_grad), 1)
    near_dk, near_dv = outer_key(trio, out, d_far, near_dk, near_dv)
    key_grad, value_grad = far_key(bias, own, (l1a, l2a, l2b, core1, core2), near_dk, near_dv)
    return attended, query_grad, key_grad, value_grad


def solution(mesh):
    return jax.shard_map(
        body,
        mesh=mesh,
        in_specs=(
            P("seq", "head"),
            P("seq", "head"),
            P("seq", "head"),
            P("head"),
            P("seq", "head"),
        ),
        out_specs=(P("seq", "head"), P("seq", "head"), P("seq", "head"), P("seq", "head")),
        check_vma=False,
    )
```

time: 152 us -> 136 us (0.89)
  waiting for transfers between devices: 50 us -> 40 us
  Pallas kernels: 34.6 us -> 38.9 us
  starting transfers between devices: 58 us -> 53.7 us
  local copies, waits for them, and re-layouts: 6.48 us -> 2.28 us
  other arithmetic: 1.55 us -> 0 us
    ppermute x6 -> x2, starting transfers between devices: 24.4 us -> 8.37 us  [exchange_outer(): return lax.ppermute(array, 'seq', pairs)]
    ppermute x24 -> x22, waiting for transfers between devices: 46.7 us -> 33.3 us  [exchange(): return lax.ppermute(array, 'seq', [(i, i ^ mask) for i in range(count)])]
    ppermute x24 -> x22, starting transfers between devices: 30 us -> 42 us  [exchange(): return lax.ppermute(array, 'seq', [(i, i ^ mask) for i in range(count)])]
    unnamed x30 -> x16, local copies, waits for them, and re-layouts: 6.48 us -> 2.28 us
    pallas_call x1, Pallas kernels: 0.63 us -> 4.18 us  [pool(): pl.pallas_call(pool_kernel, out_shape=[f32(OWN, 3 * WIDTH), f32(64, KV),...]
    ppermute x6 -> x2, waiting for transfers between devices: 0.02 us -> 3.48 us  [exchange_outer(): return lax.ppermute(array, 'seq', pairs)]
    pallas_call x3 -> x5, Pallas kernels: 19.5 us -> 22.2 us  [head_call(): pl.pallas_call(kernel, grid=(HEADS,), out_shape=outs, in_specs=in_specs,...]
    pallas_call x10 -> x8, Pallas kernels: 14.5 us -> 12.5 us  [whole_call(): pl.pallas_call(kernel, out_shape=outs, in_specs=[spec] * len(operands), o...]
  transfers between devices with their start and end apart: 33 -> 27, of which waited for: 11 -> 9; matrix products, arithmetic and copies ran while one was open for 1% -> 0% of each run, Pallas kernels for 19% -> 19%
where the time goes in v1:
time: 136 us
  starting transfers between devices  53.7 us (39%)
  waiting for transfers between devices  40 us (29%)
  Pallas kernels  38.9 us (29%)
  local copies, waits for them, and re-layouts  2.28 us (2%)
    ppermute x22, starting transfers between devices, exchange(): return lax.ppermute(array, 'seq', [(i, i ^ mask) for i in range(count)])  42 us
    ppermute x22, waiting for transfers between devices, exchange(): return lax.ppermute(array, 'seq', [(i, i ^ mask) for i in range(count)])  33.3 us
    pallas_call x5, Pallas kernels, head_call(): pl.pallas_call(kernel, grid=(HEADS,), out_shape=outs, in_specs=in_specs,...  22.2 us
    pallas_call x8, Pallas kernels, whole_call(): pl.pallas_call(kernel, out_shape=outs, in_specs=[spec] * len(operands), o...  12.5 us
    ppermute x2, starting transfers between devices, exchange_outer(): return lax.ppermute(array, 'seq', pairs)  8.37 us
    pallas_call x1, Pallas kernels, pool(): pl.pallas_call(pool_kernel, out_shape=[f32(OWN, 3 * WIDTH), f32(64, KV),...  4.18 us
    ppermute x2, waiting for transfers between devices, exchange_outer(): return lax.ppermute(array, 'seq', pairs)  3.48 us
    ppermute x3, starting transfers between devices, body(): lax.ppermute(stats, 'head', [(i, i ^ mask) for i in range(head_count)])  3.32 us
  transfers between devices with their start and end apart: 27, of which 9 were waited for; matrix products, arithmetic and copies ran while one was open for 0% of the time, Pallas kernels for 19%

profile of v1, /device:TPU:1, one launch (start us, length us, event | category | flops | bytes accessed | tf_op | source)
XLA Modules:
  0.0 135.8 jit_solution(3206167811181513508)
XLA Ops:
  0.6 4.2 %shard_map.93 = (f32[96,1536]{1,0:T(8,128)}, f32[64,1024]{1,0:T(8,128)}, f32[16,1024]{1,0:T(8,128)}, f32[4,1024]{1,0:T(4,128)}, f32[256,1536]{1,0:T(8,128)}, /*index=5*/f32[96,512]{1,0:T(8,128)}, f32[8,256]{1,0:T(8,128)}) custom-call(s32[8,512]{1,0:T(8,128)} %constant.2.clone.table_ref, f32[256,512]{1,0:T(8,128)} %k_ref.1, f32[256,512]{1,0:T(8,128)} %v_ref.1, ...), custom_call_target="tpu_custom_call" | custom-call | flops 1000000 | bytes 2000000 | tf_op jit(solution)/shard_map/pallas_call | solution.py:477
  4.8 3.3 %collective-permute-start.4 = (f32[256,1536]{1,0:T(8,128)}, f32[256,1536]{1,0:T(8,128)S(1)}, u32[]{:S(2)}, u32[]{:S(2)}) collective-permute-start(f32[256,1536]{1,0:T(8,128)} %get-tuple-element.58.q_ref.ko_ref.vo_ref.k0_ref.v0_ref.k_ref.v_ref.q0_ref), channel_id=1, source_target_pairs={{0,4},{4,0},{8,12},{12,8},{16,20},{20,16},{24,28},{28,24},{32,36},... | collective-permute-start | bytes 4718600 | tf_op jit(solution)/shard_map/ppermute | solution.py:547
  8.1 1.0 collective-permute-start.3
  9.2 0.3 collective-permute-start.2
  9.5 1.9 %collective-permute-start.1 = (f32[4,1024]{1,0:T(4,128)}, f32[4,1024]{1,0:T(4,128)S(1)}, u32[]{:S(2)}, u32[]{:S(2)}) collective-permute-start(f32[4,1024]{1,0:T(4,128)} %get-tuple-element.48), channel_id=1, source_target_pairs={{0,64},{4,68},{8,72},{12,76},{16,80},{20,84},{24,88},{28,92},{32,9... | collective-permute-start | bytes 49160 | tf_op jit(solution)/shard_map/ppermute | solution.py:547
  11.4 0.8 collective-permute-done.3.c_ref
  12.2 1.3 collective-permute-done.2.b_ref
  13.5 0.0 collective-permute-done.1.a_ref
  13.5 0.8 copy-done.5
  14.3 4.9 %collective-permute-start.11 = (f32[256,1536]{1,0:T(8,128)}, f32[256,1536]{1,0:T(8,128)S(1)}, u32[]{:S(2)}, u32[]{:S(2)}) collective-permute-start(f32[256,1536]{1,0:T(8,128)} %get-tuple-element.58.q_ref.ko_ref.vo_ref.k0_ref.v0_ref.k_ref.v_ref.q0_ref), channel_id=1, source_target_pairs={{4,8},{8,4},{12,16},{16,12},{20,24},{24,20},{28,32},{32,28},{36,40... | collective-permute-start | bytes 4718600 | tf_op jit(solution)/shard_map/ppermute | solution.py:551
  19.3 1.7 %collective-permute-start = (f32[64,1024]{1,0:T(8,128)}, f32[64,1024]{1,0:T(8,128)S(1)}, u32[]{:S(2)}, u32[]{:S(2)}) collective-permute-start(f32[64,1024]{1,0:T(8,128)} %get-tuple-element.46), channel_id=1, source_target_pairs={{0,8},{4,12},{8,0},{12,4},{16,24},{20,28},{24,16},{28,20},{32,40},... | collective-permute-start | bytes 786440 | tf_op jit(solution)/shard_map/ppermute | solution.py:547
  21.0 3.6 %collective-permute-start.7 = (f32[28,1024]{1,0:T(8,128)S(1)}, f32[28,1024]{1,0:T(8,128)S(1)}, u32[]{:S(2)}, u32[]{:S(2)}) collective-permute-start(f32[28,1024]{1,0:T(8,128)S(1)} %shard_map.94.own_ref), channel_id=1, source_target_pairs={{0,48},{4,52},{8,56},{12,60},{16,32},{20,36},{24,40},{28,44},{32,1... | collective-permute-start | bytes 344072 | tf_op jit(solution)/shard_map/ppermute | solution.py:547
  24.6 3.9 %collective-permute-start.6 = (f32[28,1024]{1,0:T(8,128)S(1)}, f32[28,1024]{1,0:T(8,128)S(1)}, u32[]{:S(2)}, u32[]{:S(2)}) collective-permute-start(f32[28,1024]{1,0:T(8,128)S(1)} %shard_map.94.own_ref), channel_id=1, source_target_pairs={{0,32},{4,36},{8,40},{12,44},{16,48},{20,52},{24,56},{28,60},{32,0... | collective-permute-start | bytes 344072 | tf_op jit(solution)/shard_map/ppermute | solution.py:547
  28.5 0.0 collective-permute-done.4.ki_ref.vi_ref.k1_ref.v1_ref.q1_ref
  28.5 0.0 collective-permute-start.5
  28.5 1.4 %copy-done = f32[256,1536]{1,0:T(8,128)S(1)} copy-done((f32[256,1536]{1,0:T(8,128)S(1)}, f32[256,1536]{1,0:T(8,128)}, u32[]{:S(2)}) %copy-start) | copy-done | bytes 1572888
  29.9 4.1 %shard_map.95 = (f32[4,256,512]{2,1,0:T(8,128)S(1)}, f32[256,512]{1,0:T(8,128)S(1)}, f32[256,512]{1,0:T(8,128)S(1)}, f32[256,512]{1,0:T(8,128)S(1)}) custom-call(f32[256,1536]{1,0:T(8,128)S(1)} %copy-done, f32[256,1536]{1,0:T(8,128)S(1)} %copy-done, f32[256,1536]{1,0:T(8,128)S(1)} %collective-permute-done.4.ki_ref.vi_ref.k1_ref.v1_ref.q1_ref, ...), custom_call_target="tpu_custom_call" | custom-call | flops 1610612736 | bytes 4000000 | tf_op jit(solution)/shard_map/pallas_call | solution.py:421
  34.0 23.8 %collective-permute-done.7.c_ref = f32[28,1024]{1,0:T(8,128)S(1)} collective-permute-done((f32[28,1024]{1,0:T(8,128)S(1)}, f32[28,1024]{1,0:T(8,128)S(1)}, u32[]{:S(2)}, u32[]{:S(2)}) %collective-permute-start.7) | collective-permute-done | bytes 114720 | tf_op jit(solution)/shard_map/ppermute | solution.py:547
  57.8 0.0 collective-permute-done.6.b_ref
  57.9 0.1 shard_map.96
  57.9 0.1 collective-permute-start.8
  58.0 3.5 %collective-permute-start.9 = (f32[160,1024]{1,0:T(8,128)S(1)}, f32[160,1024]{1,0:T(8,128)S(1)}, u32[]{:S(2)}, u32[]{:S(2)}) collective-permute-start(f32[160,1024]{1,0:T(8,128)S(1)} %get-tuple-element.53), channel_id=1, source_target_pairs={{0,4},{4,0},{8,12},{12,8},{16,20},{20,16},{24,28},{28,24},{32,36},... | collective-permute-start | bytes 1966088 | tf_op jit(solution)/shard_map/ppermute | solution.py:547
  61.6 5.5 %collective-permute-done.8.a2 = f32[96,1024]{1,0:T(8,128)S(1)} collective-permute-done((f32[96,1024]{1,0:T(8,128)S(1)}, f32[96,1024]{1,0:T(8,128)S(1)}, u32[]{:S(2)}, u32[]{:S(2)}) %collective-permute-start.8) | collective-permute-done | bytes 393248 | tf_op jit(solution)/shard_map/ppermute | solution.py:547
  67.1 2.5 %collective-permute-start.10 = (f32[96,1024]{1,0:T(8,128)S(1)}, f32[96,1024]{1,0:T(8,128)S(1)}, u32[]{:S(2)}, u32[]{:S(2)}) collective-permute-start(f32[96,1024]{1,0:T(8,128)S(1)} %collective-permute-done.8.a2), channel_id=1, source_target_pairs={{0,4},{4,0},{8,12},{12,8},{16,20},{20,16},{24,28},{28,24},{32,36},... | collective-permute-start | bytes 1179656 | tf_op jit(solution)/shard_map/ppermute | solution.py:547
  69.6 0.0 collective-permute-done.11.k_ref.v_ref.k2_ref.v2_ref.q_ref
  69.6 0.0 copy-start.3
  69.6 0.0 copy-start.4
  69.6 0.0 copy-start.7
  69.6 3.7 %shard_map.97 = (f32[4,256,256]{2,1,0:T(8,128)S(1)}, f32[256,512]{1,0:T(8,128)S(1)}, f32[256,512]{1,0:T(8,128)S(1)}, f32[256,512]{1,0:T(8,128)S(1)}) custom-call(f32[8,256]{1,0:T(8,128)S(1)} %copy-done.6, f32[256,1536]{1,0:T(8,128)S(1)} %copy-done.1, f32[256,1536]{1,0:T(8,128)S(1)} %collective-permute-done.11.k_ref.v_ref.k2_ref.v2_ref.q_ref, ...), custom_call_target="tpu_custom_call" | custom-call | flops 805306368 | bytes 4000000 | tf_op jit(solution)/shard_map/pallas_call | solution.py:421
  73.3 0.0 collective-permute-done.9.a3
  73.3 0.0 collective-permute-done.10.a4
  73.4 2.8 %shard_map.98 = (f32[256,512]{1,0:T(8,128)S(1)}, f32[256,512]{1,0:T(8,128)S(1)}, f32[8,256]{1,0:T(8,128)S(1)}) custom-call(f32[96,512]{1,0:T(8,128)S(1)} %copy-done.4, f32[96,1536]{1,0:T(8,128)S(1)} %copy-done.2, f32[64,1024]{1,0:T(8,128)S(1)} %collective-permute-done.first_ref.a0, f32[96,1024]{1,0:T(8,128)S(1)} %get-tuple-element.52.a1, ...), custom_call_target="tpu_custom_call" | custom-call | flops 402653184 | bytes 8000000 | tf_op jit(solution)/shard_map/pallas_call | solution.py:398
  76.2 2.5 %collective-permute-start.14 = (f32[8,256]{1,0:T(8,128)S(1)}, f32[8,256]{1,0:T(8,128)S(1)}, u32[]{:S(2)}, u32[]{:S(2)}) collective-permute-start(f32[8,256]{1,0:T(8,128)S(1)} %get-tuple-element.62.s0_ref), channel_id=1, source_target_pairs={{0,3},{1,2},{2,1},{3,0},{4,7},{5,6},{6,5},{7,4},{8,11},{9,10},{10,... | collective-permute-start | bytes 24584 | tf_op jit(solution)/shard_map/ppermute | solution.py:582
  78.7 0.5 collective-permute-start.13
  79.2 0.3 collective-permute-start.12
  79.5 0.5 collective-permute-done.14.s3_ref
  80.0 2.8 %collective-permute-done.13.s2_ref = f32[8,256]{1,0:T(8,128)S(1)} collective-permute-done((f32[8,256]{1,0:T(8,128)S(1)}, f32[8,256]{1,0:T(8,128)S(1)}, u32[]{:S(2)}, u32[]{:S(2)}) %collective-permute-start.13) | collective-permute-done | bytes 8224 | tf_op jit(solution)/shard_map/ppermute | solution.py:582
  82.7 1.3 shard_map.99
  84.1 1.4 %collective-permute-start.19 = (f32[264,512]{1,0:T(8,128)S(1)}, f32[264,512]{1,0:T(8,128)S(1)}, u32[]{:S(2)}, u32[]{:S(2)}) collective-permute-start(f32[264,512]{1,0:T(8,128)S(1)} %get-tuple-element.78.dout_ref.d0_ref.t0_ref), channel_id=1, source_target_pairs={{0,4},{4,0},{8,12},{12,8},{16,20},{20,16},{24,28},{28,24},{32,36},... | collective-permute-start | bytes 1622024 | tf_op jit(solution)/shard_map/ppermute | solution.py:547
  85.5 1.0 collective-permute-start.17
  86.5 0.7 collective-permute-start.16
  87.3 1.5 %collective-permute-start.15 = (f32[4,1152]{1,0:T(4,128)S(1)}, f32[4,1152]{1,0:T(4,128)S(1)}, u32[]{:S(2)}, u32[]{:S(2)}) collective-permute-start(f32[4,1152]{1,0:T(4,128)S(1)} %get-tuple-element.68.third_ref), channel_id=1, source_target_pairs={{0,64},{4,68},{8,72},{12,76},{16,80},{20,84},{24,88},{28,92},{32,9... | collective-permute-start | bytes 55304 | tf_op jit(solution)/shard_map/ppermute | solution.py:547
  88.8 0.0 collective-permute-start.18
  88.8 0.6 collective-permute-done.17.c_ref
  89.3 1.3 collective-permute-done.16.b_ref
  90.7 0.0 collective-permute-done.15.a_ref
  90.7 0.3 collective-permute-start.22
  91.0 4.8 %collective-permute-start.21 = (f32[28,1152]{1,0:T(8,128)S(1)}, f32[28,1152]{1,0:T(8,128)S(1)}, u32[]{:S(2)}, u32[]{:S(2)}) collective-permute-start(f32[28,1152]{1,0:T(8,128)S(1)} %shard_map.100.own_ref), channel_id=1, source_target_pairs={{0,32},{4,36},{8,40},{12,44},{16,48},{20,52},{24,56},{28,60},{32,0... | collective-permute-start | bytes 387080 | tf_op jit(solution)/shard_map/ppermute | solution.py:547
  95.8 0.7 collective-permute-start.20
  96.4 5.1 %shard_map.101.near_ref = f32[256,512]{1,0:T(8,128)S(1)} custom-call(f32[4,256,512]{2,1,0:T(8,128)S(1)} %get-tuple-element.50.w0_ref, f32[4,256,256]{2,1,0:T(8,128)S(1)} %get-tuple-element.69.w1_ref, f32[256,512]{1,0:T(8,128)S(1)} %get-tuple-element.54.peak0_ref, f32[256,512]{1,0:T(8,128)S(1)} %get-tuple-element.59.peak1_ref, ...), custom_call_target="tpu_custom_call" | custom-call | flops 2415919104 | bytes 4000000 | tf_op jit(solution)/shard_map/pallas_call | solution.py:421
  101.5 0.0 collective-permute-done.19.d1_ref.t1_ref
  101.5 5.6 %shard_map.103 = (f32[256,512]{1,0:T(8,128)S(1)}, f32[256,512]{1,0:T(8,128)S(1)}) custom-call(f32[256,1536]{1,0:T(8,128)S(1)} %copy-done.1, f32[256,1536]{1,0:T(8,128)S(1)} %copy-done.1, f32[256,1536]{1,0:T(8,128)S(1)} %copy-done.1, f32[256,1536]{1,0:T(8,128)S(1)} %collective-permute-done.4.ki_ref.vi_ref.k1_ref.v1_ref.q1_ref, ...), custom_call_target="tpu_custom_call" | custom-call | flops 3221225472 | bytes 4000000 | tf_op jit(solution)/shard_map/pallas_call | solution.py:421
  107.2 0.0 collective-permute-done.22.c_ref
  107.2 0.0 collective-permute-done.18.first_ref.a0
  107.2 0.1 shard_map.104
  107.3 3.4 %collective-permute-start.23 = (f32[96,1152]{1,0:T(8,128)S(1)}, f32[96,1152]{1,0:T(8,128)S(1)}, u32[]{:S(2)}, u32[]{:S(2)}) collective-permute-start(f32[96,1152]{1,0:T(8,128)S(1)} %get-tuple-element.75.a1), channel_id=1, source_target_pairs={{0,8},{4,12},{8,0},{12,4},{16,24},{20,28},{24,16},{28,20},{32,40},... | collective-permute-start | bytes 1327112 | tf_op jit(solution)/shard_map/ppermute | solution.py:547
  110.7 3.0 %collective-permute-start.24 = (f32[160,1152]{1,0:T(8,128)S(1)}, f32[160,1152]{1,0:T(8,128)S(1)}, u32[]{:S(2)}, u32[]{:S(2)}) collective-permute-start(f32[160,1152]{1,0:T(8,128)S(1)} %get-tuple-element.76), channel_id=1, source_target_pairs={{0,4},{4,0},{8,12},{12,8},{16,20},{20,16},{24,28},{28,24},{32,36},... | collective-permute-start | bytes 2211848 | tf_op jit(solution)/shard_map/ppermute | solution.py:547
  113.6 3.4 %collective-permute-start.26 = (f32[264,512]{1,0:T(8,128)S(1)}, f32[264,512]{1,0:T(8,128)S(1)}, u32[]{:S(2)}, u32[]{:S(2)}) collective-permute-start(f32[264,512]{1,0:T(8,128)S(1)} %get-tuple-element.78.dout_ref.d0_ref.t0_ref), channel_id=1, source_target_pairs={{4,8},{8,4},{12,16},{16,12},{20,24},{24,20},{28,32},{32,28},{36,40... | collective-permute-start | bytes 1622024 | tf_op jit(solution)/shard_map/ppermute | solution.py:551
  117.1 3.7 %shard_map.102 = f32[256,512]{1,0:T(8,128)} custom-call(f32[96,512]{1,0:T(8,128)S(1)} %copy-done.4, f32[96,1536]{1,0:T(8,128)S(1)} %copy-done.2, f32[64,1024]{1,0:T(8,128)S(1)} %collective-permute-done.first_ref.a0, f32[96,1024]{1,0:T(8,128)S(1)} %get-tuple-element.52.a1, f32[96,1024]{1,0:T(8,128)S(1)} %collective-permute-done.8.a2, ...), custom_call_target="tpu_custom_call" | custom-call | flops 402653184 | bytes 6000000 | tf_op jit(solution)/shard_map/pallas_call | solution.py:398
  120.8 3.3 %collective-permute-start.25 = (f32[96,1152]{1,0:T(8,128)S(1)}, f32[96,1152]{1,0:T(8,128)S(1)}, u32[]{:S(2)}, u32[]{:S(2)}) collective-permute-start(f32[96,1152]{1,0:T(8,128)S(1)} %collective-permute-done.23.a2), channel_id=1, source_target_pairs={{0,4},{4,0},{8,12},{12,8},{16,20},{20,16},{24,28},{28,24},{32,36},... | collective-permute-start | bytes 1327112 | tf_op jit(solution)/shard_map/ppermute | solution.py:547
  124.1 3.5 %collective-permute-done.26.d_ref.t_ref = f32[264,512]{1,0:T(8,128)S(1)} collective-permute-done((f32[264,512]{1,0:T(8,128)S(1)}, f32[264,512]{1,0:T(8,128)S(1)}, u32[]{:S(2)}, u32[]{:S(2)}) %collective-permute-start.26) | collective-permute-done | bytes 540704 | tf_op jit(solution)/shard_map/ppermute | solution.py:551
  127.6 3.7 %shard_map.105 = (f32[256,512]{1,0:T(8,128)S(1)}, f32[256,512]{1,0:T(8,128)S(1)}) custom-call(f32[256,1536]{1,0:T(8,128)S(1)} %copy-done.1, f32[256,1536]{1,0:T(8,128)S(1)} %copy-done.1, f32[256,1536]{1,0:T(8,128)S(1)} %collective-permute-done.11.k_ref.v_ref.k2_ref.v2_ref.q_ref, f32[264,512]{1,0:T(8,128)S(1)} %collective-permute-done.26.d_ref.t_ref, ...), custom_call_target="tpu_custom_call" | custom-call | flops 1610612736 | bytes 4000000 | tf_op jit(solution)/shard_map/pallas_call | solution.py:421
  131.3 0.0 collective-permute-done.24.a3
  131.4 4.4 %shard_map.106 = (f32[256,512]{1,0:T(8,128)}, f32[256,512]{1,0:T(8,128)}) custom-call(f32[96,512]{1,0:T(8,128)S(1)} %copy-done.4, f32[96,1536]{1,0:T(8,128)S(1)} %copy-done.2, f32[64,1152]{1,0:T(8,128)S(1)} %collective-permute-done.18.first_ref.a0, f32[96,1152]{1,0:T(8,128)S(1)} %get-tuple-element.75.a1, f32[96,1152]{1,0:T(8,128)S(1)} %collective-permute-done.23.a2, ...), custom_call_target="tpu_custom_call" | custom-call | flops 402653184 | bytes 6000000 | tf_op jit(solution)/shard_map/pallas_call | solution.py:398
  (20 shorter events, 0.1 us)
Async XLA Ops:
  4.8 23.7 %collective-permute-start.4 = (f32[256,1536]{1,0:T(8,128)}, f32[256,1536]{1,0:T(8,128)S(1)}, u32[]{:S(2)}, u32[]{:S(2)}) collective-permute-start(f32[256,1536]{1,0:T(8,128)} %get-tuple-element.58.q_ref.ko_ref.vo_ref.k0_ref.v0_ref.k_ref.v_ref.q0_ref), channel_id=1, source_target_pairs={{0,4},{4,0},{8,12},{12,8},{16,20},{20,16},{24,28},{28,24},{32,36},... | collective-permute-start | bytes 4718600 | tf_op jit(solution)/shard_map/ppermute | solution.py:547
  8.1 4.0 %collective-permute-start.3 = (f32[4,1024]{1,0:T(4,128)}, f32[4,1024]{1,0:T(4,128)S(1)}, u32[]{:S(2)}, u32[]{:S(2)}) collective-permute-start(f32[4,1024]{1,0:T(4,128)} %get-tuple-element.48), channel_id=1, source_target_pairs={{0,192},{4,196},{8,200},{12,204},{16,208},{20,212},{24,216},{28,22... | collective-permute-start | bytes 49160 | tf_op jit(solution)/shard_map/ppermute | solution.py:547
  9.2 4.3 %collective-permute-start.2 = (f32[4,1024]{1,0:T(4,128)}, f32[4,1024]{1,0:T(4,128)S(1)}, u32[]{:S(2)}, u32[]{:S(2)}) collective-permute-start(f32[4,1024]{1,0:T(4,128)} %get-tuple-element.48), channel_id=1, source_target_pairs={{0,128},{4,132},{8,136},{12,140},{16,144},{20,148},{24,152},{28,15... | collective-permute-start | bytes 49160 | tf_op jit(solution)/shard_map/ppermute | solution.py:547
  9.5 4.0 %collective-permute-start.1 = (f32[4,1024]{1,0:T(4,128)}, f32[4,1024]{1,0:T(4,128)S(1)}, u32[]{:S(2)}, u32[]{:S(2)}) collective-permute-start(f32[4,1024]{1,0:T(4,128)} %get-tuple-element.48), channel_id=1, source_target_pairs={{0,64},{4,68},{8,72},{12,76},{16,80},{20,84},{24,88},{28,92},{32,9... | collective-permute-start | bytes 49160 | tf_op jit(solution)/shard_map/ppermute | solution.py:547
  13.5 0.8 copy-start.5
  14.3 55.2 %copy-start.6 = (f32[8,256]{1,0:T(8,128)S(1)}, f32[8,256]{1,0:T(8,128)}, u32[]{:S(2)}) copy-start(f32[8,256]{1,0:T(8,128)} %get-tuple-element.57.edge_ref) | copy-start | bytes 24580
  14.3 55.2 %collective-permute-start.11 = (f32[256,1536]{1,0:T(8,128)}, f32[256,1536]{1,0:T(8,128)S(1)}, u32[]{:S(2)}, u32[]{:S(2)}) collective-permute-start(f32[256,1536]{1,0:T(8,128)} %get-tuple-element.58.q_ref.ko_ref.vo_ref.k0_ref.v0_ref.k_ref.v_ref.q0_ref), channel_id=1, source_target_pairs={{4,8},{8,4},{12,16},{16,12},{20,24},{24,20},{28,32},{32,28},{36,40... | collective-permute-start | bytes 4718600 | tf_op jit(solution)/shard_map/ppermute | solution.py:551
  19.3 38.6 %collective-permute-start = (f32[64,1024]{1,0:T(8,128)}, f32[64,1024]{1,0:T(8,128)S(1)}, u32[]{:S(2)}, u32[]{:S(2)}) collective-permute-start(f32[64,1024]{1,0:T(8,128)} %get-tuple-element.46), channel_id=1, source_target_pairs={{0,8},{4,12},{8,0},{12,4},{16,24},{20,28},{24,16},{28,20},{32,40},... | collective-permute-start | bytes 786440 | tf_op jit(solution)/shard_map/ppermute | solution.py:547
  21.0 36.8 %collective-permute-start.7 = (f32[28,1024]{1,0:T(8,128)S(1)}, f32[28,1024]{1,0:T(8,128)S(1)}, u32[]{:S(2)}, u32[]{:S(2)}) collective-permute-start(f32[28,1024]{1,0:T(8,128)S(1)} %shard_map.94.own_ref), channel_id=1, source_target_pairs={{0,48},{4,52},{8,56},{12,60},{16,32},{20,36},{24,40},{28,44},{32,1... | collective-permute-start | bytes 344072 | tf_op jit(solution)/shard_map/ppermute | solution.py:547
  24.6 33.3 %collective-permute-start.6 = (f32[28,1024]{1,0:T(8,128)S(1)}, f32[28,1024]{1,0:T(8,128)S(1)}, u32[]{:S(2)}, u32[]{:S(2)}) collective-permute-start(f32[28,1024]{1,0:T(8,128)S(1)} %shard_map.94.own_ref), channel_id=1, source_target_pairs={{0,32},{4,36},{8,40},{12,44},{16,48},{20,52},{24,56},{28,60},{32,0... | collective-permute-start | bytes 344072 | tf_op jit(solution)/shard_map/ppermute | solution.py:547
  28.5 29.3 %collective-permute-start.5 = (f32[28,1024]{1,0:T(8,128)S(1)}, f32[28,1024]{1,0:T(8,128)S(1)}, u32[]{:S(2)}, u32[]{:S(2)}) collective-permute-start(f32[28,1024]{1,0:T(8,128)S(1)} %shard_map.94.own_ref), channel_id=1, source_target_pairs={{0,16},{4,20},{8,24},{12,28},{16,0},{20,4},{24,8},{28,12},{32,48},... | collective-permute-start | bytes 344072 | tf_op jit(solution)/shard_map/ppermute | solution.py:547
  28.5 1.4 %copy-start = (f32[256,1536]{1,0:T(8,128)S(1)}, f32[256,1536]{1,0:T(8,128)}, u32[]{:S(2)}) copy-start(f32[256,1536]{1,0:T(8,128)} %get-tuple-element.58.q_ref.ko_ref.vo_ref.k0_ref.v0_ref.k_ref.v_ref.q0_ref) | copy-start | bytes 4718596
  29.9 39.6 %copy-start.1 = (f32[256,1536]{1,0:T(8,128)S(1)}, f32[256,1536]{1,0:T(8,128)}, u32[]{:S(2)}) copy-start(f32[256,1536]{1,0:T(8,128)} %get-tuple-element.58.q_ref.ko_ref.vo_ref.k0_ref.v0_ref.k_ref.v_ref.q0_ref) | copy-start | bytes 4718596
  57.9 9.2 %collective-permute-start.8 = (f32[96,1024]{1,0:T(8,128)S(1)}, f32[96,1024]{1,0:T(8,128)S(1)}, u32[]{:S(2)}, u32[]{:S(2)}) collective-permute-start(f32[96,1024]{1,0:T(8,128)S(1)} %get-tuple-element.52.a1), channel_id=1, source_target_pairs={{0,8},{4,12},{8,0},{12,4},{16,24},{20,28},{24,16},{28,20},{32,40},... | collective-permute-start | bytes 1179656 | tf_op jit(solution)/shard_map/ppermute | solution.py:547
  58.0 15.3 %collective-permute-start.9 = (f32[160,1024]{1,0:T(8,128)S(1)}, f32[160,1024]{1,0:T(8,128)S(1)}, u32[]{:S(2)}, u32[]{:S(2)}) collective-permute-start(f32[160,1024]{1,0:T(8,128)S(1)} %get-tuple-element.53), channel_id=1, source_target_pairs={{0,4},{4,0},{8,12},{12,8},{16,20},{20,16},{24,28},{28,24},{32,36},... | collective-permute-start | bytes 1966088 | tf_op jit(solution)/shard_map/ppermute | solution.py:547
  67.1 6.2 %collective-permute-start.10 = (f32[96,1024]{1,0:T(8,128)S(1)}, f32[96,1024]{1,0:T(8,128)S(1)}, u32[]{:S(2)}, u32[]{:S(2)}) collective-permute-start(f32[96,1024]{1,0:T(8,128)S(1)} %collective-permute-done.8.a2), channel_id=1, source_target_pairs={{0,4},{4,0},{8,12},{12,8},{16,20},{20,16},{24,28},{28,24},{32,36},... | collective-permute-start | bytes 1179656 | tf_op jit(solution)/shard_map/ppermute | solution.py:547
  69.6 3.8 %copy-start.2 = (f32[96,1536]{1,0:T(8,128)S(1)}, f32[96,1536]{1,0:T(8,128)}, u32[]{:S(2)}) copy-start(f32[96,1536]{1,0:T(8,128)} %get-tuple-element.45.own_ref) | copy-start | bytes 1769476
  69.6 3.8 %copy-start.3 = (f32[256,512]{1,0:T(8,128)S(1)}, f32[256,512]{1,0:T(8,128)}, u32[]{:S(2)}) copy-start(f32[256,512]{1,0:T(8,128)} %up_ref.3) | copy-start | bytes 1572868
  69.6 3.8 %copy-start.4 = (f32[96,512]{1,0:T(8,128)S(1)}, f32[96,512]{1,0:T(8,128)}, u32[]{:S(2)}) copy-start(f32[96,512]{1,0:T(8,128)} %get-tuple-element.44.bias_ref) | copy-start | bytes 589828
  69.6 3.8 %copy-start.7 = (f32[512]{0:T(512)S(1)}, f32[512]{0:T(512)}, u32[]{:S(2)}) copy-start(f32[512]{0:T(512)} %param.9) | copy-start | bytes 6148
  76.2 3.8 %collective-permute-start.14 = (f32[8,256]{1,0:T(8,128)S(1)}, f32[8,256]{1,0:T(8,128)S(1)}, u32[]{:S(2)}, u32[]{:S(2)}) collective-permute-start(f32[8,256]{1,0:T(8,128)S(1)} %get-tuple-element.62.s0_ref), channel_id=1, source_target_pairs={{0,3},{1,2},{2,1},{3,0},{4,7},{5,6},{6,5},{7,4},{8,11},{9,10},{10,... | collective-permute-start | bytes 24584 | tf_op jit(solution)/shard_map/ppermute | solution.py:582
  78.7 4.0 %collective-permute-start.13 = (f32[8,256]{1,0:T(8,128)S(1)}, f32[8,256]{1,0:T(8,128)S(1)}, u32[]{:S(2)}, u32[]{:S(2)}) collective-permute-start(f32[8,256]{1,0:T(8,128)S(1)} %get-tuple-element.62.s0_ref), channel_id=1, source_target_pairs={{0,2},{1,3},{2,0},{3,1},{4,6},{5,7},{6,4},{7,5},{8,10},{9,11},{10,... | collective-permute-start | bytes 24584 | tf_op jit(solution)/shard_map/ppermute | solution.py:582
  79.2 3.5 %collective-permute-start.12 = (f32[8,256]{1,0:T(8,128)S(1)}, f32[8,256]{1,0:T(8,128)S(1)}, u32[]{:S(2)}, u32[]{:S(2)}) collective-permute-start(f32[8,256]{1,0:T(8,128)S(1)} %get-tuple-element.62.s0_ref), channel_id=1, source_target_pairs={{0,1},{1,0},{2,3},{3,2},{4,5},{5,4},{6,7},{7,6},{8,9},{9,8},{10,11... | collective-permute-start | bytes 24584 | tf_op jit(solution)/shard_map/ppermute | solution.py:582
  84.1 17.4 %collective-permute-start.19 = (f32[264,512]{1,0:T(8,128)S(1)}, f32[264,512]{1,0:T(8,128)S(1)}, u32[]{:S(2)}, u32[]{:S(2)}) collective-permute-start(f32[264,512]{1,0:T(8,128)S(1)} %get-tuple-element.78.dout_ref.d0_ref.t0_ref), channel_id=1, source_target_pairs={{0,4},{4,0},{8,12},{12,8},{16,20},{20,16},{24,28},{28,24},{32,36},... | collective-permute-start | bytes 1622024 | tf_op jit(solution)/shard_map/ppermute | solution.py:547
  85.5 3.8 %collective-permute-start.17 = (f32[4,1152]{1,0:T(4,128)S(1)}, f32[4,1152]{1,0:T(4,128)S(1)}, u32[]{:S(2)}, u32[]{:S(2)}) collective-permute-start(f32[4,1152]{1,0:T(4,128)S(1)} %get-tuple-element.68.third_ref), channel_id=1, source_target_pairs={{0,192},{4,196},{8,200},{12,204},{16,208},{20,212},{24,216},{28,22... | collective-permute-start | bytes 55304 | tf_op jit(solution)/shard_map/ppermute | solution.py:547
  86.5 4.1 %collective-permute-start.16 = (f32[4,1152]{1,0:T(4,128)S(1)}, f32[4,1152]{1,0:T(4,128)S(1)}, u32[]{:S(2)}, u32[]{:S(2)}) collective-permute-start(f32[4,1152]{1,0:T(4,128)S(1)} %get-tuple-element.68.third_ref), channel_id=1, source_target_pairs={{0,128},{4,132},{8,136},{12,140},{16,144},{20,148},{24,152},{28,15... | collective-permute-start | bytes 55304 | tf_op jit(solution)/shard_map/ppermute | solution.py:547
  87.3 3.4 %collective-permute-start.15 = (f32[4,1152]{1,0:T(4,128)S(1)}, f32[4,1152]{1,0:T(4,128)S(1)}, u32[]{:S(2)}, u32[]{:S(2)}) collective-permute-start(f32[4,1152]{1,0:T(4,128)S(1)} %get-tuple-element.68.third_ref), channel_id=1, source_target_pairs={{0,64},{4,68},{8,72},{12,76},{16,80},{20,84},{24,88},{28,92},{32,9... | collective-permute-start | bytes 55304 | tf_op jit(solution)/shard_map/ppermute | solution.py:547
  88.8 18.4 %collective-permute-start.18 = (f32[64,1152]{1,0:T(8,128)S(1)}, f32[64,1152]{1,0:T(8,128)S(1)}, u32[]{:S(2)}, u32[]{:S(2)}) collective-permute-start(f32[64,1152]{1,0:T(8,128)S(1)} %get-tuple-element.66.first_ref), channel_id=1, source_target_pairs={{0,8},{4,12},{8,0},{12,4},{16,24},{20,28},{24,16},{28,20},{32,40},... | collective-permute-start | bytes 884744 | tf_op jit(solution)/shard_map/ppermute | solution.py:547
  90.7 16.5 %collective-permute-start.22 = (f32[28,1152]{1,0:T(8,128)S(1)}, f32[28,1152]{1,0:T(8,128)S(1)}, u32[]{:S(2)}, u32[]{:S(2)}) collective-permute-start(f32[28,1152]{1,0:T(8,128)S(1)} %shard_map.100.own_ref), channel_id=1, source_target_pairs={{0,48},{4,52},{8,56},{12,60},{16,32},{20,36},{24,40},{28,44},{32,1... | collective-permute-start | bytes 387080 | tf_op jit(solution)/shard_map/ppermute | solution.py:547
  91.0 16.2 %collective-permute-start.21 = (f32[28,1152]{1,0:T(8,128)S(1)}, f32[28,1152]{1,0:T(8,128)S(1)}, u32[]{:S(2)}, u32[]{:S(2)}) collective-permute-start(f32[28,1152]{1,0:T(8,128)S(1)} %shard_map.100.own_ref), channel_id=1, source_target_pairs={{0,32},{4,36},{8,40},{12,44},{16,48},{20,52},{24,56},{28,60},{32,0... | collective-permute-start | bytes 387080 | tf_op jit(solution)/shard_map/ppermute | solution.py:547
  95.8 11.4 %collective-permute-start.20 = (f32[28,1152]{1,0:T(8,128)S(1)}, f32[28,1152]{1,0:T(8,128)S(1)}, u32[]{:S(2)}, u32[]{:S(2)}) collective-permute-start(f32[28,1152]{1,0:T(8,128)S(1)} %shard_map.100.own_ref), channel_id=1, source_target_pairs={{0,16},{4,20},{8,24},{12,28},{16,0},{20,4},{24,8},{28,12},{32,48},... | collective-permute-start | bytes 387080 | tf_op jit(solution)/shard_map/ppermute | solution.py:547
  107.3 13.5 %collective-permute-start.23 = (f32[96,1152]{1,0:T(8,128)S(1)}, f32[96,1152]{1,0:T(8,128)S(1)}, u32[]{:S(2)}, u32[]{:S(2)}) collective-permute-start(f32[96,1152]{1,0:T(8,128)S(1)} %get-tuple-element.75.a1), channel_id=1, source_target_pairs={{0,8},{4,12},{8,0},{12,4},{16,24},{20,28},{24,16},{28,20},{32,40},... | collective-permute-start | bytes 1327112 | tf_op jit(solution)/shard_map/ppermute | solution.py:547
  110.7 20.7 %collective-permute-start.24 = (f32[160,1152]{1,0:T(8,128)S(1)}, f32[160,1152]{1,0:T(8,128)S(1)}, u32[]{:S(2)}, u32[]{:S(2)}) collective-permute-start(f32[160,1152]{1,0:T(8,128)S(1)} %get-tuple-element.76), channel_id=1, source_target_pairs={{0,4},{4,0},{8,12},{12,8},{16,20},{20,16},{24,28},{28,24},{32,36},... | collective-permute-start | bytes 2211848 | tf_op jit(solution)/shard_map/ppermute | solution.py:547
  113.6 13.9 %collective-permute-start.26 = (f32[264,512]{1,0:T(8,128)S(1)}, f32[264,512]{1,0:T(8,128)S(1)}, u32[]{:S(2)}, u32[]{:S(2)}) collective-permute-start(f32[264,512]{1,0:T(8,128)S(1)} %get-tuple-element.78.dout_ref.d0_ref.t0_ref), channel_id=1, source_target_pairs={{4,8},{8,4},{12,16},{16,12},{20,24},{24,20},{28,32},{32,28},{36,40... | collective-permute-start | bytes 1622024 | tf_op jit(solution)/shard_map/ppermute | solution.py:551
  120.8 10.5 %collective-permute-start.25 = (f32[96,1152]{1,0:T(8,128)S(1)}, f32[96,1152]{1,0:T(8,128)S(1)}, u32[]{:S(2)}, u32[]{:S(2)}) collective-permute-start(f32[96,1152]{1,0:T(8,128)S(1)} %collective-permute-done.23.a2), channel_id=1, source_target_pairs={{0,4},{4,0},{8,12},{12,8},{16,20},{20,16},{24,28},{28,24},{32,36},... | collective-permute-start | bytes 1327112 | tf_op jit(solution)/shard_map/ppermute | solution.py:547

commit v2 on v1

--- a/solution.py
+++ b/solution.py
@@ -27,21 +27,33 @@
 KV = 2 * WIDTH
 GRAD = 2 * WIDTH + DHEAD
 
-QUAD = (4, 8, 12)
+QUAD = (4, 12, 8)
 PLANES = (16, 32, 48)
-HALF2_BLOCKS = QUAD + tuple(2 ^ o for o in QUAD)
-QUARTER3_BLOCKS = tuple(y ^ o for o in (0,) + QUAD for y in PLANES)
-HALF3_BLOCKS = QUARTER3_BLOCKS + tuple(2 ^ o for o in QUARTER3_BLOCKS)
+THIRD_BLOCKS = tuple(y ^ o for o in (0,) + QUAD for y in PLANES)
+
+
+def flipped(blocks, mask):
+    return tuple(o ^ mask for o in blocks)
+
+
 SLOTS = (
-    ((2, 3), 64),
-    (HALF2_BLOCKS + tuple(1 ^ o for o in HALF2_BLOCKS), 16),
-    (HALF3_BLOCKS + tuple(1 ^ o for o in HALF3_BLOCKS), 4),
+    (1, (2, 3)),
+    (2, QUAD),
+    (2, flipped(QUAD, 1)),
+    (3, THIRD_BLOCKS),
+    (3, flipped(THIRD_BLOCKS, 1)),
+    (2, flipped(QUAD, 2)),
+    (2, flipped(QUAD, 3)),
+    (3, flipped(THIRD_BLOCKS, 2)),
+    (3, flipped(THIRD_BLOCKS, 3)),
 )
+EARLY = 320
 
 
 def slot_table():
-    offset = np.concatenate([np.repeat(np.array(blocks, np.int32), rows) for blocks, rows in SLOTS])
-    level = np.concatenate([np.full(len(blocks) * rows, n + 1, np.int32) for n, (blocks, rows) in enumerate(SLOTS)])
+    rows = {1: 64, 2: 16, 3: 4}
+    offset = np.concatenate([np.repeat(np.array(blocks, np.int32), rows[n]) for n, blocks in SLOTS])
+    level = np.concatenate([np.full(len(blocks) * rows[n], n, np.int32) for n, blocks in SLOTS])
     table = np.zeros((8, FAR), np.int32)
     table[0], table[1] = offset, level
     return table
@@ -112,18 +124,25 @@
     return jnp.broadcast_to(column, (column.shape[0], DHEAD))
 
 
+def early(refs, lanes):
+    l1a, l2a, core1 = refs
+    pieces = [l1a[:, lanes], core1[0:64, lanes], l2a[0:48, lanes], core1[64:112, lanes]]
+    return pieces + [l2a[48:96, lanes], core1[112:160, lanes]]
+
+
+def late(refs, lanes):
+    l2b, core2 = refs
+    return [l2b[0:48, lanes], core2[0:48, lanes], l2b[48:96, lanes], core2[48:96, lanes]]
+
+
 def gathered(refs, lanes):
-    l1a, l2a, l2b, core1, core2 = refs
-    pieces = [l1a[:, lanes], core1[0:64, lanes]]
-    pieces += [l2a[0:48, lanes], l2b[0:48, lanes], core1[64:112, lanes], core2[0:48, lanes]]
-    pieces += [l2a[48:96, lanes], l2b[48:96, lanes], core1[112:160, lanes], core2[48:96, lanes]]
-    return jnp.concatenate(pieces, axis=0)
+    return jnp.concatenate(early(refs[0:3], lanes) + late(refs[3:5], lanes), axis=0)
 
 
 def pool_kernel(
     table_ref, k_ref, v_ref, q_ref,
-    own_ref, first_ref, second_ref, third_ref, trio_ref, bias_ref, edge_ref,
-    e0_ref, e1_ref, e2_ref, in_ref, sems, out_sems,
+    own_ref, first_ref, second_ref, third_ref, bias_ref, edge_ref,
+    e0_ref, e1_ref, e2_ref, in_ref, sems,
 ):
     copies = []
     for i, ref in enumerate((k_ref, v_ref, q_ref)):
@@ -143,13 +162,9 @@
     alone = (place == 0) | (place == last)
     edge_ref[...] = jnp.full((8, BLOCK), jnp.where(alone, NEGATIVE_FILL, 0.0), jnp.float32)
     own_ref[84:96, :] = jnp.zeros((12, 3 * WIDTH), jnp.float32)
-    stores = []
     for part in range(3):
         for copy in copies[4 * part : 4 * part + 4]:
             copy.wait()
-        lanes = pl.ds(part * WIDTH, WIDTH)
-        stores.append(pltpu.make_async_copy(in_ref.at[part], trio_ref.at[:, lanes], out_sems.at[part]))
-        stores[-1].start()
         for h in range(HEADS):
             dst = cols(h, part * WIDTH)
             value = in_ref[part, :, cols(h)]
@@ -163,8 +178,6 @@
                 first_ref[:, dst] = one
                 second_ref[:, dst] = two
                 third_ref[:, dst] = three
-    for store in stores:
-        store.wait()
 
 
 def pack_kernel(second_ref, a_ref, b_ref, c_ref, out_ref):
@@ -174,10 +187,16 @@
     out_ref[24:28, :] = c_ref[...]
 
 
-def merge_kernel(first_ref, own_ref, a_ref, b_ref, c_ref, out_ref, bundle_ref):
+def double_kernel(own_ref, other_ref, out_ref):
+    out_ref[0:28, :] = own_ref[...]
+    out_ref[28:56, :] = other_ref[...]
+
+
+def merge_kernel(first_ref, double_ref, other_ref, out_ref, bundle_ref):
     bundle_ref[0:64, :] = first_ref[...]
-    pieces = [(16 * i, ref[0:16, :]) for i, ref in enumerate((a_ref, b_ref, c_ref))]
-    pieces += [(48 + 12 * i, ref[16:28, :]) for i, ref in enumerate((own_ref, a_ref, b_ref, c_ref))]
+    parts = (double_ref[28:56, :], other_ref[0:28, :], other_ref[28:56, :])
+    pieces = [(16 * i, part[0:16]) for i, part in enumerate(parts)]
+    pieces += [(48 + 12 * i, part[16:28]) for i, part in enumerate((double_ref[0:28, :],) + parts)]
     for start, piece in pieces:
         stop = start + piece.shape[0]
         out_ref[start:stop, :] = piece
@@ -362,23 +381,40 @@
     dv_ref[...] = dv_in_ref[...] + d_values
 
 
-def far_key_kernel(
-    bias_ref, own_ref, a0, a1, a2, a3, a4, dk_in_ref, dv_in_ref, dk_ref, dv_ref, e0_ref, e1_ref
-):
-    far = (a0, a1, a2, a3, a4)
-    bias = bias_ref[...]
-    stats = jnp.transpose(gathered(far, slice(KV, GRAD)))[0:8, :]
+def far_key_parts(own_ref, bias, pieces, h):
+    def take(lanes):
+        return jnp.concatenate(pieces(lanes), axis=0)
+
+    stats = take(slice(KV, GRAD))
+    fill = jnp.zeros((64, DHEAD), jnp.float32)
+    stats = jnp.transpose(jnp.concatenate([stats, fill], axis=0))[0:8, 0 : stats.shape[0]]
+    queries = take(cols(h, WIDTH))
+    grads = take(cols(h))
+    scores = nt3(own_ref[:, cols(h)], queries) * INV_ROOT + bias
+    weights = jnp.exp(scores - stats[h : h + 1, :])
+    d_scores = weights * (nt3(own_ref[:, cols(h, WIDTH)], grads) - stats[HEADS + h : HEADS + h + 1, :])
+    return nn3(d_scores, queries) * INV_ROOT, nn3(weights, grads)
+
+
+def early_key_kernel(bias_ref, own_ref, a0, a1, a2, dk_ref, dv_ref):
+    bias = bias_ref[:, 0:EARLY]
     for h in range(HEADS):
         k = cols(h)
-        queries = gathered(far, cols(h, WIDTH))
-        grads = gathered(far, k)
-        scores = nt3(own_ref[:, k], queries) * INV_ROOT + bias
-        weights = jnp.exp(scores - stats[h : h + 1, :])
-        d_scores = weights * (nt3(own_ref[:, cols(h, WIDTH)], grads) - stats[HEADS + h : HEADS + h + 1, :])
-        scales = [1.0 / 4**n for n in (1, 2, 3)]
-        d_keys = nn3(d_scores, queries) * INV_ROOT
+        dk_ref[:, k], dv_ref[:, k] = far_key_parts(own_ref, bias, lambda lanes: early((a0, a1, a2), lanes), h)
+
+
+def late_key_kernel(
+    bias_ref, own_ref, a0, a1, far_dk_ref, far_dv_ref, dk_in_ref, dv_in_ref, dk_ref, dv_ref, e0_ref, e1_ref
+):
+    bias = bias_ref[:, EARLY:FAR]
+    scales = [1.0 / 4**n for n in (1, 2, 3)]
+    for h in range(HEADS):
+        k = cols(h)
+        d_keys, d_values = far_key_parts(own_ref, bias, lambda lanes: late((a0, a1), lanes), h)
+        d_keys = far_dk_ref[:, k] + d_keys
+        d_values = far_dv_ref[:, k] + d_values
         dk_ref[:, k] = dk_in_ref[:, k] + expand_levels(e0_ref.at[h % 2], d_keys, scales)
-        dv_ref[:, k] = dv_in_ref[:, k] + expand_levels(e1_ref.at[h % 2], nn3(weights, grads), scales)
+        dv_ref[:, k] = dv_in_ref[:, k] + expand_levels(e1_ref.at[h % 2], d_values, scales)
 
 
 def f32(*shape):
@@ -409,8 +445,8 @@
 BLOCK_FLOPS = 2.0 * BLOCK * BLOCK * DHEAD * HEADS * 6
 
 
-def column_at(first):
-    return pl.BlockSpec((BLOCK, DHEAD), lambda h: (0, first + h))
+def column():
+    return pl.BlockSpec((BLOCK, DHEAD), lambda h: (0, h))
 
 
 def slab(blocks):
@@ -429,25 +465,24 @@
     )(*operands)
 
 
-def near_inner(trio, inn):
-    k, v, q = column_at(0), column_at(HEADS), column_at(2 * HEADS)
+def near_inner(query, keys, values):
+    k = column()
     outs = [f32(HEADS, BLOCK, 2 * BLOCK)] + [f32(BLOCK, WIDTH)] * 3
-    return head_call(near_inner_kernel, outs, [slab(2), k, k, k], [q, k, k, v, v], 4, trio, trio, inn, trio, inn)
-
-
-def near_outer(edge, trio, out):
-    k, v, q = column_at(0), column_at(HEADS), column_at(2 * HEADS)
+    return head_call(near_inner_kernel, outs, [slab(2), k, k, k], [k] * 5, 4, query, *keys, *values)
+
+
+def near_outer(edge, query, keys, values):
+    k = column()
     outs = [f32(HEADS, BLOCK, BLOCK)] + [f32(BLOCK, WIDTH)] * 3
     edge_spec = pl.BlockSpec((8, BLOCK), lambda h: (0, 0))
-    return head_call(near_outer_kernel, outs, [slab(1), k, k, k], [edge_spec, q, k, v], 2, edge, trio, out, out)
-
-
-def near_query(w0, w1, peak0, peak1, lse, delta, d_out, trio, inn, out):
-    k, v = column_at(0), column_at(HEADS)
-    specs = [slab(2), slab(1)] + [k] * 8 + [v] * 3
+    return head_call(near_outer_kernel, outs, [slab(1), k, k, k], [edge_spec, k, k, k], 2, edge, query, keys, values)
+
+
+def near_query(w0, w1, peak0, peak1, lse, delta, d_out, keys, values):
+    k = column()
+    specs = [slab(2), slab(1)] + [k] * 11
     return head_call(
-        near_query_kernel, f32(BLOCK, WIDTH), k, specs, 6,
-        w0, w1, peak0, peak1, lse, delta, d_out, trio, inn, out, trio, inn, out,
+        near_query_kernel, f32(BLOCK, WIDTH), k, specs, 6, w0, w1, peak0, peak1, lse, delta, d_out, *keys, *values
     )
 
 
@@ -455,19 +490,19 @@
     return pl.BlockSpec((8, 256), lambda h: (BLOCK // 8, 0))
 
 
-def inner_key(trio, inn, d_out, d_in):
-    k, v, q, t = column_at(0), column_at(HEADS), column_at(2 * HEADS), stat_rows()
+def inner_key(key, value, query, query_in, d_out, d_in):
+    k, t = column(), stat_rows()
     return head_call(
-        inner_key_kernel, [f32(BLOCK, WIDTH)] * 2, [k, k], [k, v, q, q, k, k, t, t], 8,
-        trio, trio, trio, inn, d_out, d_in, d_out, d_in,
-    )
-
-
-def outer_key(trio, out, d_far, dk, dv):
-    k, v, q, t = column_at(0), column_at(HEADS), column_at(2 * HEADS), stat_rows()
+        inner_key_kernel, [f32(BLOCK, WIDTH)] * 2, [k, k], [k] * 6 + [t, t], 8,
+        key, value, query, query_in, d_out, d_in, d_out, d_in,
+    )
+
+
+def outer_key(key, value, query_out, d_far, dk, dv):
+    k, t = column(), stat_rows()
     return head_call(
-        outer_key_kernel, [f32(BLOCK, WIDTH)] * 2, [k, k], [k, v, q, k, t, k, k], 4,
-        trio, trio, out, d_far, d_far, dk, dv,
+        outer_key_kernel, [f32(BLOCK, WIDTH)] * 2, [k, k], [k] * 4 + [t, k, k], 4,
+        key, value, query_out, d_far, d_far, dk, dv,
     )
 
 
@@ -477,17 +512,16 @@
     return pl.pallas_call(
         pool_kernel,
         out_shape=[
-            f32(OWN, 3 * WIDTH), f32(64, KV), f32(16, KV), f32(4, KV), f32(BLOCK, 3 * WIDTH), f32(OWN, FAR), f32(8, BLOCK),
+            f32(OWN, 3 * WIDTH), f32(64, KV), f32(16, KV), f32(4, KV), f32(OWN, FAR), f32(8, BLOCK),
         ],
         in_specs=[vmem] + [hbm] * 3,
-        out_specs=[vmem] * 4 + [hbm] + [vmem] * 2,
+        out_specs=[vmem] * 6,
         scratch_shapes=[
             pltpu.VMEM((2, BLOCK, DHEAD), jnp.float32),
             pltpu.VMEM((64, DHEAD), jnp.float32),
             pltpu.VMEM((16, DHEAD), jnp.float32),
             pltpu.VMEM((3, BLOCK, WIDTH), jnp.float32),
             pltpu.SemaphoreType.DMA((3, 4)),
-            pltpu.SemaphoreType.DMA((3,)),
         ],
         compiler_params=pltpu.CompilerParams(vmem_limit_bytes=POOL_VMEM_BYTES),
         cost_estimate=cost(1e6, 2e6),
@@ -528,14 +562,18 @@
     return grad
 
 
-def far_key(bias, own, grads, near_dk, near_dv):
+def early_key(bias, own, grads):
+    return whole_call(early_key_kernel, [f32(OWN, WIDTH)] * 2, [], BLOCK_FLOPS, 3e6, bias, own, *grads)
+
+
+def late_key(bias, own, grads, far_dk, far_dv, near_dk, near_dv):
     return whole_call(
-        far_key_kernel,
+        late_key_kernel,
         [f32(BLOCK, WIDTH)] * 2,
         [(2, BLOCK, DHEAD)] * 2,
         BLOCK_FLOPS,
-        6e6,
-        bias, own, *grads, near_dk, near_dv,
+        3e6,
+        bias, own, *grads, far_dk, far_dv, near_dk, near_dv,
     )
 
 
@@ -556,48 +594,60 @@
     def packed(second, thirds):
         return whole_call(pack_kernel, [f32(28, second.shape[1])], [], 1e4, 1e5, second, *thirds)[0]
 
-    def merged(first, pack, quads):
+    def doubled(pack, other):
+        return whole_call(double_kernel, [f32(56, pack.shape[1])], [], 1e4, 1e5, pack, other)[0]
+
+    def merged(first, double, other):
         width = first.shape[1]
-        return whole_call(merge_kernel, [f32(96, width), f32(160, width)], [], 1e4, 1e5, first, pack, *quads)
+        return whole_call(merge_kernel, [f32(96, width), f32(160, width)], [], 1e4, 1e5, first, double, other)
 
     gain = norm_gain.reshape(1, WIDTH)
-    own, first, second, third, trio, bias, edge = pool(key, value, query)
+    out_k, out_v = exchange_outer(key), exchange_outer(value)
+    own, first, second, third, bias, edge = pool(key, value, query)
 
     planes = [exchange(third, mask) for mask in PLANES]
     l1a = exchange(first, 2)
-    inn = exchange(trio, 1)
-    pack = packed(second, planes)
-    quads = [exchange(pack, mask) for mask in QUAD]
-    out = exchange_outer(after(trio, pack))
-    w0, *inner = near_inner(trio, inn)
-    l2a, bundle = merged(l1a, after(pack, w0), quads)
+    pack = packed(after(second, out_k, out_v), planes)
+    in_k, in_v = exchange(after(key, pack), 1), exchange(after(value, pack), 1)
+    double = doubled(after(pack, l1a), exchange(pack, 4))
+    other = exchange(double, 12)
+    w0, *inner = near_inner(query, (key, after(in_k, double)), (value, in_v))
+    w1, *outer = near_outer(edge, query, after(out_k, double), out_v)
+    l2a, bundle = merged(l1a, after(double, w0, w1), other)
     l2b = exchange(l2a, 2)
     core1 = exchange(bundle, 1)
     core2 = exchange(l2b, 1)
-    w1, *outer = near_outer(edge, trio, out)
-    far = (l1a, l2a, l2b, core1, core2)
+    query_in = exchange(after(query, core2), 1)
+    query_out = exchange_outer(after(query, core2))
+    far = (l1a, l2a, core1, l2b, core2)
     attention, lse, stats = far_forward(bias, own, far, inner, outer, upstream, gain)
 
     others = [
         lax.ppermute(stats, "head", [(i, i ^ mask) for i in range(head_count)]) for mask in range(1, head_count)
     ]
+    attention = after(attention, query_in, query_out)
     attended, d_out, delta, g1, g2, g3 = cotangent(stats, others, own, attention, lse, upstream, gain)
 
+    d_far = exchange_outer(d_out)
     planes = [exchange(g3, mask) for mask in PLANES]
     l1a = exchange(g1, 2)
-    d_in = exchange(d_out, 1)
-    pack = packed(g2, planes)
-    quads = [exchange(pack, mask) for mask in QUAD]
-    near_dq = near_query(w0, w1, inner[0], outer[0], lse, delta, after(d_out, pack), trio, inn, out)
-    near_dk, near_dv = inner_key(trio, inn, d_out, d_in)
-    l2a, bundle = merged(l1a, after(pack, near_dq, near_dk), quads)
+    pack = packed(after(g2, d_far), planes)
+    d_in = exchange(after(d_out, pack), 1)
+    quad = exchange(pack, 4)
+    near_dq = near_query(
+        w0, w1, inner[0], outer[0], lse, delta, after(d_out, pack), (key, in_k, out_k), (value, in_v, out_v)
+    )
+    double = doubled(after(pack, near_dq, l1a), quad)
+    other = exchange(double, 12)
+    near_dk, near_dv = inner_key(key, value, query, query_in, d_out, after(d_in, double))
+    query_grad = far_query(bias, own, far, after(g1, double), g2, g3, near_dq)
+    l2a, bundle = merged(l1a, after(double, near_dk, query_grad), other)
     l2b = exchange(l2a, 2)
     core1 = exchange(bundle, 1)
-    d_far = exchange_outer(after(d_out, l2a))
-    query_grad = far_query(bias, own, far, g1, g2, g3, near_dq)
-    core2 = exchange(after(l2b, query_grad), 1)
-    near_dk, near_dv = outer_key(trio, out, d_far, near_dk, near_dv)
-    key_grad, value_grad = far_key(bias, own, (l1a, l2a, l2b, core1, core2), near_dk, near_dv)
+    near_dk, near_dv = outer_key(key, value, query_out, after(d_far, l2a), near_dk, near_dv)
+    far_dk, far_dv = early_key(bias, own, (l1a, after(l2a, near_dk), core1))
+    core2 = exchange(after(l2b, near_dk), 1)
+    key_grad, value_grad = late_key(bias, own, (l2b, core2), far_dk, far_dv, near_dk, near_dv)
     return attended, query_grad, key_grad, value_grad
 
 

time: 136 us -> 138 us (1.015)
  waiting for transfers between devices: 40 us -> 50.6 us
  starting transfers between devices: 53.7 us -> 44.8 us
    ppermute x22, starting transfers between devices: 42 us -> 26.8 us  [exchange(): return lax.ppermute(array, 'seq', [(i, i ^ mask) for i in range(count)])]
    ppermute x22, waiting for transfers between devices: 33.3 us -> 40.5 us  [exchange(): return lax.ppermute(array, 'seq', [(i, i ^ mask) for i in range(count)])]
    ppermute x2 -> x4, starting transfers between devices: 8.37 us -> 14.1 us  [exchange_outer(): return lax.ppermute(array, 'seq', pairs)]
    ppermute x2 -> x4, waiting for transfers between devices: 3.48 us -> 8.07 us  [exchange_outer(): return lax.ppermute(array, 'seq', pairs)]
    pallas_call x8 -> x11, Pallas kernels: 12.5 us -> 14 us  [whole_call(): pl.pallas_call(kernel, out_shape=outs, in_specs=[spec] * len(operands), o...]
  transfers between devices with their start and end apart: 27 -> 29, of which waited for: 9 -> 13; matrix products, arithmetic and copies ran while one was open for 0% -> 0% of each run, Pallas kernels for 19% -> 25%
where the time goes in v2:
time: 138 us; the launch traced here: 137 us
  waiting for transfers between devices  50.6 us (37%)
  starting transfers between devices  44.8 us (32%)
  Pallas kernels  39.4 us (29%)
  local copies, waits for them, and re-layouts  1.58 us (1%)
    ppermute x22, waiting for transfers between devices, exchange(): return lax.ppermute(array, 'seq', [(i, i ^ mask) for i in range(count)])  40.5 us
    ppermute x22, starting transfers between devices, exchange(): return lax.ppermute(array, 'seq', [(i, i ^ mask) for i in range(count)])  26.8 us
    pallas_call x5, Pallas kernels, head_call(): pl.pallas_call(kernel, grid=(HEADS,), out_shape=outs, in_specs=in_specs,...  22.1 us
    ppermute x4, starting transfers between devices, exchange_outer(): return lax.ppermute(array, 'seq', pairs)  14.1 us
    pallas_call x11, Pallas kernels, whole_call(): pl.pallas_call(kernel, out_shape=outs, in_specs=[spec] * len(operands), o...  14 us
    ppermute x4, waiting for transfers between devices, exchange_outer(): return lax.ppermute(array, 'seq', pairs)  8.07 us
    ppermute x3, starting transfers between devices, body(): lax.ppermute(stats, 'head', [(i, i ^ mask) for i in range(head_count)])  3.95 us
    pallas_call x1, Pallas kernels, pool(): pl.pallas_call(pool_kernel, out_shape=[f32(OWN, 3 * WIDTH), f32(64, KV),...  3.27 us
  transfers between devices with their start and end apart: 29, of which 13 were waited for; matrix products, arithmetic and copies ran while one was open for 0% of the time, Pallas kernels for 25%

profile of v2, /device:TPU:1, one launch (start us, length us, event | category | flops | bytes accessed | tf_op | source)
XLA Modules:
  0.0 137.3 jit_solution(3632618107962087511)
XLA Ops:
  0.6 5.1 %collective-permute-start.1 = (f32[256,512]{1,0:T(8,128)}, f32[256,512]{1,0:T(8,128)S(1)}, u32[]{:S(2)}, u32[]{:S(2)}) collective-permute-start(f32[256,512]{1,0:T(8,128)} %k_ref.5), channel_id=1, source_target_pairs={{4,8},{8,4},{12,16},{16,12},{20,24},{24,20},{28,32},{32,28},{36,40... | collective-permute-start | bytes 1572872 | tf_op jit(solution)/shard_map/ppermute | solution.py:589
  5.7 1.9 %collective-permute-start.2 = (f32[256,512]{1,0:T(8,128)}, f32[256,512]{1,0:T(8,128)S(1)}, u32[]{:S(2)}, u32[]{:S(2)}) collective-permute-start(f32[256,512]{1,0:T(8,128)} %v_ref.5), channel_id=1, source_target_pairs={{4,8},{8,4},{12,16},{16,12},{20,24},{24,20},{28,32},{32,28},{36,40... | collective-permute-start | bytes 1572872 | tf_op jit(solution)/shard_map/ppermute | solution.py:589
  7.6 3.3 %shard_map.93 = (f32[96,1536]{1,0:T(8,128)}, f32[64,1024]{1,0:T(8,128)}, f32[16,1024]{1,0:T(8,128)}, f32[4,1024]{1,0:T(4,128)}, f32[96,512]{1,0:T(8,128)}, /*index=5*/f32[8,256]{1,0:T(8,128)}) custom-call(s32[8,512]{1,0:T(8,128)} %constant.2.clone.table_ref, f32[256,512]{1,0:T(8,128)} %k_ref.5, f32[256,512]{1,0:T(8,128)} %v_ref.5, f32[256,512]{1,0:T(8,128)} %q0_ref.1), custom_call_target="tpu_custom_call" | custom-call | flops 1000000 | bytes 2000000 | tf_op jit(solution)/shard_map/pallas_call | solution.py:512
  10.9 0.0 copy-start.3
  10.9 0.0 copy-start.4
  10.9 1.4 %collective-permute-start.3 = (f32[4,1024]{1,0:T(4,128)}, f32[4,1024]{1,0:T(4,128)S(1)}, u32[]{:S(2)}, u32[]{:S(2)}) collective-permute-start(f32[4,1024]{1,0:T(4,128)} %get-tuple-element.62), channel_id=1, source_target_pairs={{0,64},{4,68},{8,72},{12,76},{16,80},{20,84},{24,88},{28,92},{32,9... | collective-permute-start | bytes 49160 | tf_op jit(solution)/shard_map/ppermute | solution.py:585
  12.3 2.6 %collective-permute-start.4 = (f32[4,1024]{1,0:T(4,128)}, f32[4,1024]{1,0:T(4,128)S(1)}, u32[]{:S(2)}, u32[]{:S(2)}) collective-permute-start(f32[4,1024]{1,0:T(4,128)} %get-tuple-element.62), channel_id=1, source_target_pairs={{0,128},{4,132},{8,136},{12,140},{16,144},{20,148},{24,152},{28,15... | collective-permute-start | bytes 49160 | tf_op jit(solution)/shard_map/ppermute | solution.py:585
  15.0 0.0 collective-permute-start.5
  15.0 0.0 collective-permute-done.1.k_ref.k2_ref
  15.0 3.4 %collective-permute-done.2.v_ref.v2_ref = f32[256,512]{1,0:T(8,128)S(1)} collective-permute-done((f32[256,512]{1,0:T(8,128)}, f32[256,512]{1,0:T(8,128)S(1)}, u32[]{:S(2)}, u32[]{:S(2)}) %collective-permute-start.2) | collective-permute-done | bytes 524320 | tf_op jit(solution)/shard_map/ppermute | solution.py:589
  18.4 0.0 collective-permute-done.3.a_ref
  18.4 6.2 %collective-permute-done.4.b_ref = f32[4,1024]{1,0:T(4,128)S(1)} collective-permute-done((f32[4,1024]{1,0:T(4,128)}, f32[4,1024]{1,0:T(4,128)S(1)}, u32[]{:S(2)}, u32[]{:S(2)}) %collective-permute-start.4) | collective-permute-done | bytes 16416 | tf_op jit(solution)/shard_map/ppermute | solution.py:585
  24.6 0.8 copy-done.6
  25.5 1.0 collective-permute-start.7
  26.4 0.1 collective-permute-start.8
  26.6 0.2 collective-permute-start.6
  26.7 10.4 %collective-permute-done.first_ref.a0 = f32[64,1024]{1,0:T(8,128)S(1)} collective-permute-done((f32[64,1024]{1,0:T(8,128)}, f32[64,1024]{1,0:T(8,128)S(1)}, u32[]{:S(2)}, u32[]{:S(2)}) %collective-permute-start) | collective-permute-done | bytes 262176 | tf_op jit(solution)/shard_map/ppermute | solution.py:585
  37.1 0.0 collective-permute-done.6.other_ref
  37.2 2.6 %collective-permute-start.9 = (f32[56,1024]{1,0:T(8,128)S(1)}, f32[56,1024]{1,0:T(8,128)S(1)}, u32[]{:S(2)}, u32[]{:S(2)}) collective-permute-start(f32[56,1024]{1,0:T(8,128)S(1)} %shard_map.95.double_ref), channel_id=1, source_target_pairs={{0,48},{4,52},{8,56},{12,60},{16,32},{20,36},{24,40},{28,44},{32,1... | collective-permute-start | bytes 688136 | tf_op jit(solution)/shard_map/ppermute | solution.py:585
  39.8 0.7 copy-done.8
  40.5 3.6 %shard_map.97 = (f32[4,256,256]{2,1,0:T(8,128)S(1)}, f32[256,512]{1,0:T(8,128)S(1)}, f32[256,512]{1,0:T(8,128)S(1)}, f32[256,512]{1,0:T(8,128)S(1)}) custom-call(f32[8,256]{1,0:T(8,128)S(1)} %copy-done.8, f32[256,512]{1,0:T(8,128)S(1)} %copy-done.5, f32[256,512]{1,0:T(8,128)S(1)} %collective-permute-done.1.k_ref.k2_ref, ...), custom_call_target="tpu_custom_call" | custom-call | flops 805306368 | bytes 4000000 | tf_op jit(solution)/shard_map/pallas_call | solution.py:457
  44.2 0.0 copy-start.1
  44.2 0.0 copy-start.2
  44.2 0.0 copy-start.7
  44.2 0.0 collective-permute-done.8.vi_ref.v1_ref
  44.2 4.1 %shard_map.96 = (f32[4,256,512]{2,1,0:T(8,128)S(1)}, f32[256,512]{1,0:T(8,128)S(1)}, f32[256,512]{1,0:T(8,128)S(1)}, f32[256,512]{1,0:T(8,128)S(1)}) custom-call(f32[256,512]{1,0:T(8,128)S(1)} %copy-done.5, f32[256,512]{1,0:T(8,128)S(1)} %copy-done.3, f32[256,512]{1,0:T(8,128)S(1)} %collective-permute-done.7.ki_ref.k1_ref, f32[256,512]{1,0:T(8,128)S(1)} %copy-done.4, ...), custom_call_target="tpu_custom_call" | custom-call | flops 1610612736 | bytes 4000000 | tf_op jit(solution)/shard_map/pallas_call | solution.py:457
  48.3 1.1 collective-permute-done.9.other_ref
  49.4 0.1 shard_map.98
  49.5 0.3 collective-permute-start.11
  49.7 10.0 %collective-permute-done.11.a3 = f32[96,1024]{1,0:T(8,128)S(1)} collective-permute-done((f32[96,1024]{1,0:T(8,128)S(1)}, f32[96,1024]{1,0:T(8,128)S(1)}, u32[]{:S(2)}, u32[]{:S(2)}) %collective-permute-start.11) | collective-permute-done | bytes 393248 | tf_op jit(solution)/shard_map/ppermute | solution.py:585
  59.7 1.4 collective-permute-start.12
  61.1 0.0 collective-permute-start.10
  61.1 1.3 collective-permute-done.12.a4
  62.5 0.4 collective-permute-start.16
  62.8 2.1 %collective-permute-start.17 = (f32[256,512]{1,0:T(8,128)S(1)}, f32[256,512]{1,0:T(8,128)S(1)}, u32[]{:S(2)}, u32[]{:S(2)}) collective-permute-start(f32[256,512]{1,0:T(8,128)S(1)} %copy-done.5), channel_id=1, source_target_pairs={{4,8},{8,4},{12,16},{16,12},{20,24},{24,20},{28,32},{32,28},{36,40... | collective-permute-start | bytes 1572872 | tf_op jit(solution)/shard_map/ppermute | solution.py:589
  64.9 0.0 collective-permute-done.10.a2
  65.0 2.8 %shard_map.99 = (f32[256,512]{1,0:T(8,128)S(1)}, f32[256,512]{1,0:T(8,128)S(1)}, f32[8,256]{1,0:T(8,128)S(1)}) custom-call(f32[96,512]{1,0:T(8,128)S(1)} %copy-done.1, f32[96,1536]{1,0:T(8,128)S(1)} %copy-done, f32[64,1024]{1,0:T(8,128)S(1)} %collective-permute-done.first_ref.a0, f32[96,1024]{1,0:T(8,128)S(1)} %get-tuple-element.72.a1, ...), custom_call_target="tpu_custom_call" | custom-call | flops 402653184 | bytes 8000000 | tf_op jit(solution)/shard_map/pallas_call | solution.py:434
  67.8 1.3 collective-permute-start.13
  69.0 2.5 %collective-permute-start.14 = (f32[8,256]{1,0:T(8,128)S(1)}, f32[8,256]{1,0:T(8,128)S(1)}, u32[]{:S(2)}, u32[]{:S(2)}) collective-permute-start(f32[8,256]{1,0:T(8,128)S(1)} %get-tuple-element.80.s0_ref), channel_id=1, source_target_pairs={{0,2},{1,3},{2,0},{3,1},{4,6},{5,7},{6,4},{7,5},{8,10},{9,11},{10,... | collective-permute-start | bytes 24584 | tf_op jit(solution)/shard_map/ppermute | solution.py:626
  71.5 0.2 collective-permute-start.15
  71.7 1.6 %collective-permute-done.17.q_ref = f32[256,512]{1,0:T(8,128)S(1)} collective-permute-done((f32[256,512]{1,0:T(8,128)S(1)}, f32[256,512]{1,0:T(8,128)S(1)}, u32[]{:S(2)}, u32[]{:S(2)}) %collective-permute-start.17) | collective-permute-done | bytes 524320 | tf_op jit(solution)/shard_map/ppermute | solution.py:589
  73.3 2.0 %collective-permute-done.15.s3_ref = f32[8,256]{1,0:T(8,128)S(1)} collective-permute-done((f32[8,256]{1,0:T(8,128)S(1)}, f32[8,256]{1,0:T(8,128)S(1)}, u32[]{:S(2)}, u32[]{:S(2)}) %collective-permute-start.15) | collective-permute-done | bytes 8224 | tf_op jit(solution)/shard_map/ppermute | solution.py:626
  75.3 1.4 shard_map.100
  76.7 5.0 %collective-permute-start.18 = (f32[264,512]{1,0:T(8,128)S(1)}, f32[264,512]{1,0:T(8,128)S(1)}, u32[]{:S(2)}, u32[]{:S(2)}) collective-permute-start(f32[264,512]{1,0:T(8,128)S(1)} %get-tuple-element.92.dout_ref.d0_ref.t0_ref), channel_id=1, source_target_pairs={{4,8},{8,4},{12,16},{16,12},{20,24},{24,20},{28,32},{32,28},{36,40... | collective-permute-start | bytes 1622024 | tf_op jit(solution)/shard_map/ppermute | solution.py:589
  81.7 1.5 %collective-permute-start.19 = (f32[4,1152]{1,0:T(4,128)S(1)}, f32[4,1152]{1,0:T(4,128)S(1)}, u32[]{:S(2)}, u32[]{:S(2)}) collective-permute-start(f32[4,1152]{1,0:T(4,128)S(1)} %get-tuple-element.90.third_ref), channel_id=1, source_target_pairs={{0,64},{4,68},{8,72},{12,76},{16,80},{20,84},{24,88},{28,92},{32,9... | collective-permute-start | bytes 55304 | tf_op jit(solution)/shard_map/ppermute | solution.py:585
  83.2 2.0 %collective-permute-start.20 = (f32[4,1152]{1,0:T(4,128)S(1)}, f32[4,1152]{1,0:T(4,128)S(1)}, u32[]{:S(2)}, u32[]{:S(2)}) collective-permute-start(f32[4,1152]{1,0:T(4,128)S(1)} %get-tuple-element.90.third_ref), channel_id=1, source_target_pairs={{0,128},{4,132},{8,136},{12,140},{16,144},{20,148},{24,152},{28,15... | collective-permute-start | bytes 55304 | tf_op jit(solution)/shard_map/ppermute | solution.py:585
  85.2 0.5 collective-permute-start.21
  85.7 3.0 %collective-permute-done.18.d_ref.t_ref = f32[264,512]{1,0:T(8,128)S(1)} collective-permute-done((f32[264,512]{1,0:T(8,128)S(1)}, f32[264,512]{1,0:T(8,128)S(1)}, u32[]{:S(2)}, u32[]{:S(2)}) %collective-permute-start.18) | collective-permute-done | bytes 540704 | tf_op jit(solution)/shard_map/ppermute | solution.py:589
  88.8 0.3 collective-permute-done.21.c_ref
  89.1 5.4 %collective-permute-start.24 = (f32[264,512]{1,0:T(8,128)S(1)}, f32[264,512]{1,0:T(8,128)S(1)}, u32[]{:S(2)}, u32[]{:S(2)}) collective-permute-start(f32[264,512]{1,0:T(8,128)S(1)} %get-tuple-element.92.dout_ref.d0_ref.t0_ref), channel_id=1, source_target_pairs={{0,4},{4,0},{8,12},{12,8},{16,20},{20,16},{24,28},{28,24},{32,36},... | collective-permute-start | bytes 1622024 | tf_op jit(solution)/shard_map/ppermute | solution.py:585
  94.4 5.0 %shard_map.102.near_ref = f32[256,512]{1,0:T(8,128)S(1)} custom-call(f32[4,256,512]{2,1,0:T(8,128)S(1)} %get-tuple-element.67.w0_ref, f32[4,256,256]{2,1,0:T(8,128)S(1)} %get-tuple-element.70.w1_ref, f32[256,512]{1,0:T(8,128)S(1)} %get-tuple-element.74.peak0_ref, f32[256,512]{1,0:T(8,128)S(1)} %get-tuple-element.77.peak1_ref, ...), custom_call_target="tpu_custom_call" | custom-call | flops 2415919104 | bytes 4000000 | tf_op jit(solution)/shard_map/pallas_call | solution.py:457
  99.5 6.7 %collective-permute-done.22.first_ref.a0 = f32[64,1152]{1,0:T(8,128)S(1)} collective-permute-done((f32[64,1152]{1,0:T(8,128)S(1)}, f32[64,1152]{1,0:T(8,128)S(1)}, u32[]{:S(2)}, u32[]{:S(2)}) %collective-permute-start.22) | collective-permute-done | bytes 294944 | tf_op jit(solution)/shard_map/ppermute | solution.py:585
  106.2 0.1 collective-permute-start.25
  106.3 3.7 %shard_map.104 = f32[256,512]{1,0:T(8,128)} custom-call(f32[96,512]{1,0:T(8,128)S(1)} %copy-done.1, f32[96,1536]{1,0:T(8,128)S(1)} %copy-done, f32[64,1024]{1,0:T(8,128)S(1)} %collective-permute-done.first_ref.a0, f32[96,1024]{1,0:T(8,128)S(1)} %get-tuple-element.72.a1, f32[160,1024]{1,0:T(8,128)S(1)} %collective-permute-done.10.a2, ...), custom_call_target="tpu_custom_call" | custom-call | flops 402653184 | bytes 6000000 | tf_op jit(solution)/shard_map/pallas_call | solution.py:434
  110.0 5.6 %shard_map.105 = (f32[256,512]{1,0:T(8,128)S(1)}, f32[256,512]{1,0:T(8,128)S(1)}) custom-call(f32[256,512]{1,0:T(8,128)S(1)} %copy-done.3, f32[256,512]{1,0:T(8,128)S(1)} %copy-done.4, f32[256,512]{1,0:T(8,128)S(1)} %copy-done.5, f32[256,512]{1,0:T(8,128)S(1)} %collective-permute-done.16.q1_ref, f32[264,512]{1,0:T(8,128)S(1)} %get-tuple-element.92.dout_ref.d0_ref.t0_ref, ...), custom_call_target="tpu_custom_call" | custom-call | flops 3221225472 | bytes 4000000 | tf_op jit(solution)/shard_map/pallas_call | solution.py:457
  115.6 1.5 %collective-permute-done.25.other_ref = f32[56,1152]{1,0:T(8,128)S(1)} collective-permute-done((f32[56,1152]{1,0:T(8,128)S(1)}, f32[56,1152]{1,0:T(8,128)S(1)}, u32[]{:S(2)}, u32[]{:S(2)}) %collective-permute-start.25) | collective-permute-done | bytes 258080 | tf_op jit(solution)/shard_map/ppermute | solution.py:585
  117.1 0.1 shard_map.106
  117.2 3.0 %collective-permute-start.26 = (f32[96,1152]{1,0:T(8,128)S(1)}, f32[96,1152]{1,0:T(8,128)S(1)}, u32[]{:S(2)}, u32[]{:S(2)}) collective-permute-start(f32[96,1152]{1,0:T(8,128)S(1)} %get-tuple-element.103.a1), channel_id=1, source_target_pairs={{0,8},{4,12},{8,0},{12,4},{16,24},{20,28},{24,16},{28,20},{32,40},... | collective-permute-start | bytes 1327112 | tf_op jit(solution)/shard_map/ppermute | solution.py:585
  120.2 2.1 %collective-permute-start.28 = (f32[160,1152]{1,0:T(8,128)S(1)}, f32[160,1152]{1,0:T(8,128)S(1)}, u32[]{:S(2)}, u32[]{:S(2)}) collective-permute-start(f32[160,1152]{1,0:T(8,128)S(1)} %get-tuple-element.104), channel_id=1, source_target_pairs={{0,4},{4,0},{8,12},{12,8},{16,20},{20,16},{24,28},{28,24},{32,36},... | collective-permute-start | bytes 2211848 | tf_op jit(solution)/shard_map/ppermute | solution.py:585
  122.3 3.7 %shard_map.107 = (f32[256,512]{1,0:T(8,128)S(1)}, f32[256,512]{1,0:T(8,128)S(1)}) custom-call(f32[256,512]{1,0:T(8,128)S(1)} %copy-done.3, f32[256,512]{1,0:T(8,128)S(1)} %copy-done.4, f32[256,512]{1,0:T(8,128)S(1)} %collective-permute-done.17.q_ref, f32[264,512]{1,0:T(8,128)S(1)} %collective-permute-done.18.d_ref.t_ref, ...), custom_call_target="tpu_custom_call" | custom-call | flops 1610612736 | bytes 4000000 | tf_op jit(solution)/shard_map/pallas_call | solution.py:457
  126.0 2.9 %collective-permute-done.26.a0 = f32[96,1152]{1,0:T(8,128)S(1)} collective-permute-done((f32[96,1152]{1,0:T(8,128)S(1)}, f32[96,1152]{1,0:T(8,128)S(1)}, u32[]{:S(2)}, u32[]{:S(2)}) %collective-permute-start.26) | collective-permute-done | bytes 442400 | tf_op jit(solution)/shard_map/ppermute | solution.py:585
  128.9 2.4 %collective-permute-start.27 = (f32[96,1152]{1,0:T(8,128)S(1)}, f32[96,1152]{1,0:T(8,128)S(1)}, u32[]{:S(2)}, u32[]{:S(2)}) collective-permute-start(f32[96,1152]{1,0:T(8,128)S(1)} %collective-permute-done.26.a0), channel_id=1, source_target_pairs={{0,4},{4,0},{8,12},{12,8},{16,20},{20,16},{24,28},{28,24},{32,36},... | collective-permute-start | bytes 1327112 | tf_op jit(solution)/shard_map/ppermute | solution.py:585
  131.4 2.7 %shard_map.108 = (f32[96,512]{1,0:T(8,128)S(1)}, f32[96,512]{1,0:T(8,128)S(1)}) custom-call(f32[96,512]{1,0:T(8,128)S(1)} %copy-done.1, f32[96,1536]{1,0:T(8,128)S(1)} %copy-done, f32[64,1152]{1,0:T(8,128)S(1)} %collective-permute-done.22.first_ref.a0, f32[96,1152]{1,0:T(8,128)S(1)} %get-tuple-element.103.a1, f32[160,1152]{1,0:T(8,128)S(1)} %collective-permute-done.28.a2), custom_call_target="tpu_custom_call" | custom-call | flops 402653184 | bytes 3000000 | tf_op jit(solution)/shard_map/pallas_call | solution.py:434
  134.1 3.2 %shard_map.109 = (f32[256,512]{1,0:T(8,128)}, f32[256,512]{1,0:T(8,128)}) custom-call(f32[96,512]{1,0:T(8,128)S(1)} %copy-done.1, f32[96,1536]{1,0:T(8,128)S(1)} %copy-done, f32[96,1152]{1,0:T(8,128)S(1)} %collective-permute-done.26.a0, f32[96,1152]{1,0:T(8,128)S(1)} %collective-permute-done.27.a1, f32[96,512]{1,0:T(8,128)S(1)} %get-tuple-element.105.far_dk_ref, ...), custom_call_target="tpu_custom_call" | custom-call | flops 402653184 | bytes 3000000 | tf_op jit(solution)/shard_map/pallas_call | solution.py:434
  (29 shorter events, 0.1 us)
Async XLA Ops:
  0.6 39.2 %copy-start.5 = (f32[256,512]{1,0:T(8,128)S(1)}, f32[256,512]{1,0:T(8,128)}, u32[]{:S(2)}) copy-start(f32[256,512]{1,0:T(8,128)} %q0_ref.1) | copy-start | bytes 1572868
  0.6 14.3 %collective-permute-start.1 = (f32[256,512]{1,0:T(8,128)}, f32[256,512]{1,0:T(8,128)S(1)}, u32[]{:S(2)}, u32[]{:S(2)}) collective-permute-start(f32[256,512]{1,0:T(8,128)} %k_ref.5), channel_id=1, source_target_pairs={{4,8},{8,4},{12,16},{16,12},{20,24},{24,20},{28,32},{32,28},{36,40... | collective-permute-start | bytes 1572872 | tf_op jit(solution)/shard_map/ppermute | solution.py:589
  5.7 12.7 %collective-permute-start.2 = (f32[256,512]{1,0:T(8,128)}, f32[256,512]{1,0:T(8,128)S(1)}, u32[]{:S(2)}, u32[]{:S(2)}) collective-permute-start(f32[256,512]{1,0:T(8,128)} %v_ref.5), channel_id=1, source_target_pairs={{4,8},{8,4},{12,16},{16,12},{20,24},{24,20},{28,32},{32,28},{36,40... | collective-permute-start | bytes 1572872 | tf_op jit(solution)/shard_map/ppermute | solution.py:589
  10.9 33.3 %copy-start.3 = (f32[256,512]{1,0:T(8,128)S(1)}, f32[256,512]{1,0:T(8,128)}, u32[]{:S(2)}) copy-start(f32[256,512]{1,0:T(8,128)} %k_ref.5) | copy-start | bytes 1572868
  10.9 33.3 %copy-start.4 = (f32[256,512]{1,0:T(8,128)S(1)}, f32[256,512]{1,0:T(8,128)}, u32[]{:S(2)}) copy-start(f32[256,512]{1,0:T(8,128)} %v_ref.5) | copy-start | bytes 1572868
  10.9 7.5 %collective-permute-start.3 = (f32[4,1024]{1,0:T(4,128)}, f32[4,1024]{1,0:T(4,128)S(1)}, u32[]{:S(2)}, u32[]{:S(2)}) collective-permute-start(f32[4,1024]{1,0:T(4,128)} %get-tuple-element.62), channel_id=1, source_target_pairs={{0,64},{4,68},{8,72},{12,76},{16,80},{20,84},{24,88},{28,92},{32,9... | collective-permute-start | bytes 49160 | tf_op jit(solution)/shard_map/ppermute | solution.py:585
  12.3 12.3 %collective-permute-start.4 = (f32[4,1024]{1,0:T(4,128)}, f32[4,1024]{1,0:T(4,128)S(1)}, u32[]{:S(2)}, u32[]{:S(2)}) collective-permute-start(f32[4,1024]{1,0:T(4,128)} %get-tuple-element.62), channel_id=1, source_target_pairs={{0,128},{4,132},{8,136},{12,140},{16,144},{20,148},{24,152},{28,15... | collective-permute-start | bytes 49160 | tf_op jit(solution)/shard_map/ppermute | solution.py:585
  15.0 9.7 %collective-permute-start.5 = (f32[4,1024]{1,0:T(4,128)}, f32[4,1024]{1,0:T(4,128)S(1)}, u32[]{:S(2)}, u32[]{:S(2)}) collective-permute-start(f32[4,1024]{1,0:T(4,128)} %get-tuple-element.62), channel_id=1, source_target_pairs={{0,192},{4,196},{8,200},{12,204},{16,208},{20,212},{24,216},{28,22... | collective-permute-start | bytes 49160 | tf_op jit(solution)/shard_map/ppermute | solution.py:585
  24.6 0.8 copy-start.6
  25.5 18.7 %collective-permute-start.7 = (f32[256,512]{1,0:T(8,128)}, f32[256,512]{1,0:T(8,128)S(1)}, u32[]{:S(2)}, u32[]{:S(2)}) collective-permute-start(f32[256,512]{1,0:T(8,128)} %k_ref.5), channel_id=1, source_target_pairs={{0,4},{4,0},{8,12},{12,8},{16,20},{20,16},{24,28},{28,24},{32,36},... | collective-permute-start | bytes 1572872 | tf_op jit(solution)/shard_map/ppermute | solution.py:585
  26.4 17.8 %collective-permute-start.8 = (f32[256,512]{1,0:T(8,128)}, f32[256,512]{1,0:T(8,128)S(1)}, u32[]{:S(2)}, u32[]{:S(2)}) collective-permute-start(f32[256,512]{1,0:T(8,128)} %v_ref.5), channel_id=1, source_target_pairs={{0,4},{4,0},{8,12},{12,8},{16,20},{20,16},{24,28},{28,24},{32,36},... | collective-permute-start | bytes 1572872 | tf_op jit(solution)/shard_map/ppermute | solution.py:585
  26.6 10.6 %collective-permute-start = (f32[64,1024]{1,0:T(8,128)}, f32[64,1024]{1,0:T(8,128)S(1)}, u32[]{:S(2)}, u32[]{:S(2)}) collective-permute-start(f32[64,1024]{1,0:T(8,128)} %get-tuple-element.59), channel_id=1, source_target_pairs={{0,8},{4,12},{8,0},{12,4},{16,24},{20,28},{24,16},{28,20},{32,40},... | collective-permute-start | bytes 786440 | tf_op jit(solution)/shard_map/ppermute | solution.py:585
  26.6 10.6 %collective-permute-start.6 = (f32[28,1024]{1,0:T(8,128)S(1)}, f32[28,1024]{1,0:T(8,128)S(1)}, u32[]{:S(2)}, u32[]{:S(2)}) collective-permute-start(f32[28,1024]{1,0:T(8,128)S(1)} %shard_map.94.own_ref), channel_id=1, source_target_pairs={{0,16},{4,20},{8,24},{12,28},{16,0},{20,4},{24,8},{28,12},{32,48},... | collective-permute-start | bytes 344072 | tf_op jit(solution)/shard_map/ppermute | solution.py:585
  37.2 12.2 %collective-permute-start.9 = (f32[56,1024]{1,0:T(8,128)S(1)}, f32[56,1024]{1,0:T(8,128)S(1)}, u32[]{:S(2)}, u32[]{:S(2)}) collective-permute-start(f32[56,1024]{1,0:T(8,128)S(1)} %shard_map.95.double_ref), channel_id=1, source_target_pairs={{0,48},{4,52},{8,56},{12,60},{16,32},{20,36},{24,40},{28,44},{32,1... | collective-permute-start | bytes 688136 | tf_op jit(solution)/shard_map/ppermute | solution.py:585
  39.8 0.7 copy-start.8
  44.1 20.8 %copy-start = (f32[96,1536]{1,0:T(8,128)S(1)}, f32[96,1536]{1,0:T(8,128)}, u32[]{:S(2)}) copy-start(f32[96,1536]{1,0:T(8,128)} %get-tuple-element.58.own_ref) | copy-start | bytes 1769476
  44.2 20.8 %copy-start.1 = (f32[96,512]{1,0:T(8,128)S(1)}, f32[96,512]{1,0:T(8,128)}, u32[]{:S(2)}) copy-start(f32[96,512]{1,0:T(8,128)} %get-tuple-element.57.bias_ref) | copy-start | bytes 589828
  44.2 20.8 %copy-start.2 = (f32[256,512]{1,0:T(8,128)S(1)}, f32[256,512]{1,0:T(8,128)}, u32[]{:S(2)}) copy-start(f32[256,512]{1,0:T(8,128)} %up_ref.3) | copy-start | bytes 1572868
  44.2 20.8 %copy-start.7 = (f32[512]{0:T(512)S(1)}, f32[512]{0:T(512)}, u32[]{:S(2)}) copy-start(f32[512]{0:T(512)} %param.9) | copy-start | bytes 6148
  49.5 10.3 %collective-permute-start.11 = (f32[96,1024]{1,0:T(8,128)S(1)}, f32[96,1024]{1,0:T(8,128)S(1)}, u32[]{:S(2)}, u32[]{:S(2)}) collective-permute-start(f32[96,1024]{1,0:T(8,128)S(1)} %get-tuple-element.72.a1), channel_id=1, source_target_pairs={{0,8},{4,12},{8,0},{12,4},{16,24},{20,28},{24,16},{28,20},{32,40},... | collective-permute-start | bytes 1179656 | tf_op jit(solution)/shard_map/ppermute | solution.py:585
  59.7 2.7 %collective-permute-start.12 = (f32[96,1024]{1,0:T(8,128)S(1)}, f32[96,1024]{1,0:T(8,128)S(1)}, u32[]{:S(2)}, u32[]{:S(2)}) collective-permute-start(f32[96,1024]{1,0:T(8,128)S(1)} %collective-permute-done.11.a3), channel_id=1, source_target_pairs={{0,4},{4,0},{8,12},{12,8},{16,20},{20,16},{24,28},{28,24},{32,36},... | collective-permute-start | bytes 1179656 | tf_op jit(solution)/shard_map/ppermute | solution.py:585
  61.1 3.8 %collective-permute-start.10 = (f32[160,1024]{1,0:T(8,128)S(1)}, f32[160,1024]{1,0:T(8,128)S(1)}, u32[]{:S(2)}, u32[]{:S(2)}) collective-permute-start(f32[160,1024]{1,0:T(8,128)S(1)} %get-tuple-element.73), channel_id=1, source_target_pairs={{0,4},{4,0},{8,12},{12,8},{16,20},{20,16},{24,28},{28,24},{32,36},... | collective-permute-start | bytes 1966088 | tf_op jit(solution)/shard_map/ppermute | solution.py:585
  62.5 9.3 %collective-permute-start.16 = (f32[256,512]{1,0:T(8,128)S(1)}, f32[256,512]{1,0:T(8,128)S(1)}, u32[]{:S(2)}, u32[]{:S(2)}) collective-permute-start(f32[256,512]{1,0:T(8,128)S(1)} %copy-done.5), channel_id=1, source_target_pairs={{0,4},{4,0},{8,12},{12,8},{16,20},{20,16},{24,28},{28,24},{32,36},... | collective-permute-start | bytes 1572872 | tf_op jit(solution)/shard_map/ppermute | solution.py:585
  62.8 10.5 %collective-permute-start.17 = (f32[256,512]{1,0:T(8,128)S(1)}, f32[256,512]{1,0:T(8,128)S(1)}, u32[]{:S(2)}, u32[]{:S(2)}) collective-permute-start(f32[256,512]{1,0:T(8,128)S(1)} %copy-done.5), channel_id=1, source_target_pairs={{4,8},{8,4},{12,16},{16,12},{20,24},{24,20},{28,32},{32,28},{36,40... | collective-permute-start | bytes 1572872 | tf_op jit(solution)/shard_map/ppermute | solution.py:589
  67.8 5.5 %collective-permute-start.13 = (f32[8,256]{1,0:T(8,128)S(1)}, f32[8,256]{1,0:T(8,128)S(1)}, u32[]{:S(2)}, u32[]{:S(2)}) collective-permute-start(f32[8,256]{1,0:T(8,128)S(1)} %get-tuple-element.80.s0_ref), channel_id=1, source_target_pairs={{0,1},{1,0},{2,3},{3,2},{4,5},{5,4},{6,7},{7,6},{8,9},{9,8},{10,11... | collective-permute-start | bytes 24584 | tf_op jit(solution)/shard_map/ppermute | solution.py:626
  69.0 4.3 %collective-permute-start.14 = (f32[8,256]{1,0:T(8,128)S(1)}, f32[8,256]{1,0:T(8,128)S(1)}, u32[]{:S(2)}, u32[]{:S(2)}) collective-permute-start(f32[8,256]{1,0:T(8,128)S(1)} %get-tuple-element.80.s0_ref), channel_id=1, source_target_pairs={{0,2},{1,3},{2,0},{3,1},{4,6},{5,7},{6,4},{7,5},{8,10},{9,11},{10,... | collective-permute-start | bytes 24584 | tf_op jit(solution)/shard_map/ppermute | solution.py:626
  71.5 3.8 %collective-permute-start.15 = (f32[8,256]{1,0:T(8,128)S(1)}, f32[8,256]{1,0:T(8,128)S(1)}, u32[]{:S(2)}, u32[]{:S(2)}) collective-permute-start(f32[8,256]{1,0:T(8,128)S(1)} %get-tuple-element.80.s0_ref), channel_id=1, source_target_pairs={{0,3},{1,2},{2,1},{3,0},{4,7},{5,6},{6,5},{7,4},{8,11},{9,10},{10,... | collective-permute-start | bytes 24584 | tf_op jit(solution)/shard_map/ppermute | solution.py:626
  76.7 12.1 %collective-permute-start.18 = (f32[264,512]{1,0:T(8,128)S(1)}, f32[264,512]{1,0:T(8,128)S(1)}, u32[]{:S(2)}, u32[]{:S(2)}) collective-permute-start(f32[264,512]{1,0:T(8,128)S(1)} %get-tuple-element.92.dout_ref.d0_ref.t0_ref), channel_id=1, source_target_pairs={{4,8},{8,4},{12,16},{16,12},{20,24},{24,20},{28,32},{32,28},{36,40... | collective-permute-start | bytes 1622024 | tf_op jit(solution)/shard_map/ppermute | solution.py:589
  81.7 7.0 %collective-permute-start.19 = (f32[4,1152]{1,0:T(4,128)S(1)}, f32[4,1152]{1,0:T(4,128)S(1)}, u32[]{:S(2)}, u32[]{:S(2)}) collective-permute-start(f32[4,1152]{1,0:T(4,128)S(1)} %get-tuple-element.90.third_ref), channel_id=1, source_target_pairs={{0,64},{4,68},{8,72},{12,76},{16,80},{20,84},{24,88},{28,92},{32,9... | collective-permute-start | bytes 55304 | tf_op jit(solution)/shard_map/ppermute | solution.py:585
  83.2 5.5 %collective-permute-start.20 = (f32[4,1152]{1,0:T(4,128)S(1)}, f32[4,1152]{1,0:T(4,128)S(1)}, u32[]{:S(2)}, u32[]{:S(2)}) collective-permute-start(f32[4,1152]{1,0:T(4,128)S(1)} %get-tuple-element.90.third_ref), channel_id=1, source_target_pairs={{0,128},{4,132},{8,136},{12,140},{16,144},{20,148},{24,152},{28,15... | collective-permute-start | bytes 55304 | tf_op jit(solution)/shard_map/ppermute | solution.py:585
  85.2 3.8 %collective-permute-start.21 = (f32[4,1152]{1,0:T(4,128)S(1)}, f32[4,1152]{1,0:T(4,128)S(1)}, u32[]{:S(2)}, u32[]{:S(2)}) collective-permute-start(f32[4,1152]{1,0:T(4,128)S(1)} %get-tuple-element.90.third_ref), channel_id=1, source_target_pairs={{0,192},{4,196},{8,200},{12,204},{16,208},{20,212},{24,216},{28,22... | collective-permute-start | bytes 55304 | tf_op jit(solution)/shard_map/ppermute | solution.py:585
  89.1 20.9 %collective-permute-start.24 = (f32[264,512]{1,0:T(8,128)S(1)}, f32[264,512]{1,0:T(8,128)S(1)}, u32[]{:S(2)}, u32[]{:S(2)}) collective-permute-start(f32[264,512]{1,0:T(8,128)S(1)} %get-tuple-element.92.dout_ref.d0_ref.t0_ref), channel_id=1, source_target_pairs={{0,4},{4,0},{8,12},{12,8},{16,20},{20,16},{24,28},{28,24},{32,36},... | collective-permute-start | bytes 1622024 | tf_op jit(solution)/shard_map/ppermute | solution.py:585
  94.4 11.7 %collective-permute-start.22 = (f32[64,1152]{1,0:T(8,128)S(1)}, f32[64,1152]{1,0:T(8,128)S(1)}, u32[]{:S(2)}, u32[]{:S(2)}) collective-permute-start(f32[64,1152]{1,0:T(8,128)S(1)} %get-tuple-element.94.first_ref), channel_id=1, source_target_pairs={{0,8},{4,12},{8,0},{12,4},{16,24},{20,28},{24,16},{28,20},{32,40},... | collective-permute-start | bytes 884744 | tf_op jit(solution)/shard_map/ppermute | solution.py:585
  94.4 11.7 %collective-permute-start.23 = (f32[28,1152]{1,0:T(8,128)S(1)}, f32[28,1152]{1,0:T(8,128)S(1)}, u32[]{:S(2)}, u32[]{:S(2)}) collective-permute-start(f32[28,1152]{1,0:T(8,128)S(1)} %shard_map.101.own_ref), channel_id=1, source_target_pairs={{0,16},{4,20},{8,24},{12,28},{16,0},{20,4},{24,8},{28,12},{32,48},... | collective-permute-start | bytes 387080 | tf_op jit(solution)/shard_map/ppermute | solution.py:585
  106.2 10.9 %collective-permute-start.25 = (f32[56,1152]{1,0:T(8,128)S(1)}, f32[56,1152]{1,0:T(8,128)S(1)}, u32[]{:S(2)}, u32[]{:S(2)}) collective-permute-start(f32[56,1152]{1,0:T(8,128)S(1)} %shard_map.103.double_ref), channel_id=1, source_target_pairs={{0,48},{4,52},{8,56},{12,60},{16,32},{20,36},{24,40},{28,44},{32,1... | collective-permute-start | bytes 774152 | tf_op jit(solution)/shard_map/ppermute | solution.py:585
  117.2 11.7 %collective-permute-start.26 = (f32[96,1152]{1,0:T(8,128)S(1)}, f32[96,1152]{1,0:T(8,128)S(1)}, u32[]{:S(2)}, u32[]{:S(2)}) collective-permute-start(f32[96,1152]{1,0:T(8,128)S(1)} %get-tuple-element.103.a1), channel_id=1, source_target_pairs={{0,8},{4,12},{8,0},{12,4},{16,24},{20,28},{24,16},{28,20},{32,40},... | collective-permute-start | bytes 1327112 | tf_op jit(solution)/shard_map/ppermute | solution.py:585
  120.2 11.1 %collective-permute-start.28 = (f32[160,1152]{1,0:T(8,128)S(1)}, f32[160,1152]{1,0:T(8,128)S(1)}, u32[]{:S(2)}, u32[]{:S(2)}) collective-permute-start(f32[160,1152]{1,0:T(8,128)S(1)} %get-tuple-element.104), channel_id=1, source_target_pairs={{0,4},{4,0},{8,12},{12,8},{16,20},{20,16},{24,28},{28,24},{32,36},... | collective-permute-start | bytes 2211848 | tf_op jit(solution)/shard_map/ppermute | solution.py:585
  128.9 5.2 %collective-permute-start.27 = (f32[96,1152]{1,0:T(8,128)S(1)}, f32[96,1152]{1,0:T(8,128)S(1)}, u32[]{:S(2)}, u32[]{:S(2)}) collective-permute-start(f32[96,1152]{1,0:T(8,128)S(1)} %collective-permute-done.26.a0), channel_id=1, source_target_pairs={{0,4},{4,0},{8,12},{12,8},{16,20},{20,16},{24,28},{28,24},{32,36},... | collective-permute-start | bytes 1327112 | tf_op jit(solution)/shard_map/ppermute | solution.py:585

commit v3 on v2

--- a/solution.py
+++ b/solution.py
@@ -605,18 +605,18 @@
     out_k, out_v = exchange_outer(key), exchange_outer(value)
     own, first, second, third, bias, edge = pool(key, value, query)
 
-    planes = [exchange(third, mask) for mask in PLANES]
+    planes = [exchange(after(third, out_k), PLANES[0])] + [exchange(third, mask) for mask in PLANES[1:]]
     l1a = exchange(first, 2)
-    pack = packed(after(second, out_k, out_v), planes)
+    pack = packed(after(second, out_k, out_v, l1a), planes)
     in_k, in_v = exchange(after(key, pack), 1), exchange(after(value, pack), 1)
-    double = doubled(after(pack, l1a), exchange(pack, 4))
+    double = doubled(pack, exchange(pack, 4))
     other = exchange(double, 12)
     w0, *inner = near_inner(query, (key, after(in_k, double)), (value, in_v))
     w1, *outer = near_outer(edge, query, after(out_k, double), out_v)
     l2a, bundle = merged(l1a, after(double, w0, w1), other)
     l2b = exchange(l2a, 2)
     core1 = exchange(bundle, 1)
-    core2 = exchange(l2b, 1)
+    core2 = exchange(after(l2b, core1), 1)
     query_in = exchange(after(query, core2), 1)
     query_out = exchange_outer(after(query, core2))
     far = (l1a, l2a, core1, l2b, core2)
@@ -628,25 +628,26 @@
     attention = after(attention, query_in, query_out)
     attended, d_out, delta, g1, g2, g3 = cotangent(stats, others, own, attention, lse, upstream, gain)
 
-    d_far = exchange_outer(d_out)
     planes = [exchange(g3, mask) for mask in PLANES]
     l1a = exchange(g1, 2)
-    pack = packed(after(g2, d_far), planes)
-    d_in = exchange(after(d_out, pack), 1)
+    d_in = exchange(d_out, 1)
+    pack = packed(g2, planes)
     quad = exchange(pack, 4)
     near_dq = near_query(
-        w0, w1, inner[0], outer[0], lse, delta, after(d_out, pack), (key, in_k, out_k), (value, in_v, out_v)
+        w0, w1, inner[0], outer[0], lse, delta, after(d_out, pack),
+        (key, in_k, out_k), (value, in_v, out_v),
     )
     double = doubled(after(pack, near_dq, l1a), quad)
     other = exchange(double, 12)
+    query_grad = far_query(bias, own, far, after(g1, double), g2, g3, near_dq)
+    d_far = exchange_outer(after(d_out, query_grad))
     near_dk, near_dv = inner_key(key, value, query, query_in, d_out, after(d_in, double))
-    query_grad = far_query(bias, own, far, after(g1, double), g2, g3, near_dq)
-    l2a, bundle = merged(l1a, after(double, near_dk, query_grad), other)
+    l2a, bundle = merged(l1a, after(double, near_dk, query_grad, d_far), other)
     l2b = exchange(l2a, 2)
     core1 = exchange(bundle, 1)
     near_dk, near_dv = outer_key(key, value, query_out, after(d_far, l2a), near_dk, near_dv)
     far_dk, far_dv = early_key(bias, own, (l1a, after(l2a, near_dk), core1))
-    core2 = exchange(after(l2b, near_dk), 1)
+    core2 = exchange(after(l2b, far_dk), 1)
     key_grad, value_grad = late_key(bias, own, (l2b, core2), far_dk, far_dv, near_dk, near_dv)
     return attended, query_grad, key_grad, value_grad
 

time: 138 us -> 142 us (1.029)
  starting transfers between devices: 44.8 us -> 50.8 us
  waiting for transfers between devices: 50.6 us -> 48.9 us
    ppermute x22, starting transfers between devices: 26.8 us -> 34.8 us  [exchange(): return lax.ppermute(array, 'seq', [(i, i ^ mask) for i in range(count)])]
    ppermute x4, waiting for transfers between devices: 8.07 us -> 4.1 us  [exchange_outer(): return lax.ppermute(array, 'seq', pairs)]
    ppermute x22, waiting for transfers between devices: 40.5 us -> 42.2 us  [exchange(): return lax.ppermute(array, 'seq', [(i, i ^ mask) for i in range(count)])]
    ppermute x4, starting transfers between devices: 14.1 us -> 12.5 us  [exchange_outer(): return lax.ppermute(array, 'seq', pairs)]
  transfers between devices with their start and end apart: 29 -> 29, of which waited for: 13 -> 15; matrix products, arithmetic and copies ran while one was open for 0% -> 0% of each run, Pallas kernels for 25% -> 24%
where the time goes in v3:
time: 142 us
  starting transfers between devices  50.8 us (36%)
  waiting for transfers between devices  48.9 us (34%)
  Pallas kernels  39.4 us (28%)
  local copies, waits for them, and re-layouts  1.58 us (1%)
    ppermute x22, waiting for transfers between devices, exchange(): return lax.ppermute(array, 'seq', [(i, i ^ mask) for i in range(count)])  42.2 us
    ppermute x22, starting transfers between devices, exchange(): return lax.ppermute(array, 'seq', [(i, i ^ mask) for i in range(count)])  34.8 us
    pallas_call x5, Pallas kernels, head_call(): pl.pallas_call(kernel, grid=(HEADS,), out_shape=outs, in_specs=in_specs,...  22.1 us
    pallas_call x11, Pallas kernels, whole_call(): pl.pallas_call(kernel, out_shape=outs, in_specs=[spec] * len(operands), o...  14 us
    ppermute x4, starting transfers between devices, exchange_outer(): return lax.ppermute(array, 'seq', pairs)  12.5 us
    ppermute x4, waiting for transfers between devices, exchange_outer(): return lax.ppermute(array, 'seq', pairs)  4.1 us
    ppermute x3, starting transfers between devices, body(): lax.ppermute(stats, 'head', [(i, i ^ mask) for i in range(head_count)])  3.4 us
    pallas_call x1, Pallas kernels, pool(): pl.pallas_call(pool_kernel, out_shape=[f32(OWN, 3 * WIDTH), f32(64, KV),...  3.27 us
  transfers between devices with their start and end apart: 29, of which 15 were waited for; matrix products, arithmetic and copies ran while one was open for 0% of the time, Pallas kernels for 24%

profile of v3, /device:TPU:1, one launch (start us, length us, event | category | flops | bytes accessed | tf_op | source)
XLA Modules:
  0.0 141.5 jit_solution(4403061819477584570)
XLA Ops:
  0.6 5.1 %collective-permute-start.1 = (f32[256,512]{1,0:T(8,128)}, f32[256,512]{1,0:T(8,128)S(1)}, u32[]{:S(2)}, u32[]{:S(2)}) collective-permute-start(f32[256,512]{1,0:T(8,128)} %k_ref.5), channel_id=1, source_target_pairs={{4,8},{8,4},{12,16},{16,12},{20,24},{24,20},{28,32},{32,28},{36,40... | collective-permute-start | bytes 1572872 | tf_op jit(solution)/shard_map/ppermute | solution.py:589
  5.7 1.9 %collective-permute-start.2 = (f32[256,512]{1,0:T(8,128)}, f32[256,512]{1,0:T(8,128)S(1)}, u32[]{:S(2)}, u32[]{:S(2)}) collective-permute-start(f32[256,512]{1,0:T(8,128)} %v_ref.5), channel_id=1, source_target_pairs={{4,8},{8,4},{12,16},{16,12},{20,24},{24,20},{28,32},{32,28},{36,40... | collective-permute-start | bytes 1572872 | tf_op jit(solution)/shard_map/ppermute | solution.py:589
  7.6 3.3 %shard_map.93 = (f32[96,1536]{1,0:T(8,128)}, f32[64,1024]{1,0:T(8,128)}, f32[16,1024]{1,0:T(8,128)}, f32[4,1024]{1,0:T(4,128)}, f32[96,512]{1,0:T(8,128)}, /*index=5*/f32[8,256]{1,0:T(8,128)}) custom-call(s32[8,512]{1,0:T(8,128)} %constant.2.clone.table_ref, f32[256,512]{1,0:T(8,128)} %k_ref.5, f32[256,512]{1,0:T(8,128)} %v_ref.5, f32[256,512]{1,0:T(8,128)} %q0_ref.1), custom_call_target="tpu_custom_call" | custom-call | flops 1000000 | bytes 2000000 | tf_op jit(solution)/shard_map/pallas_call | solution.py:512
  10.9 0.0 copy-start.3
  10.9 0.0 copy-start.4
  10.9 1.7 %collective-permute-start = (f32[64,1024]{1,0:T(8,128)}, f32[64,1024]{1,0:T(8,128)S(1)}, u32[]{:S(2)}, u32[]{:S(2)}) collective-permute-start(f32[64,1024]{1,0:T(8,128)} %get-tuple-element.60), channel_id=1, source_target_pairs={{0,8},{4,12},{8,0},{12,4},{16,24},{20,28},{24,16},{28,20},{32,40},... | collective-permute-start | bytes 786440 | tf_op jit(solution)/shard_map/ppermute | solution.py:585
  12.7 2.7 %collective-permute-start.5 = (f32[4,1024]{1,0:T(4,128)}, f32[4,1024]{1,0:T(4,128)S(1)}, u32[]{:S(2)}, u32[]{:S(2)}) collective-permute-start(f32[4,1024]{1,0:T(4,128)} %get-tuple-element.64), channel_id=1, source_target_pairs={{0,192},{4,196},{8,200},{12,204},{16,208},{20,212},{24,216},{28,22... | collective-permute-start | bytes 49160 | tf_op jit(solution)/shard_map/ppermute | solution.py:585
  15.4 0.3 collective-permute-start.4
  15.8 0.2 collective-permute-start.3
  16.0 7.4 %collective-permute-done.first_ref.a0 = f32[64,1024]{1,0:T(8,128)S(1)} collective-permute-done((f32[64,1024]{1,0:T(8,128)}, f32[64,1024]{1,0:T(8,128)S(1)}, u32[]{:S(2)}, u32[]{:S(2)}) %collective-permute-start) | collective-permute-done | bytes 262176 | tf_op jit(solution)/shard_map/ppermute | solution.py:585
  23.4 1.4 %collective-permute-done.4.b_ref = f32[4,1024]{1,0:T(4,128)S(1)} collective-permute-done((f32[4,1024]{1,0:T(4,128)}, f32[4,1024]{1,0:T(4,128)S(1)}, u32[]{:S(2)}, u32[]{:S(2)}) %collective-permute-start.4) | collective-permute-done | bytes 16416 | tf_op jit(solution)/shard_map/ppermute | solution.py:585
  24.8 0.8 copy-done.6
  25.7 0.7 collective-permute-start.7
  26.3 0.1 collective-permute-start.8
  26.4 2.3 %collective-permute-start.6 = (f32[28,1024]{1,0:T(8,128)S(1)}, f32[28,1024]{1,0:T(8,128)S(1)}, u32[]{:S(2)}, u32[]{:S(2)}) collective-permute-start(f32[28,1024]{1,0:T(8,128)S(1)} %shard_map.94.own_ref), channel_id=1, source_target_pairs={{0,16},{4,20},{8,24},{12,28},{16,0},{20,4},{24,8},{28,12},{32,48},... | collective-permute-start | bytes 344072 | tf_op jit(solution)/shard_map/ppermute | solution.py:585
  28.8 6.3 %collective-permute-done.6.other_ref = f32[28,1024]{1,0:T(8,128)S(1)} collective-permute-done((f32[28,1024]{1,0:T(8,128)S(1)}, f32[28,1024]{1,0:T(8,128)S(1)}, u32[]{:S(2)}, u32[]{:S(2)}) %collective-permute-start.6) | collective-permute-done | bytes 114720 | tf_op jit(solution)/shard_map/ppermute | solution.py:585
  35.1 3.4 %collective-permute-start.9 = (f32[56,1024]{1,0:T(8,128)S(1)}, f32[56,1024]{1,0:T(8,128)S(1)}, u32[]{:S(2)}, u32[]{:S(2)}) collective-permute-start(f32[56,1024]{1,0:T(8,128)S(1)} %shard_map.95.double_ref), channel_id=1, source_target_pairs={{0,48},{4,52},{8,56},{12,60},{16,32},{20,36},{24,40},{28,44},{32,1... | collective-permute-start | bytes 688136 | tf_op jit(solution)/shard_map/ppermute | solution.py:585
  38.5 0.7 copy-done.8
  39.2 3.6 %shard_map.97 = (f32[4,256,256]{2,1,0:T(8,128)S(1)}, f32[256,512]{1,0:T(8,128)S(1)}, f32[256,512]{1,0:T(8,128)S(1)}, f32[256,512]{1,0:T(8,128)S(1)}) custom-call(f32[8,256]{1,0:T(8,128)S(1)} %copy-done.8, f32[256,512]{1,0:T(8,128)S(1)} %copy-done.5, f32[256,512]{1,0:T(8,128)S(1)} %collective-permute-done.1.k_ref.k2_ref, ...), custom_call_target="tpu_custom_call" | custom-call | flops 805306368 | bytes 4000000 | tf_op jit(solution)/shard_map/pallas_call | solution.py:457
  42.8 0.0 copy-start.1
  42.8 0.0 copy-start.2
  42.8 0.0 copy-start.7
  42.9 4.1 %shard_map.96 = (f32[4,256,512]{2,1,0:T(8,128)S(1)}, f32[256,512]{1,0:T(8,128)S(1)}, f32[256,512]{1,0:T(8,128)S(1)}, f32[256,512]{1,0:T(8,128)S(1)}) custom-call(f32[256,512]{1,0:T(8,128)S(1)} %copy-done.5, f32[256,512]{1,0:T(8,128)S(1)} %copy-done.3, f32[256,512]{1,0:T(8,128)S(1)} %collective-permute-done.7.ki_ref.k1_ref, f32[256,512]{1,0:T(8,128)S(1)} %copy-done.4, ...), custom_call_target="tpu_custom_call" | custom-call | flops 1610612736 | bytes 4000000 | tf_op jit(solution)/shard_map/pallas_call | solution.py:457
  47.0 0.7 collective-permute-done.9.other_ref
  47.6 0.1 shard_map.98
  47.7 1.6 %collective-permute-start.10 = (f32[160,1024]{1,0:T(8,128)S(1)}, f32[160,1024]{1,0:T(8,128)S(1)}, u32[]{:S(2)}, u32[]{:S(2)}) collective-permute-start(f32[160,1024]{1,0:T(8,128)S(1)} %get-tuple-element.74), channel_id=1, source_target_pairs={{0,4},{4,0},{8,12},{12,8},{16,20},{20,16},{24,28},{28,24},{32,36},... | collective-permute-start | bytes 1966088 | tf_op jit(solution)/shard_map/ppermute | solution.py:585
  49.4 2.2 %collective-permute-start.11 = (f32[96,1024]{1,0:T(8,128)S(1)}, f32[96,1024]{1,0:T(8,128)S(1)}, u32[]{:S(2)}, u32[]{:S(2)}) collective-permute-start(f32[96,1024]{1,0:T(8,128)S(1)} %get-tuple-element.73.a1), channel_id=1, source_target_pairs={{0,8},{4,12},{8,0},{12,4},{16,24},{20,28},{24,16},{28,20},{32,40},... | collective-permute-start | bytes 1179656 | tf_op jit(solution)/shard_map/ppermute | solution.py:585
  51.6 9.4 %collective-permute-done.11.a3 = f32[96,1024]{1,0:T(8,128)S(1)} collective-permute-done((f32[96,1024]{1,0:T(8,128)S(1)}, f32[96,1024]{1,0:T(8,128)S(1)}, u32[]{:S(2)}, u32[]{:S(2)}) %collective-permute-start.11) | collective-permute-done | bytes 393248 | tf_op jit(solution)/shard_map/ppermute | solution.py:585
  60.9 0.7 collective-permute-start.12
  61.6 1.3 collective-permute-done.12.a4
  63.0 3.6 %collective-permute-start.17 = (f32[256,512]{1,0:T(8,128)S(1)}, f32[256,512]{1,0:T(8,128)S(1)}, u32[]{:S(2)}, u32[]{:S(2)}) collective-permute-start(f32[256,512]{1,0:T(8,128)S(1)} %copy-done.5), channel_id=1, source_target_pairs={{4,8},{8,4},{12,16},{16,12},{20,24},{24,20},{28,32},{32,28},{36,40... | collective-permute-start | bytes 1572872 | tf_op jit(solution)/shard_map/ppermute | solution.py:589
  66.6 0.1 collective-permute-start.16
  66.7 2.8 %shard_map.99 = (f32[256,512]{1,0:T(8,128)S(1)}, f32[256,512]{1,0:T(8,128)S(1)}, f32[8,256]{1,0:T(8,128)S(1)}) custom-call(f32[96,512]{1,0:T(8,128)S(1)} %copy-done.1, f32[96,1536]{1,0:T(8,128)S(1)} %copy-done, f32[64,1024]{1,0:T(8,128)S(1)} %collective-permute-done.first_ref.a0, f32[96,1024]{1,0:T(8,128)S(1)} %get-tuple-element.73.a1, ...), custom_call_target="tpu_custom_call" | custom-call | flops 402653184 | bytes 8000000 | tf_op jit(solution)/shard_map/pallas_call | solution.py:434
  69.6 2.5 %collective-permute-start.15 = (f32[8,256]{1,0:T(8,128)S(1)}, f32[8,256]{1,0:T(8,128)S(1)}, u32[]{:S(2)}, u32[]{:S(2)}) collective-permute-start(f32[8,256]{1,0:T(8,128)S(1)} %get-tuple-element.82.s0_ref), channel_id=1, source_target_pairs={{0,3},{1,2},{2,1},{3,0},{4,7},{5,6},{6,5},{7,4},{8,11},{9,10},{10,... | collective-permute-start | bytes 24584 | tf_op jit(solution)/shard_map/ppermute | solution.py:626
  72.1 0.5 collective-permute-start.14
  72.6 0.3 collective-permute-start.13
  73.0 0.5 collective-permute-done.17.q_ref
  73.5 2.6 %collective-permute-done.14.s2_ref = f32[8,256]{1,0:T(8,128)S(1)} collective-permute-done((f32[8,256]{1,0:T(8,128)S(1)}, f32[8,256]{1,0:T(8,128)S(1)}, u32[]{:S(2)}, u32[]{:S(2)}) %collective-permute-start.14) | collective-permute-done | bytes 8224 | tf_op jit(solution)/shard_map/ppermute | solution.py:626
  76.1 1.4 shard_map.100
  77.5 2.0 %collective-permute-start.21 = (f32[64,1152]{1,0:T(8,128)S(1)}, f32[64,1152]{1,0:T(8,128)S(1)}, u32[]{:S(2)}, u32[]{:S(2)}) collective-permute-start(f32[64,1152]{1,0:T(8,128)S(1)} %get-tuple-element.95.first_ref), channel_id=1, source_target_pairs={{0,8},{4,12},{8,0},{12,4},{16,24},{20,28},{24,16},{28,20},{32,40},... | collective-permute-start | bytes 884744 | tf_op jit(solution)/shard_map/ppermute | solution.py:585
  79.4 2.2 %collective-permute-start.23 = (f32[264,512]{1,0:T(8,128)S(1)}, f32[264,512]{1,0:T(8,128)S(1)}, u32[]{:S(2)}, u32[]{:S(2)}) collective-permute-start(f32[264,512]{1,0:T(8,128)S(1)} %get-tuple-element.98.dout_ref.d0_ref.t0_ref), channel_id=1, source_target_pairs={{0,4},{4,0},{8,12},{12,8},{16,20},{20,16},{24,28},{28,24},{32,36},... | collective-permute-start | bytes 1622024 | tf_op jit(solution)/shard_map/ppermute | solution.py:585
  81.6 2.7 %collective-permute-start.20 = (f32[4,1152]{1,0:T(4,128)S(1)}, f32[4,1152]{1,0:T(4,128)S(1)}, u32[]{:S(2)}, u32[]{:S(2)}) collective-permute-start(f32[4,1152]{1,0:T(4,128)S(1)} %get-tuple-element.90.third_ref), channel_id=1, source_target_pairs={{0,192},{4,196},{8,200},{12,204},{16,208},{20,212},{24,216},{28,22... | collective-permute-start | bytes 55304 | tf_op jit(solution)/shard_map/ppermute | solution.py:585
  84.3 0.3 collective-permute-start.19
  84.7 0.2 collective-permute-start.18
  84.9 0.6 collective-permute-done.20.c_ref
  85.5 3.0 %collective-permute-done.19.b_ref = f32[4,1152]{1,0:T(4,128)S(1)} collective-permute-done((f32[4,1152]{1,0:T(4,128)S(1)}, f32[4,1152]{1,0:T(4,128)S(1)}, u32[]{:S(2)}, u32[]{:S(2)}) %collective-permute-start.19) | collective-permute-done | bytes 18464 | tf_op jit(solution)/shard_map/ppermute | solution.py:585
  88.5 0.9 collective-permute-start.22
  89.4 5.0 %shard_map.102.near_ref = f32[256,512]{1,0:T(8,128)S(1)} custom-call(f32[4,256,512]{2,1,0:T(8,128)S(1)} %get-tuple-element.68.w0_ref, f32[4,256,256]{2,1,0:T(8,128)S(1)} %get-tuple-element.71.w1_ref, f32[256,512]{1,0:T(8,128)S(1)} %get-tuple-element.76.peak0_ref, f32[256,512]{1,0:T(8,128)S(1)} %get-tuple-element.79.peak1_ref, ...), custom_call_target="tpu_custom_call" | custom-call | flops 2415919104 | bytes 4000000 | tf_op jit(solution)/shard_map/pallas_call | solution.py:457
  94.5 3.7 %collective-permute-done.22.other_ref = f32[28,1152]{1,0:T(8,128)S(1)} collective-permute-done((f32[28,1152]{1,0:T(8,128)S(1)}, f32[28,1152]{1,0:T(8,128)S(1)}, u32[]{:S(2)}, u32[]{:S(2)}) %collective-permute-start.22) | collective-permute-done | bytes 129056 | tf_op jit(solution)/shard_map/ppermute | solution.py:585
  98.2 3.7 %shard_map.104 = f32[256,512]{1,0:T(8,128)} custom-call(f32[96,512]{1,0:T(8,128)S(1)} %copy-done.1, f32[96,1536]{1,0:T(8,128)S(1)} %copy-done, f32[64,1024]{1,0:T(8,128)S(1)} %collective-permute-done.first_ref.a0, f32[96,1024]{1,0:T(8,128)S(1)} %get-tuple-element.73.a1, f32[160,1024]{1,0:T(8,128)S(1)} %collective-permute-done.10.a2, ...), custom_call_target="tpu_custom_call" | custom-call | flops 402653184 | bytes 6000000 | tf_op jit(solution)/shard_map/pallas_call | solution.py:434
  101.9 1.9 %collective-permute-start.24 = (f32[264,512]{1,0:T(8,128)S(1)}, f32[264,512]{1,0:T(8,128)S(1)}, u32[]{:S(2)}, u32[]{:S(2)}) collective-permute-start(f32[264,512]{1,0:T(8,128)S(1)} %get-tuple-element.98.dout_ref.d0_ref.t0_ref), channel_id=1, source_target_pairs={{4,8},{8,4},{12,16},{16,12},{20,24},{24,20},{28,32},{32,28},{36,40... | collective-permute-start | bytes 1622024 | tf_op jit(solution)/shard_map/ppermute | solution.py:589
  103.8 2.3 %collective-permute-start.25 = (f32[56,1152]{1,0:T(8,128)S(1)}, f32[56,1152]{1,0:T(8,128)S(1)}, u32[]{:S(2)}, u32[]{:S(2)}) collective-permute-start(f32[56,1152]{1,0:T(8,128)S(1)} %shard_map.103.double_ref), channel_id=1, source_target_pairs={{0,48},{4,52},{8,56},{12,60},{16,32},{20,36},{24,40},{28,44},{32,1... | collective-permute-start | bytes 774152 | tf_op jit(solution)/shard_map/ppermute | solution.py:585
  106.1 5.6 %shard_map.105 = (f32[256,512]{1,0:T(8,128)S(1)}, f32[256,512]{1,0:T(8,128)S(1)}) custom-call(f32[256,512]{1,0:T(8,128)S(1)} %copy-done.3, f32[256,512]{1,0:T(8,128)S(1)} %copy-done.4, f32[256,512]{1,0:T(8,128)S(1)} %copy-done.5, f32[256,512]{1,0:T(8,128)S(1)} %collective-permute-done.16.q1_ref, f32[264,512]{1,0:T(8,128)S(1)} %get-tuple-element.98.dout_ref.d0_ref.t0_ref, ...), custom_call_target="tpu_custom_call" | custom-call | flops 3221225472 | bytes 4000000 | tf_op jit(solution)/shard_map/pallas_call | solution.py:457
  111.7 3.6 %collective-permute-done.24.d_ref.t_ref = f32[264,512]{1,0:T(8,128)S(1)} collective-permute-done((f32[264,512]{1,0:T(8,128)S(1)}, f32[264,512]{1,0:T(8,128)S(1)}, u32[]{:S(2)}, u32[]{:S(2)}) %collective-permute-start.24) | collective-permute-done | bytes 540704 | tf_op jit(solution)/shard_map/ppermute | solution.py:589
  115.3 3.1 %collective-permute-done.25.other_ref = f32[56,1152]{1,0:T(8,128)S(1)} collective-permute-done((f32[56,1152]{1,0:T(8,128)S(1)}, f32[56,1152]{1,0:T(8,128)S(1)}, u32[]{:S(2)}, u32[]{:S(2)}) %collective-permute-start.25) | collective-permute-done | bytes 258080 | tf_op jit(solution)/shard_map/ppermute | solution.py:585
  118.4 0.1 shard_map.106
  118.5 0.1 collective-permute-start.27
  118.6 7.2 %collective-permute-start.26 = (f32[96,1152]{1,0:T(8,128)S(1)}, f32[96,1152]{1,0:T(8,128)S(1)}, u32[]{:S(2)}, u32[]{:S(2)}) collective-permute-start(f32[96,1152]{1,0:T(8,128)S(1)} %get-tuple-element.104.a1), channel_id=1, source_target_pairs={{0,8},{4,12},{8,0},{12,4},{16,24},{20,28},{24,16},{28,20},{32,40},... | collective-permute-start | bytes 1327112 | tf_op jit(solution)/shard_map/ppermute | solution.py:585
  125.8 3.7 %shard_map.107 = (f32[256,512]{1,0:T(8,128)S(1)}, f32[256,512]{1,0:T(8,128)S(1)}) custom-call(f32[256,512]{1,0:T(8,128)S(1)} %copy-done.3, f32[256,512]{1,0:T(8,128)S(1)} %copy-done.4, f32[256,512]{1,0:T(8,128)S(1)} %collective-permute-done.17.q_ref, f32[264,512]{1,0:T(8,128)S(1)} %collective-permute-done.24.d_ref.t_ref, ...), custom_call_target="tpu_custom_call" | custom-call | flops 1610612736 | bytes 4000000 | tf_op jit(solution)/shard_map/pallas_call | solution.py:457
  129.6 2.7 %shard_map.108 = (f32[96,512]{1,0:T(8,128)S(1)}, f32[96,512]{1,0:T(8,128)S(1)}) custom-call(f32[96,512]{1,0:T(8,128)S(1)} %copy-done.1, f32[96,1536]{1,0:T(8,128)S(1)} %copy-done, f32[64,1152]{1,0:T(8,128)S(1)} %collective-permute-done.21.first_ref.a0, f32[96,1152]{1,0:T(8,128)S(1)} %get-tuple-element.104.a1, f32[160,1152]{1,0:T(8,128)S(1)} %collective-permute-done.27.a2), custom_call_target="tpu_custom_call" | custom-call | flops 402653184 | bytes 3000000 | tf_op jit(solution)/shard_map/pallas_call | solution.py:434
  132.3 4.0 %collective-permute-done.26.a0 = f32[96,1152]{1,0:T(8,128)S(1)} collective-permute-done((f32[96,1152]{1,0:T(8,128)S(1)}, f32[96,1152]{1,0:T(8,128)S(1)}, u32[]{:S(2)}, u32[]{:S(2)}) %collective-permute-start.26) | collective-permute-done | bytes 442400 | tf_op jit(solution)/shard_map/ppermute | solution.py:585
  136.3 0.7 collective-permute-start.28
  137.0 1.4 %collective-permute-done.28.a1 = f32[96,1152]{1,0:T(8,128)S(1)} collective-permute-done((f32[96,1152]{1,0:T(8,128)S(1)}, f32[96,1152]{1,0:T(8,128)S(1)}, u32[]{:S(2)}, u32[]{:S(2)}) %collective-permute-start.28) | collective-permute-done | bytes 442400 | tf_op jit(solution)/shard_map/ppermute | solution.py:585
  138.4 3.2 %shard_map.109 = (f32[256,512]{1,0:T(8,128)}, f32[256,512]{1,0:T(8,128)}) custom-call(f32[96,512]{1,0:T(8,128)S(1)} %copy-done.1, f32[96,1536]{1,0:T(8,128)S(1)} %copy-done, f32[96,1152]{1,0:T(8,128)S(1)} %collective-permute-done.26.a0, f32[96,1152]{1,0:T(8,128)S(1)} %collective-permute-done.28.a1, f32[96,512]{1,0:T(8,128)S(1)} %get-tuple-element.106.far_dk_ref, ...), custom_call_target="tpu_custom_call" | custom-call | flops 402653184 | bytes 3000000 | tf_op jit(solution)/shard_map/pallas_call | solution.py:434
  (29 shorter events, 0.1 us)
Async XLA Ops:
  0.6 37.8 %copy-start.5 = (f32[256,512]{1,0:T(8,128)S(1)}, f32[256,512]{1,0:T(8,128)}, u32[]{:S(2)}) copy-start(f32[256,512]{1,0:T(8,128)} %q0_ref.1) | copy-start | bytes 1572868
  0.6 15.1 %collective-permute-start.1 = (f32[256,512]{1,0:T(8,128)}, f32[256,512]{1,0:T(8,128)S(1)}, u32[]{:S(2)}, u32[]{:S(2)}) collective-permute-start(f32[256,512]{1,0:T(8,128)} %k_ref.5), channel_id=1, source_target_pairs={{4,8},{8,4},{12,16},{16,12},{20,24},{24,20},{28,32},{32,28},{36,40... | collective-permute-start | bytes 1572872 | tf_op jit(solution)/shard_map/ppermute | solution.py:589
  5.7 17.7 %collective-permute-start.2 = (f32[256,512]{1,0:T(8,128)}, f32[256,512]{1,0:T(8,128)S(1)}, u32[]{:S(2)}, u32[]{:S(2)}) collective-permute-start(f32[256,512]{1,0:T(8,128)} %v_ref.5), channel_id=1, source_target_pairs={{4,8},{8,4},{12,16},{16,12},{20,24},{24,20},{28,32},{32,28},{36,40... | collective-permute-start | bytes 1572872 | tf_op jit(solution)/shard_map/ppermute | solution.py:589
  10.9 32.0 %copy-start.3 = (f32[256,512]{1,0:T(8,128)S(1)}, f32[256,512]{1,0:T(8,128)}, u32[]{:S(2)}) copy-start(f32[256,512]{1,0:T(8,128)} %k_ref.5) | copy-start | bytes 1572868
  10.9 32.0 %copy-start.4 = (f32[256,512]{1,0:T(8,128)S(1)}, f32[256,512]{1,0:T(8,128)}, u32[]{:S(2)}) copy-start(f32[256,512]{1,0:T(8,128)} %v_ref.5) | copy-start | bytes 1572868
  10.9 12.4 %collective-permute-start = (f32[64,1024]{1,0:T(8,128)}, f32[64,1024]{1,0:T(8,128)S(1)}, u32[]{:S(2)}, u32[]{:S(2)}) collective-permute-start(f32[64,1024]{1,0:T(8,128)} %get-tuple-element.60), channel_id=1, source_target_pairs={{0,8},{4,12},{8,0},{12,4},{16,24},{20,28},{24,16},{28,20},{32,40},... | collective-permute-start | bytes 786440 | tf_op jit(solution)/shard_map/ppermute | solution.py:585
  12.7 10.7 %collective-permute-start.5 = (f32[4,1024]{1,0:T(4,128)}, f32[4,1024]{1,0:T(4,128)S(1)}, u32[]{:S(2)}, u32[]{:S(2)}) collective-permute-start(f32[4,1024]{1,0:T(4,128)} %get-tuple-element.64), channel_id=1, source_target_pairs={{0,192},{4,196},{8,200},{12,204},{16,208},{20,212},{24,216},{28,22... | collective-permute-start | bytes 49160 | tf_op jit(solution)/shard_map/ppermute | solution.py:585
  15.4 9.4 %collective-permute-start.4 = (f32[4,1024]{1,0:T(4,128)}, f32[4,1024]{1,0:T(4,128)S(1)}, u32[]{:S(2)}, u32[]{:S(2)}) collective-permute-start(f32[4,1024]{1,0:T(4,128)} %get-tuple-element.64), channel_id=1, source_target_pairs={{0,128},{4,132},{8,136},{12,140},{16,144},{20,148},{24,152},{28,15... | collective-permute-start | bytes 49160 | tf_op jit(solution)/shard_map/ppermute | solution.py:585
  15.8 9.0 %collective-permute-start.3 = (f32[4,1024]{1,0:T(4,128)}, f32[4,1024]{1,0:T(4,128)S(1)}, u32[]{:S(2)}, u32[]{:S(2)}) collective-permute-start(f32[4,1024]{1,0:T(4,128)} %get-tuple-element.64), channel_id=1, source_target_pairs={{0,64},{4,68},{8,72},{12,76},{16,80},{20,84},{24,88},{28,92},{32,9... | collective-permute-start | bytes 49160 | tf_op jit(solution)/shard_map/ppermute | solution.py:585
  24.8 0.8 copy-start.6
  25.7 17.2 %collective-permute-start.7 = (f32[256,512]{1,0:T(8,128)}, f32[256,512]{1,0:T(8,128)S(1)}, u32[]{:S(2)}, u32[]{:S(2)}) collective-permute-start(f32[256,512]{1,0:T(8,128)} %k_ref.5), channel_id=1, source_target_pairs={{0,4},{4,0},{8,12},{12,8},{16,20},{20,16},{24,28},{28,24},{32,36},... | collective-permute-start | bytes 1572872 | tf_op jit(solution)/shard_map/ppermute | solution.py:585
  26.3 16.5 %collective-permute-start.8 = (f32[256,512]{1,0:T(8,128)}, f32[256,512]{1,0:T(8,128)S(1)}, u32[]{:S(2)}, u32[]{:S(2)}) collective-permute-start(f32[256,512]{1,0:T(8,128)} %v_ref.5), channel_id=1, source_target_pairs={{0,4},{4,0},{8,12},{12,8},{16,20},{20,16},{24,28},{28,24},{32,36},... | collective-permute-start | bytes 1572872 | tf_op jit(solution)/shard_map/ppermute | solution.py:585
  26.4 8.6 %collective-permute-start.6 = (f32[28,1024]{1,0:T(8,128)S(1)}, f32[28,1024]{1,0:T(8,128)S(1)}, u32[]{:S(2)}, u32[]{:S(2)}) collective-permute-start(f32[28,1024]{1,0:T(8,128)S(1)} %shard_map.94.own_ref), channel_id=1, source_target_pairs={{0,16},{4,20},{8,24},{12,28},{16,0},{20,4},{24,8},{28,12},{32,48},... | collective-permute-start | bytes 344072 | tf_op jit(solution)/shard_map/ppermute | solution.py:585
  35.1 12.6 %collective-permute-start.9 = (f32[56,1024]{1,0:T(8,128)S(1)}, f32[56,1024]{1,0:T(8,128)S(1)}, u32[]{:S(2)}, u32[]{:S(2)}) collective-permute-start(f32[56,1024]{1,0:T(8,128)S(1)} %shard_map.95.double_ref), channel_id=1, source_target_pairs={{0,48},{4,52},{8,56},{12,60},{16,32},{20,36},{24,40},{28,44},{32,1... | collective-permute-start | bytes 688136 | tf_op jit(solution)/shard_map/ppermute | solution.py:585
  38.5 0.7 copy-start.8
  42.8 23.9 %copy-start = (f32[96,1536]{1,0:T(8,128)S(1)}, f32[96,1536]{1,0:T(8,128)}, u32[]{:S(2)}) copy-start(f32[96,1536]{1,0:T(8,128)} %get-tuple-element.59.own_ref) | copy-start | bytes 1769476
  42.8 23.9 %copy-start.1 = (f32[96,512]{1,0:T(8,128)S(1)}, f32[96,512]{1,0:T(8,128)}, u32[]{:S(2)}) copy-start(f32[96,512]{1,0:T(8,128)} %get-tuple-element.58.bias_ref) | copy-start | bytes 589828
  42.8 23.9 %copy-start.2 = (f32[256,512]{1,0:T(8,128)S(1)}, f32[256,512]{1,0:T(8,128)}, u32[]{:S(2)}) copy-start(f32[256,512]{1,0:T(8,128)} %up_ref.3) | copy-start | bytes 1572868
  42.8 23.9 %copy-start.7 = (f32[512]{0:T(512)S(1)}, f32[512]{0:T(512)}, u32[]{:S(2)}) copy-start(f32[512]{0:T(512)} %param.9) | copy-start | bytes 6148
  47.7 13.2 %collective-permute-start.10 = (f32[160,1024]{1,0:T(8,128)S(1)}, f32[160,1024]{1,0:T(8,128)S(1)}, u32[]{:S(2)}, u32[]{:S(2)}) collective-permute-start(f32[160,1024]{1,0:T(8,128)S(1)} %get-tuple-element.74), channel_id=1, source_target_pairs={{0,4},{4,0},{8,12},{12,8},{16,20},{20,16},{24,28},{28,24},{32,36},... | collective-permute-start | bytes 1966088 | tf_op jit(solution)/shard_map/ppermute | solution.py:585
  49.4 11.6 %collective-permute-start.11 = (f32[96,1024]{1,0:T(8,128)S(1)}, f32[96,1024]{1,0:T(8,128)S(1)}, u32[]{:S(2)}, u32[]{:S(2)}) collective-permute-start(f32[96,1024]{1,0:T(8,128)S(1)} %get-tuple-element.73.a1), channel_id=1, source_target_pairs={{0,8},{4,12},{8,0},{12,4},{16,24},{20,28},{24,16},{28,20},{32,40},... | collective-permute-start | bytes 1179656 | tf_op jit(solution)/shard_map/ppermute | solution.py:585
  60.9 2.0 %collective-permute-start.12 = (f32[96,1024]{1,0:T(8,128)S(1)}, f32[96,1024]{1,0:T(8,128)S(1)}, u32[]{:S(2)}, u32[]{:S(2)}) collective-permute-start(f32[96,1024]{1,0:T(8,128)S(1)} %collective-permute-done.11.a3), channel_id=1, source_target_pairs={{0,4},{4,0},{8,12},{12,8},{16,20},{20,16},{24,28},{28,24},{32,36},... | collective-permute-start | bytes 1179656 | tf_op jit(solution)/shard_map/ppermute | solution.py:585
  63.0 10.5 %collective-permute-start.17 = (f32[256,512]{1,0:T(8,128)S(1)}, f32[256,512]{1,0:T(8,128)S(1)}, u32[]{:S(2)}, u32[]{:S(2)}) collective-permute-start(f32[256,512]{1,0:T(8,128)S(1)} %copy-done.5), channel_id=1, source_target_pairs={{4,8},{8,4},{12,16},{16,12},{20,24},{24,20},{28,32},{32,28},{36,40... | collective-permute-start | bytes 1572872 | tf_op jit(solution)/shard_map/ppermute | solution.py:589
  66.6 6.9 %collective-permute-start.16 = (f32[256,512]{1,0:T(8,128)S(1)}, f32[256,512]{1,0:T(8,128)S(1)}, u32[]{:S(2)}, u32[]{:S(2)}) collective-permute-start(f32[256,512]{1,0:T(8,128)S(1)} %copy-done.5), channel_id=1, source_target_pairs={{0,4},{4,0},{8,12},{12,8},{16,20},{20,16},{24,28},{28,24},{32,36},... | collective-permute-start | bytes 1572872 | tf_op jit(solution)/shard_map/ppermute | solution.py:585
  69.6 3.9 %collective-permute-start.15 = (f32[8,256]{1,0:T(8,128)S(1)}, f32[8,256]{1,0:T(8,128)S(1)}, u32[]{:S(2)}, u32[]{:S(2)}) collective-permute-start(f32[8,256]{1,0:T(8,128)S(1)} %get-tuple-element.82.s0_ref), channel_id=1, source_target_pairs={{0,3},{1,2},{2,1},{3,0},{4,7},{5,6},{6,5},{7,4},{8,11},{9,10},{10,... | collective-permute-start | bytes 24584 | tf_op jit(solution)/shard_map/ppermute | solution.py:626
  72.1 4.0 %collective-permute-start.14 = (f32[8,256]{1,0:T(8,128)S(1)}, f32[8,256]{1,0:T(8,128)S(1)}, u32[]{:S(2)}, u32[]{:S(2)}) collective-permute-start(f32[8,256]{1,0:T(8,128)S(1)} %get-tuple-element.82.s0_ref), channel_id=1, source_target_pairs={{0,2},{1,3},{2,0},{3,1},{4,6},{5,7},{6,4},{7,5},{8,10},{9,11},{10,... | collective-permute-start | bytes 24584 | tf_op jit(solution)/shard_map/ppermute | solution.py:626
  72.6 3.5 %collective-permute-start.13 = (f32[8,256]{1,0:T(8,128)S(1)}, f32[8,256]{1,0:T(8,128)S(1)}, u32[]{:S(2)}, u32[]{:S(2)}) collective-permute-start(f32[8,256]{1,0:T(8,128)S(1)} %get-tuple-element.82.s0_ref), channel_id=1, source_target_pairs={{0,1},{1,0},{2,3},{3,2},{4,5},{5,4},{6,7},{7,6},{8,9},{9,8},{10,11... | collective-permute-start | bytes 24584 | tf_op jit(solution)/shard_map/ppermute | solution.py:626
  77.5 17.0 %collective-permute-start.21 = (f32[64,1152]{1,0:T(8,128)S(1)}, f32[64,1152]{1,0:T(8,128)S(1)}, u32[]{:S(2)}, u32[]{:S(2)}) collective-permute-start(f32[64,1152]{1,0:T(8,128)S(1)} %get-tuple-element.95.first_ref), channel_id=1, source_target_pairs={{0,8},{4,12},{8,0},{12,4},{16,24},{20,28},{24,16},{28,20},{32,40},... | collective-permute-start | bytes 884744 | tf_op jit(solution)/shard_map/ppermute | solution.py:585
  79.4 26.7 %collective-permute-start.23 = (f32[264,512]{1,0:T(8,128)S(1)}, f32[264,512]{1,0:T(8,128)S(1)}, u32[]{:S(2)}, u32[]{:S(2)}) collective-permute-start(f32[264,512]{1,0:T(8,128)S(1)} %get-tuple-element.98.dout_ref.d0_ref.t0_ref), channel_id=1, source_target_pairs={{0,4},{4,0},{8,12},{12,8},{16,20},{20,16},{24,28},{28,24},{32,36},... | collective-permute-start | bytes 1622024 | tf_op jit(solution)/shard_map/ppermute | solution.py:585
  81.6 3.9 %collective-permute-start.20 = (f32[4,1152]{1,0:T(4,128)S(1)}, f32[4,1152]{1,0:T(4,128)S(1)}, u32[]{:S(2)}, u32[]{:S(2)}) collective-permute-start(f32[4,1152]{1,0:T(4,128)S(1)} %get-tuple-element.90.third_ref), channel_id=1, source_target_pairs={{0,192},{4,196},{8,200},{12,204},{16,208},{20,212},{24,216},{28,22... | collective-permute-start | bytes 55304 | tf_op jit(solution)/shard_map/ppermute | solution.py:585
  84.3 4.1 %collective-permute-start.19 = (f32[4,1152]{1,0:T(4,128)S(1)}, f32[4,1152]{1,0:T(4,128)S(1)}, u32[]{:S(2)}, u32[]{:S(2)}) collective-permute-start(f32[4,1152]{1,0:T(4,128)S(1)} %get-tuple-element.90.third_ref), channel_id=1, source_target_pairs={{0,128},{4,132},{8,136},{12,140},{16,144},{20,148},{24,152},{28,15... | collective-permute-start | bytes 55304 | tf_op jit(solution)/shard_map/ppermute | solution.py:585
  84.7 3.8 %collective-permute-start.18 = (f32[4,1152]{1,0:T(4,128)S(1)}, f32[4,1152]{1,0:T(4,128)S(1)}, u32[]{:S(2)}, u32[]{:S(2)}) collective-permute-start(f32[4,1152]{1,0:T(4,128)S(1)} %get-tuple-element.90.third_ref), channel_id=1, source_target_pairs={{0,64},{4,68},{8,72},{12,76},{16,80},{20,84},{24,88},{28,92},{32,9... | collective-permute-start | bytes 55304 | tf_op jit(solution)/shard_map/ppermute | solution.py:585
  88.5 9.7 %collective-permute-start.22 = (f32[28,1152]{1,0:T(8,128)S(1)}, f32[28,1152]{1,0:T(8,128)S(1)}, u32[]{:S(2)}, u32[]{:S(2)}) collective-permute-start(f32[28,1152]{1,0:T(8,128)S(1)} %shard_map.101.own_ref), channel_id=1, source_target_pairs={{0,16},{4,20},{8,24},{12,28},{16,0},{20,4},{24,8},{28,12},{32,48},... | collective-permute-start | bytes 387080 | tf_op jit(solution)/shard_map/ppermute | solution.py:585
  101.9 13.4 %collective-permute-start.24 = (f32[264,512]{1,0:T(8,128)S(1)}, f32[264,512]{1,0:T(8,128)S(1)}, u32[]{:S(2)}, u32[]{:S(2)}) collective-permute-start(f32[264,512]{1,0:T(8,128)S(1)} %get-tuple-element.98.dout_ref.d0_ref.t0_ref), channel_id=1, source_target_pairs={{4,8},{8,4},{12,16},{16,12},{20,24},{24,20},{28,32},{32,28},{36,40... | collective-permute-start | bytes 1622024 | tf_op jit(solution)/shard_map/ppermute | solution.py:589
  103.8 14.6 %collective-permute-start.25 = (f32[56,1152]{1,0:T(8,128)S(1)}, f32[56,1152]{1,0:T(8,128)S(1)}, u32[]{:S(2)}, u32[]{:S(2)}) collective-permute-start(f32[56,1152]{1,0:T(8,128)S(1)} %shard_map.103.double_ref), channel_id=1, source_target_pairs={{0,48},{4,52},{8,56},{12,60},{16,32},{20,36},{24,40},{28,44},{32,1... | collective-permute-start | bytes 774152 | tf_op jit(solution)/shard_map/ppermute | solution.py:585
  118.5 11.1 %collective-permute-start.27 = (f32[160,1152]{1,0:T(8,128)S(1)}, f32[160,1152]{1,0:T(8,128)S(1)}, u32[]{:S(2)}, u32[]{:S(2)}) collective-permute-start(f32[160,1152]{1,0:T(8,128)S(1)} %get-tuple-element.105), channel_id=1, source_target_pairs={{0,4},{4,0},{8,12},{12,8},{16,20},{20,16},{24,28},{28,24},{32,36},... | collective-permute-start | bytes 2211848 | tf_op jit(solution)/shard_map/ppermute | solution.py:585
  118.6 17.7 %collective-permute-start.26 = (f32[96,1152]{1,0:T(8,128)S(1)}, f32[96,1152]{1,0:T(8,128)S(1)}, u32[]{:S(2)}, u32[]{:S(2)}) collective-permute-start(f32[96,1152]{1,0:T(8,128)S(1)} %get-tuple-element.104.a1), channel_id=1, source_target_pairs={{0,8},{4,12},{8,0},{12,4},{16,24},{20,28},{24,16},{28,20},{32,40},... | collective-permute-start | bytes 1327112 | tf_op jit(solution)/shard_map/ppermute | solution.py:585
  136.3 2.1 %collective-permute-start.28 = (f32[96,1152]{1,0:T(8,128)S(1)}, f32[96,1152]{1,0:T(8,128)S(1)}, u32[]{:S(2)}, u32[]{:S(2)}) collective-permute-start(f32[96,1152]{1,0:T(8,128)S(1)} %collective-permute-done.26.a0), channel_id=1, source_target_pairs={{0,4},{4,0},{8,12},{12,8},{16,20},{20,16},{24,28},{28,24},{32,36},... | collective-permute-start | bytes 1327112 | tf_op jit(solution)/shard_map/ppermute | solution.py:585

commit v4 on v3

--- a/solution.py
+++ b/solution.py
@@ -284,7 +284,7 @@
 
 
 def cotangent_kernel(
-    s0_ref, s1_ref, s2_ref, s3_ref, own_ref, att_ref, lse_ref, up_ref, gain_ref,
+    s0_ref, s1_ref, s2_ref, s3_ref, own_ref, query_ref, att_ref, lse_ref, up_ref, gain_ref,
     out_ref, dout_ref, delta_ref, first_ref, second_ref, third_ref,
     e0_ref, e1_ref, e2_ref,
 ):
@@ -305,6 +305,7 @@
         out_ref[:, k] = attention * inverse * gain_ref[0:1, k]
         d_out = inverse * (up_ref[:, k] * gain_ref[0:1, k]) - attention * pull
         dout_ref[0:BLOCK, k] = d_out
+        dout_ref[0:BLOCK, cols(h, WIDTH)] = query_ref[:, k]
         delta = wide(jnp.sum(d_out * attention, axis=1, keepdims=True))
         delta_ref[:, k] = delta
         packed = jnp.where(lane == h, lse_ref[:, k], packed)
@@ -320,7 +321,7 @@
     second_ref[:, KV:] = stats[1]
     third_ref[:, KV:] = stats[2]
     dout_ref[BLOCK:, 0:256] = jnp.transpose(packed)[0:8, :]
-    dout_ref[BLOCK:, 256:] = jnp.zeros((8, 256), jnp.float32)
+    dout_ref[BLOCK:, 256:] = jnp.zeros((8, KV - 256), jnp.float32)
 
 
 def near_query_kernel(
@@ -445,8 +446,8 @@
 BLOCK_FLOPS = 2.0 * BLOCK * BLOCK * DHEAD * HEADS * 6
 
 
-def column():
-    return pl.BlockSpec((BLOCK, DHEAD), lambda h: (0, h))
+def column(first=0):
+    return pl.BlockSpec((BLOCK, DHEAD), lambda h: (0, first + h))
 
 
 def slab(blocks):
@@ -490,19 +491,19 @@
     return pl.BlockSpec((8, 256), lambda h: (BLOCK // 8, 0))
 
 
-def inner_key(key, value, query, query_in, d_out, d_in):
-    k, t = column(), stat_rows()
+def inner_key(key, value, d_out, d_in):
+    k, q, t = column(), column(HEADS), stat_rows()
     return head_call(
-        inner_key_kernel, [f32(BLOCK, WIDTH)] * 2, [k, k], [k] * 6 + [t, t], 8,
-        key, value, query, query_in, d_out, d_in, d_out, d_in,
-    )
-
-
-def outer_key(key, value, query_out, d_far, dk, dv):
-    k, t = column(), stat_rows()
+        inner_key_kernel, [f32(BLOCK, WIDTH)] * 2, [k, k], [k, k, q, q, k, k, t, t], 8,
+        key, value, d_out, d_in, d_out, d_in, d_out, d_in,
+    )
+
+
+def outer_key(key, value, d_far, dk, dv):
+    k, q, t = column(), column(HEADS), stat_rows()
     return head_call(
-        outer_key_kernel, [f32(BLOCK, WIDTH)] * 2, [k, k], [k] * 4 + [t, k, k], 4,
-        key, value, query_out, d_far, d_far, dk, dv,
+        outer_key_kernel, [f32(BLOCK, WIDTH)] * 2, [k, k], [k, k, q, k, t, k, k], 4,
+        key, value, d_far, d_far, d_far, dk, dv,
     )
 
 
@@ -539,14 +540,14 @@
     )
 
 
-def cotangent(stats, others, own, attention, lse, upstream, gain):
+def cotangent(stats, others, own, query, attention, lse, upstream, gain):
     return whole_call(
         cotangent_kernel,
-        [f32(BLOCK, WIDTH), f32(BLOCK + 8, WIDTH), f32(BLOCK, WIDTH), f32(64, GRAD), f32(16, GRAD), f32(4, GRAD)],
+        [f32(BLOCK, WIDTH), f32(BLOCK + 8, KV), f32(BLOCK, WIDTH), f32(64, GRAD), f32(16, GRAD), f32(4, GRAD)],
         [(2, BLOCK, DHEAD)] * 3,
         1e6,
         4e6,
-        stats, *others, own, attention, lse, upstream, gain,
+        stats, *others, own, query, attention, lse, upstream, gain,
     )
 
 
@@ -603,13 +604,14 @@
 
     gain = norm_gain.reshape(1, WIDTH)
     out_k, out_v = exchange_outer(key), exchange_outer(value)
+    in_k, in_v = exchange(key, 1), exchange(value, 1)
     own, first, second, third, bias, edge = pool(key, value, query)
 
-    planes = [exchange(after(third, out_k), PLANES[0])] + [exchange(third, mask) for mask in PLANES[1:]]
+    held = after(third, in_k, in_v)
+    planes = [exchange(after(held, out_k), PLANES[0])] + [exchange(held, mask) for mask in PLANES[1:]]
     l1a = exchange(first, 2)
-    pack = packed(after(second, out_k, out_v, l1a), planes)
-    in_k, in_v = exchange(after(key, pack), 1), exchange(after(value, pack), 1)
-    double = doubled(pack, exchange(pack, 4))
+    pack = packed(after(second, out_k), planes)
+    double = doubled(after(pack, l1a), exchange(pack, 4))
     other = exchange(double, 12)
     w0, *inner = near_inner(query, (key, after(in_k, double)), (value, in_v))
     w1, *outer = near_outer(edge, query, after(out_k, double), out_v)
@@ -617,35 +619,32 @@
     l2b = exchange(l2a, 2)
     core1 = exchange(bundle, 1)
     core2 = exchange(after(l2b, core1), 1)
-    query_in = exchange(after(query, core2), 1)
-    query_out = exchange_outer(after(query, core2))
     far = (l1a, l2a, core1, l2b, core2)
     attention, lse, stats = far_forward(bias, own, far, inner, outer, upstream, gain)
 
     others = [
         lax.ppermute(stats, "head", [(i, i ^ mask) for i in range(head_count)]) for mask in range(1, head_count)
     ]
-    attention = after(attention, query_in, query_out)
-    attended, d_out, delta, g1, g2, g3 = cotangent(stats, others, own, attention, lse, upstream, gain)
+    attended, d_out, delta, g1, g2, g3 = cotangent(stats, others, own, query, attention, lse, upstream, gain)
 
     planes = [exchange(g3, mask) for mask in PLANES]
     l1a = exchange(g1, 2)
-    d_in = exchange(d_out, 1)
+    d_far = exchange_outer(d_out)
     pack = packed(g2, planes)
+    d_in = exchange(after(d_out, pack), 1)
     quad = exchange(pack, 4)
     near_dq = near_query(
         w0, w1, inner[0], outer[0], lse, delta, after(d_out, pack),
         (key, in_k, out_k), (value, in_v, out_v),
     )
-    double = doubled(after(pack, near_dq, l1a), quad)
+    double = doubled(after(pack, near_dq, d_far), quad)
     other = exchange(double, 12)
+    near_dk, near_dv = inner_key(key, value, d_out, after(d_in, double))
     query_grad = far_query(bias, own, far, after(g1, double), g2, g3, near_dq)
-    d_far = exchange_outer(after(d_out, query_grad))
-    near_dk, near_dv = inner_key(key, value, query, query_in, d_out, after(d_in, double))
-    l2a, bundle = merged(l1a, after(double, near_dk, query_grad, d_far), other)
+    l2a, bundle = merged(l1a, after(double, near_dk, query_grad), other)
     l2b = exchange(l2a, 2)
     core1 = exchange(bundle, 1)
-    near_dk, near_dv = outer_key(key, value, query_out, after(d_far, l2a), near_dk, near_dv)
+    near_dk, near_dv = outer_key(key, value, after(d_far, l2a), near_dk, near_dv)
     far_dk, far_dv = early_key(bias, own, (l1a, after(l2a, near_dk), core1))
     core2 = exchange(after(l2b, far_dk), 1)
     key_grad, value_grad = late_key(bias, own, (l2b, core2), far_dk, far_dv, near_dk, near_dv)

time: 142 us -> 133 us (0.937)
  starting transfers between devices: 50.8 us -> 37.3 us
  waiting for transfers between devices: 48.9 us -> 53.6 us
    ppermute x22 -> x21, starting transfers between devices: 34.8 us -> 23.4 us  [exchange(): return lax.ppermute(array, 'seq', [(i, i ^ mask) for i in range(count)])]
    ppermute x22 -> x21, waiting for transfers between devices: 42.2 us -> 48.7 us  [exchange(): return lax.ppermute(array, 'seq', [(i, i ^ mask) for i in range(count)])]
    ppermute x4 -> x3, waiting for transfers between devices: 4.1 us -> 1.66 us  [exchange_outer(): return lax.ppermute(array, 'seq', pairs)]
    ppermute x4 -> x3, starting transfers between devices: 12.5 us -> 10.6 us  [exchange_outer(): return lax.ppermute(array, 'seq', pairs)]
  transfers between devices with their start and end apart: 29 -> 27, of which waited for: 15 -> 14; matrix products, arithmetic and copies ran while one was open for 0% -> 0% of each run, Pallas kernels for 24% -> 24%
where the time goes in v4:
time: 133 us
  waiting for transfers between devices  53.6 us (40%)
  Pallas kernels  39.6 us (30%)
  starting transfers between devices  37.3 us (28%)
  local copies, waits for them, and re-layouts  1.56 us (1%)
    ppermute x21, waiting for transfers between devices, exchange(): return lax.ppermute(array, 'seq', [(i, i ^ mask) for i in range(count)])  48.7 us
    ppermute x21, starting transfers between devices, exchange(): return lax.ppermute(array, 'seq', [(i, i ^ mask) for i in range(count)])  23.4 us
    pallas_call x5, Pallas kernels, head_call(): pl.pallas_call(kernel, grid=(HEADS,), out_shape=outs, in_specs=in_specs,...  22.1 us
    pallas_call x11, Pallas kernels, whole_call(): pl.pallas_call(kernel, out_shape=outs, in_specs=[spec] * len(operands), o...  14.2 us
    ppermute x3, starting transfers between devices, exchange_outer(): return lax.ppermute(array, 'seq', pairs)  10.6 us
    ppermute x3, starting transfers between devices, body(): lax.ppermute(stats, 'head', [(i, i ^ mask) for i in range(head_count)])  3.32 us
    pallas_call x1, Pallas kernels, pool(): pl.pallas_call(pool_kernel, out_shape=[f32(OWN, 3 * WIDTH), f32(64, KV),...  3.27 us
    ppermute x3, waiting for transfers between devices, body(): lax.ppermute(stats, 'head', [(i, i ^ mask) for i in range(head_count)])  3.23 us
  transfers between devices with their start and end apart: 27, of which 14 were waited for; matrix products, arithmetic and copies ran while one was open for 0% of the time, Pallas kernels for 24%

profile of v4, /device:TPU:1, one launch (start us, length us, event | category | flops | bytes accessed | tf_op | source)
XLA Modules:
  0.0 133.0 jit_solution(18281349036340557388)
XLA Ops:
  0.6 3.3 %collective-permute-start.2 = (f32[256,512]{1,0:T(8,128)}, f32[256,512]{1,0:T(8,128)S(1)}, u32[]{:S(2)}, u32[]{:S(2)}) collective-permute-start(f32[256,512]{1,0:T(8,128)} %k_ref.5), channel_id=1, source_target_pairs={{0,4},{4,0},{8,12},{12,8},{16,20},{20,16},{24,28},{28,24},{32,36},... | collective-permute-start | bytes 1572872 | tf_op jit(solution)/shard_map/ppermute | solution.py:586
  4.0 0.1 collective-permute-start.3
  4.1 2.1 %collective-permute-start.1 = (f32[256,512]{1,0:T(8,128)}, f32[256,512]{1,0:T(8,128)S(1)}, u32[]{:S(2)}, u32[]{:S(2)}) collective-permute-start(f32[256,512]{1,0:T(8,128)} %k_ref.5), channel_id=1, source_target_pairs={{4,8},{8,4},{12,16},{16,12},{20,24},{24,20},{28,32},{32,28},{36,40... | collective-permute-start | bytes 1572872 | tf_op jit(solution)/shard_map/ppermute | solution.py:590
  6.2 3.5 %collective-permute-start.8 = (f32[256,512]{1,0:T(8,128)}, f32[256,512]{1,0:T(8,128)S(1)}, u32[]{:S(2)}, u32[]{:S(2)}) collective-permute-start(f32[256,512]{1,0:T(8,128)} %v_ref.5), channel_id=1, source_target_pairs={{4,8},{8,4},{12,16},{16,12},{20,24},{24,20},{28,32},{32,28},{36,40... | collective-permute-start | bytes 1572872 | tf_op jit(solution)/shard_map/ppermute | solution.py:590
  9.6 3.3 %shard_map.93 = (f32[96,1536]{1,0:T(8,128)}, f32[64,1024]{1,0:T(8,128)}, f32[16,1024]{1,0:T(8,128)}, f32[4,1024]{1,0:T(4,128)}, f32[96,512]{1,0:T(8,128)}, /*index=5*/f32[8,256]{1,0:T(8,128)}) custom-call(s32[8,512]{1,0:T(8,128)} %constant.2.clone.table_ref, f32[256,512]{1,0:T(8,128)} %k_ref.5, f32[256,512]{1,0:T(8,128)} %v_ref.5, f32[256,512]{1,0:T(8,128)} %query_ref.1), custom_call_target="tpu_custom_call" | custom-call | flops 1000000 | bytes 2000000 | tf_op jit(solution)/shard_map/pallas_call | solution.py:513
  12.9 0.2 collective-permute-start
  13.1 1.7 %collective-permute-done.1.k_ref.k2_ref = f32[256,512]{1,0:T(8,128)S(1)} collective-permute-done((f32[256,512]{1,0:T(8,128)}, f32[256,512]{1,0:T(8,128)S(1)}, u32[]{:S(2)}, u32[]{:S(2)}) %collective-permute-start.1) | collective-permute-done | bytes 524320 | tf_op jit(solution)/shard_map/ppermute | solution.py:590
  14.8 0.1 collective-permute-start.4
  14.8 1.9 %collective-permute-start.6 = (f32[4,1024]{1,0:T(4,128)}, f32[4,1024]{1,0:T(4,128)S(1)}, u32[]{:S(2)}, u32[]{:S(2)}) collective-permute-start(f32[4,1024]{1,0:T(4,128)} %get-tuple-element.62), channel_id=1, source_target_pairs={{0,192},{4,196},{8,200},{12,204},{16,208},{20,212},{24,216},{28,22... | collective-permute-start | bytes 49160 | tf_op jit(solution)/shard_map/ppermute | solution.py:586
  16.7 1.3 collective-permute-start.5
  18.0 0.8 collective-permute-done.6.c_ref
  18.8 6.5 %collective-permute-done.5.b_ref = f32[4,1024]{1,0:T(4,128)S(1)} collective-permute-done((f32[4,1024]{1,0:T(4,128)}, f32[4,1024]{1,0:T(4,128)S(1)}, u32[]{:S(2)}, u32[]{:S(2)}) %collective-permute-start.5) | collective-permute-done | bytes 16416 | tf_op jit(solution)/shard_map/ppermute | solution.py:586
  25.4 0.8 copy-done.6
  26.2 0.1 collective-permute-start.7
  26.3 0.0 collective-permute-done.first_ref.a0
  26.3 7.2 %collective-permute-done.7.other_ref = f32[28,1024]{1,0:T(8,128)S(1)} collective-permute-done((f32[28,1024]{1,0:T(8,128)S(1)}, f32[28,1024]{1,0:T(8,128)S(1)}, u32[]{:S(2)}, u32[]{:S(2)}) %collective-permute-start.7) | collective-permute-done | bytes 114720 | tf_op jit(solution)/shard_map/ppermute | solution.py:586
  33.6 0.1 collective-permute-start.9
  33.7 0.7 copy-done.8
  34.4 3.6 %shard_map.97 = (f32[4,256,256]{2,1,0:T(8,128)S(1)}, f32[256,512]{1,0:T(8,128)S(1)}, f32[256,512]{1,0:T(8,128)S(1)}, f32[256,512]{1,0:T(8,128)S(1)}) custom-call(f32[8,256]{1,0:T(8,128)S(1)} %copy-done.8, f32[256,512]{1,0:T(8,128)S(1)} %copy-done.4, f32[256,512]{1,0:T(8,128)S(1)} %collective-permute-done.1.k_ref.k2_ref, ...), custom_call_target="tpu_custom_call" | custom-call | flops 805306368 | bytes 4000000 | tf_op jit(solution)/shard_map/pallas_call | solution.py:458
  38.1 0.0 copy-start.1
  38.1 0.0 copy-start.5
  38.1 0.0 copy-start.7
  38.1 4.1 %shard_map.96 = (f32[4,256,512]{2,1,0:T(8,128)S(1)}, f32[256,512]{1,0:T(8,128)S(1)}, f32[256,512]{1,0:T(8,128)S(1)}, f32[256,512]{1,0:T(8,128)S(1)}) custom-call(f32[256,512]{1,0:T(8,128)S(1)} %copy-done.4, f32[256,512]{1,0:T(8,128)S(1)} %copy-done.2, f32[256,512]{1,0:T(8,128)S(1)} %collective-permute-done.2.ki_ref.k1_ref, f32[256,512]{1,0:T(8,128)S(1)} %copy-done.3, ...), custom_call_target="tpu_custom_call" | custom-call | flops 1610612736 | bytes 4000000 | tf_op jit(solution)/shard_map/pallas_call | solution.py:458
  42.2 0.1 shard_map.98
  42.3 2.8 %collective-permute-start.10 = (f32[160,1024]{1,0:T(8,128)S(1)}, f32[160,1024]{1,0:T(8,128)S(1)}, u32[]{:S(2)}, u32[]{:S(2)}) collective-permute-start(f32[160,1024]{1,0:T(8,128)S(1)} %get-tuple-element.71), channel_id=1, source_target_pairs={{0,4},{4,0},{8,12},{12,8},{16,20},{20,16},{24,28},{28,24},{32,36},... | collective-permute-start | bytes 1966088 | tf_op jit(solution)/shard_map/ppermute | solution.py:586
  45.1 5.0 %collective-permute-start.11 = (f32[96,1024]{1,0:T(8,128)S(1)}, f32[96,1024]{1,0:T(8,128)S(1)}, u32[]{:S(2)}, u32[]{:S(2)}) collective-permute-start(f32[96,1024]{1,0:T(8,128)S(1)} %get-tuple-element.70.a1), channel_id=1, source_target_pairs={{0,8},{4,12},{8,0},{12,4},{16,24},{20,28},{24,16},{28,20},{32,40},... | collective-permute-start | bytes 1179656 | tf_op jit(solution)/shard_map/ppermute | solution.py:586
  50.1 9.4 %collective-permute-done.11.a3 = f32[96,1024]{1,0:T(8,128)S(1)} collective-permute-done((f32[96,1024]{1,0:T(8,128)S(1)}, f32[96,1024]{1,0:T(8,128)S(1)}, u32[]{:S(2)}, u32[]{:S(2)}) %collective-permute-start.11) | collective-permute-done | bytes 393248 | tf_op jit(solution)/shard_map/ppermute | solution.py:586
  59.4 0.0 collective-permute-done.10.a2
  59.4 0.7 collective-permute-start.12
  60.1 1.3 %collective-permute-done.12.a4 = f32[96,1024]{1,0:T(8,128)S(1)} collective-permute-done((f32[96,1024]{1,0:T(8,128)S(1)}, f32[96,1024]{1,0:T(8,128)S(1)}, u32[]{:S(2)}, u32[]{:S(2)}) %collective-permute-start.12) | collective-permute-done | bytes 393248 | tf_op jit(solution)/shard_map/ppermute | solution.py:586
  61.5 2.8 %shard_map.99 = (f32[256,512]{1,0:T(8,128)S(1)}, f32[256,512]{1,0:T(8,128)S(1)}, f32[8,256]{1,0:T(8,128)S(1)}) custom-call(f32[96,512]{1,0:T(8,128)S(1)} %copy-done.1, f32[96,1536]{1,0:T(8,128)S(1)} %copy-done, f32[64,1024]{1,0:T(8,128)S(1)} %collective-permute-done.first_ref.a0, f32[96,1024]{1,0:T(8,128)S(1)} %get-tuple-element.70.a1, ...), custom_call_target="tpu_custom_call" | custom-call | flops 402653184 | bytes 8000000 | tf_op jit(solution)/shard_map/pallas_call | solution.py:435
  64.3 2.5 %collective-permute-start.15 = (f32[8,256]{1,0:T(8,128)S(1)}, f32[8,256]{1,0:T(8,128)S(1)}, u32[]{:S(2)}, u32[]{:S(2)}) collective-permute-start(f32[8,256]{1,0:T(8,128)S(1)} %get-tuple-element.79.s0_ref), channel_id=1, source_target_pairs={{0,3},{1,2},{2,1},{3,0},{4,7},{5,6},{6,5},{7,4},{8,11},{9,10},{10,... | collective-permute-start | bytes 24584 | tf_op jit(solution)/shard_map/ppermute | solution.py:626
  66.8 0.5 collective-permute-start.14
  67.4 0.3 collective-permute-start.13
  67.6 0.5 collective-permute-done.15.s3_ref
  68.1 2.8 %collective-permute-done.14.s2_ref = f32[8,256]{1,0:T(8,128)S(1)} collective-permute-done((f32[8,256]{1,0:T(8,128)S(1)}, f32[8,256]{1,0:T(8,128)S(1)}, u32[]{:S(2)}, u32[]{:S(2)}) %collective-permute-start.14) | collective-permute-done | bytes 8224 | tf_op jit(solution)/shard_map/ppermute | solution.py:626
  70.8 0.0 collective-permute-done.13.s1_ref
  70.8 1.6 %shard_map.100 = (f32[256,512]{1,0:T(8,128)}, f32[264,1024]{1,0:T(8,128)S(1)}, f32[256,512]{1,0:T(8,128)S(1)}, f32[64,1152]{1,0:T(8,128)S(1)}, f32[16,1152]{1,0:T(8,128)S(1)}, /*index=5*/f32[4,1152]{1,0:T(4,128)S(1)}) custom-call(f32[8,256]{1,0:T(8,128)S(1)} %get-tuple-element.79.s0_ref, f32[8,256]{1,0:T(8,128)S(1)} %collective-permute-done.13.s1_ref, ...), custom_call_target="tpu_custom_call" | custom-call | flops 1000000 | bytes 4000000 | tf_op jit(solution)/shard_map/pallas_call | solution.py:435
  72.4 5.1 %collective-permute-start.19 = (f32[264,1024]{1,0:T(8,128)S(1)}, f32[264,1024]{1,0:T(8,128)S(1)}, u32[]{:S(2)}, u32[]{:S(2)}) collective-permute-start(f32[264,1024]{1,0:T(8,128)S(1)} %get-tuple-element.88.dout_ref.q0_ref.d0_ref.t0_ref), channel_id=1, source_target_pairs={{4,8},{8,4},{12,16},{16,12},{20,24},{24,20},{28,32},{32,28},{36,40... | collective-permute-start | bytes 3244040 | tf_op jit(solution)/shard_map/ppermute | solution.py:590
  77.5 0.4 collective-permute-start.18
  77.9 1.0 collective-permute-start.17
  78.9 1.9 %collective-permute-start.16 = (f32[4,1152]{1,0:T(4,128)S(1)}, f32[4,1152]{1,0:T(4,128)S(1)}, u32[]{:S(2)}, u32[]{:S(2)}) collective-permute-start(f32[4,1152]{1,0:T(4,128)S(1)} %get-tuple-element.85.third_ref), channel_id=1, source_target_pairs={{0,64},{4,68},{8,72},{12,76},{16,80},{20,84},{24,88},{28,92},{32,9... | collective-permute-start | bytes 55304 | tf_op jit(solution)/shard_map/ppermute | solution.py:586
  80.8 0.9 collective-permute-done.18.c_ref
  81.7 11.1 %collective-permute-done.17.b_ref = f32[4,1152]{1,0:T(4,128)S(1)} collective-permute-done((f32[4,1152]{1,0:T(4,128)S(1)}, f32[4,1152]{1,0:T(4,128)S(1)}, u32[]{:S(2)}, u32[]{:S(2)}) %collective-permute-start.17) | collective-permute-done | bytes 18464 | tf_op jit(solution)/shard_map/ppermute | solution.py:586
  92.8 0.0 collective-permute-done.16.a_ref
  92.8 0.5 collective-permute-start.22
  93.3 0.0 collective-permute-start.21
  93.3 0.0 collective-permute-start.20
  93.3 5.1 %shard_map.102.near_ref = f32[256,512]{1,0:T(8,128)S(1)} custom-call(f32[4,256,512]{2,1,0:T(8,128)S(1)} %get-tuple-element.65.w0_ref, f32[4,256,256]{2,1,0:T(8,128)S(1)} %get-tuple-element.68.w1_ref, f32[256,512]{1,0:T(8,128)S(1)} %get-tuple-element.73.peak0_ref, f32[256,512]{1,0:T(8,128)S(1)} %get-tuple-element.76.peak1_ref, ...), custom_call_target="tpu_custom_call" | custom-call | flops 2415919104 | bytes 4000000 | tf_op jit(solution)/shard_map/pallas_call | solution.py:458
  98.4 4.6 %collective-permute-done.20.other_ref = f32[28,1152]{1,0:T(8,128)S(1)} collective-permute-done((f32[28,1152]{1,0:T(8,128)S(1)}, f32[28,1152]{1,0:T(8,128)S(1)}, u32[]{:S(2)}, u32[]{:S(2)}) %collective-permute-start.20) | collective-permute-done | bytes 129056 | tf_op jit(solution)/shard_map/ppermute | solution.py:586
  103.0 0.1 collective-permute-start.23
  103.1 3.7 %shard_map.104 = f32[256,512]{1,0:T(8,128)} custom-call(f32[96,512]{1,0:T(8,128)S(1)} %copy-done.1, f32[96,1536]{1,0:T(8,128)S(1)} %copy-done, f32[64,1024]{1,0:T(8,128)S(1)} %collective-permute-done.first_ref.a0, f32[96,1024]{1,0:T(8,128)S(1)} %get-tuple-element.70.a1, f32[160,1024]{1,0:T(8,128)S(1)} %collective-permute-done.10.a2, ...), custom_call_target="tpu_custom_call" | custom-call | flops 402653184 | bytes 6000000 | tf_op jit(solution)/shard_map/pallas_call | solution.py:435
  106.8 5.6 %shard_map.105 = (f32[256,512]{1,0:T(8,128)S(1)}, f32[256,512]{1,0:T(8,128)S(1)}) custom-call(f32[256,512]{1,0:T(8,128)S(1)} %copy-done.2, f32[256,512]{1,0:T(8,128)S(1)} %copy-done.3, f32[264,1024]{1,0:T(8,128)S(1)} %get-tuple-element.88.dout_ref.q0_ref.d0_ref.t0_ref, f32[264,1024]{1,0:T(8,128)S(1)} %collective-permute-done.22.q1_ref.d1_ref.t1_ref, ...), custom_call_target="tpu_custom_call" | custom-call | flops 3221225472 | bytes 4000000 | tf_op jit(solution)/shard_map/pallas_call | solution.py:458
  112.4 0.0 collective-permute-done.21.first_ref.a0
  112.4 1.6 %collective-permute-done.23.other_ref = f32[56,1152]{1,0:T(8,128)S(1)} collective-permute-done((f32[56,1152]{1,0:T(8,128)S(1)}, f32[56,1152]{1,0:T(8,128)S(1)}, u32[]{:S(2)}, u32[]{:S(2)}) %collective-permute-start.23) | collective-permute-done | bytes 258080 | tf_op jit(solution)/shard_map/ppermute | solution.py:586
  114.0 0.1 shard_map.106
  114.1 1.1 collective-permute-start.25
  115.2 2.0 %collective-permute-start.24 = (f32[96,1152]{1,0:T(8,128)S(1)}, f32[96,1152]{1,0:T(8,128)S(1)}, u32[]{:S(2)}, u32[]{:S(2)}) collective-permute-start(f32[96,1152]{1,0:T(8,128)S(1)} %get-tuple-element.98.a1), channel_id=1, source_target_pairs={{0,8},{4,12},{8,0},{12,4},{16,24},{20,28},{24,16},{28,20},{32,40},... | collective-permute-start | bytes 1327112 | tf_op jit(solution)/shard_map/ppermute | solution.py:586
  117.3 3.7 %shard_map.107 = (f32[256,512]{1,0:T(8,128)S(1)}, f32[256,512]{1,0:T(8,128)S(1)}) custom-call(f32[256,512]{1,0:T(8,128)S(1)} %copy-done.2, f32[256,512]{1,0:T(8,128)S(1)} %copy-done.3, f32[264,1024]{1,0:T(8,128)S(1)} %collective-permute-done.19.q_ref.d_ref.t_ref, f32[264,1024]{1,0:T(8,128)S(1)} %collective-permute-done.19.q_ref.d_ref.t_ref, ...), custom_call_target="tpu_custom_call" | custom-call | flops 1610612736 | bytes 4000000 | tf_op jit(solution)/shard_map/pallas_call | solution.py:458
  121.0 2.7 %shard_map.108 = (f32[96,512]{1,0:T(8,128)S(1)}, f32[96,512]{1,0:T(8,128)S(1)}) custom-call(f32[96,512]{1,0:T(8,128)S(1)} %copy-done.1, f32[96,1536]{1,0:T(8,128)S(1)} %copy-done, f32[64,1152]{1,0:T(8,128)S(1)} %collective-permute-done.21.first_ref.a0, f32[96,1152]{1,0:T(8,128)S(1)} %get-tuple-element.98.a1, f32[160,1152]{1,0:T(8,128)S(1)} %collective-permute-done.25.a2), custom_call_target="tpu_custom_call" | custom-call | flops 402653184 | bytes 3000000 | tf_op jit(solution)/shard_map/pallas_call | solution.py:435
  123.7 3.8 %collective-permute-done.24.a0 = f32[96,1152]{1,0:T(8,128)S(1)} collective-permute-done((f32[96,1152]{1,0:T(8,128)S(1)}, f32[96,1152]{1,0:T(8,128)S(1)}, u32[]{:S(2)}, u32[]{:S(2)}) %collective-permute-start.24) | collective-permute-done | bytes 442400 | tf_op jit(solution)/shard_map/ppermute | solution.py:586
  127.6 0.8 collective-permute-start.26
  128.4 1.4 %collective-permute-done.26.a1 = f32[96,1152]{1,0:T(8,128)S(1)} collective-permute-done((f32[96,1152]{1,0:T(8,128)S(1)}, f32[96,1152]{1,0:T(8,128)S(1)}, u32[]{:S(2)}, u32[]{:S(2)}) %collective-permute-start.26) | collective-permute-done | bytes 442400 | tf_op jit(solution)/shard_map/ppermute | solution.py:586
  129.8 3.2 %shard_map.109 = (f32[256,512]{1,0:T(8,128)}, f32[256,512]{1,0:T(8,128)}) custom-call(f32[96,512]{1,0:T(8,128)S(1)} %copy-done.1, f32[96,1536]{1,0:T(8,128)S(1)} %copy-done, f32[96,1152]{1,0:T(8,128)S(1)} %collective-permute-done.24.a0, f32[96,1152]{1,0:T(8,128)S(1)} %collective-permute-done.26.a1, f32[96,512]{1,0:T(8,128)S(1)} %get-tuple-element.100.far_dk_ref, ...), custom_call_target="tpu_custom_call" | custom-call | flops 402653184 | bytes 3000000 | tf_op jit(solution)/shard_map/pallas_call | solution.py:435
  (25 shorter events, 0.1 us)
Async XLA Ops:
  0.6 33.0 %copy-start.4 = (f32[256,512]{1,0:T(8,128)S(1)}, f32[256,512]{1,0:T(8,128)}, u32[]{:S(2)}) copy-start(f32[256,512]{1,0:T(8,128)} %query_ref.1) | copy-start | bytes 1572868
  0.6 12.5 %collective-permute-start.2 = (f32[256,512]{1,0:T(8,128)}, f32[256,512]{1,0:T(8,128)S(1)}, u32[]{:S(2)}, u32[]{:S(2)}) collective-permute-start(f32[256,512]{1,0:T(8,128)} %k_ref.5), channel_id=1, source_target_pairs={{0,4},{4,0},{8,12},{12,8},{16,20},{20,16},{24,28},{28,24},{32,36},... | collective-permute-start | bytes 1572872 | tf_op jit(solution)/shard_map/ppermute | solution.py:586
  4.0 9.1 %collective-permute-start.3 = (f32[256,512]{1,0:T(8,128)}, f32[256,512]{1,0:T(8,128)S(1)}, u32[]{:S(2)}, u32[]{:S(2)}) collective-permute-start(f32[256,512]{1,0:T(8,128)} %v_ref.5), channel_id=1, source_target_pairs={{0,4},{4,0},{8,12},{12,8},{16,20},{20,16},{24,28},{28,24},{32,36},... | collective-permute-start | bytes 1572872 | tf_op jit(solution)/shard_map/ppermute | solution.py:586
  4.1 10.7 %collective-permute-start.1 = (f32[256,512]{1,0:T(8,128)}, f32[256,512]{1,0:T(8,128)S(1)}, u32[]{:S(2)}, u32[]{:S(2)}) collective-permute-start(f32[256,512]{1,0:T(8,128)} %k_ref.5), channel_id=1, source_target_pairs={{4,8},{8,4},{12,16},{16,12},{20,24},{24,20},{28,32},{32,28},{36,40... | collective-permute-start | bytes 1572872 | tf_op jit(solution)/shard_map/ppermute | solution.py:590
  6.2 27.5 %collective-permute-start.8 = (f32[256,512]{1,0:T(8,128)}, f32[256,512]{1,0:T(8,128)S(1)}, u32[]{:S(2)}, u32[]{:S(2)}) collective-permute-start(f32[256,512]{1,0:T(8,128)} %v_ref.5), channel_id=1, source_target_pairs={{4,8},{8,4},{12,16},{16,12},{20,24},{24,20},{28,32},{32,28},{36,40... | collective-permute-start | bytes 1572872 | tf_op jit(solution)/shard_map/ppermute | solution.py:590
  12.9 13.4 %collective-permute-start = (f32[64,1024]{1,0:T(8,128)}, f32[64,1024]{1,0:T(8,128)S(1)}, u32[]{:S(2)}, u32[]{:S(2)}) collective-permute-start(f32[64,1024]{1,0:T(8,128)} %get-tuple-element.57), channel_id=1, source_target_pairs={{0,8},{4,12},{8,0},{12,4},{16,24},{20,28},{24,16},{28,20},{32,40},... | collective-permute-start | bytes 786440 | tf_op jit(solution)/shard_map/ppermute | solution.py:586
  14.8 3.3 %collective-permute-start.4 = (f32[4,1024]{1,0:T(4,128)}, f32[4,1024]{1,0:T(4,128)S(1)}, u32[]{:S(2)}, u32[]{:S(2)}) collective-permute-start(f32[4,1024]{1,0:T(4,128)} %get-tuple-element.62), channel_id=1, source_target_pairs={{0,64},{4,68},{8,72},{12,76},{16,80},{20,84},{24,88},{28,92},{32,9... | collective-permute-start | bytes 49160 | tf_op jit(solution)/shard_map/ppermute | solution.py:586
  14.8 4.0 %collective-permute-start.6 = (f32[4,1024]{1,0:T(4,128)}, f32[4,1024]{1,0:T(4,128)S(1)}, u32[]{:S(2)}, u32[]{:S(2)}) collective-permute-start(f32[4,1024]{1,0:T(4,128)} %get-tuple-element.62), channel_id=1, source_target_pairs={{0,192},{4,196},{8,200},{12,204},{16,208},{20,212},{24,216},{28,22... | collective-permute-start | bytes 49160 | tf_op jit(solution)/shard_map/ppermute | solution.py:586
  16.7 8.6 %collective-permute-start.5 = (f32[4,1024]{1,0:T(4,128)}, f32[4,1024]{1,0:T(4,128)S(1)}, u32[]{:S(2)}, u32[]{:S(2)}) collective-permute-start(f32[4,1024]{1,0:T(4,128)} %get-tuple-element.62), channel_id=1, source_target_pairs={{0,128},{4,132},{8,136},{12,140},{16,144},{20,148},{24,152},{28,15... | collective-permute-start | bytes 49160 | tf_op jit(solution)/shard_map/ppermute | solution.py:586
  25.4 0.8 copy-start.6
  26.2 7.3 %collective-permute-start.7 = (f32[28,1024]{1,0:T(8,128)S(1)}, f32[28,1024]{1,0:T(8,128)S(1)}, u32[]{:S(2)}, u32[]{:S(2)}) collective-permute-start(f32[28,1024]{1,0:T(8,128)S(1)} %shard_map.94.own_ref), channel_id=1, source_target_pairs={{0,16},{4,20},{8,24},{12,28},{16,0},{20,4},{24,8},{28,12},{32,48},... | collective-permute-start | bytes 344072 | tf_op jit(solution)/shard_map/ppermute | solution.py:586
  33.6 8.6 %collective-permute-start.9 = (f32[56,1024]{1,0:T(8,128)S(1)}, f32[56,1024]{1,0:T(8,128)S(1)}, u32[]{:S(2)}, u32[]{:S(2)}) collective-permute-start(f32[56,1024]{1,0:T(8,128)S(1)} %shard_map.95.double_ref), channel_id=1, source_target_pairs={{0,48},{4,52},{8,56},{12,60},{16,32},{20,36},{24,40},{28,44},{32,1... | collective-permute-start | bytes 688136 | tf_op jit(solution)/shard_map/ppermute | solution.py:586
  33.7 0.7 copy-start.8
  34.4 3.7 %copy-start.2 = (f32[256,512]{1,0:T(8,128)S(1)}, f32[256,512]{1,0:T(8,128)}, u32[]{:S(2)}) copy-start(f32[256,512]{1,0:T(8,128)} %k_ref.5) | copy-start | bytes 1572868
  34.4 3.7 %copy-start.3 = (f32[256,512]{1,0:T(8,128)S(1)}, f32[256,512]{1,0:T(8,128)}, u32[]{:S(2)}) copy-start(f32[256,512]{1,0:T(8,128)} %v_ref.5) | copy-start | bytes 1572868
  38.1 23.4 %copy-start.1 = (f32[96,512]{1,0:T(8,128)S(1)}, f32[96,512]{1,0:T(8,128)}, u32[]{:S(2)}) copy-start(f32[96,512]{1,0:T(8,128)} %get-tuple-element.55.bias_ref) | copy-start | bytes 589828
  38.1 23.4 %copy-start.5 = (f32[256,512]{1,0:T(8,128)S(1)}, f32[256,512]{1,0:T(8,128)}, u32[]{:S(2)}) copy-start(f32[256,512]{1,0:T(8,128)} %up_ref.3) | copy-start | bytes 1572868
  38.1 23.4 %copy-start.7 = (f32[512]{0:T(512)S(1)}, f32[512]{0:T(512)}, u32[]{:S(2)}) copy-start(f32[512]{0:T(512)} %param.9) | copy-start | bytes 6148
  42.2 19.3 %copy-start = (f32[96,1536]{1,0:T(8,128)S(1)}, f32[96,1536]{1,0:T(8,128)}, u32[]{:S(2)}) copy-start(f32[96,1536]{1,0:T(8,128)} %get-tuple-element.56.own_ref) | copy-start | bytes 1769476
  42.3 17.1 %collective-permute-start.10 = (f32[160,1024]{1,0:T(8,128)S(1)}, f32[160,1024]{1,0:T(8,128)S(1)}, u32[]{:S(2)}, u32[]{:S(2)}) collective-permute-start(f32[160,1024]{1,0:T(8,128)S(1)} %get-tuple-element.71), channel_id=1, source_target_pairs={{0,4},{4,0},{8,12},{12,8},{16,20},{20,16},{24,28},{28,24},{32,36},... | collective-permute-start | bytes 1966088 | tf_op jit(solution)/shard_map/ppermute | solution.py:586
  45.1 14.3 %collective-permute-start.11 = (f32[96,1024]{1,0:T(8,128)S(1)}, f32[96,1024]{1,0:T(8,128)S(1)}, u32[]{:S(2)}, u32[]{:S(2)}) collective-permute-start(f32[96,1024]{1,0:T(8,128)S(1)} %get-tuple-element.70.a1), channel_id=1, source_target_pairs={{0,8},{4,12},{8,0},{12,4},{16,24},{20,28},{24,16},{28,20},{32,40},... | collective-permute-start | bytes 1179656 | tf_op jit(solution)/shard_map/ppermute | solution.py:586
  59.4 2.0 %collective-permute-start.12 = (f32[96,1024]{1,0:T(8,128)S(1)}, f32[96,1024]{1,0:T(8,128)S(1)}, u32[]{:S(2)}, u32[]{:S(2)}) collective-permute-start(f32[96,1024]{1,0:T(8,128)S(1)} %collective-permute-done.11.a3), channel_id=1, source_target_pairs={{0,4},{4,0},{8,12},{12,8},{16,20},{20,16},{24,28},{28,24},{32,36},... | collective-permute-start | bytes 1179656 | tf_op jit(solution)/shard_map/ppermute | solution.py:586
  64.3 3.8 %collective-permute-start.15 = (f32[8,256]{1,0:T(8,128)S(1)}, f32[8,256]{1,0:T(8,128)S(1)}, u32[]{:S(2)}, u32[]{:S(2)}) collective-permute-start(f32[8,256]{1,0:T(8,128)S(1)} %get-tuple-element.79.s0_ref), channel_id=1, source_target_pairs={{0,3},{1,2},{2,1},{3,0},{4,7},{5,6},{6,5},{7,4},{8,11},{9,10},{10,... | collective-permute-start | bytes 24584 | tf_op jit(solution)/shard_map/ppermute | solution.py:626
  66.8 4.0 %collective-permute-start.14 = (f32[8,256]{1,0:T(8,128)S(1)}, f32[8,256]{1,0:T(8,128)S(1)}, u32[]{:S(2)}, u32[]{:S(2)}) collective-permute-start(f32[8,256]{1,0:T(8,128)S(1)} %get-tuple-element.79.s0_ref), channel_id=1, source_target_pairs={{0,2},{1,3},{2,0},{3,1},{4,6},{5,7},{6,4},{7,5},{8,10},{9,11},{10,... | collective-permute-start | bytes 24584 | tf_op jit(solution)/shard_map/ppermute | solution.py:626
  67.4 3.5 %collective-permute-start.13 = (f32[8,256]{1,0:T(8,128)S(1)}, f32[8,256]{1,0:T(8,128)S(1)}, u32[]{:S(2)}, u32[]{:S(2)}) collective-permute-start(f32[8,256]{1,0:T(8,128)S(1)} %get-tuple-element.79.s0_ref), channel_id=1, source_target_pairs={{0,1},{1,0},{2,3},{3,2},{4,5},{5,4},{6,7},{7,6},{8,9},{9,8},{10,11... | collective-permute-start | bytes 24584 | tf_op jit(solution)/shard_map/ppermute | solution.py:626
  72.4 26.0 %collective-permute-start.19 = (f32[264,1024]{1,0:T(8,128)S(1)}, f32[264,1024]{1,0:T(8,128)S(1)}, u32[]{:S(2)}, u32[]{:S(2)}) collective-permute-start(f32[264,1024]{1,0:T(8,128)S(1)} %get-tuple-element.88.dout_ref.q0_ref.d0_ref.t0_ref), channel_id=1, source_target_pairs={{4,8},{8,4},{12,16},{16,12},{20,24},{24,20},{28,32},{32,28},{36,40... | collective-permute-start | bytes 3244040 | tf_op jit(solution)/shard_map/ppermute | solution.py:590
  77.5 4.2 %collective-permute-start.18 = (f32[4,1152]{1,0:T(4,128)S(1)}, f32[4,1152]{1,0:T(4,128)S(1)}, u32[]{:S(2)}, u32[]{:S(2)}) collective-permute-start(f32[4,1152]{1,0:T(4,128)S(1)} %get-tuple-element.85.third_ref), channel_id=1, source_target_pairs={{0,192},{4,196},{8,200},{12,204},{16,208},{20,212},{24,216},{28,22... | collective-permute-start | bytes 55304 | tf_op jit(solution)/shard_map/ppermute | solution.py:586
  77.9 14.9 %collective-permute-start.17 = (f32[4,1152]{1,0:T(4,128)S(1)}, f32[4,1152]{1,0:T(4,128)S(1)}, u32[]{:S(2)}, u32[]{:S(2)}) collective-permute-start(f32[4,1152]{1,0:T(4,128)S(1)} %get-tuple-element.85.third_ref), channel_id=1, source_target_pairs={{0,128},{4,132},{8,136},{12,140},{16,144},{20,148},{24,152},{28,15... | collective-permute-start | bytes 55304 | tf_op jit(solution)/shard_map/ppermute | solution.py:586
  78.9 13.9 %collective-permute-start.16 = (f32[4,1152]{1,0:T(4,128)S(1)}, f32[4,1152]{1,0:T(4,128)S(1)}, u32[]{:S(2)}, u32[]{:S(2)}) collective-permute-start(f32[4,1152]{1,0:T(4,128)S(1)} %get-tuple-element.85.third_ref), channel_id=1, source_target_pairs={{0,64},{4,68},{8,72},{12,76},{16,80},{20,84},{24,88},{28,92},{32,9... | collective-permute-start | bytes 55304 | tf_op jit(solution)/shard_map/ppermute | solution.py:586
  92.8 14.0 %collective-permute-start.22 = (f32[264,1024]{1,0:T(8,128)S(1)}, f32[264,1024]{1,0:T(8,128)S(1)}, u32[]{:S(2)}, u32[]{:S(2)}) collective-permute-start(f32[264,1024]{1,0:T(8,128)S(1)} %get-tuple-element.88.dout_ref.q0_ref.d0_ref.t0_ref), channel_id=1, source_target_pairs={{0,4},{4,0},{8,12},{12,8},{16,20},{20,16},{24,28},{28,24},{32,36},... | collective-permute-start | bytes 3244040 | tf_op jit(solution)/shard_map/ppermute | solution.py:586
  93.3 19.2 %collective-permute-start.21 = (f32[64,1152]{1,0:T(8,128)S(1)}, f32[64,1152]{1,0:T(8,128)S(1)}, u32[]{:S(2)}, u32[]{:S(2)}) collective-permute-start(f32[64,1152]{1,0:T(8,128)S(1)} %get-tuple-element.90.first_ref), channel_id=1, source_target_pairs={{0,8},{4,12},{8,0},{12,4},{16,24},{20,28},{24,16},{28,20},{32,40},... | collective-permute-start | bytes 884744 | tf_op jit(solution)/shard_map/ppermute | solution.py:586
  93.3 9.7 %collective-permute-start.20 = (f32[28,1152]{1,0:T(8,128)S(1)}, f32[28,1152]{1,0:T(8,128)S(1)}, u32[]{:S(2)}, u32[]{:S(2)}) collective-permute-start(f32[28,1152]{1,0:T(8,128)S(1)} %shard_map.101.own_ref), channel_id=1, source_target_pairs={{0,16},{4,20},{8,24},{12,28},{16,0},{20,4},{24,8},{28,12},{32,48},... | collective-permute-start | bytes 387080 | tf_op jit(solution)/shard_map/ppermute | solution.py:586
  103.0 11.0 %collective-permute-start.23 = (f32[56,1152]{1,0:T(8,128)S(1)}, f32[56,1152]{1,0:T(8,128)S(1)}, u32[]{:S(2)}, u32[]{:S(2)}) collective-permute-start(f32[56,1152]{1,0:T(8,128)S(1)} %shard_map.103.double_ref), channel_id=1, source_target_pairs={{0,48},{4,52},{8,56},{12,60},{16,32},{20,36},{24,40},{28,44},{32,1... | collective-permute-start | bytes 774152 | tf_op jit(solution)/shard_map/ppermute | solution.py:586
  114.1 6.8 %collective-permute-start.25 = (f32[160,1152]{1,0:T(8,128)S(1)}, f32[160,1152]{1,0:T(8,128)S(1)}, u32[]{:S(2)}, u32[]{:S(2)}) collective-permute-start(f32[160,1152]{1,0:T(8,128)S(1)} %get-tuple-element.99), channel_id=1, source_target_pairs={{0,4},{4,0},{8,12},{12,8},{16,20},{20,16},{24,28},{28,24},{32,36},... | collective-permute-start | bytes 2211848 | tf_op jit(solution)/shard_map/ppermute | solution.py:586
  115.2 12.3 %collective-permute-start.24 = (f32[96,1152]{1,0:T(8,128)S(1)}, f32[96,1152]{1,0:T(8,128)S(1)}, u32[]{:S(2)}, u32[]{:S(2)}) collective-permute-start(f32[96,1152]{1,0:T(8,128)S(1)} %get-tuple-element.98.a1), channel_id=1, source_target_pairs={{0,8},{4,12},{8,0},{12,4},{16,24},{20,28},{24,16},{28,20},{32,40},... | collective-permute-start | bytes 1327112 | tf_op jit(solution)/shard_map/ppermute | solution.py:586
  127.6 2.2 %collective-permute-start.26 = (f32[96,1152]{1,0:T(8,128)S(1)}, f32[96,1152]{1,0:T(8,128)S(1)}, u32[]{:S(2)}, u32[]{:S(2)}) collective-permute-start(f32[96,1152]{1,0:T(8,128)S(1)} %collective-permute-done.24.a0), channel_id=1, source_target_pairs={{0,4},{4,0},{8,12},{12,8},{16,20},{20,16},{24,28},{28,24},{32,36},... | collective-permute-start | bytes 1327112 | tf_op jit(solution)/shard_map/ppermute | solution.py:586

commit v5 on v3

--- a/solution.py
+++ b/solution.py
@@ -603,13 +603,14 @@
 
     gain = norm_gain.reshape(1, WIDTH)
     out_k, out_v = exchange_outer(key), exchange_outer(value)
+    in_k, in_v = exchange(key, 1), exchange(value, 1)
     own, first, second, third, bias, edge = pool(key, value, query)
 
-    planes = [exchange(after(third, out_k), PLANES[0])] + [exchange(third, mask) for mask in PLANES[1:]]
+    held = after(third, in_k, in_v)
+    planes = [exchange(after(held, out_k), PLANES[0])] + [exchange(held, mask) for mask in PLANES[1:]]
     l1a = exchange(first, 2)
-    pack = packed(after(second, out_k, out_v, l1a), planes)
-    in_k, in_v = exchange(after(key, pack), 1), exchange(after(value, pack), 1)
-    double = doubled(pack, exchange(pack, 4))
+    pack = packed(after(second, out_k), planes)
+    double = doubled(after(pack, l1a), exchange(pack, 4))
     other = exchange(double, 12)
     w0, *inner = near_inner(query, (key, after(in_k, double)), (value, in_v))
     w1, *outer = near_outer(edge, query, after(out_k, double), out_v)
@@ -617,8 +618,8 @@
     l2b = exchange(l2a, 2)
     core1 = exchange(bundle, 1)
     core2 = exchange(after(l2b, core1), 1)
-    query_in = exchange(after(query, core2), 1)
-    query_out = exchange_outer(after(query, core2))
+    query_in = exchange(after(query, l2a), 1)
+    query_out = exchange_outer(after(query, l2a))
     far = (l1a, l2a, core1, l2b, core2)
     attention, lse, stats = far_forward(bias, own, far, inner, outer, upstream, gain)
 
@@ -634,14 +635,13 @@
     pack = packed(g2, planes)
     quad = exchange(pack, 4)
     near_dq = near_query(
-        w0, w1, inner[0], outer[0], lse, delta, after(d_out, pack),
-        (key, in_k, out_k), (value, in_v, out_v),
+        w0, w1, inner[0], outer[0], lse, delta, after(d_out, pack), (key, in_k, out_k), (value, in_v, out_v)
     )
     double = doubled(after(pack, near_dq, l1a), quad)
     other = exchange(double, 12)
+    d_far = exchange_outer(after(d_out, double))
+    near_dk, near_dv = inner_key(key, value, query, query_in, d_out, after(d_in, double))
     query_grad = far_query(bias, own, far, after(g1, double), g2, g3, near_dq)
-    d_far = exchange_outer(after(d_out, query_grad))
-    near_dk, near_dv = inner_key(key, value, query, query_in, d_out, after(d_in, double))
     l2a, bundle = merged(l1a, after(double, near_dk, query_grad, d_far), other)
     l2b = exchange(l2a, 2)
     core1 = exchange(bundle, 1)

time: 142 us -> 132 us (0.930)
  waiting for transfers between devices: 48.9 us -> 42.5 us
  starting transfers between devices: 50.8 us -> 47 us
    ppermute x22, waiting for transfers between devices: 42.2 us -> 37.3 us  [exchange(): return lax.ppermute(array, 'seq', [(i, i ^ mask) for i in range(count)])]
    ppermute x4, starting transfers between devices: 12.5 us -> 9.38 us  [exchange_outer(): return lax.ppermute(array, 'seq', pairs)]
    ppermute x4, waiting for transfers between devices: 4.1 us -> 2.01 us  [exchange_outer(): return lax.ppermute(array, 'seq', pairs)]
  transfers between devices with their start and end apart: 29 -> 29, of which waited for: 15 -> 16; matrix products, arithmetic and copies ran while one was open for 0% -> 0% of each run, Pallas kernels for 24% -> 26%
where the time goes in v5:
time: 132 us; the launch traced here: 131 us
  starting transfers between devices  47 us (36%)
  waiting for transfers between devices  42.5 us (32%)
  Pallas kernels  39.4 us (30%)
  local copies, waits for them, and re-layouts  1.57 us (1%)
    ppermute x22, waiting for transfers between devices, exchange(): return lax.ppermute(array, 'seq', [(i, i ^ mask) for i in range(count)])  37.3 us
    ppermute x22, starting transfers between devices, exchange(): return lax.ppermute(array, 'seq', [(i, i ^ mask) for i in range(count)])  34.2 us
    pallas_call x5, Pallas kernels, head_call(): pl.pallas_call(kernel, grid=(HEADS,), out_shape=outs, in_specs=in_specs,...  22.1 us
    pallas_call x11, Pallas kernels, whole_call(): pl.pallas_call(kernel, out_shape=outs, in_specs=[spec] * len(operands), o...  14.1 us
    ppermute x4, starting transfers between devices, exchange_outer(): return lax.ppermute(array, 'seq', pairs)  9.38 us
    ppermute x3, starting transfers between devices, body(): lax.ppermute(stats, 'head', [(i, i ^ mask) for i in range(head_count)])  3.4 us
    pallas_call x1, Pallas kernels, pool(): pl.pallas_call(pool_kernel, out_shape=[f32(OWN, 3 * WIDTH), f32(64, KV),...  3.27 us
    ppermute x3, waiting for transfers between devices, body(): lax.ppermute(stats, 'head', [(i, i ^ mask) for i in range(head_count)])  3.14 us
  transfers between devices with their start and end apart: 29, of which 16 were waited for; matrix products, arithmetic and copies ran while one was open for 0% of the time, Pallas kernels for 26%

profile of v5, /device:TPU:1, one launch (start us, length us, event | category | flops | bytes accessed | tf_op | source)
XLA Modules:
  0.0 131.4 jit_solution(14473309674211564021)
XLA Ops:
  0.6 3.3 %collective-permute-start.2 = (f32[256,512]{1,0:T(8,128)}, f32[256,512]{1,0:T(8,128)S(1)}, u32[]{:S(2)}, u32[]{:S(2)}) collective-permute-start(f32[256,512]{1,0:T(8,128)} %k_ref.5), channel_id=1, source_target_pairs={{0,4},{4,0},{8,12},{12,8},{16,20},{20,16},{24,28},{28,24},{32,36},... | collective-permute-start | bytes 1572872 | tf_op jit(solution)/shard_map/ppermute | solution.py:585
  4.0 0.1 collective-permute-start.3
  4.1 2.1 %collective-permute-start.1 = (f32[256,512]{1,0:T(8,128)}, f32[256,512]{1,0:T(8,128)S(1)}, u32[]{:S(2)}, u32[]{:S(2)}) collective-permute-start(f32[256,512]{1,0:T(8,128)} %k_ref.5), channel_id=1, source_target_pairs={{4,8},{8,4},{12,16},{16,12},{20,24},{24,20},{28,32},{32,28},{36,40... | collective-permute-start | bytes 1572872 | tf_op jit(solution)/shard_map/ppermute | solution.py:589
  6.2 3.5 %collective-permute-start.8 = (f32[256,512]{1,0:T(8,128)}, f32[256,512]{1,0:T(8,128)S(1)}, u32[]{:S(2)}, u32[]{:S(2)}) collective-permute-start(f32[256,512]{1,0:T(8,128)} %v_ref.5), channel_id=1, source_target_pairs={{4,8},{8,4},{12,16},{16,12},{20,24},{24,20},{28,32},{32,28},{36,40... | collective-permute-start | bytes 1572872 | tf_op jit(solution)/shard_map/ppermute | solution.py:589
  9.6 3.3 %shard_map.93 = (f32[96,1536]{1,0:T(8,128)}, f32[64,1024]{1,0:T(8,128)}, f32[16,1024]{1,0:T(8,128)}, f32[4,1024]{1,0:T(4,128)}, f32[96,512]{1,0:T(8,128)}, /*index=5*/f32[8,256]{1,0:T(8,128)}) custom-call(s32[8,512]{1,0:T(8,128)} %constant.2.clone.table_ref, f32[256,512]{1,0:T(8,128)} %k_ref.5, f32[256,512]{1,0:T(8,128)} %v_ref.5, f32[256,512]{1,0:T(8,128)} %q0_ref.1), custom_call_target="tpu_custom_call" | custom-call | flops 1000000 | bytes 2000000 | tf_op jit(solution)/shard_map/pallas_call | solution.py:512
  12.9 0.0 copy-start.3
  12.9 0.0 copy-start.4
  12.9 0.2 collective-permute-start
  13.1 1.6 %collective-permute-done.1.k_ref.k2_ref = f32[256,512]{1,0:T(8,128)S(1)} collective-permute-done((f32[256,512]{1,0:T(8,128)}, f32[256,512]{1,0:T(8,128)S(1)}, u32[]{:S(2)}, u32[]{:S(2)}) %collective-permute-start.1) | collective-permute-done | bytes 524320 | tf_op jit(solution)/shard_map/ppermute | solution.py:589
  14.8 0.1 collective-permute-start.4
  14.8 1.9 %collective-permute-start.6 = (f32[4,1024]{1,0:T(4,128)}, f32[4,1024]{1,0:T(4,128)S(1)}, u32[]{:S(2)}, u32[]{:S(2)}) collective-permute-start(f32[4,1024]{1,0:T(4,128)} %get-tuple-element.65), channel_id=1, source_target_pairs={{0,192},{4,196},{8,200},{12,204},{16,208},{20,212},{24,216},{28,22... | collective-permute-start | bytes 49160 | tf_op jit(solution)/shard_map/ppermute | solution.py:585
  16.7 1.3 collective-permute-start.5
  18.0 0.8 collective-permute-done.6.c_ref
  18.8 6.5 %collective-permute-done.5.b_ref = f32[4,1024]{1,0:T(4,128)S(1)} collective-permute-done((f32[4,1024]{1,0:T(4,128)}, f32[4,1024]{1,0:T(4,128)S(1)}, u32[]{:S(2)}, u32[]{:S(2)}) %collective-permute-start.5) | collective-permute-done | bytes 16416 | tf_op jit(solution)/shard_map/ppermute | solution.py:585
  25.4 0.8 copy-done.6
  26.2 0.1 collective-permute-start.7
  26.3 7.2 %collective-permute-done.7.other_ref = f32[28,1024]{1,0:T(8,128)S(1)} collective-permute-done((f32[28,1024]{1,0:T(8,128)S(1)}, f32[28,1024]{1,0:T(8,128)S(1)}, u32[]{:S(2)}, u32[]{:S(2)}) %collective-permute-start.7) | collective-permute-done | bytes 114720 | tf_op jit(solution)/shard_map/ppermute | solution.py:585
  33.5 0.1 collective-permute-start.9
  33.7 0.7 copy-done.8
  34.4 3.6 %shard_map.97 = (f32[4,256,256]{2,1,0:T(8,128)S(1)}, f32[256,512]{1,0:T(8,128)S(1)}, f32[256,512]{1,0:T(8,128)S(1)}, f32[256,512]{1,0:T(8,128)S(1)}) custom-call(f32[8,256]{1,0:T(8,128)S(1)} %copy-done.8, f32[256,512]{1,0:T(8,128)S(1)} %copy-done.5, f32[256,512]{1,0:T(8,128)S(1)} %collective-permute-done.1.k_ref.k2_ref, ...), custom_call_target="tpu_custom_call" | custom-call | flops 805306368 | bytes 4000000 | tf_op jit(solution)/shard_map/pallas_call | solution.py:457
  38.0 0.0 copy-start.1
  38.1 0.0 copy-start.2
  38.1 4.1 %shard_map.96 = (f32[4,256,512]{2,1,0:T(8,128)S(1)}, f32[256,512]{1,0:T(8,128)S(1)}, f32[256,512]{1,0:T(8,128)S(1)}, f32[256,512]{1,0:T(8,128)S(1)}) custom-call(f32[256,512]{1,0:T(8,128)S(1)} %copy-done.5, f32[256,512]{1,0:T(8,128)S(1)} %copy-done.3, f32[256,512]{1,0:T(8,128)S(1)} %collective-permute-done.2.ki_ref.k1_ref, f32[256,512]{1,0:T(8,128)S(1)} %copy-done.4, ...), custom_call_target="tpu_custom_call" | custom-call | flops 1610612736 | bytes 4000000 | tf_op jit(solution)/shard_map/pallas_call | solution.py:457
  42.2 0.1 shard_map.98
  42.3 2.8 %collective-permute-start.10 = (f32[160,1024]{1,0:T(8,128)S(1)}, f32[160,1024]{1,0:T(8,128)S(1)}, u32[]{:S(2)}, u32[]{:S(2)}) collective-permute-start(f32[160,1024]{1,0:T(8,128)S(1)} %get-tuple-element.74), channel_id=1, source_target_pairs={{0,4},{4,0},{8,12},{12,8},{16,20},{20,16},{24,28},{28,24},{32,36},... | collective-permute-start | bytes 1966088 | tf_op jit(solution)/shard_map/ppermute | solution.py:585
  45.1 5.0 %collective-permute-start.11 = (f32[96,1024]{1,0:T(8,128)S(1)}, f32[96,1024]{1,0:T(8,128)S(1)}, u32[]{:S(2)}, u32[]{:S(2)}) collective-permute-start(f32[96,1024]{1,0:T(8,128)S(1)} %get-tuple-element.73.a1), channel_id=1, source_target_pairs={{0,8},{4,12},{8,0},{12,4},{16,24},{20,28},{24,16},{28,20},{32,40},... | collective-permute-start | bytes 1179656 | tf_op jit(solution)/shard_map/ppermute | solution.py:585
  50.0 1.9 %collective-permute-start.17 = (f32[256,512]{1,0:T(8,128)S(1)}, f32[256,512]{1,0:T(8,128)S(1)}, u32[]{:S(2)}, u32[]{:S(2)}) collective-permute-start(f32[256,512]{1,0:T(8,128)S(1)} %copy-done.5), channel_id=1, source_target_pairs={{4,8},{8,4},{12,16},{16,12},{20,24},{24,20},{28,32},{32,28},{36,40... | collective-permute-start | bytes 1572872 | tf_op jit(solution)/shard_map/ppermute | solution.py:589
  52.0 0.1 collective-permute-start.16
  52.1 7.4 %collective-permute-done.11.a3 = f32[96,1024]{1,0:T(8,128)S(1)} collective-permute-done((f32[96,1024]{1,0:T(8,128)S(1)}, f32[96,1024]{1,0:T(8,128)S(1)}, u32[]{:S(2)}, u32[]{:S(2)}) %collective-permute-start.11) | collective-permute-done | bytes 393248 | tf_op jit(solution)/shard_map/ppermute | solution.py:585
  59.4 0.7 collective-permute-start.12
  60.1 1.3 %collective-permute-done.12.a4 = f32[96,1024]{1,0:T(8,128)S(1)} collective-permute-done((f32[96,1024]{1,0:T(8,128)S(1)}, f32[96,1024]{1,0:T(8,128)S(1)}, u32[]{:S(2)}, u32[]{:S(2)}) %collective-permute-start.12) | collective-permute-done | bytes 393248 | tf_op jit(solution)/shard_map/ppermute | solution.py:585
  61.5 2.8 %shard_map.99 = (f32[256,512]{1,0:T(8,128)S(1)}, f32[256,512]{1,0:T(8,128)S(1)}, f32[8,256]{1,0:T(8,128)S(1)}) custom-call(f32[96,512]{1,0:T(8,128)S(1)} %copy-done.1, f32[96,1536]{1,0:T(8,128)S(1)} %copy-done, f32[64,1024]{1,0:T(8,128)S(1)} %collective-permute-done.first_ref.a0, f32[96,1024]{1,0:T(8,128)S(1)} %get-tuple-element.73.a1, ...), custom_call_target="tpu_custom_call" | custom-call | flops 402653184 | bytes 8000000 | tf_op jit(solution)/shard_map/pallas_call | solution.py:434
  64.3 2.5 %collective-permute-start.15 = (f32[8,256]{1,0:T(8,128)S(1)}, f32[8,256]{1,0:T(8,128)S(1)}, u32[]{:S(2)}, u32[]{:S(2)}) collective-permute-start(f32[8,256]{1,0:T(8,128)S(1)} %get-tuple-element.82.s0_ref), channel_id=1, source_target_pairs={{0,3},{1,2},{2,1},{3,0},{4,7},{5,6},{6,5},{7,4},{8,11},{9,10},{10,... | collective-permute-start | bytes 24584 | tf_op jit(solution)/shard_map/ppermute | solution.py:627
  66.8 0.6 collective-permute-start.14
  67.4 0.3 collective-permute-start.13
  67.7 0.4 collective-permute-done.15.s3_ref
  68.1 2.8 %collective-permute-done.14.s2_ref = f32[8,256]{1,0:T(8,128)S(1)} collective-permute-done((f32[8,256]{1,0:T(8,128)S(1)}, f32[8,256]{1,0:T(8,128)S(1)}, u32[]{:S(2)}, u32[]{:S(2)}) %collective-permute-start.14) | collective-permute-done | bytes 8224 | tf_op jit(solution)/shard_map/ppermute | solution.py:627
  70.8 1.4 %shard_map.100 = (f32[256,512]{1,0:T(8,128)}, f32[264,512]{1,0:T(8,128)S(1)}, f32[256,512]{1,0:T(8,128)S(1)}, f32[64,1152]{1,0:T(8,128)S(1)}, f32[16,1152]{1,0:T(8,128)S(1)}, /*index=5*/f32[4,1152]{1,0:T(4,128)S(1)}) custom-call(f32[8,256]{1,0:T(8,128)S(1)} %get-tuple-element.82.s0_ref, f32[8,256]{1,0:T(8,128)S(1)} %collective-permute-done.13.s1_ref, ...), custom_call_target="tpu_custom_call" | custom-call | flops 1000000 | bytes 4000000 | tf_op jit(solution)/shard_map/pallas_call | solution.py:434
  72.2 1.8 %collective-permute-start.23 = (f32[264,512]{1,0:T(8,128)S(1)}, f32[264,512]{1,0:T(8,128)S(1)}, u32[]{:S(2)}, u32[]{:S(2)}) collective-permute-start(f32[264,512]{1,0:T(8,128)S(1)} %get-tuple-element.98.dout_ref.d0_ref.t0_ref), channel_id=1, source_target_pairs={{0,4},{4,0},{8,12},{12,8},{16,20},{20,16},{24,28},{28,24},{32,36},... | collective-permute-start | bytes 1622024 | tf_op jit(solution)/shard_map/ppermute | solution.py:585
  74.0 2.0 %collective-permute-start.21 = (f32[64,1152]{1,0:T(8,128)S(1)}, f32[64,1152]{1,0:T(8,128)S(1)}, u32[]{:S(2)}, u32[]{:S(2)}) collective-permute-start(f32[64,1152]{1,0:T(8,128)S(1)} %get-tuple-element.95.first_ref), channel_id=1, source_target_pairs={{0,8},{4,12},{8,0},{12,4},{16,24},{20,28},{24,16},{28,20},{32,40},... | collective-permute-start | bytes 884744 | tf_op jit(solution)/shard_map/ppermute | solution.py:585
  76.0 0.4 collective-permute-start.20
  76.3 0.9 collective-permute-start.19
  77.2 2.0 %collective-permute-start.18 = (f32[4,1152]{1,0:T(4,128)S(1)}, f32[4,1152]{1,0:T(4,128)S(1)}, u32[]{:S(2)}, u32[]{:S(2)}) collective-permute-start(f32[4,1152]{1,0:T(4,128)S(1)} %get-tuple-element.90.third_ref), channel_id=1, source_target_pairs={{0,64},{4,68},{8,72},{12,76},{16,80},{20,84},{24,88},{28,92},{32,9... | collective-permute-start | bytes 55304 | tf_op jit(solution)/shard_map/ppermute | solution.py:585
  79.2 0.6 collective-permute-done.20.c_ref
  79.8 0.7 collective-permute-done.19.b_ref
  80.5 0.4 collective-permute-done.18.a_ref
  80.9 0.1 collective-permute-start.22
  81.0 5.1 %shard_map.102.near_ref = f32[256,512]{1,0:T(8,128)S(1)} custom-call(f32[4,256,512]{2,1,0:T(8,128)S(1)} %get-tuple-element.68.w0_ref, f32[4,256,256]{2,1,0:T(8,128)S(1)} %get-tuple-element.71.w1_ref, f32[256,512]{1,0:T(8,128)S(1)} %get-tuple-element.76.peak0_ref, f32[256,512]{1,0:T(8,128)S(1)} %get-tuple-element.79.peak1_ref, ...), custom_call_target="tpu_custom_call" | custom-call | flops 2415919104 | bytes 4000000 | tf_op jit(solution)/shard_map/pallas_call | solution.py:457
  86.1 4.5 %collective-permute-done.22.other_ref = f32[28,1152]{1,0:T(8,128)S(1)} collective-permute-done((f32[28,1152]{1,0:T(8,128)S(1)}, f32[28,1152]{1,0:T(8,128)S(1)}, u32[]{:S(2)}, u32[]{:S(2)}) %collective-permute-start.22) | collective-permute-done | bytes 129056 | tf_op jit(solution)/shard_map/ppermute | solution.py:585
  90.5 1.9 %collective-permute-start.24 = (f32[264,512]{1,0:T(8,128)S(1)}, f32[264,512]{1,0:T(8,128)S(1)}, u32[]{:S(2)}, u32[]{:S(2)}) collective-permute-start(f32[264,512]{1,0:T(8,128)S(1)} %get-tuple-element.98.dout_ref.d0_ref.t0_ref), channel_id=1, source_target_pairs={{4,8},{8,4},{12,16},{16,12},{20,24},{24,20},{28,32},{32,28},{36,40... | collective-permute-start | bytes 1622024 | tf_op jit(solution)/shard_map/ppermute | solution.py:589
  92.5 1.5 %collective-permute-start.25 = (f32[56,1152]{1,0:T(8,128)S(1)}, f32[56,1152]{1,0:T(8,128)S(1)}, u32[]{:S(2)}, u32[]{:S(2)}) collective-permute-start(f32[56,1152]{1,0:T(8,128)S(1)} %shard_map.103.double_ref), channel_id=1, source_target_pairs={{0,48},{4,52},{8,56},{12,60},{16,32},{20,36},{24,40},{28,44},{32,1... | collective-permute-start | bytes 774152 | tf_op jit(solution)/shard_map/ppermute | solution.py:585
  94.0 3.7 %shard_map.104 = f32[256,512]{1,0:T(8,128)} custom-call(f32[96,512]{1,0:T(8,128)S(1)} %copy-done.1, f32[96,1536]{1,0:T(8,128)S(1)} %copy-done, f32[64,1024]{1,0:T(8,128)S(1)} %collective-permute-done.first_ref.a0, f32[96,1024]{1,0:T(8,128)S(1)} %get-tuple-element.73.a1, f32[160,1024]{1,0:T(8,128)S(1)} %collective-permute-done.10.a2, ...), custom_call_target="tpu_custom_call" | custom-call | flops 402653184 | bytes 6000000 | tf_op jit(solution)/shard_map/pallas_call | solution.py:434
  97.7 5.6 %shard_map.105 = (f32[256,512]{1,0:T(8,128)S(1)}, f32[256,512]{1,0:T(8,128)S(1)}) custom-call(f32[256,512]{1,0:T(8,128)S(1)} %copy-done.3, f32[256,512]{1,0:T(8,128)S(1)} %copy-done.4, f32[256,512]{1,0:T(8,128)S(1)} %copy-done.5, f32[256,512]{1,0:T(8,128)S(1)} %collective-permute-done.16.q1_ref, f32[264,512]{1,0:T(8,128)S(1)} %get-tuple-element.98.dout_ref.d0_ref.t0_ref, ...), custom_call_target="tpu_custom_call" | custom-call | flops 3221225472 | bytes 4000000 | tf_op jit(solution)/shard_map/pallas_call | solution.py:457
  103.3 0.4 collective-permute-done.24.d_ref.t_ref
  103.7 2.6 %collective-permute-done.25.other_ref = f32[56,1152]{1,0:T(8,128)S(1)} collective-permute-done((f32[56,1152]{1,0:T(8,128)S(1)}, f32[56,1152]{1,0:T(8,128)S(1)}, u32[]{:S(2)}, u32[]{:S(2)}) %collective-permute-start.25) | collective-permute-done | bytes 258080 | tf_op jit(solution)/shard_map/ppermute | solution.py:585
  106.2 0.1 shard_map.106
  106.3 0.1 collective-permute-start.27
  106.4 9.3 %collective-permute-start.26 = (f32[96,1152]{1,0:T(8,128)S(1)}, f32[96,1152]{1,0:T(8,128)S(1)}, u32[]{:S(2)}, u32[]{:S(2)}) collective-permute-start(f32[96,1152]{1,0:T(8,128)S(1)} %get-tuple-element.104.a1), channel_id=1, source_target_pairs={{0,8},{4,12},{8,0},{12,4},{16,24},{20,28},{24,16},{28,20},{32,40},... | collective-permute-start | bytes 1327112 | tf_op jit(solution)/shard_map/ppermute | solution.py:585
  115.7 3.7 %shard_map.107 = (f32[256,512]{1,0:T(8,128)S(1)}, f32[256,512]{1,0:T(8,128)S(1)}) custom-call(f32[256,512]{1,0:T(8,128)S(1)} %copy-done.3, f32[256,512]{1,0:T(8,128)S(1)} %copy-done.4, f32[256,512]{1,0:T(8,128)S(1)} %collective-permute-done.17.q_ref, f32[264,512]{1,0:T(8,128)S(1)} %collective-permute-done.24.d_ref.t_ref, ...), custom_call_target="tpu_custom_call" | custom-call | flops 1610612736 | bytes 4000000 | tf_op jit(solution)/shard_map/pallas_call | solution.py:457
  119.4 2.7 %shard_map.108 = (f32[96,512]{1,0:T(8,128)S(1)}, f32[96,512]{1,0:T(8,128)S(1)}) custom-call(f32[96,512]{1,0:T(8,128)S(1)} %copy-done.1, f32[96,1536]{1,0:T(8,128)S(1)} %copy-done, f32[64,1152]{1,0:T(8,128)S(1)} %collective-permute-done.21.first_ref.a0, f32[96,1152]{1,0:T(8,128)S(1)} %get-tuple-element.104.a1, f32[160,1152]{1,0:T(8,128)S(1)} %collective-permute-done.27.a2), custom_call_target="tpu_custom_call" | custom-call | flops 402653184 | bytes 3000000 | tf_op jit(solution)/shard_map/pallas_call | solution.py:434
  122.2 4.0 %collective-permute-done.26.a0 = f32[96,1152]{1,0:T(8,128)S(1)} collective-permute-done((f32[96,1152]{1,0:T(8,128)S(1)}, f32[96,1152]{1,0:T(8,128)S(1)}, u32[]{:S(2)}, u32[]{:S(2)}) %collective-permute-start.26) | collective-permute-done | bytes 442400 | tf_op jit(solution)/shard_map/ppermute | solution.py:585
  126.1 0.7 collective-permute-start.28
  126.8 1.4 %collective-permute-done.28.a1 = f32[96,1152]{1,0:T(8,128)S(1)} collective-permute-done((f32[96,1152]{1,0:T(8,128)S(1)}, f32[96,1152]{1,0:T(8,128)S(1)}, u32[]{:S(2)}, u32[]{:S(2)}) %collective-permute-start.28) | collective-permute-done | bytes 442400 | tf_op jit(solution)/shard_map/ppermute | solution.py:585
  128.2 3.2 %shard_map.109 = (f32[256,512]{1,0:T(8,128)}, f32[256,512]{1,0:T(8,128)}) custom-call(f32[96,512]{1,0:T(8,128)S(1)} %copy-done.1, f32[96,1536]{1,0:T(8,128)S(1)} %copy-done, f32[96,1152]{1,0:T(8,128)S(1)} %collective-permute-done.26.a0, f32[96,1152]{1,0:T(8,128)S(1)} %collective-permute-done.28.a1, f32[96,512]{1,0:T(8,128)S(1)} %get-tuple-element.106.far_dk_ref, ...), custom_call_target="tpu_custom_call" | custom-call | flops 402653184 | bytes 3000000 | tf_op jit(solution)/shard_map/pallas_call | solution.py:434
  (29 shorter events, 0.1 us)
Async XLA Ops:
  0.6 33.0 %copy-start.5 = (f32[256,512]{1,0:T(8,128)S(1)}, f32[256,512]{1,0:T(8,128)}, u32[]{:S(2)}) copy-start(f32[256,512]{1,0:T(8,128)} %q0_ref.1) | copy-start | bytes 1572868
  0.6 12.5 %collective-permute-start.2 = (f32[256,512]{1,0:T(8,128)}, f32[256,512]{1,0:T(8,128)S(1)}, u32[]{:S(2)}, u32[]{:S(2)}) collective-permute-start(f32[256,512]{1,0:T(8,128)} %k_ref.5), channel_id=1, source_target_pairs={{0,4},{4,0},{8,12},{12,8},{16,20},{20,16},{24,28},{28,24},{32,36},... | collective-permute-start | bytes 1572872 | tf_op jit(solution)/shard_map/ppermute | solution.py:585
  4.0 9.2 %collective-permute-start.3 = (f32[256,512]{1,0:T(8,128)}, f32[256,512]{1,0:T(8,128)S(1)}, u32[]{:S(2)}, u32[]{:S(2)}) collective-permute-start(f32[256,512]{1,0:T(8,128)} %v_ref.5), channel_id=1, source_target_pairs={{0,4},{4,0},{8,12},{12,8},{16,20},{20,16},{24,28},{28,24},{32,36},... | collective-permute-start | bytes 1572872 | tf_op jit(solution)/shard_map/ppermute | solution.py:585
  4.1 10.7 %collective-permute-start.1 = (f32[256,512]{1,0:T(8,128)}, f32[256,512]{1,0:T(8,128)S(1)}, u32[]{:S(2)}, u32[]{:S(2)}) collective-permute-start(f32[256,512]{1,0:T(8,128)} %k_ref.5), channel_id=1, source_target_pairs={{4,8},{8,4},{12,16},{16,12},{20,24},{24,20},{28,32},{32,28},{36,40... | collective-permute-start | bytes 1572872 | tf_op jit(solution)/shard_map/ppermute | solution.py:589
  6.2 27.5 %collective-permute-start.8 = (f32[256,512]{1,0:T(8,128)}, f32[256,512]{1,0:T(8,128)S(1)}, u32[]{:S(2)}, u32[]{:S(2)}) collective-permute-start(f32[256,512]{1,0:T(8,128)} %v_ref.5), channel_id=1, source_target_pairs={{4,8},{8,4},{12,16},{16,12},{20,24},{24,20},{28,32},{32,28},{36,40... | collective-permute-start | bytes 1572872 | tf_op jit(solution)/shard_map/ppermute | solution.py:589
  12.9 25.1 %copy-start.3 = (f32[256,512]{1,0:T(8,128)S(1)}, f32[256,512]{1,0:T(8,128)}, u32[]{:S(2)}) copy-start(f32[256,512]{1,0:T(8,128)} %k_ref.5) | copy-start | bytes 1572868
  12.9 25.1 %copy-start.4 = (f32[256,512]{1,0:T(8,128)S(1)}, f32[256,512]{1,0:T(8,128)}, u32[]{:S(2)}) copy-start(f32[256,512]{1,0:T(8,128)} %v_ref.5) | copy-start | bytes 1572868
  12.9 13.4 %collective-permute-start = (f32[64,1024]{1,0:T(8,128)}, f32[64,1024]{1,0:T(8,128)S(1)}, u32[]{:S(2)}, u32[]{:S(2)}) collective-permute-start(f32[64,1024]{1,0:T(8,128)} %get-tuple-element.60), channel_id=1, source_target_pairs={{0,8},{4,12},{8,0},{12,4},{16,24},{20,28},{24,16},{28,20},{32,40},... | collective-permute-start | bytes 786440 | tf_op jit(solution)/shard_map/ppermute | solution.py:585
  14.8 3.3 %collective-permute-start.4 = (f32[4,1024]{1,0:T(4,128)}, f32[4,1024]{1,0:T(4,128)S(1)}, u32[]{:S(2)}, u32[]{:S(2)}) collective-permute-start(f32[4,1024]{1,0:T(4,128)} %get-tuple-element.65), channel_id=1, source_target_pairs={{0,64},{4,68},{8,72},{12,76},{16,80},{20,84},{24,88},{28,92},{32,9... | collective-permute-start | bytes 49160 | tf_op jit(solution)/shard_map/ppermute | solution.py:585
  14.8 4.0 %collective-permute-start.6 = (f32[4,1024]{1,0:T(4,128)}, f32[4,1024]{1,0:T(4,128)S(1)}, u32[]{:S(2)}, u32[]{:S(2)}) collective-permute-start(f32[4,1024]{1,0:T(4,128)} %get-tuple-element.65), channel_id=1, source_target_pairs={{0,192},{4,196},{8,200},{12,204},{16,208},{20,212},{24,216},{28,22... | collective-permute-start | bytes 49160 | tf_op jit(solution)/shard_map/ppermute | solution.py:585
  16.7 8.6 %collective-permute-start.5 = (f32[4,1024]{1,0:T(4,128)}, f32[4,1024]{1,0:T(4,128)S(1)}, u32[]{:S(2)}, u32[]{:S(2)}) collective-permute-start(f32[4,1024]{1,0:T(4,128)} %get-tuple-element.65), channel_id=1, source_target_pairs={{0,128},{4,132},{8,136},{12,140},{16,144},{20,148},{24,152},{28,15... | collective-permute-start | bytes 49160 | tf_op jit(solution)/shard_map/ppermute | solution.py:585
  25.4 0.8 copy-start.6
  26.2 7.3 %collective-permute-start.7 = (f32[28,1024]{1,0:T(8,128)S(1)}, f32[28,1024]{1,0:T(8,128)S(1)}, u32[]{:S(2)}, u32[]{:S(2)}) collective-permute-start(f32[28,1024]{1,0:T(8,128)S(1)} %shard_map.94.own_ref), channel_id=1, source_target_pairs={{0,16},{4,20},{8,24},{12,28},{16,0},{20,4},{24,8},{28,12},{32,48},... | collective-permute-start | bytes 344072 | tf_op jit(solution)/shard_map/ppermute | solution.py:585
  33.5 8.6 %collective-permute-start.9 = (f32[56,1024]{1,0:T(8,128)S(1)}, f32[56,1024]{1,0:T(8,128)S(1)}, u32[]{:S(2)}, u32[]{:S(2)}) collective-permute-start(f32[56,1024]{1,0:T(8,128)S(1)} %shard_map.95.double_ref), channel_id=1, source_target_pairs={{0,48},{4,52},{8,56},{12,60},{16,32},{20,36},{24,40},{28,44},{32,1... | collective-permute-start | bytes 688136 | tf_op jit(solution)/shard_map/ppermute | solution.py:585
  33.7 0.7 copy-start.8
  38.0 23.4 %copy-start = (f32[96,1536]{1,0:T(8,128)S(1)}, f32[96,1536]{1,0:T(8,128)}, u32[]{:S(2)}) copy-start(f32[96,1536]{1,0:T(8,128)} %get-tuple-element.59.own_ref) | copy-start | bytes 1769476
  38.0 23.4 %copy-start.1 = (f32[96,512]{1,0:T(8,128)S(1)}, f32[96,512]{1,0:T(8,128)}, u32[]{:S(2)}) copy-start(f32[96,512]{1,0:T(8,128)} %get-tuple-element.58.bias_ref) | copy-start | bytes 589828
  38.1 23.4 %copy-start.2 = (f32[256,512]{1,0:T(8,128)S(1)}, f32[256,512]{1,0:T(8,128)}, u32[]{:S(2)}) copy-start(f32[256,512]{1,0:T(8,128)} %up_ref.3) | copy-start | bytes 1572868
  38.1 23.4 %copy-start.7 = (f32[512]{0:T(512)S(1)}, f32[512]{0:T(512)}, u32[]{:S(2)}) copy-start(f32[512]{0:T(512)} %param.9) | copy-start | bytes 6148
  42.3 17.1 %collective-permute-start.10 = (f32[160,1024]{1,0:T(8,128)S(1)}, f32[160,1024]{1,0:T(8,128)S(1)}, u32[]{:S(2)}, u32[]{:S(2)}) collective-permute-start(f32[160,1024]{1,0:T(8,128)S(1)} %get-tuple-element.74), channel_id=1, source_target_pairs={{0,4},{4,0},{8,12},{12,8},{16,20},{20,16},{24,28},{28,24},{32,36},... | collective-permute-start | bytes 1966088 | tf_op jit(solution)/shard_map/ppermute | solution.py:585
  45.1 14.3 %collective-permute-start.11 = (f32[96,1024]{1,0:T(8,128)S(1)}, f32[96,1024]{1,0:T(8,128)S(1)}, u32[]{:S(2)}, u32[]{:S(2)}) collective-permute-start(f32[96,1024]{1,0:T(8,128)S(1)} %get-tuple-element.73.a1), channel_id=1, source_target_pairs={{0,8},{4,12},{8,0},{12,4},{16,24},{20,28},{24,16},{28,20},{32,40},... | collective-permute-start | bytes 1179656 | tf_op jit(solution)/shard_map/ppermute | solution.py:585
  50.0 17.7 %collective-permute-start.17 = (f32[256,512]{1,0:T(8,128)S(1)}, f32[256,512]{1,0:T(8,128)S(1)}, u32[]{:S(2)}, u32[]{:S(2)}) collective-permute-start(f32[256,512]{1,0:T(8,128)S(1)} %copy-done.5), channel_id=1, source_target_pairs={{4,8},{8,4},{12,16},{16,12},{20,24},{24,20},{28,32},{32,28},{36,40... | collective-permute-start | bytes 1572872 | tf_op jit(solution)/shard_map/ppermute | solution.py:589
  52.0 15.7 %collective-permute-start.16 = (f32[256,512]{1,0:T(8,128)S(1)}, f32[256,512]{1,0:T(8,128)S(1)}, u32[]{:S(2)}, u32[]{:S(2)}) collective-permute-start(f32[256,512]{1,0:T(8,128)S(1)} %copy-done.5), channel_id=1, source_target_pairs={{0,4},{4,0},{8,12},{12,8},{16,20},{20,16},{24,28},{28,24},{32,36},... | collective-permute-start | bytes 1572872 | tf_op jit(solution)/shard_map/ppermute | solution.py:585
  59.4 2.0 %collective-permute-start.12 = (f32[96,1024]{1,0:T(8,128)S(1)}, f32[96,1024]{1,0:T(8,128)S(1)}, u32[]{:S(2)}, u32[]{:S(2)}) collective-permute-start(f32[96,1024]{1,0:T(8,128)S(1)} %collective-permute-done.11.a3), channel_id=1, source_target_pairs={{0,4},{4,0},{8,12},{12,8},{16,20},{20,16},{24,28},{28,24},{32,36},... | collective-permute-start | bytes 1179656 | tf_op jit(solution)/shard_map/ppermute | solution.py:585
  64.3 3.8 %collective-permute-start.15 = (f32[8,256]{1,0:T(8,128)S(1)}, f32[8,256]{1,0:T(8,128)S(1)}, u32[]{:S(2)}, u32[]{:S(2)}) collective-permute-start(f32[8,256]{1,0:T(8,128)S(1)} %get-tuple-element.82.s0_ref), channel_id=1, source_target_pairs={{0,3},{1,2},{2,1},{3,0},{4,7},{5,6},{6,5},{7,4},{8,11},{9,10},{10,... | collective-permute-start | bytes 24584 | tf_op jit(solution)/shard_map/ppermute | solution.py:627
  66.8 4.0 %collective-permute-start.14 = (f32[8,256]{1,0:T(8,128)S(1)}, f32[8,256]{1,0:T(8,128)S(1)}, u32[]{:S(2)}, u32[]{:S(2)}) collective-permute-start(f32[8,256]{1,0:T(8,128)S(1)} %get-tuple-element.82.s0_ref), channel_id=1, source_target_pairs={{0,2},{1,3},{2,0},{3,1},{4,6},{5,7},{6,4},{7,5},{8,10},{9,11},{10,... | collective-permute-start | bytes 24584 | tf_op jit(solution)/shard_map/ppermute | solution.py:627
  67.4 3.5 %collective-permute-start.13 = (f32[8,256]{1,0:T(8,128)S(1)}, f32[8,256]{1,0:T(8,128)S(1)}, u32[]{:S(2)}, u32[]{:S(2)}) collective-permute-start(f32[8,256]{1,0:T(8,128)S(1)} %get-tuple-element.82.s0_ref), channel_id=1, source_target_pairs={{0,1},{1,0},{2,3},{3,2},{4,5},{5,4},{6,7},{7,6},{8,9},{9,8},{10,11... | collective-permute-start | bytes 24584 | tf_op jit(solution)/shard_map/ppermute | solution.py:627
  72.2 25.5 %collective-permute-start.23 = (f32[264,512]{1,0:T(8,128)S(1)}, f32[264,512]{1,0:T(8,128)S(1)}, u32[]{:S(2)}, u32[]{:S(2)}) collective-permute-start(f32[264,512]{1,0:T(8,128)S(1)} %get-tuple-element.98.dout_ref.d0_ref.t0_ref), channel_id=1, source_target_pairs={{0,4},{4,0},{8,12},{12,8},{16,20},{20,16},{24,28},{28,24},{32,36},... | collective-permute-start | bytes 1622024 | tf_op jit(solution)/shard_map/ppermute | solution.py:585
  74.0 12.0 %collective-permute-start.21 = (f32[64,1152]{1,0:T(8,128)S(1)}, f32[64,1152]{1,0:T(8,128)S(1)}, u32[]{:S(2)}, u32[]{:S(2)}) collective-permute-start(f32[64,1152]{1,0:T(8,128)S(1)} %get-tuple-element.95.first_ref), channel_id=1, source_target_pairs={{0,8},{4,12},{8,0},{12,4},{16,24},{20,28},{24,16},{28,20},{32,40},... | collective-permute-start | bytes 884744 | tf_op jit(solution)/shard_map/ppermute | solution.py:585
  76.0 3.8 %collective-permute-start.20 = (f32[4,1152]{1,0:T(4,128)S(1)}, f32[4,1152]{1,0:T(4,128)S(1)}, u32[]{:S(2)}, u32[]{:S(2)}) collective-permute-start(f32[4,1152]{1,0:T(4,128)S(1)} %get-tuple-element.90.third_ref), channel_id=1, source_target_pairs={{0,192},{4,196},{8,200},{12,204},{16,208},{20,212},{24,216},{28,22... | collective-permute-start | bytes 55304 | tf_op jit(solution)/shard_map/ppermute | solution.py:585
  76.3 4.1 %collective-permute-start.19 = (f32[4,1152]{1,0:T(4,128)S(1)}, f32[4,1152]{1,0:T(4,128)S(1)}, u32[]{:S(2)}, u32[]{:S(2)}) collective-permute-start(f32[4,1152]{1,0:T(4,128)S(1)} %get-tuple-element.90.third_ref), channel_id=1, source_target_pairs={{0,128},{4,132},{8,136},{12,140},{16,144},{20,148},{24,152},{28,15... | collective-permute-start | bytes 55304 | tf_op jit(solution)/shard_map/ppermute | solution.py:585
  77.2 3.7 %collective-permute-start.18 = (f32[4,1152]{1,0:T(4,128)S(1)}, f32[4,1152]{1,0:T(4,128)S(1)}, u32[]{:S(2)}, u32[]{:S(2)}) collective-permute-start(f32[4,1152]{1,0:T(4,128)S(1)} %get-tuple-element.90.third_ref), channel_id=1, source_target_pairs={{0,64},{4,68},{8,72},{12,76},{16,80},{20,84},{24,88},{28,92},{32,9... | collective-permute-start | bytes 55304 | tf_op jit(solution)/shard_map/ppermute | solution.py:585
  80.9 9.6 %collective-permute-start.22 = (f32[28,1152]{1,0:T(8,128)S(1)}, f32[28,1152]{1,0:T(8,128)S(1)}, u32[]{:S(2)}, u32[]{:S(2)}) collective-permute-start(f32[28,1152]{1,0:T(8,128)S(1)} %shard_map.101.own_ref), channel_id=1, source_target_pairs={{0,16},{4,20},{8,24},{12,28},{16,0},{20,4},{24,8},{28,12},{32,48},... | collective-permute-start | bytes 387080 | tf_op jit(solution)/shard_map/ppermute | solution.py:585
  90.5 13.1 %collective-permute-start.24 = (f32[264,512]{1,0:T(8,128)S(1)}, f32[264,512]{1,0:T(8,128)S(1)}, u32[]{:S(2)}, u32[]{:S(2)}) collective-permute-start(f32[264,512]{1,0:T(8,128)S(1)} %get-tuple-element.98.dout_ref.d0_ref.t0_ref), channel_id=1, source_target_pairs={{4,8},{8,4},{12,16},{16,12},{20,24},{24,20},{28,32},{32,28},{36,40... | collective-permute-start | bytes 1622024 | tf_op jit(solution)/shard_map/ppermute | solution.py:589
  92.5 13.8 %collective-permute-start.25 = (f32[56,1152]{1,0:T(8,128)S(1)}, f32[56,1152]{1,0:T(8,128)S(1)}, u32[]{:S(2)}, u32[]{:S(2)}) collective-permute-start(f32[56,1152]{1,0:T(8,128)S(1)} %shard_map.103.double_ref), channel_id=1, source_target_pairs={{0,48},{4,52},{8,56},{12,60},{16,32},{20,36},{24,40},{28,44},{32,1... | collective-permute-start | bytes 774152 | tf_op jit(solution)/shard_map/ppermute | solution.py:585
  106.3 13.1 %collective-permute-start.27 = (f32[160,1152]{1,0:T(8,128)S(1)}, f32[160,1152]{1,0:T(8,128)S(1)}, u32[]{:S(2)}, u32[]{:S(2)}) collective-permute-start(f32[160,1152]{1,0:T(8,128)S(1)} %get-tuple-element.105), channel_id=1, source_target_pairs={{0,4},{4,0},{8,12},{12,8},{16,20},{20,16},{24,28},{28,24},{32,36},... | collective-permute-start | bytes 2211848 | tf_op jit(solution)/shard_map/ppermute | solution.py:585
  106.4 19.7 %collective-permute-start.26 = (f32[96,1152]{1,0:T(8,128)S(1)}, f32[96,1152]{1,0:T(8,128)S(1)}, u32[]{:S(2)}, u32[]{:S(2)}) collective-permute-start(f32[96,1152]{1,0:T(8,128)S(1)} %get-tuple-element.104.a1), channel_id=1, source_target_pairs={{0,8},{4,12},{8,0},{12,4},{16,24},{20,28},{24,16},{28,20},{32,40},... | collective-permute-start | bytes 1327112 | tf_op jit(solution)/shard_map/ppermute | solution.py:585
  126.1 2.1 %collective-permute-start.28 = (f32[96,1152]{1,0:T(8,128)S(1)}, f32[96,1152]{1,0:T(8,128)S(1)}, u32[]{:S(2)}, u32[]{:S(2)}) collective-permute-start(f32[96,1152]{1,0:T(8,128)S(1)} %collective-permute-done.26.a0), channel_id=1, source_target_pairs={{0,4},{4,0},{8,12},{12,8},{16,20},{20,16},{24,28},{28,24},{32,36},... | collective-permute-start | bytes 1327112 | tf_op jit(solution)/shard_map/ppermute | solution.py:585

commit v6 on v5

--- a/solution.py
+++ b/solution.py
@@ -39,15 +39,15 @@
 SLOTS = (
     (1, (2, 3)),
     (2, QUAD),
+    (3, THIRD_BLOCKS),
     (2, flipped(QUAD, 1)),
-    (3, THIRD_BLOCKS),
     (3, flipped(THIRD_BLOCKS, 1)),
     (2, flipped(QUAD, 2)),
     (2, flipped(QUAD, 3)),
     (3, flipped(THIRD_BLOCKS, 2)),
     (3, flipped(THIRD_BLOCKS, 3)),
 )
-EARLY = 320
+EARLY = 224
 
 
 def slot_table():
@@ -125,18 +125,18 @@
 
 
 def early(refs, lanes):
-    l1a, l2a, core1 = refs
-    pieces = [l1a[:, lanes], core1[0:64, lanes], l2a[0:48, lanes], core1[64:112, lanes]]
-    return pieces + [l2a[48:96, lanes], core1[112:160, lanes]]
+    l1a, l1b, l2a = refs
+    return [l1a[:, lanes], l1b[:, lanes], l2a[:, lanes]]
 
 
 def late(refs, lanes):
-    l2b, core2 = refs
-    return [l2b[0:48, lanes], core2[0:48, lanes], l2b[48:96, lanes], core2[48:96, lanes]]
+    core1, l2b, core2 = refs
+    pieces = [core1[:, lanes], l2b[0:48, lanes], core2[0:48, lanes]]
+    return pieces + [l2b[48:96, lanes], core2[48:96, lanes]]
 
 
 def gathered(refs, lanes):
-    return jnp.concatenate(early(refs[0:3], lanes) + late(refs[3:5], lanes), axis=0)
+    return jnp.concatenate(early(refs[0:3], lanes) + late(refs[3:6], lanes), axis=0)
 
 
 def pool_kernel(
@@ -192,15 +192,13 @@
     out_ref[28:56, :] = other_ref[...]
 
 
-def merge_kernel(first_ref, double_ref, other_ref, out_ref, bundle_ref):
-    bundle_ref[0:64, :] = first_ref[...]
+def merge_kernel(double_ref, other_ref, out_ref):
     parts = (double_ref[28:56, :], other_ref[0:28, :], other_ref[28:56, :])
     pieces = [(16 * i, part[0:16]) for i, part in enumerate(parts)]
     pieces += [(48 + 12 * i, part[16:28]) for i, part in enumerate((double_ref[0:28, :],) + parts)]
     for start, piece in pieces:
         stop = start + piece.shape[0]
         out_ref[start:stop, :] = piece
-        bundle_ref[64 + start : 64 + stop, :] = piece
 
 
 def near_state(scores, values, w_ref, peak_ref, mass_ref, sum_ref):
@@ -230,12 +228,12 @@
 
 
 def far_forward_kernel(
-    bias_ref, own_ref, a0, a1, a2, a3, a4,
+    bias_ref, own_ref, a0, a1, a2, a3, a4, a5,
     peak0_ref, mass0_ref, sum0_ref, peak1_ref, mass1_ref, sum1_ref, up_ref, gain_ref,
     att_ref, lse_ref, stat_ref,
     e0_ref, e1_ref, e2_ref, square_ref, cross_ref,
 ):
-    far = (a0, a1, a2, a3, a4)
+    far = (a0, a1, a2, a3, a4, a5)
     bias = bias_ref[...]
     for h in range(HEADS):
         k = cols(h)
@@ -338,9 +336,9 @@
 
 
 def far_query_kernel(
-    bias_ref, own_ref, a0, a1, a2, a3, a4, first_ref, second_ref, third_ref, near_ref, dq_ref, e0_ref
+    bias_ref, own_ref, a0, a1, a2, a3, a4, a5, first_ref, second_ref, third_ref, near_ref, dq_ref, e0_ref
 ):
-    far = (a0, a1, a2, a3, a4)
+    far = (a0, a1, a2, a3, a4, a5)
     bias = bias_ref[...]
 
     def grads(lanes):
@@ -386,7 +384,7 @@
         return jnp.concatenate(pieces(lanes), axis=0)
 
     stats = take(slice(KV, GRAD))
-    fill = jnp.zeros((64, DHEAD), jnp.float32)
+    fill = jnp.zeros((-stats.shape[0] % DHEAD, DHEAD), jnp.float32)
     stats = jnp.transpose(jnp.concatenate([stats, fill], axis=0))[0:8, 0 : stats.shape[0]]
     queries = take(cols(h, WIDTH))
     grads = take(cols(h))
@@ -404,13 +402,13 @@
 
 
 def late_key_kernel(
-    bias_ref, own_ref, a0, a1, far_dk_ref, far_dv_ref, dk_in_ref, dv_in_ref, dk_ref, dv_ref, e0_ref, e1_ref
+    bias_ref, own_ref, a0, a1, a2, far_dk_ref, far_dv_ref, dk_in_ref, dv_in_ref, dk_ref, dv_ref, e0_ref, e1_ref
 ):
     bias = bias_ref[:, EARLY:FAR]
     scales = [1.0 / 4**n for n in (1, 2, 3)]
     for h in range(HEADS):
         k = cols(h)
-        d_keys, d_values = far_key_parts(own_ref, bias, lambda lanes: late((a0, a1), lanes), h)
+        d_keys, d_values = far_key_parts(own_ref, bias, lambda lanes: late((a0, a1, a2), lanes), h)
         d_keys = far_dk_ref[:, k] + d_keys
         d_values = far_dv_ref[:, k] + d_values
         dk_ref[:, k] = dk_in_ref[:, k] + expand_levels(e0_ref.at[h % 2], d_keys, scales)
@@ -597,9 +595,8 @@
     def doubled(pack, other):
         return whole_call(double_kernel, [f32(56, pack.shape[1])], [], 1e4, 1e5, pack, other)[0]
 
-    def merged(first, double, other):
-        width = first.shape[1]
-        return whole_call(merge_kernel, [f32(96, width), f32(160, width)], [], 1e4, 1e5, first, double, other)
+    def merged(double, other):
+        return whole_call(merge_kernel, [f32(96, double.shape[1])], [], 1e4, 1e5, double, other)[0]
 
     gain = norm_gain.reshape(1, WIDTH)
     out_k, out_v = exchange_outer(key), exchange_outer(value)
@@ -614,13 +611,14 @@
     other = exchange(double, 12)
     w0, *inner = near_inner(query, (key, after(in_k, double)), (value, in_v))
     w1, *outer = near_outer(edge, query, after(out_k, double), out_v)
-    l2a, bundle = merged(l1a, after(double, w0, w1), other)
+    l1b = exchange(after(l1a, double), 1)
+    l2a = merged(after(double, w0, w1, l1b), other)
     l2b = exchange(l2a, 2)
-    core1 = exchange(bundle, 1)
+    core1 = exchange(l2a, 1)
     core2 = exchange(after(l2b, core1), 1)
     query_in = exchange(after(query, l2a), 1)
     query_out = exchange_outer(after(query, l2a))
-    far = (l1a, l2a, core1, l2b, core2)
+    far = (l1a, l1b, l2a, core1, l2b, core2)
     attention, lse, stats = far_forward(bias, own, far, inner, outer, upstream, gain)
 
     others = [
@@ -642,13 +640,14 @@
     d_far = exchange_outer(after(d_out, double))
     near_dk, near_dv = inner_key(key, value, query, query_in, d_out, after(d_in, double))
     query_grad = far_query(bias, own, far, after(g1, double), g2, g3, near_dq)
-    l2a, bundle = merged(l1a, after(double, near_dk, query_grad, d_far), other)
+    l1b = exchange(after(l1a, double), 1)
+    l2a = merged(after(double, near_dk, query_grad, d_far, l1b), other)
     l2b = exchange(l2a, 2)
-    core1 = exchange(bundle, 1)
+    core1 = exchange(l2a, 1)
     near_dk, near_dv = outer_key(key, value, query_out, after(d_far, l2a), near_dk, near_dv)
-    far_dk, far_dv = early_key(bias, own, (l1a, after(l2a, near_dk), core1))
+    far_dk, far_dv = early_key(bias, own, (l1a, l1b, after(l2a, near_dk)))
     core2 = exchange(after(l2b, far_dk), 1)
-    key_grad, value_grad = late_key(bias, own, (l2b, core2), far_dk, far_dv, near_dk, near_dv)
+    key_grad, value_grad = late_key(bias, own, (core1, l2b, core2), far_dk, far_dv, near_dk, near_dv)
     return attended, query_grad, key_grad, value_grad
 
 

time: 132 us -> 131 us (level)
  waiting for transfers between devices: 42.5 us -> 40 us
    ppermute x22 -> x24, waiting for transfers between devices: 37.3 us -> 35.1 us  [exchange(): return lax.ppermute(array, 'seq', [(i, i ^ mask) for i in range(count)])]
    ppermute x22 -> x24, starting transfers between devices: 34.2 us -> 35 us  [exchange(): return lax.ppermute(array, 'seq', [(i, i ^ mask) for i in range(count)])]
  transfers between devices with their start and end apart: 29 -> 31, of which waited for: 16 -> 16; matrix products, arithmetic and copies ran while one was open for 0% -> 0% of each run, Pallas kernels for 26% -> 26%
where the time goes in v6:
time: 131 us; the launch traced here: 130 us
  starting transfers between devices  47.9 us (37%)
  waiting for transfers between devices  40 us (31%)
  Pallas kernels  39.3 us (30%)
  local copies, waits for them, and re-layouts  1.58 us (1%)
    ppermute x24, waiting for transfers between devices, exchange(): return lax.ppermute(array, 'seq', [(i, i ^ mask) for i in range(count)])  35.1 us
    ppermute x24, starting transfers between devices, exchange(): return lax.ppermute(array, 'seq', [(i, i ^ mask) for i in range(count)])  35 us
    pallas_call x5, Pallas kernels, head_call(): pl.pallas_call(kernel, grid=(HEADS,), out_shape=outs, in_specs=in_specs,...  22.1 us
    pallas_call x11, Pallas kernels, whole_call(): pl.pallas_call(kernel, out_shape=outs, in_specs=[spec] * len(operands), o...  14 us
    ppermute x4, starting transfers between devices, exchange_outer(): return lax.ppermute(array, 'seq', pairs)  9.38 us
    ppermute x3, starting transfers between devices, body(): lax.ppermute(stats, 'head', [(i, i ^ mask) for i in range(head_count)])  3.5 us
    pallas_call x1, Pallas kernels, pool(): pl.pallas_call(pool_kernel, out_shape=[f32(OWN, 3 * WIDTH), f32(64, KV),...  3.27 us
    ppermute x3, waiting for transfers between devices, body(): lax.ppermute(stats, 'head', [(i, i ^ mask) for i in range(head_count)])  3.23 us
  transfers between devices with their start and end apart: 31, of which 16 were waited for; matrix products, arithmetic and copies ran while one was open for 0% of the time, Pallas kernels for 26%

profile of v6, /device:TPU:1, one launch (start us, length us, event | category | flops | bytes accessed | tf_op | source)
XLA Modules:
  0.0 129.7 jit_solution(9377539428953401495)
XLA Ops:
  0.6 3.3 %collective-permute-start.2 = (f32[256,512]{1,0:T(8,128)}, f32[256,512]{1,0:T(8,128)S(1)}, u32[]{:S(2)}, u32[]{:S(2)}) collective-permute-start(f32[256,512]{1,0:T(8,128)} %k_ref.5), channel_id=1, source_target_pairs={{0,4},{4,0},{8,12},{12,8},{16,20},{20,16},{24,28},{28,24},{32,36},... | collective-permute-start | bytes 1572872 | tf_op jit(solution)/shard_map/ppermute | solution.py:583
  4.0 0.1 collective-permute-start.3
  4.1 2.1 %collective-permute-start.1 = (f32[256,512]{1,0:T(8,128)}, f32[256,512]{1,0:T(8,128)S(1)}, u32[]{:S(2)}, u32[]{:S(2)}) collective-permute-start(f32[256,512]{1,0:T(8,128)} %k_ref.5), channel_id=1, source_target_pairs={{4,8},{8,4},{12,16},{16,12},{20,24},{24,20},{28,32},{32,28},{36,40... | collective-permute-start | bytes 1572872 | tf_op jit(solution)/shard_map/ppermute | solution.py:587
  6.2 3.5 %collective-permute-start.9 = (f32[256,512]{1,0:T(8,128)}, f32[256,512]{1,0:T(8,128)S(1)}, u32[]{:S(2)}, u32[]{:S(2)}) collective-permute-start(f32[256,512]{1,0:T(8,128)} %v_ref.5), channel_id=1, source_target_pairs={{4,8},{8,4},{12,16},{16,12},{20,24},{24,20},{28,32},{32,28},{36,40... | collective-permute-start | bytes 1572872 | tf_op jit(solution)/shard_map/ppermute | solution.py:587
  9.6 3.3 %shard_map.93 = (f32[96,1536]{1,0:T(8,128)}, f32[64,1024]{1,0:T(8,128)}, f32[16,1024]{1,0:T(8,128)}, f32[4,1024]{1,0:T(4,128)}, f32[96,512]{1,0:T(8,128)}, /*index=5*/f32[8,256]{1,0:T(8,128)}) custom-call(s32[8,512]{1,0:T(8,128)} %constant.2.clone.table_ref, f32[256,512]{1,0:T(8,128)} %k_ref.5, f32[256,512]{1,0:T(8,128)} %v_ref.5, f32[256,512]{1,0:T(8,128)} %q0_ref.1), custom_call_target="tpu_custom_call" | custom-call | flops 1000000 | bytes 2000000 | tf_op jit(solution)/shard_map/pallas_call | solution.py:510
  12.9 0.0 copy-start.3
  12.9 0.0 copy-start.4
  12.9 0.2 collective-permute-start
  13.1 1.6 %collective-permute-done.1.k_ref.k2_ref = f32[256,512]{1,0:T(8,128)S(1)} collective-permute-done((f32[256,512]{1,0:T(8,128)}, f32[256,512]{1,0:T(8,128)S(1)}, u32[]{:S(2)}, u32[]{:S(2)}) %collective-permute-start.1) | collective-permute-done | bytes 524320 | tf_op jit(solution)/shard_map/ppermute | solution.py:587
  14.8 0.1 collective-permute-start.4
  14.8 1.9 %collective-permute-start.6 = (f32[4,1024]{1,0:T(4,128)}, f32[4,1024]{1,0:T(4,128)S(1)}, u32[]{:S(2)}, u32[]{:S(2)}) collective-permute-start(f32[4,1024]{1,0:T(4,128)} %get-tuple-element.63), channel_id=1, source_target_pairs={{0,192},{4,196},{8,200},{12,204},{16,208},{20,212},{24,216},{28,22... | collective-permute-start | bytes 49160 | tf_op jit(solution)/shard_map/ppermute | solution.py:583
  16.7 1.3 %collective-permute-start.5 = (f32[4,1024]{1,0:T(4,128)}, f32[4,1024]{1,0:T(4,128)S(1)}, u32[]{:S(2)}, u32[]{:S(2)}) collective-permute-start(f32[4,1024]{1,0:T(4,128)} %get-tuple-element.63), channel_id=1, source_target_pairs={{0,128},{4,132},{8,136},{12,140},{16,144},{20,148},{24,152},{28,15... | collective-permute-start | bytes 49160 | tf_op jit(solution)/shard_map/ppermute | solution.py:583
  18.0 0.0 collective-permute-done.4.a_ref
  18.0 0.8 collective-permute-done.6.c_ref
  18.8 6.5 %collective-permute-done.5.b_ref = f32[4,1024]{1,0:T(4,128)S(1)} collective-permute-done((f32[4,1024]{1,0:T(4,128)}, f32[4,1024]{1,0:T(4,128)S(1)}, u32[]{:S(2)}, u32[]{:S(2)}) %collective-permute-start.5) | collective-permute-done | bytes 16416 | tf_op jit(solution)/shard_map/ppermute | solution.py:583
  25.4 0.8 copy-done.6
  26.2 0.1 collective-permute-start.7
  26.3 7.2 %collective-permute-done.7.other_ref = f32[28,1024]{1,0:T(8,128)S(1)} collective-permute-done((f32[28,1024]{1,0:T(8,128)S(1)}, f32[28,1024]{1,0:T(8,128)S(1)}, u32[]{:S(2)}, u32[]{:S(2)}) %collective-permute-start.7) | collective-permute-done | bytes 114720 | tf_op jit(solution)/shard_map/ppermute | solution.py:583
  33.5 1.5 %collective-permute-start.8 = (f32[64,1024]{1,0:T(8,128)S(1)}, f32[64,1024]{1,0:T(8,128)S(1)}, u32[]{:S(2)}, u32[]{:S(2)}) collective-permute-start(f32[64,1024]{1,0:T(8,128)S(1)} %collective-permute-done.a0), channel_id=1, source_target_pairs={{0,4},{4,0},{8,12},{12,8},{16,20},{20,16},{24,28},{28,24},{32,36},... | collective-permute-start | bytes 786440 | tf_op jit(solution)/shard_map/ppermute | solution.py:583
  35.1 1.1 collective-permute-start.10
  36.1 0.7 copy-done.8
  36.8 3.6 %shard_map.97 = (f32[4,256,256]{2,1,0:T(8,128)S(1)}, f32[256,512]{1,0:T(8,128)S(1)}, f32[256,512]{1,0:T(8,128)S(1)}, f32[256,512]{1,0:T(8,128)S(1)}) custom-call(f32[8,256]{1,0:T(8,128)S(1)} %copy-done.8, f32[256,512]{1,0:T(8,128)S(1)} %copy-done.5, f32[256,512]{1,0:T(8,128)S(1)} %collective-permute-done.1.k_ref.k2_ref, ...), custom_call_target="tpu_custom_call" | custom-call | flops 805306368 | bytes 4000000 | tf_op jit(solution)/shard_map/pallas_call | solution.py:455
  40.5 0.0 copy-start.1
  40.5 0.0 copy-start.2
  40.5 0.0 copy-start.7
  40.5 4.1 %shard_map.96 = (f32[4,256,512]{2,1,0:T(8,128)S(1)}, f32[256,512]{1,0:T(8,128)S(1)}, f32[256,512]{1,0:T(8,128)S(1)}, f32[256,512]{1,0:T(8,128)S(1)}) custom-call(f32[256,512]{1,0:T(8,128)S(1)} %copy-done.5, f32[256,512]{1,0:T(8,128)S(1)} %copy-done.3, f32[256,512]{1,0:T(8,128)S(1)} %collective-permute-done.2.ki_ref.k1_ref, f32[256,512]{1,0:T(8,128)S(1)} %copy-done.4, ...), custom_call_target="tpu_custom_call" | custom-call | flops 1610612736 | bytes 4000000 | tf_op jit(solution)/shard_map/pallas_call | solution.py:455
  44.6 1.2 collective-permute-done.10.other_ref
  45.9 4.7 %collective-permute-start.12 = (f32[96,1024]{1,0:T(8,128)S(1)}, f32[96,1024]{1,0:T(8,128)S(1)}, u32[]{:S(2)}, u32[]{:S(2)}) collective-permute-start(f32[96,1024]{1,0:T(8,128)S(1)} %shard_map.98.a2), channel_id=1, source_target_pairs={{0,8},{4,12},{8,0},{12,4},{16,24},{20,28},{24,16},{28,20},{32,40},... | collective-permute-start | bytes 1179656 | tf_op jit(solution)/shard_map/ppermute | solution.py:583
  50.5 0.9 collective-permute-start.11
  51.5 1.9 %collective-permute-start.18 = (f32[256,512]{1,0:T(8,128)S(1)}, f32[256,512]{1,0:T(8,128)S(1)}, u32[]{:S(2)}, u32[]{:S(2)}) collective-permute-start(f32[256,512]{1,0:T(8,128)S(1)} %copy-done.5), channel_id=1, source_target_pairs={{4,8},{8,4},{12,16},{16,12},{20,24},{24,20},{28,32},{32,28},{36,40... | collective-permute-start | bytes 1572872 | tf_op jit(solution)/shard_map/ppermute | solution.py:587
  53.4 0.1 collective-permute-start.17
  53.5 5.9 %collective-permute-done.12.a4 = f32[96,1024]{1,0:T(8,128)S(1)} collective-permute-done((f32[96,1024]{1,0:T(8,128)S(1)}, f32[96,1024]{1,0:T(8,128)S(1)}, u32[]{:S(2)}, u32[]{:S(2)}) %collective-permute-start.12) | collective-permute-done | bytes 393248 | tf_op jit(solution)/shard_map/ppermute | solution.py:583
  59.4 1.6 %collective-permute-start.13 = (f32[96,1024]{1,0:T(8,128)S(1)}, f32[96,1024]{1,0:T(8,128)S(1)}, u32[]{:S(2)}, u32[]{:S(2)}) collective-permute-start(f32[96,1024]{1,0:T(8,128)S(1)} %collective-permute-done.12.a4), channel_id=1, source_target_pairs={{0,4},{4,0},{8,12},{12,8},{16,20},{20,16},{24,28},{28,24},{32,36},... | collective-permute-start | bytes 1179656 | tf_op jit(solution)/shard_map/ppermute | solution.py:583
  61.0 1.3 %collective-permute-done.13.a5 = f32[96,1024]{1,0:T(8,128)S(1)} collective-permute-done((f32[96,1024]{1,0:T(8,128)S(1)}, f32[96,1024]{1,0:T(8,128)S(1)}, u32[]{:S(2)}, u32[]{:S(2)}) %collective-permute-start.13) | collective-permute-done | bytes 393248 | tf_op jit(solution)/shard_map/ppermute | solution.py:583
  62.4 2.8 %shard_map.99 = (f32[256,512]{1,0:T(8,128)S(1)}, f32[256,512]{1,0:T(8,128)S(1)}, f32[8,256]{1,0:T(8,128)S(1)}) custom-call(f32[96,512]{1,0:T(8,128)S(1)} %copy-done.1, f32[96,1536]{1,0:T(8,128)S(1)} %copy-done, f32[64,1024]{1,0:T(8,128)S(1)} %collective-permute-done.a0, f32[64,1024]{1,0:T(8,128)S(1)} %collective-permute-done.8.a1, ...), custom_call_target="tpu_custom_call" | custom-call | flops 402653184 | bytes 8000000 | tf_op jit(solution)/shard_map/pallas_call | solution.py:432
  65.2 2.7 %collective-permute-start.16 = (f32[8,256]{1,0:T(8,128)S(1)}, f32[8,256]{1,0:T(8,128)S(1)}, u32[]{:S(2)}, u32[]{:S(2)}) collective-permute-start(f32[8,256]{1,0:T(8,128)S(1)} %get-tuple-element.79.s0_ref), channel_id=1, source_target_pairs={{0,3},{1,2},{2,1},{3,0},{4,7},{5,6},{6,5},{7,4},{8,11},{9,10},{10,... | collective-permute-start | bytes 24584 | tf_op jit(solution)/shard_map/ppermute | solution.py:625
  67.9 0.5 collective-permute-start.15
  68.4 0.3 collective-permute-start.14
  68.7 0.5 collective-permute-done.16.s3_ref
  69.1 2.8 %collective-permute-done.15.s2_ref = f32[8,256]{1,0:T(8,128)S(1)} collective-permute-done((f32[8,256]{1,0:T(8,128)S(1)}, f32[8,256]{1,0:T(8,128)S(1)}, u32[]{:S(2)}, u32[]{:S(2)}) %collective-permute-start.15) | collective-permute-done | bytes 8224 | tf_op jit(solution)/shard_map/ppermute | solution.py:625
  71.9 1.4 %shard_map.100 = (f32[256,512]{1,0:T(8,128)}, f32[264,512]{1,0:T(8,128)S(1)}, f32[256,512]{1,0:T(8,128)S(1)}, f32[64,1152]{1,0:T(8,128)S(1)}, f32[16,1152]{1,0:T(8,128)S(1)}, /*index=5*/f32[4,1152]{1,0:T(4,128)S(1)}) custom-call(f32[8,256]{1,0:T(8,128)S(1)} %get-tuple-element.79.s0_ref, f32[8,256]{1,0:T(8,128)S(1)} %collective-permute-done.14.s1_ref, ...), custom_call_target="tpu_custom_call" | custom-call | flops 1000000 | bytes 4000000 | tf_op jit(solution)/shard_map/pallas_call | solution.py:432
  73.3 1.8 %collective-permute-start.24 = (f32[264,512]{1,0:T(8,128)S(1)}, f32[264,512]{1,0:T(8,128)S(1)}, u32[]{:S(2)}, u32[]{:S(2)}) collective-permute-start(f32[264,512]{1,0:T(8,128)S(1)} %get-tuple-element.95.dout_ref.d0_ref.t0_ref), channel_id=1, source_target_pairs={{0,4},{4,0},{8,12},{12,8},{16,20},{20,16},{24,28},{28,24},{32,36},... | collective-permute-start | bytes 1622024 | tf_op jit(solution)/shard_map/ppermute | solution.py:583
  75.1 2.2 %collective-permute-start.22 = (f32[64,1152]{1,0:T(8,128)S(1)}, f32[64,1152]{1,0:T(8,128)S(1)}, u32[]{:S(2)}, u32[]{:S(2)}) collective-permute-start(f32[64,1152]{1,0:T(8,128)S(1)} %get-tuple-element.92.first_ref), channel_id=1, source_target_pairs={{0,8},{4,12},{8,0},{12,4},{16,24},{20,28},{24,16},{28,20},{32,40},... | collective-permute-start | bytes 884744 | tf_op jit(solution)/shard_map/ppermute | solution.py:583
  77.3 0.4 collective-permute-start.21
  77.7 1.7 %collective-permute-start.20 = (f32[4,1152]{1,0:T(4,128)S(1)}, f32[4,1152]{1,0:T(4,128)S(1)}, u32[]{:S(2)}, u32[]{:S(2)}) collective-permute-start(f32[4,1152]{1,0:T(4,128)S(1)} %get-tuple-element.87.third_ref), channel_id=1, source_target_pairs={{0,128},{4,132},{8,136},{12,140},{16,144},{20,148},{24,152},{28,15... | collective-permute-start | bytes 55304 | tf_op jit(solution)/shard_map/ppermute | solution.py:583
  79.4 1.1 collective-permute-start.19
  80.5 0.6 collective-permute-done.21.c_ref
  81.1 0.7 collective-permute-done.20.b_ref
  81.8 0.5 collective-permute-done.19.a_ref
  82.3 0.1 collective-permute-start.23
  82.4 5.1 %shard_map.102.near_ref = f32[256,512]{1,0:T(8,128)S(1)} custom-call(f32[4,256,512]{2,1,0:T(8,128)S(1)} %get-tuple-element.67.w0_ref, f32[4,256,256]{2,1,0:T(8,128)S(1)} %get-tuple-element.70.w1_ref, f32[256,512]{1,0:T(8,128)S(1)} %get-tuple-element.73.peak0_ref, f32[256,512]{1,0:T(8,128)S(1)} %get-tuple-element.76.peak1_ref, ...), custom_call_target="tpu_custom_call" | custom-call | flops 2415919104 | bytes 4000000 | tf_op jit(solution)/shard_map/pallas_call | solution.py:455
  87.5 4.2 %collective-permute-done.23.other_ref = f32[28,1152]{1,0:T(8,128)S(1)} collective-permute-done((f32[28,1152]{1,0:T(8,128)S(1)}, f32[28,1152]{1,0:T(8,128)S(1)}, u32[]{:S(2)}, u32[]{:S(2)}) %collective-permute-start.23) | collective-permute-done | bytes 129056 | tf_op jit(solution)/shard_map/ppermute | solution.py:583
  91.8 1.9 %collective-permute-start.25 = (f32[264,512]{1,0:T(8,128)S(1)}, f32[264,512]{1,0:T(8,128)S(1)}, u32[]{:S(2)}, u32[]{:S(2)}) collective-permute-start(f32[264,512]{1,0:T(8,128)S(1)} %get-tuple-element.95.dout_ref.d0_ref.t0_ref), channel_id=1, source_target_pairs={{4,8},{8,4},{12,16},{16,12},{20,24},{24,20},{28,32},{32,28},{36,40... | collective-permute-start | bytes 1622024 | tf_op jit(solution)/shard_map/ppermute | solution.py:587
  93.7 1.9 %collective-permute-start.27 = (f32[56,1152]{1,0:T(8,128)S(1)}, f32[56,1152]{1,0:T(8,128)S(1)}, u32[]{:S(2)}, u32[]{:S(2)}) collective-permute-start(f32[56,1152]{1,0:T(8,128)S(1)} %shard_map.103.double_ref), channel_id=1, source_target_pairs={{0,48},{4,52},{8,56},{12,60},{16,32},{20,36},{24,40},{28,44},{32,1... | collective-permute-start | bytes 774152 | tf_op jit(solution)/shard_map/ppermute | solution.py:583
  95.6 3.7 %shard_map.104 = f32[256,512]{1,0:T(8,128)} custom-call(f32[96,512]{1,0:T(8,128)S(1)} %copy-done.1, f32[96,1536]{1,0:T(8,128)S(1)} %copy-done, f32[64,1024]{1,0:T(8,128)S(1)} %collective-permute-done.a0, f32[64,1024]{1,0:T(8,128)S(1)} %collective-permute-done.8.a1, f32[96,1024]{1,0:T(8,128)S(1)} %shard_map.98.a2, f32[96,1024]{1,0:T(8,128)S(1)} %collective-permute-done.11.a3, ...), custom_call_target="tpu_custom_call" | custom-call | flops 402653184 | bytes 6000000 | tf_op jit(solution)/shard_map/pallas_call | solution.py:432
  99.3 5.6 %shard_map.105 = (f32[256,512]{1,0:T(8,128)S(1)}, f32[256,512]{1,0:T(8,128)S(1)}) custom-call(f32[256,512]{1,0:T(8,128)S(1)} %copy-done.3, f32[256,512]{1,0:T(8,128)S(1)} %copy-done.4, f32[256,512]{1,0:T(8,128)S(1)} %copy-done.5, f32[256,512]{1,0:T(8,128)S(1)} %collective-permute-done.17.q1_ref, f32[264,512]{1,0:T(8,128)S(1)} %get-tuple-element.95.dout_ref.d0_ref.t0_ref, ...), custom_call_target="tpu_custom_call" | custom-call | flops 3221225472 | bytes 4000000 | tf_op jit(solution)/shard_map/pallas_call | solution.py:455
  104.9 2.9 %collective-permute-done.27.other_ref = f32[56,1152]{1,0:T(8,128)S(1)} collective-permute-done((f32[56,1152]{1,0:T(8,128)S(1)}, f32[56,1152]{1,0:T(8,128)S(1)}, u32[]{:S(2)}, u32[]{:S(2)}) %collective-permute-start.27) | collective-permute-done | bytes 258080 | tf_op jit(solution)/shard_map/ppermute | solution.py:583
  107.9 8.9 %collective-permute-start.29 = (f32[96,1152]{1,0:T(8,128)S(1)}, f32[96,1152]{1,0:T(8,128)S(1)}, u32[]{:S(2)}, u32[]{:S(2)}) collective-permute-start(f32[96,1152]{1,0:T(8,128)S(1)} %shard_map.106.a2), channel_id=1, source_target_pairs={{0,8},{4,12},{8,0},{12,4},{16,24},{20,28},{24,16},{28,20},{32,40},... | collective-permute-start | bytes 1327112 | tf_op jit(solution)/shard_map/ppermute | solution.py:583
  116.8 0.0 collective-permute-start.28
  116.8 3.7 %shard_map.107 = (f32[256,512]{1,0:T(8,128)S(1)}, f32[256,512]{1,0:T(8,128)S(1)}) custom-call(f32[256,512]{1,0:T(8,128)S(1)} %copy-done.3, f32[256,512]{1,0:T(8,128)S(1)} %copy-done.4, f32[256,512]{1,0:T(8,128)S(1)} %collective-permute-done.18.q_ref, f32[264,512]{1,0:T(8,128)S(1)} %collective-permute-done.25.d_ref.t_ref, ...), custom_call_target="tpu_custom_call" | custom-call | flops 1610612736 | bytes 4000000 | tf_op jit(solution)/shard_map/pallas_call | solution.py:455
  120.5 2.2 %shard_map.108 = (f32[96,512]{1,0:T(8,128)S(1)}, f32[96,512]{1,0:T(8,128)S(1)}) custom-call(f32[96,512]{1,0:T(8,128)S(1)} %copy-done.1, f32[96,1536]{1,0:T(8,128)S(1)} %copy-done, f32[64,1152]{1,0:T(8,128)S(1)} %collective-permute-done.22.a0, f32[64,1152]{1,0:T(8,128)S(1)} %collective-permute-done.26.a1, f32[96,1152]{1,0:T(8,128)S(1)} %shard_map.106.a2), custom_call_target="tpu_custom_call" | custom-call | flops 402653184 | bytes 3000000 | tf_op jit(solution)/shard_map/pallas_call | solution.py:432
  122.7 1.4 %collective-permute-done.29.a1 = f32[96,1152]{1,0:T(8,128)S(1)} collective-permute-done((f32[96,1152]{1,0:T(8,128)S(1)}, f32[96,1152]{1,0:T(8,128)S(1)}, u32[]{:S(2)}, u32[]{:S(2)}) %collective-permute-start.29) | collective-permute-done | bytes 442400 | tf_op jit(solution)/shard_map/ppermute | solution.py:583
  124.1 1.8 %collective-permute-done.30.a2 = f32[96,1152]{1,0:T(8,128)S(1)} collective-permute-done((f32[96,1152]{1,0:T(8,128)S(1)}, f32[96,1152]{1,0:T(8,128)S(1)}, u32[]{:S(2)}, u32[]{:S(2)}) %collective-permute-start.30) | collective-permute-done | bytes 442400 | tf_op jit(solution)/shard_map/ppermute | solution.py:583
  125.9 3.7 %shard_map.109 = (f32[256,512]{1,0:T(8,128)}, f32[256,512]{1,0:T(8,128)}) custom-call(f32[96,512]{1,0:T(8,128)S(1)} %copy-done.1, f32[96,1536]{1,0:T(8,128)S(1)} %copy-done, f32[96,1152]{1,0:T(8,128)S(1)} %collective-permute-done.28.a0, f32[96,1152]{1,0:T(8,128)S(1)} %collective-permute-done.29.a1, f32[96,1152]{1,0:T(8,128)S(1)} %collective-permute-done.30.a2, ...), custom_call_target="tpu_custom_call" | custom-call | flops 402653184 | bytes 3000000 | tf_op jit(solution)/shard_map/pallas_call | solution.py:432
  (33 shorter events, 0.2 us)
Async XLA Ops:
  0.6 35.5 %copy-start.5 = (f32[256,512]{1,0:T(8,128)S(1)}, f32[256,512]{1,0:T(8,128)}, u32[]{:S(2)}) copy-start(f32[256,512]{1,0:T(8,128)} %q0_ref.1) | copy-start | bytes 1572868
  0.6 12.5 %collective-permute-start.2 = (f32[256,512]{1,0:T(8,128)}, f32[256,512]{1,0:T(8,128)S(1)}, u32[]{:S(2)}, u32[]{:S(2)}) collective-permute-start(f32[256,512]{1,0:T(8,128)} %k_ref.5), channel_id=1, source_target_pairs={{0,4},{4,0},{8,12},{12,8},{16,20},{20,16},{24,28},{28,24},{32,36},... | collective-permute-start | bytes 1572872 | tf_op jit(solution)/shard_map/ppermute | solution.py:583
  4.0 9.2 %collective-permute-start.3 = (f32[256,512]{1,0:T(8,128)}, f32[256,512]{1,0:T(8,128)S(1)}, u32[]{:S(2)}, u32[]{:S(2)}) collective-permute-start(f32[256,512]{1,0:T(8,128)} %v_ref.5), channel_id=1, source_target_pairs={{0,4},{4,0},{8,12},{12,8},{16,20},{20,16},{24,28},{28,24},{32,36},... | collective-permute-start | bytes 1572872 | tf_op jit(solution)/shard_map/ppermute | solution.py:583
  4.1 10.7 %collective-permute-start.1 = (f32[256,512]{1,0:T(8,128)}, f32[256,512]{1,0:T(8,128)S(1)}, u32[]{:S(2)}, u32[]{:S(2)}) collective-permute-start(f32[256,512]{1,0:T(8,128)} %k_ref.5), channel_id=1, source_target_pairs={{4,8},{8,4},{12,16},{16,12},{20,24},{24,20},{28,32},{32,28},{36,40... | collective-permute-start | bytes 1572872 | tf_op jit(solution)/shard_map/ppermute | solution.py:587
  6.2 30.0 %collective-permute-start.9 = (f32[256,512]{1,0:T(8,128)}, f32[256,512]{1,0:T(8,128)S(1)}, u32[]{:S(2)}, u32[]{:S(2)}) collective-permute-start(f32[256,512]{1,0:T(8,128)} %v_ref.5), channel_id=1, source_target_pairs={{4,8},{8,4},{12,16},{16,12},{20,24},{24,20},{28,32},{32,28},{36,40... | collective-permute-start | bytes 1572872 | tf_op jit(solution)/shard_map/ppermute | solution.py:587
  12.9 27.6 %copy-start.3 = (f32[256,512]{1,0:T(8,128)S(1)}, f32[256,512]{1,0:T(8,128)}, u32[]{:S(2)}) copy-start(f32[256,512]{1,0:T(8,128)} %k_ref.5) | copy-start | bytes 1572868
  12.9 27.6 %copy-start.4 = (f32[256,512]{1,0:T(8,128)S(1)}, f32[256,512]{1,0:T(8,128)}, u32[]{:S(2)}) copy-start(f32[256,512]{1,0:T(8,128)} %v_ref.5) | copy-start | bytes 1572868
  12.9 13.4 %collective-permute-start = (f32[64,1024]{1,0:T(8,128)}, f32[64,1024]{1,0:T(8,128)S(1)}, u32[]{:S(2)}, u32[]{:S(2)}) collective-permute-start(f32[64,1024]{1,0:T(8,128)} %get-tuple-element.58), channel_id=1, source_target_pairs={{0,8},{4,12},{8,0},{12,4},{16,24},{20,28},{24,16},{28,20},{32,40},... | collective-permute-start | bytes 786440 | tf_op jit(solution)/shard_map/ppermute | solution.py:583
  14.8 3.3 %collective-permute-start.4 = (f32[4,1024]{1,0:T(4,128)}, f32[4,1024]{1,0:T(4,128)S(1)}, u32[]{:S(2)}, u32[]{:S(2)}) collective-permute-start(f32[4,1024]{1,0:T(4,128)} %get-tuple-element.63), channel_id=1, source_target_pairs={{0,64},{4,68},{8,72},{12,76},{16,80},{20,84},{24,88},{28,92},{32,9... | collective-permute-start | bytes 49160 | tf_op jit(solution)/shard_map/ppermute | solution.py:583
  14.8 4.0 %collective-permute-start.6 = (f32[4,1024]{1,0:T(4,128)}, f32[4,1024]{1,0:T(4,128)S(1)}, u32[]{:S(2)}, u32[]{:S(2)}) collective-permute-start(f32[4,1024]{1,0:T(4,128)} %get-tuple-element.63), channel_id=1, source_target_pairs={{0,192},{4,196},{8,200},{12,204},{16,208},{20,212},{24,216},{28,22... | collective-permute-start | bytes 49160 | tf_op jit(solution)/shard_map/ppermute | solution.py:583
  16.7 8.6 %collective-permute-start.5 = (f32[4,1024]{1,0:T(4,128)}, f32[4,1024]{1,0:T(4,128)S(1)}, u32[]{:S(2)}, u32[]{:S(2)}) collective-permute-start(f32[4,1024]{1,0:T(4,128)} %get-tuple-element.63), channel_id=1, source_target_pairs={{0,128},{4,132},{8,136},{12,140},{16,144},{20,148},{24,152},{28,15... | collective-permute-start | bytes 49160 | tf_op jit(solution)/shard_map/ppermute | solution.py:583
  25.4 0.8 copy-start.6
  26.2 7.3 %collective-permute-start.7 = (f32[28,1024]{1,0:T(8,128)S(1)}, f32[28,1024]{1,0:T(8,128)S(1)}, u32[]{:S(2)}, u32[]{:S(2)}) collective-permute-start(f32[28,1024]{1,0:T(8,128)S(1)} %shard_map.94.own_ref), channel_id=1, source_target_pairs={{0,16},{4,20},{8,24},{12,28},{16,0},{20,4},{24,8},{28,12},{32,48},... | collective-permute-start | bytes 344072 | tf_op jit(solution)/shard_map/ppermute | solution.py:583
  33.5 11.1 %collective-permute-start.8 = (f32[64,1024]{1,0:T(8,128)S(1)}, f32[64,1024]{1,0:T(8,128)S(1)}, u32[]{:S(2)}, u32[]{:S(2)}) collective-permute-start(f32[64,1024]{1,0:T(8,128)S(1)} %collective-permute-done.a0), channel_id=1, source_target_pairs={{0,4},{4,0},{8,12},{12,8},{16,20},{20,16},{24,28},{28,24},{32,36},... | collective-permute-start | bytes 786440 | tf_op jit(solution)/shard_map/ppermute | solution.py:583
  35.1 10.8 %collective-permute-start.10 = (f32[56,1024]{1,0:T(8,128)S(1)}, f32[56,1024]{1,0:T(8,128)S(1)}, u32[]{:S(2)}, u32[]{:S(2)}) collective-permute-start(f32[56,1024]{1,0:T(8,128)S(1)} %shard_map.95.double_ref), channel_id=1, source_target_pairs={{0,48},{4,52},{8,56},{12,60},{16,32},{20,36},{24,40},{28,44},{32,1... | collective-permute-start | bytes 688136 | tf_op jit(solution)/shard_map/ppermute | solution.py:583
  36.1 0.7 copy-start.8
  40.5 21.9 %copy-start = (f32[96,1536]{1,0:T(8,128)S(1)}, f32[96,1536]{1,0:T(8,128)}, u32[]{:S(2)}) copy-start(f32[96,1536]{1,0:T(8,128)} %get-tuple-element.57.own_ref) | copy-start | bytes 1769476
  40.5 21.9 %copy-start.1 = (f32[96,512]{1,0:T(8,128)S(1)}, f32[96,512]{1,0:T(8,128)}, u32[]{:S(2)}) copy-start(f32[96,512]{1,0:T(8,128)} %get-tuple-element.56.bias_ref) | copy-start | bytes 589828
  40.5 21.9 %copy-start.2 = (f32[256,512]{1,0:T(8,128)S(1)}, f32[256,512]{1,0:T(8,128)}, u32[]{:S(2)}) copy-start(f32[256,512]{1,0:T(8,128)} %up_ref.3) | copy-start | bytes 1572868
  40.5 21.9 %copy-start.7 = (f32[512]{0:T(512)S(1)}, f32[512]{0:T(512)}, u32[]{:S(2)}) copy-start(f32[512]{0:T(512)} %param.9) | copy-start | bytes 6148
  45.9 13.5 %collective-permute-start.12 = (f32[96,1024]{1,0:T(8,128)S(1)}, f32[96,1024]{1,0:T(8,128)S(1)}, u32[]{:S(2)}, u32[]{:S(2)}) collective-permute-start(f32[96,1024]{1,0:T(8,128)S(1)} %shard_map.98.a2), channel_id=1, source_target_pairs={{0,8},{4,12},{8,0},{12,4},{16,24},{20,28},{24,16},{28,20},{32,40},... | collective-permute-start | bytes 1179656 | tf_op jit(solution)/shard_map/ppermute | solution.py:583
  50.5 8.8 %collective-permute-start.11 = (f32[96,1024]{1,0:T(8,128)S(1)}, f32[96,1024]{1,0:T(8,128)S(1)}, u32[]{:S(2)}, u32[]{:S(2)}) collective-permute-start(f32[96,1024]{1,0:T(8,128)S(1)} %shard_map.98.a2), channel_id=1, source_target_pairs={{0,4},{4,0},{8,12},{12,8},{16,20},{20,16},{24,28},{28,24},{32,36},... | collective-permute-start | bytes 1179656 | tf_op jit(solution)/shard_map/ppermute | solution.py:583
  51.5 17.2 %collective-permute-start.18 = (f32[256,512]{1,0:T(8,128)S(1)}, f32[256,512]{1,0:T(8,128)S(1)}, u32[]{:S(2)}, u32[]{:S(2)}) collective-permute-start(f32[256,512]{1,0:T(8,128)S(1)} %copy-done.5), channel_id=1, source_target_pairs={{4,8},{8,4},{12,16},{16,12},{20,24},{24,20},{28,32},{32,28},{36,40... | collective-permute-start | bytes 1572872 | tf_op jit(solution)/shard_map/ppermute | solution.py:587
  53.4 15.3 %collective-permute-start.17 = (f32[256,512]{1,0:T(8,128)S(1)}, f32[256,512]{1,0:T(8,128)S(1)}, u32[]{:S(2)}, u32[]{:S(2)}) collective-permute-start(f32[256,512]{1,0:T(8,128)S(1)} %copy-done.5), channel_id=1, source_target_pairs={{0,4},{4,0},{8,12},{12,8},{16,20},{20,16},{24,28},{28,24},{32,36},... | collective-permute-start | bytes 1572872 | tf_op jit(solution)/shard_map/ppermute | solution.py:583
  59.4 3.0 %collective-permute-start.13 = (f32[96,1024]{1,0:T(8,128)S(1)}, f32[96,1024]{1,0:T(8,128)S(1)}, u32[]{:S(2)}, u32[]{:S(2)}) collective-permute-start(f32[96,1024]{1,0:T(8,128)S(1)} %collective-permute-done.12.a4), channel_id=1, source_target_pairs={{0,4},{4,0},{8,12},{12,8},{16,20},{20,16},{24,28},{28,24},{32,36},... | collective-permute-start | bytes 1179656 | tf_op jit(solution)/shard_map/ppermute | solution.py:583
  65.2 4.0 %collective-permute-start.16 = (f32[8,256]{1,0:T(8,128)S(1)}, f32[8,256]{1,0:T(8,128)S(1)}, u32[]{:S(2)}, u32[]{:S(2)}) collective-permute-start(f32[8,256]{1,0:T(8,128)S(1)} %get-tuple-element.79.s0_ref), channel_id=1, source_target_pairs={{0,3},{1,2},{2,1},{3,0},{4,7},{5,6},{6,5},{7,4},{8,11},{9,10},{10,... | collective-permute-start | bytes 24584 | tf_op jit(solution)/shard_map/ppermute | solution.py:625
  67.9 4.0 %collective-permute-start.15 = (f32[8,256]{1,0:T(8,128)S(1)}, f32[8,256]{1,0:T(8,128)S(1)}, u32[]{:S(2)}, u32[]{:S(2)}) collective-permute-start(f32[8,256]{1,0:T(8,128)S(1)} %get-tuple-element.79.s0_ref), channel_id=1, source_target_pairs={{0,2},{1,3},{2,0},{3,1},{4,6},{5,7},{6,4},{7,5},{8,10},{9,11},{10,... | collective-permute-start | bytes 24584 | tf_op jit(solution)/shard_map/ppermute | solution.py:625
  68.4 3.5 %collective-permute-start.14 = (f32[8,256]{1,0:T(8,128)S(1)}, f32[8,256]{1,0:T(8,128)S(1)}, u32[]{:S(2)}, u32[]{:S(2)}) collective-permute-start(f32[8,256]{1,0:T(8,128)S(1)} %get-tuple-element.79.s0_ref), channel_id=1, source_target_pairs={{0,1},{1,0},{2,3},{3,2},{4,5},{5,4},{6,7},{7,6},{8,9},{9,8},{10,11... | collective-permute-start | bytes 24584 | tf_op jit(solution)/shard_map/ppermute | solution.py:625
  73.3 26.1 %collective-permute-start.24 = (f32[264,512]{1,0:T(8,128)S(1)}, f32[264,512]{1,0:T(8,128)S(1)}, u32[]{:S(2)}, u32[]{:S(2)}) collective-permute-start(f32[264,512]{1,0:T(8,128)S(1)} %get-tuple-element.95.dout_ref.d0_ref.t0_ref), channel_id=1, source_target_pairs={{0,4},{4,0},{8,12},{12,8},{16,20},{20,16},{24,28},{28,24},{32,36},... | collective-permute-start | bytes 1622024 | tf_op jit(solution)/shard_map/ppermute | solution.py:583
  75.1 12.4 %collective-permute-start.22 = (f32[64,1152]{1,0:T(8,128)S(1)}, f32[64,1152]{1,0:T(8,128)S(1)}, u32[]{:S(2)}, u32[]{:S(2)}) collective-permute-start(f32[64,1152]{1,0:T(8,128)S(1)} %get-tuple-element.92.first_ref), channel_id=1, source_target_pairs={{0,8},{4,12},{8,0},{12,4},{16,24},{20,28},{24,16},{28,20},{32,40},... | collective-permute-start | bytes 884744 | tf_op jit(solution)/shard_map/ppermute | solution.py:583
  77.3 3.8 %collective-permute-start.21 = (f32[4,1152]{1,0:T(4,128)S(1)}, f32[4,1152]{1,0:T(4,128)S(1)}, u32[]{:S(2)}, u32[]{:S(2)}) collective-permute-start(f32[4,1152]{1,0:T(4,128)S(1)} %get-tuple-element.87.third_ref), channel_id=1, source_target_pairs={{0,192},{4,196},{8,200},{12,204},{16,208},{20,212},{24,216},{28,22... | collective-permute-start | bytes 55304 | tf_op jit(solution)/shard_map/ppermute | solution.py:583
  77.7 4.1 %collective-permute-start.20 = (f32[4,1152]{1,0:T(4,128)S(1)}, f32[4,1152]{1,0:T(4,128)S(1)}, u32[]{:S(2)}, u32[]{:S(2)}) collective-permute-start(f32[4,1152]{1,0:T(4,128)S(1)} %get-tuple-element.87.third_ref), channel_id=1, source_target_pairs={{0,128},{4,132},{8,136},{12,140},{16,144},{20,148},{24,152},{28,15... | collective-permute-start | bytes 55304 | tf_op jit(solution)/shard_map/ppermute | solution.py:583
  79.4 2.9 %collective-permute-start.19 = (f32[4,1152]{1,0:T(4,128)S(1)}, f32[4,1152]{1,0:T(4,128)S(1)}, u32[]{:S(2)}, u32[]{:S(2)}) collective-permute-start(f32[4,1152]{1,0:T(4,128)S(1)} %get-tuple-element.87.third_ref), channel_id=1, source_target_pairs={{0,64},{4,68},{8,72},{12,76},{16,80},{20,84},{24,88},{28,92},{32,9... | collective-permute-start | bytes 55304 | tf_op jit(solution)/shard_map/ppermute | solution.py:583
  82.3 9.4 %collective-permute-start.23 = (f32[28,1152]{1,0:T(8,128)S(1)}, f32[28,1152]{1,0:T(8,128)S(1)}, u32[]{:S(2)}, u32[]{:S(2)}) collective-permute-start(f32[28,1152]{1,0:T(8,128)S(1)} %shard_map.101.own_ref), channel_id=1, source_target_pairs={{0,16},{4,20},{8,24},{12,28},{16,0},{20,4},{24,8},{28,12},{32,48},... | collective-permute-start | bytes 387080 | tf_op jit(solution)/shard_map/ppermute | solution.py:583
  91.8 13.1 %collective-permute-start.25 = (f32[264,512]{1,0:T(8,128)S(1)}, f32[264,512]{1,0:T(8,128)S(1)}, u32[]{:S(2)}, u32[]{:S(2)}) collective-permute-start(f32[264,512]{1,0:T(8,128)S(1)} %get-tuple-element.95.dout_ref.d0_ref.t0_ref), channel_id=1, source_target_pairs={{4,8},{8,4},{12,16},{16,12},{20,24},{24,20},{28,32},{32,28},{36,40... | collective-permute-start | bytes 1622024 | tf_op jit(solution)/shard_map/ppermute | solution.py:587
  93.7 14.2 %collective-permute-start.27 = (f32[56,1152]{1,0:T(8,128)S(1)}, f32[56,1152]{1,0:T(8,128)S(1)}, u32[]{:S(2)}, u32[]{:S(2)}) collective-permute-start(f32[56,1152]{1,0:T(8,128)S(1)} %shard_map.103.double_ref), channel_id=1, source_target_pairs={{0,48},{4,52},{8,56},{12,60},{16,32},{20,36},{24,40},{28,44},{32,1... | collective-permute-start | bytes 774152 | tf_op jit(solution)/shard_map/ppermute | solution.py:583
  95.6 9.3 %collective-permute-start.26 = (f32[64,1152]{1,0:T(8,128)S(1)}, f32[64,1152]{1,0:T(8,128)S(1)}, u32[]{:S(2)}, u32[]{:S(2)}) collective-permute-start(f32[64,1152]{1,0:T(8,128)S(1)} %collective-permute-done.22.a0), channel_id=1, source_target_pairs={{0,4},{4,0},{8,12},{12,8},{16,20},{20,16},{24,28},{28,24},{32,36},... | collective-permute-start | bytes 884744 | tf_op jit(solution)/shard_map/ppermute | solution.py:583
  107.9 16.2 %collective-permute-start.29 = (f32[96,1152]{1,0:T(8,128)S(1)}, f32[96,1152]{1,0:T(8,128)S(1)}, u32[]{:S(2)}, u32[]{:S(2)}) collective-permute-start(f32[96,1152]{1,0:T(8,128)S(1)} %shard_map.106.a2), channel_id=1, source_target_pairs={{0,8},{4,12},{8,0},{12,4},{16,24},{20,28},{24,16},{28,20},{32,40},... | collective-permute-start | bytes 1327112 | tf_op jit(solution)/shard_map/ppermute | solution.py:583
  116.8 7.3 %collective-permute-start.28 = (f32[96,1152]{1,0:T(8,128)S(1)}, f32[96,1152]{1,0:T(8,128)S(1)}, u32[]{:S(2)}, u32[]{:S(2)}) collective-permute-start(f32[96,1152]{1,0:T(8,128)S(1)} %shard_map.106.a2), channel_id=1, source_target_pairs={{0,4},{4,0},{8,12},{12,8},{16,20},{20,16},{24,28},{28,24},{32,36},... | collective-permute-start | bytes 1327112 | tf_op jit(solution)/shard_map/ppermute | solution.py:583
  124.1 1.8 %collective-permute-start.30 = (f32[96,1152]{1,0:T(8,128)S(1)}, f32[96,1152]{1,0:T(8,128)S(1)}, u32[]{:S(2)}, u32[]{:S(2)}) collective-permute-start(f32[96,1152]{1,0:T(8,128)S(1)} %collective-permute-done.29.a1), channel_id=1, source_target_pairs={{0,4},{4,0},{8,12},{12,8},{16,20},{20,16},{24,28},{28,24},{32,36},... | collective-permute-start | bytes 1327112 | tf_op jit(solution)/shard_map/ppermute | solution.py:583

commit v7 on v6

--- a/solution.py
+++ b/solution.py
@@ -611,8 +611,8 @@
     other = exchange(double, 12)
     w0, *inner = near_inner(query, (key, after(in_k, double)), (value, in_v))
     w1, *outer = near_outer(edge, query, after(out_k, double), out_v)
-    l1b = exchange(after(l1a, double), 1)
-    l2a = merged(after(double, w0, w1, l1b), other)
+    l2a = merged(after(double, w0, w1), other)
+    l1b = exchange(after(l1a, l2a), 1)
     l2b = exchange(l2a, 2)
     core1 = exchange(l2a, 1)
     core2 = exchange(after(l2b, core1), 1)

time: 131 us -> 130 us (level)
    ppermute x24, waiting for transfers between devices: 35.1 us -> 33.8 us  [exchange(): return lax.ppermute(array, 'seq', [(i, i ^ mask) for i in range(count)])]
  transfers between devices with their start and end apart: 31 -> 31, of which waited for: 16 -> 16; matrix products, arithmetic and copies ran while one was open for 0% -> 0% of each run, Pallas kernels for 26% -> 27%
where the time goes in v7:
time: 130 us; the launch traced here: 129 us
  starting transfers between devices  47.2 us (36%)
  waiting for transfers between devices  39.7 us (31%)
  Pallas kernels  39.3 us (30%)
  local copies, waits for them, and re-layouts  1.57 us (1%)
    ppermute x24, starting transfers between devices, exchange(): return lax.ppermute(array, 'seq', [(i, i ^ mask) for i in range(count)])  34.3 us
    ppermute x24, waiting for transfers between devices, exchange(): return lax.ppermute(array, 'seq', [(i, i ^ mask) for i in range(count)])  33.8 us
    pallas_call x5, Pallas kernels, head_call(): pl.pallas_call(kernel, grid=(HEADS,), out_shape=outs, in_specs=in_specs,...  22.1 us
    pallas_call x11, Pallas kernels, whole_call(): pl.pallas_call(kernel, out_shape=outs, in_specs=[spec] * len(operands), o...  14 us
    ppermute x4, starting transfers between devices, exchange_outer(): return lax.ppermute(array, 'seq', pairs)  9.38 us
    ppermute x3, starting transfers between devices, body(): lax.ppermute(stats, 'head', [(i, i ^ mask) for i in range(head_count)])  3.5 us
    pallas_call x1, Pallas kernels, pool(): pl.pallas_call(pool_kernel, out_shape=[f32(OWN, 3 * WIDTH), f32(64, KV),...  3.27 us
    ppermute x3, waiting for transfers between devices, body(): lax.ppermute(stats, 'head', [(i, i ^ mask) for i in range(head_count)])  3.22 us
  transfers between devices with their start and end apart: 31, of which 16 were waited for; matrix products, arithmetic and copies ran while one was open for 0% of the time, Pallas kernels for 27%

profile of v7, /device:TPU:1, one launch (start us, length us, event | category | flops | bytes accessed | tf_op | source)
XLA Modules:
  0.0 128.7 jit_solution(6261250949191730924)
XLA Ops:
  0.6 3.3 %collective-permute-start.2 = (f32[256,512]{1,0:T(8,128)}, f32[256,512]{1,0:T(8,128)S(1)}, u32[]{:S(2)}, u32[]{:S(2)}) collective-permute-start(f32[256,512]{1,0:T(8,128)} %k_ref.5), channel_id=1, source_target_pairs={{0,4},{4,0},{8,12},{12,8},{16,20},{20,16},{24,28},{28,24},{32,36},... | collective-permute-start | bytes 1572872 | tf_op jit(solution)/shard_map/ppermute | solution.py:583
  4.0 0.1 collective-permute-start.3
  4.1 2.1 %collective-permute-start.1 = (f32[256,512]{1,0:T(8,128)}, f32[256,512]{1,0:T(8,128)S(1)}, u32[]{:S(2)}, u32[]{:S(2)}) collective-permute-start(f32[256,512]{1,0:T(8,128)} %k_ref.5), channel_id=1, source_target_pairs={{4,8},{8,4},{12,16},{16,12},{20,24},{24,20},{28,32},{32,28},{36,40... | collective-permute-start | bytes 1572872 | tf_op jit(solution)/shard_map/ppermute | solution.py:587
  6.2 3.5 %collective-permute-start.8 = (f32[256,512]{1,0:T(8,128)}, f32[256,512]{1,0:T(8,128)S(1)}, u32[]{:S(2)}, u32[]{:S(2)}) collective-permute-start(f32[256,512]{1,0:T(8,128)} %v_ref.5), channel_id=1, source_target_pairs={{4,8},{8,4},{12,16},{16,12},{20,24},{24,20},{28,32},{32,28},{36,40... | collective-permute-start | bytes 1572872 | tf_op jit(solution)/shard_map/ppermute | solution.py:587
  9.6 3.3 %shard_map.93 = (f32[96,1536]{1,0:T(8,128)}, f32[64,1024]{1,0:T(8,128)}, f32[16,1024]{1,0:T(8,128)}, f32[4,1024]{1,0:T(4,128)}, f32[96,512]{1,0:T(8,128)}, /*index=5*/f32[8,256]{1,0:T(8,128)}) custom-call(s32[8,512]{1,0:T(8,128)} %constant.2.clone.table_ref, f32[256,512]{1,0:T(8,128)} %k_ref.5, f32[256,512]{1,0:T(8,128)} %v_ref.5, f32[256,512]{1,0:T(8,128)} %q0_ref.1), custom_call_target="tpu_custom_call" | custom-call | flops 1000000 | bytes 2000000 | tf_op jit(solution)/shard_map/pallas_call | solution.py:510
  12.9 0.0 copy-start.3
  12.9 0.0 copy-start.4
  12.9 0.2 collective-permute-start
  13.1 1.6 %collective-permute-done.1.k_ref.k2_ref = f32[256,512]{1,0:T(8,128)S(1)} collective-permute-done((f32[256,512]{1,0:T(8,128)}, f32[256,512]{1,0:T(8,128)S(1)}, u32[]{:S(2)}, u32[]{:S(2)}) %collective-permute-start.1) | collective-permute-done | bytes 524320 | tf_op jit(solution)/shard_map/ppermute | solution.py:587
  14.8 0.1 collective-permute-start.4
  14.8 1.9 %collective-permute-start.6 = (f32[4,1024]{1,0:T(4,128)}, f32[4,1024]{1,0:T(4,128)S(1)}, u32[]{:S(2)}, u32[]{:S(2)}) collective-permute-start(f32[4,1024]{1,0:T(4,128)} %get-tuple-element.63), channel_id=1, source_target_pairs={{0,192},{4,196},{8,200},{12,204},{16,208},{20,212},{24,216},{28,22... | collective-permute-start | bytes 49160 | tf_op jit(solution)/shard_map/ppermute | solution.py:583
  16.7 1.3 %collective-permute-start.5 = (f32[4,1024]{1,0:T(4,128)}, f32[4,1024]{1,0:T(4,128)S(1)}, u32[]{:S(2)}, u32[]{:S(2)}) collective-permute-start(f32[4,1024]{1,0:T(4,128)} %get-tuple-element.63), channel_id=1, source_target_pairs={{0,128},{4,132},{8,136},{12,140},{16,144},{20,148},{24,152},{28,15... | collective-permute-start | bytes 49160 | tf_op jit(solution)/shard_map/ppermute | solution.py:583
  18.0 0.8 collective-permute-done.6.c_ref
  18.8 6.5 %collective-permute-done.5.b_ref = f32[4,1024]{1,0:T(4,128)S(1)} collective-permute-done((f32[4,1024]{1,0:T(4,128)}, f32[4,1024]{1,0:T(4,128)S(1)}, u32[]{:S(2)}, u32[]{:S(2)}) %collective-permute-start.5) | collective-permute-done | bytes 16416 | tf_op jit(solution)/shard_map/ppermute | solution.py:583
  25.4 0.8 copy-done.6
  26.2 0.1 collective-permute-start.7
  26.3 0.0 collective-permute-done.a0
  26.3 7.2 %collective-permute-done.7.other_ref = f32[28,1024]{1,0:T(8,128)S(1)} collective-permute-done((f32[28,1024]{1,0:T(8,128)S(1)}, f32[28,1024]{1,0:T(8,128)S(1)}, u32[]{:S(2)}, u32[]{:S(2)}) %collective-permute-start.7) | collective-permute-done | bytes 114720 | tf_op jit(solution)/shard_map/ppermute | solution.py:583
  33.5 0.1 collective-permute-start.9
  33.7 0.7 copy-done.8
  34.4 3.6 %shard_map.97 = (f32[4,256,256]{2,1,0:T(8,128)S(1)}, f32[256,512]{1,0:T(8,128)S(1)}, f32[256,512]{1,0:T(8,128)S(1)}, f32[256,512]{1,0:T(8,128)S(1)}) custom-call(f32[8,256]{1,0:T(8,128)S(1)} %copy-done.8, f32[256,512]{1,0:T(8,128)S(1)} %copy-done.5, f32[256,512]{1,0:T(8,128)S(1)} %collective-permute-done.1.k_ref.k2_ref, ...), custom_call_target="tpu_custom_call" | custom-call | flops 805306368 | bytes 4000000 | tf_op jit(solution)/shard_map/pallas_call | solution.py:455
  38.0 0.0 copy-start.1
  38.1 0.0 copy-start.2
  38.1 0.0 copy-start.7
  38.1 4.1 %shard_map.96 = (f32[4,256,512]{2,1,0:T(8,128)S(1)}, f32[256,512]{1,0:T(8,128)S(1)}, f32[256,512]{1,0:T(8,128)S(1)}, f32[256,512]{1,0:T(8,128)S(1)}) custom-call(f32[256,512]{1,0:T(8,128)S(1)} %copy-done.5, f32[256,512]{1,0:T(8,128)S(1)} %copy-done.3, f32[256,512]{1,0:T(8,128)S(1)} %collective-permute-done.2.ki_ref.k1_ref, f32[256,512]{1,0:T(8,128)S(1)} %copy-done.4, ...), custom_call_target="tpu_custom_call" | custom-call | flops 1610612736 | bytes 4000000 | tf_op jit(solution)/shard_map/pallas_call | solution.py:455
  42.2 7.3 %collective-permute-start.12 = (f32[96,1024]{1,0:T(8,128)S(1)}, f32[96,1024]{1,0:T(8,128)S(1)}, u32[]{:S(2)}, u32[]{:S(2)}) collective-permute-start(f32[96,1024]{1,0:T(8,128)S(1)} %shard_map.98.a2), channel_id=1, source_target_pairs={{0,8},{4,12},{8,0},{12,4},{16,24},{20,28},{24,16},{28,20},{32,40},... | collective-permute-start | bytes 1179656 | tf_op jit(solution)/shard_map/ppermute | solution.py:583
  49.5 0.7 collective-permute-start.11
  50.3 1.9 %collective-permute-start.18 = (f32[256,512]{1,0:T(8,128)S(1)}, f32[256,512]{1,0:T(8,128)S(1)}, u32[]{:S(2)}, u32[]{:S(2)}) collective-permute-start(f32[256,512]{1,0:T(8,128)S(1)} %copy-done.5), channel_id=1, source_target_pairs={{4,8},{8,4},{12,16},{16,12},{20,24},{24,20},{28,32},{32,28},{36,40... | collective-permute-start | bytes 1572872 | tf_op jit(solution)/shard_map/ppermute | solution.py:587
  52.2 0.1 collective-permute-start.17
  52.3 6.3 %collective-permute-done.12.a4 = f32[96,1024]{1,0:T(8,128)S(1)} collective-permute-done((f32[96,1024]{1,0:T(8,128)S(1)}, f32[96,1024]{1,0:T(8,128)S(1)}, u32[]{:S(2)}, u32[]{:S(2)}) %collective-permute-start.12) | collective-permute-done | bytes 393248 | tf_op jit(solution)/shard_map/ppermute | solution.py:583
  58.6 1.1 collective-permute-start.13
  59.8 0.0 collective-permute-start.10
  59.8 1.7 %collective-permute-done.10.a1 = f32[64,1024]{1,0:T(8,128)S(1)} collective-permute-done((f32[64,1024]{1,0:T(8,128)S(1)}, f32[64,1024]{1,0:T(8,128)S(1)}, u32[]{:S(2)}, u32[]{:S(2)}) %collective-permute-start.10) | collective-permute-done | bytes 262176 | tf_op jit(solution)/shard_map/ppermute | solution.py:583
  61.5 2.8 %shard_map.99 = (f32[256,512]{1,0:T(8,128)S(1)}, f32[256,512]{1,0:T(8,128)S(1)}, f32[8,256]{1,0:T(8,128)S(1)}) custom-call(f32[96,512]{1,0:T(8,128)S(1)} %copy-done.1, f32[96,1536]{1,0:T(8,128)S(1)} %copy-done, f32[64,1024]{1,0:T(8,128)S(1)} %collective-permute-done.a0, f32[64,1024]{1,0:T(8,128)S(1)} %collective-permute-done.10.a1, ...), custom_call_target="tpu_custom_call" | custom-call | flops 402653184 | bytes 8000000 | tf_op jit(solution)/shard_map/pallas_call | solution.py:432
  64.3 2.7 %collective-permute-start.16 = (f32[8,256]{1,0:T(8,128)S(1)}, f32[8,256]{1,0:T(8,128)S(1)}, u32[]{:S(2)}, u32[]{:S(2)}) collective-permute-start(f32[8,256]{1,0:T(8,128)S(1)} %get-tuple-element.79.s0_ref), channel_id=1, source_target_pairs={{0,3},{1,2},{2,1},{3,0},{4,7},{5,6},{6,5},{7,4},{8,11},{9,10},{10,... | collective-permute-start | bytes 24584 | tf_op jit(solution)/shard_map/ppermute | solution.py:625
  67.0 0.5 collective-permute-start.15
  67.5 0.3 collective-permute-start.14
  67.8 0.5 collective-permute-done.16.s3_ref
  68.3 2.8 %collective-permute-done.15.s2_ref = f32[8,256]{1,0:T(8,128)S(1)} collective-permute-done((f32[8,256]{1,0:T(8,128)S(1)}, f32[8,256]{1,0:T(8,128)S(1)}, u32[]{:S(2)}, u32[]{:S(2)}) %collective-permute-start.15) | collective-permute-done | bytes 8224 | tf_op jit(solution)/shard_map/ppermute | solution.py:625
  71.0 1.4 %shard_map.100 = (f32[256,512]{1,0:T(8,128)}, f32[264,512]{1,0:T(8,128)S(1)}, f32[256,512]{1,0:T(8,128)S(1)}, f32[64,1152]{1,0:T(8,128)S(1)}, f32[16,1152]{1,0:T(8,128)S(1)}, /*index=5*/f32[4,1152]{1,0:T(4,128)S(1)}) custom-call(f32[8,256]{1,0:T(8,128)S(1)} %get-tuple-element.79.s0_ref, f32[8,256]{1,0:T(8,128)S(1)} %collective-permute-done.14.s1_ref, ...), custom_call_target="tpu_custom_call" | custom-call | flops 1000000 | bytes 4000000 | tf_op jit(solution)/shard_map/pallas_call | solution.py:432
  72.4 1.8 %collective-permute-start.24 = (f32[264,512]{1,0:T(8,128)S(1)}, f32[264,512]{1,0:T(8,128)S(1)}, u32[]{:S(2)}, u32[]{:S(2)}) collective-permute-start(f32[264,512]{1,0:T(8,128)S(1)} %get-tuple-element.95.dout_ref.d0_ref.t0_ref), channel_id=1, source_target_pairs={{0,4},{4,0},{8,12},{12,8},{16,20},{20,16},{24,28},{28,24},{32,36},... | collective-permute-start | bytes 1622024 | tf_op jit(solution)/shard_map/ppermute | solution.py:583
  74.2 2.2 %collective-permute-start.22 = (f32[64,1152]{1,0:T(8,128)S(1)}, f32[64,1152]{1,0:T(8,128)S(1)}, u32[]{:S(2)}, u32[]{:S(2)}) collective-permute-start(f32[64,1152]{1,0:T(8,128)S(1)} %get-tuple-element.92.first_ref), channel_id=1, source_target_pairs={{0,8},{4,12},{8,0},{12,4},{16,24},{20,28},{24,16},{28,20},{32,40},... | collective-permute-start | bytes 884744 | tf_op jit(solution)/shard_map/ppermute | solution.py:583
  76.4 0.4 collective-permute-start.21
  76.8 0.9 collective-permute-start.20
  77.6 2.0 %collective-permute-start.19 = (f32[4,1152]{1,0:T(4,128)S(1)}, f32[4,1152]{1,0:T(4,128)S(1)}, u32[]{:S(2)}, u32[]{:S(2)}) collective-permute-start(f32[4,1152]{1,0:T(4,128)S(1)} %get-tuple-element.87.third_ref), channel_id=1, source_target_pairs={{0,64},{4,68},{8,72},{12,76},{16,80},{20,84},{24,88},{28,92},{32,9... | collective-permute-start | bytes 55304 | tf_op jit(solution)/shard_map/ppermute | solution.py:583
  79.6 0.6 collective-permute-done.21.c_ref
  80.2 0.7 collective-permute-done.20.b_ref
  80.9 0.4 collective-permute-done.19.a_ref
  81.3 0.1 collective-permute-start.23
  81.4 5.1 %shard_map.102.near_ref = f32[256,512]{1,0:T(8,128)S(1)} custom-call(f32[4,256,512]{2,1,0:T(8,128)S(1)} %get-tuple-element.66.w0_ref, f32[4,256,256]{2,1,0:T(8,128)S(1)} %get-tuple-element.69.w1_ref, f32[256,512]{1,0:T(8,128)S(1)} %get-tuple-element.73.peak0_ref, f32[256,512]{1,0:T(8,128)S(1)} %get-tuple-element.76.peak1_ref, ...), custom_call_target="tpu_custom_call" | custom-call | flops 2415919104 | bytes 4000000 | tf_op jit(solution)/shard_map/pallas_call | solution.py:455
  86.5 4.4 %collective-permute-done.23.other_ref = f32[28,1152]{1,0:T(8,128)S(1)} collective-permute-done((f32[28,1152]{1,0:T(8,128)S(1)}, f32[28,1152]{1,0:T(8,128)S(1)}, u32[]{:S(2)}, u32[]{:S(2)}) %collective-permute-start.23) | collective-permute-done | bytes 129056 | tf_op jit(solution)/shard_map/ppermute | solution.py:583
  91.0 1.9 %collective-permute-start.25 = (f32[264,512]{1,0:T(8,128)S(1)}, f32[264,512]{1,0:T(8,128)S(1)}, u32[]{:S(2)}, u32[]{:S(2)}) collective-permute-start(f32[264,512]{1,0:T(8,128)S(1)} %get-tuple-element.95.dout_ref.d0_ref.t0_ref), channel_id=1, source_target_pairs={{4,8},{8,4},{12,16},{16,12},{20,24},{24,20},{28,32},{32,28},{36,40... | collective-permute-start | bytes 1622024 | tf_op jit(solution)/shard_map/ppermute | solution.py:587
  92.9 0.8 collective-permute-start.27
  93.7 3.7 %shard_map.104 = f32[256,512]{1,0:T(8,128)} custom-call(f32[96,512]{1,0:T(8,128)S(1)} %copy-done.1, f32[96,1536]{1,0:T(8,128)S(1)} %copy-done, f32[64,1024]{1,0:T(8,128)S(1)} %collective-permute-done.a0, f32[64,1024]{1,0:T(8,128)S(1)} %collective-permute-done.10.a1, f32[96,1024]{1,0:T(8,128)S(1)} %shard_map.98.a2, ...), custom_call_target="tpu_custom_call" | custom-call | flops 402653184 | bytes 6000000 | tf_op jit(solution)/shard_map/pallas_call | solution.py:432
  97.5 5.6 %shard_map.105 = (f32[256,512]{1,0:T(8,128)S(1)}, f32[256,512]{1,0:T(8,128)S(1)}) custom-call(f32[256,512]{1,0:T(8,128)S(1)} %copy-done.3, f32[256,512]{1,0:T(8,128)S(1)} %copy-done.4, f32[256,512]{1,0:T(8,128)S(1)} %copy-done.5, f32[256,512]{1,0:T(8,128)S(1)} %collective-permute-done.17.q1_ref, f32[264,512]{1,0:T(8,128)S(1)} %get-tuple-element.95.dout_ref.d0_ref.t0_ref, ...), custom_call_target="tpu_custom_call" | custom-call | flops 3221225472 | bytes 4000000 | tf_op jit(solution)/shard_map/pallas_call | solution.py:455
  103.0 1.0 collective-permute-done.25.d_ref.t_ref
  104.1 1.9 %collective-permute-done.27.other_ref = f32[56,1152]{1,0:T(8,128)S(1)} collective-permute-done((f32[56,1152]{1,0:T(8,128)S(1)}, f32[56,1152]{1,0:T(8,128)S(1)}, u32[]{:S(2)}, u32[]{:S(2)}) %collective-permute-start.27) | collective-permute-done | bytes 258080 | tf_op jit(solution)/shard_map/ppermute | solution.py:583
  106.0 9.8 %collective-permute-start.29 = (f32[96,1152]{1,0:T(8,128)S(1)}, f32[96,1152]{1,0:T(8,128)S(1)}, u32[]{:S(2)}, u32[]{:S(2)}) collective-permute-start(f32[96,1152]{1,0:T(8,128)S(1)} %shard_map.106.a2), channel_id=1, source_target_pairs={{0,8},{4,12},{8,0},{12,4},{16,24},{20,28},{24,16},{28,20},{32,40},... | collective-permute-start | bytes 1327112 | tf_op jit(solution)/shard_map/ppermute | solution.py:583
  115.8 0.0 collective-permute-start.28
  115.8 3.7 %shard_map.107 = (f32[256,512]{1,0:T(8,128)S(1)}, f32[256,512]{1,0:T(8,128)S(1)}) custom-call(f32[256,512]{1,0:T(8,128)S(1)} %copy-done.3, f32[256,512]{1,0:T(8,128)S(1)} %copy-done.4, f32[256,512]{1,0:T(8,128)S(1)} %collective-permute-done.18.q_ref, f32[264,512]{1,0:T(8,128)S(1)} %collective-permute-done.25.d_ref.t_ref, ...), custom_call_target="tpu_custom_call" | custom-call | flops 1610612736 | bytes 4000000 | tf_op jit(solution)/shard_map/pallas_call | solution.py:455
  119.6 2.2 %shard_map.108 = (f32[96,512]{1,0:T(8,128)S(1)}, f32[96,512]{1,0:T(8,128)S(1)}) custom-call(f32[96,512]{1,0:T(8,128)S(1)} %copy-done.1, f32[96,1536]{1,0:T(8,128)S(1)} %copy-done, f32[64,1152]{1,0:T(8,128)S(1)} %collective-permute-done.22.a0, f32[64,1152]{1,0:T(8,128)S(1)} %collective-permute-done.26.a1, f32[96,1152]{1,0:T(8,128)S(1)} %shard_map.106.a2), custom_call_target="tpu_custom_call" | custom-call | flops 402653184 | bytes 3000000 | tf_op jit(solution)/shard_map/pallas_call | solution.py:432
  121.8 1.4 %collective-permute-done.29.a1 = f32[96,1152]{1,0:T(8,128)S(1)} collective-permute-done((f32[96,1152]{1,0:T(8,128)S(1)}, f32[96,1152]{1,0:T(8,128)S(1)}, u32[]{:S(2)}, u32[]{:S(2)}) %collective-permute-start.29) | collective-permute-done | bytes 442400 | tf_op jit(solution)/shard_map/ppermute | solution.py:583
  123.2 1.8 %collective-permute-done.30.a2 = f32[96,1152]{1,0:T(8,128)S(1)} collective-permute-done((f32[96,1152]{1,0:T(8,128)S(1)}, f32[96,1152]{1,0:T(8,128)S(1)}, u32[]{:S(2)}, u32[]{:S(2)}) %collective-permute-start.30) | collective-permute-done | bytes 442400 | tf_op jit(solution)/shard_map/ppermute | solution.py:583
  125.0 3.7 %shard_map.109 = (f32[256,512]{1,0:T(8,128)}, f32[256,512]{1,0:T(8,128)}) custom-call(f32[96,512]{1,0:T(8,128)S(1)} %copy-done.1, f32[96,1536]{1,0:T(8,128)S(1)} %copy-done, f32[96,1152]{1,0:T(8,128)S(1)} %collective-permute-done.28.a0, f32[96,1152]{1,0:T(8,128)S(1)} %collective-permute-done.29.a1, f32[96,1152]{1,0:T(8,128)S(1)} %collective-permute-done.30.a2, ...), custom_call_target="tpu_custom_call" | custom-call | flops 402653184 | bytes 3000000 | tf_op jit(solution)/shard_map/pallas_call | solution.py:432
  (33 shorter events, 0.2 us)
Async XLA Ops:
  0.6 33.0 %copy-start.5 = (f32[256,512]{1,0:T(8,128)S(1)}, f32[256,512]{1,0:T(8,128)}, u32[]{:S(2)}) copy-start(f32[256,512]{1,0:T(8,128)} %q0_ref.1) | copy-start | bytes 1572868
  0.6 12.5 %collective-permute-start.2 = (f32[256,512]{1,0:T(8,128)}, f32[256,512]{1,0:T(8,128)S(1)}, u32[]{:S(2)}, u32[]{:S(2)}) collective-permute-start(f32[256,512]{1,0:T(8,128)} %k_ref.5), channel_id=1, source_target_pairs={{0,4},{4,0},{8,12},{12,8},{16,20},{20,16},{24,28},{28,24},{32,36},... | collective-permute-start | bytes 1572872 | tf_op jit(solution)/shard_map/ppermute | solution.py:583
  4.0 9.2 %collective-permute-start.3 = (f32[256,512]{1,0:T(8,128)}, f32[256,512]{1,0:T(8,128)S(1)}, u32[]{:S(2)}, u32[]{:S(2)}) collective-permute-start(f32[256,512]{1,0:T(8,128)} %v_ref.5), channel_id=1, source_target_pairs={{0,4},{4,0},{8,12},{12,8},{16,20},{20,16},{24,28},{28,24},{32,36},... | collective-permute-start | bytes 1572872 | tf_op jit(solution)/shard_map/ppermute | solution.py:583
  4.1 10.7 %collective-permute-start.1 = (f32[256,512]{1,0:T(8,128)}, f32[256,512]{1,0:T(8,128)S(1)}, u32[]{:S(2)}, u32[]{:S(2)}) collective-permute-start(f32[256,512]{1,0:T(8,128)} %k_ref.5), channel_id=1, source_target_pairs={{4,8},{8,4},{12,16},{16,12},{20,24},{24,20},{28,32},{32,28},{36,40... | collective-permute-start | bytes 1572872 | tf_op jit(solution)/shard_map/ppermute | solution.py:587
  6.2 27.5 %collective-permute-start.8 = (f32[256,512]{1,0:T(8,128)}, f32[256,512]{1,0:T(8,128)S(1)}, u32[]{:S(2)}, u32[]{:S(2)}) collective-permute-start(f32[256,512]{1,0:T(8,128)} %v_ref.5), channel_id=1, source_target_pairs={{4,8},{8,4},{12,16},{16,12},{20,24},{24,20},{28,32},{32,28},{36,40... | collective-permute-start | bytes 1572872 | tf_op jit(solution)/shard_map/ppermute | solution.py:587
  12.9 25.1 %copy-start.3 = (f32[256,512]{1,0:T(8,128)S(1)}, f32[256,512]{1,0:T(8,128)}, u32[]{:S(2)}) copy-start(f32[256,512]{1,0:T(8,128)} %k_ref.5) | copy-start | bytes 1572868
  12.9 25.1 %copy-start.4 = (f32[256,512]{1,0:T(8,128)S(1)}, f32[256,512]{1,0:T(8,128)}, u32[]{:S(2)}) copy-start(f32[256,512]{1,0:T(8,128)} %v_ref.5) | copy-start | bytes 1572868
  12.9 13.4 %collective-permute-start = (f32[64,1024]{1,0:T(8,128)}, f32[64,1024]{1,0:T(8,128)S(1)}, u32[]{:S(2)}, u32[]{:S(2)}) collective-permute-start(f32[64,1024]{1,0:T(8,128)} %get-tuple-element.58), channel_id=1, source_target_pairs={{0,8},{4,12},{8,0},{12,4},{16,24},{20,28},{24,16},{28,20},{32,40},... | collective-permute-start | bytes 786440 | tf_op jit(solution)/shard_map/ppermute | solution.py:583
  14.8 3.3 %collective-permute-start.4 = (f32[4,1024]{1,0:T(4,128)}, f32[4,1024]{1,0:T(4,128)S(1)}, u32[]{:S(2)}, u32[]{:S(2)}) collective-permute-start(f32[4,1024]{1,0:T(4,128)} %get-tuple-element.63), channel_id=1, source_target_pairs={{0,64},{4,68},{8,72},{12,76},{16,80},{20,84},{24,88},{28,92},{32,9... | collective-permute-start | bytes 49160 | tf_op jit(solution)/shard_map/ppermute | solution.py:583
  14.8 4.0 %collective-permute-start.6 = (f32[4,1024]{1,0:T(4,128)}, f32[4,1024]{1,0:T(4,128)S(1)}, u32[]{:S(2)}, u32[]{:S(2)}) collective-permute-start(f32[4,1024]{1,0:T(4,128)} %get-tuple-element.63), channel_id=1, source_target_pairs={{0,192},{4,196},{8,200},{12,204},{16,208},{20,212},{24,216},{28,22... | collective-permute-start | bytes 49160 | tf_op jit(solution)/shard_map/ppermute | solution.py:583
  16.7 8.6 %collective-permute-start.5 = (f32[4,1024]{1,0:T(4,128)}, f32[4,1024]{1,0:T(4,128)S(1)}, u32[]{:S(2)}, u32[]{:S(2)}) collective-permute-start(f32[4,1024]{1,0:T(4,128)} %get-tuple-element.63), channel_id=1, source_target_pairs={{0,128},{4,132},{8,136},{12,140},{16,144},{20,148},{24,152},{28,15... | collective-permute-start | bytes 49160 | tf_op jit(solution)/shard_map/ppermute | solution.py:583
  25.4 0.8 copy-start.6
  26.2 7.3 %collective-permute-start.7 = (f32[28,1024]{1,0:T(8,128)S(1)}, f32[28,1024]{1,0:T(8,128)S(1)}, u32[]{:S(2)}, u32[]{:S(2)}) collective-permute-start(f32[28,1024]{1,0:T(8,128)S(1)} %shard_map.94.own_ref), channel_id=1, source_target_pairs={{0,16},{4,20},{8,24},{12,28},{16,0},{20,4},{24,8},{28,12},{32,48},... | collective-permute-start | bytes 344072 | tf_op jit(solution)/shard_map/ppermute | solution.py:583
  33.5 8.6 %collective-permute-start.9 = (f32[56,1024]{1,0:T(8,128)S(1)}, f32[56,1024]{1,0:T(8,128)S(1)}, u32[]{:S(2)}, u32[]{:S(2)}) collective-permute-start(f32[56,1024]{1,0:T(8,128)S(1)} %shard_map.95.double_ref), channel_id=1, source_target_pairs={{0,48},{4,52},{8,56},{12,60},{16,32},{20,36},{24,40},{28,44},{32,1... | collective-permute-start | bytes 688136 | tf_op jit(solution)/shard_map/ppermute | solution.py:583
  33.7 0.7 copy-start.8
  38.0 23.5 %copy-start = (f32[96,1536]{1,0:T(8,128)S(1)}, f32[96,1536]{1,0:T(8,128)}, u32[]{:S(2)}) copy-start(f32[96,1536]{1,0:T(8,128)} %get-tuple-element.57.own_ref) | copy-start | bytes 1769476
  38.0 23.4 %copy-start.1 = (f32[96,512]{1,0:T(8,128)S(1)}, f32[96,512]{1,0:T(8,128)}, u32[]{:S(2)}) copy-start(f32[96,512]{1,0:T(8,128)} %get-tuple-element.56.bias_ref) | copy-start | bytes 589828
  38.1 23.4 %copy-start.2 = (f32[256,512]{1,0:T(8,128)S(1)}, f32[256,512]{1,0:T(8,128)}, u32[]{:S(2)}) copy-start(f32[256,512]{1,0:T(8,128)} %up_ref.3) | copy-start | bytes 1572868
  38.1 23.4 %copy-start.7 = (f32[512]{0:T(512)S(1)}, f32[512]{0:T(512)}, u32[]{:S(2)}) copy-start(f32[512]{0:T(512)} %param.9) | copy-start | bytes 6148
  42.2 16.4 %collective-permute-start.12 = (f32[96,1024]{1,0:T(8,128)S(1)}, f32[96,1024]{1,0:T(8,128)S(1)}, u32[]{:S(2)}, u32[]{:S(2)}) collective-permute-start(f32[96,1024]{1,0:T(8,128)S(1)} %shard_map.98.a2), channel_id=1, source_target_pairs={{0,8},{4,12},{8,0},{12,4},{16,24},{20,28},{24,16},{28,20},{32,40},... | collective-permute-start | bytes 1179656 | tf_op jit(solution)/shard_map/ppermute | solution.py:583
  49.5 9.1 %collective-permute-start.11 = (f32[96,1024]{1,0:T(8,128)S(1)}, f32[96,1024]{1,0:T(8,128)S(1)}, u32[]{:S(2)}, u32[]{:S(2)}) collective-permute-start(f32[96,1024]{1,0:T(8,128)S(1)} %shard_map.98.a2), channel_id=1, source_target_pairs={{0,4},{4,0},{8,12},{12,8},{16,20},{20,16},{24,28},{28,24},{32,36},... | collective-permute-start | bytes 1179656 | tf_op jit(solution)/shard_map/ppermute | solution.py:583
  50.3 17.5 %collective-permute-start.18 = (f32[256,512]{1,0:T(8,128)S(1)}, f32[256,512]{1,0:T(8,128)S(1)}, u32[]{:S(2)}, u32[]{:S(2)}) collective-permute-start(f32[256,512]{1,0:T(8,128)S(1)} %copy-done.5), channel_id=1, source_target_pairs={{4,8},{8,4},{12,16},{16,12},{20,24},{24,20},{28,32},{32,28},{36,40... | collective-permute-start | bytes 1572872 | tf_op jit(solution)/shard_map/ppermute | solution.py:587
  52.2 15.6 %collective-permute-start.17 = (f32[256,512]{1,0:T(8,128)S(1)}, f32[256,512]{1,0:T(8,128)S(1)}, u32[]{:S(2)}, u32[]{:S(2)}) collective-permute-start(f32[256,512]{1,0:T(8,128)S(1)} %copy-done.5), channel_id=1, source_target_pairs={{0,4},{4,0},{8,12},{12,8},{16,20},{20,16},{24,28},{28,24},{32,36},... | collective-permute-start | bytes 1572872 | tf_op jit(solution)/shard_map/ppermute | solution.py:583
  58.6 2.9 %collective-permute-start.13 = (f32[96,1024]{1,0:T(8,128)S(1)}, f32[96,1024]{1,0:T(8,128)S(1)}, u32[]{:S(2)}, u32[]{:S(2)}) collective-permute-start(f32[96,1024]{1,0:T(8,128)S(1)} %collective-permute-done.12.a4), channel_id=1, source_target_pairs={{0,4},{4,0},{8,12},{12,8},{16,20},{20,16},{24,28},{28,24},{32,36},... | collective-permute-start | bytes 1179656 | tf_op jit(solution)/shard_map/ppermute | solution.py:583
  59.8 1.7 %collective-permute-start.10 = (f32[64,1024]{1,0:T(8,128)S(1)}, f32[64,1024]{1,0:T(8,128)S(1)}, u32[]{:S(2)}, u32[]{:S(2)}) collective-permute-start(f32[64,1024]{1,0:T(8,128)S(1)} %collective-permute-done.a0), channel_id=1, source_target_pairs={{0,4},{4,0},{8,12},{12,8},{16,20},{20,16},{24,28},{28,24},{32,36},... | collective-permute-start | bytes 786440 | tf_op jit(solution)/shard_map/ppermute | solution.py:583
  64.3 4.0 %collective-permute-start.16 = (f32[8,256]{1,0:T(8,128)S(1)}, f32[8,256]{1,0:T(8,128)S(1)}, u32[]{:S(2)}, u32[]{:S(2)}) collective-permute-start(f32[8,256]{1,0:T(8,128)S(1)} %get-tuple-element.79.s0_ref), channel_id=1, source_target_pairs={{0,3},{1,2},{2,1},{3,0},{4,7},{5,6},{6,5},{7,4},{8,11},{9,10},{10,... | collective-permute-start | bytes 24584 | tf_op jit(solution)/shard_map/ppermute | solution.py:625
  67.0 4.0 %collective-permute-start.15 = (f32[8,256]{1,0:T(8,128)S(1)}, f32[8,256]{1,0:T(8,128)S(1)}, u32[]{:S(2)}, u32[]{:S(2)}) collective-permute-start(f32[8,256]{1,0:T(8,128)S(1)} %get-tuple-element.79.s0_ref), channel_id=1, source_target_pairs={{0,2},{1,3},{2,0},{3,1},{4,6},{5,7},{6,4},{7,5},{8,10},{9,11},{10,... | collective-permute-start | bytes 24584 | tf_op jit(solution)/shard_map/ppermute | solution.py:625
  67.5 3.5 %collective-permute-start.14 = (f32[8,256]{1,0:T(8,128)S(1)}, f32[8,256]{1,0:T(8,128)S(1)}, u32[]{:S(2)}, u32[]{:S(2)}) collective-permute-start(f32[8,256]{1,0:T(8,128)S(1)} %get-tuple-element.79.s0_ref), channel_id=1, source_target_pairs={{0,1},{1,0},{2,3},{3,2},{4,5},{5,4},{6,7},{7,6},{8,9},{9,8},{10,11... | collective-permute-start | bytes 24584 | tf_op jit(solution)/shard_map/ppermute | solution.py:625
  72.4 25.1 %collective-permute-start.24 = (f32[264,512]{1,0:T(8,128)S(1)}, f32[264,512]{1,0:T(8,128)S(1)}, u32[]{:S(2)}, u32[]{:S(2)}) collective-permute-start(f32[264,512]{1,0:T(8,128)S(1)} %get-tuple-element.95.dout_ref.d0_ref.t0_ref), channel_id=1, source_target_pairs={{0,4},{4,0},{8,12},{12,8},{16,20},{20,16},{24,28},{28,24},{32,36},... | collective-permute-start | bytes 1622024 | tf_op jit(solution)/shard_map/ppermute | solution.py:583
  74.2 12.3 %collective-permute-start.22 = (f32[64,1152]{1,0:T(8,128)S(1)}, f32[64,1152]{1,0:T(8,128)S(1)}, u32[]{:S(2)}, u32[]{:S(2)}) collective-permute-start(f32[64,1152]{1,0:T(8,128)S(1)} %get-tuple-element.92.first_ref), channel_id=1, source_target_pairs={{0,8},{4,12},{8,0},{12,4},{16,24},{20,28},{24,16},{28,20},{32,40},... | collective-permute-start | bytes 884744 | tf_op jit(solution)/shard_map/ppermute | solution.py:583
  76.4 3.8 %collective-permute-start.21 = (f32[4,1152]{1,0:T(4,128)S(1)}, f32[4,1152]{1,0:T(4,128)S(1)}, u32[]{:S(2)}, u32[]{:S(2)}) collective-permute-start(f32[4,1152]{1,0:T(4,128)S(1)} %get-tuple-element.87.third_ref), channel_id=1, source_target_pairs={{0,192},{4,196},{8,200},{12,204},{16,208},{20,212},{24,216},{28,22... | collective-permute-start | bytes 55304 | tf_op jit(solution)/shard_map/ppermute | solution.py:583
  76.8 4.1 %collective-permute-start.20 = (f32[4,1152]{1,0:T(4,128)S(1)}, f32[4,1152]{1,0:T(4,128)S(1)}, u32[]{:S(2)}, u32[]{:S(2)}) collective-permute-start(f32[4,1152]{1,0:T(4,128)S(1)} %get-tuple-element.87.third_ref), channel_id=1, source_target_pairs={{0,128},{4,132},{8,136},{12,140},{16,144},{20,148},{24,152},{28,15... | collective-permute-start | bytes 55304 | tf_op jit(solution)/shard_map/ppermute | solution.py:583
  77.6 3.7 %collective-permute-start.19 = (f32[4,1152]{1,0:T(4,128)S(1)}, f32[4,1152]{1,0:T(4,128)S(1)}, u32[]{:S(2)}, u32[]{:S(2)}) collective-permute-start(f32[4,1152]{1,0:T(4,128)S(1)} %get-tuple-element.87.third_ref), channel_id=1, source_target_pairs={{0,64},{4,68},{8,72},{12,76},{16,80},{20,84},{24,88},{28,92},{32,9... | collective-permute-start | bytes 55304 | tf_op jit(solution)/shard_map/ppermute | solution.py:583
  81.3 9.6 %collective-permute-start.23 = (f32[28,1152]{1,0:T(8,128)S(1)}, f32[28,1152]{1,0:T(8,128)S(1)}, u32[]{:S(2)}, u32[]{:S(2)}) collective-permute-start(f32[28,1152]{1,0:T(8,128)S(1)} %shard_map.101.own_ref), channel_id=1, source_target_pairs={{0,16},{4,20},{8,24},{12,28},{16,0},{20,4},{24,8},{28,12},{32,48},... | collective-permute-start | bytes 387080 | tf_op jit(solution)/shard_map/ppermute | solution.py:583
  91.0 13.1 %collective-permute-start.25 = (f32[264,512]{1,0:T(8,128)S(1)}, f32[264,512]{1,0:T(8,128)S(1)}, u32[]{:S(2)}, u32[]{:S(2)}) collective-permute-start(f32[264,512]{1,0:T(8,128)S(1)} %get-tuple-element.95.dout_ref.d0_ref.t0_ref), channel_id=1, source_target_pairs={{4,8},{8,4},{12,16},{16,12},{20,24},{24,20},{28,32},{32,28},{36,40... | collective-permute-start | bytes 1622024 | tf_op jit(solution)/shard_map/ppermute | solution.py:587
  92.9 13.1 %collective-permute-start.27 = (f32[56,1152]{1,0:T(8,128)S(1)}, f32[56,1152]{1,0:T(8,128)S(1)}, u32[]{:S(2)}, u32[]{:S(2)}) collective-permute-start(f32[56,1152]{1,0:T(8,128)S(1)} %shard_map.103.double_ref), channel_id=1, source_target_pairs={{0,48},{4,52},{8,56},{12,60},{16,32},{20,36},{24,40},{28,44},{32,1... | collective-permute-start | bytes 774152 | tf_op jit(solution)/shard_map/ppermute | solution.py:583
  93.7 9.3 %collective-permute-start.26 = (f32[64,1152]{1,0:T(8,128)S(1)}, f32[64,1152]{1,0:T(8,128)S(1)}, u32[]{:S(2)}, u32[]{:S(2)}) collective-permute-start(f32[64,1152]{1,0:T(8,128)S(1)} %collective-permute-done.22.a0), channel_id=1, source_target_pairs={{0,4},{4,0},{8,12},{12,8},{16,20},{20,16},{24,28},{28,24},{32,36},... | collective-permute-start | bytes 884744 | tf_op jit(solution)/shard_map/ppermute | solution.py:583
  106.0 17.1 %collective-permute-start.29 = (f32[96,1152]{1,0:T(8,128)S(1)}, f32[96,1152]{1,0:T(8,128)S(1)}, u32[]{:S(2)}, u32[]{:S(2)}) collective-permute-start(f32[96,1152]{1,0:T(8,128)S(1)} %shard_map.106.a2), channel_id=1, source_target_pairs={{0,8},{4,12},{8,0},{12,4},{16,24},{20,28},{24,16},{28,20},{32,40},... | collective-permute-start | bytes 1327112 | tf_op jit(solution)/shard_map/ppermute | solution.py:583
  115.8 7.3 %collective-permute-start.28 = (f32[96,1152]{1,0:T(8,128)S(1)}, f32[96,1152]{1,0:T(8,128)S(1)}, u32[]{:S(2)}, u32[]{:S(2)}) collective-permute-start(f32[96,1152]{1,0:T(8,128)S(1)} %shard_map.106.a2), channel_id=1, source_target_pairs={{0,4},{4,0},{8,12},{12,8},{16,20},{20,16},{24,28},{28,24},{32,36},... | collective-permute-start | bytes 1327112 | tf_op jit(solution)/shard_map/ppermute | solution.py:583
  123.2 1.8 %collective-permute-start.30 = (f32[96,1152]{1,0:T(8,128)S(1)}, f32[96,1152]{1,0:T(8,128)S(1)}, u32[]{:S(2)}, u32[]{:S(2)}) collective-permute-start(f32[96,1152]{1,0:T(8,128)S(1)} %collective-permute-done.29.a1), channel_id=1, source_target_pairs={{0,4},{4,0},{8,12},{12,8},{16,20},{20,16},{24,28},{28,24},{32,36},... | collective-permute-start | bytes 1327112 | tf_op jit(solution)/shard_map/ppermute | solution.py:583
